TPU v7x, 512 devices: a whole 4x4x16 slice. The times are simulated.
512 devices in a mesh: dp: 32 (over x, z_lo, core), tensor: 16 (over y, z_hi).
Axes of the slice: x: 4, y: 4, z: 16 (z_hi: 4, z_lo: 4; z = z_hi * 4 + z_lo), core: 2. Of those that a mesh axis runs over, the one named last changes fastest.
Arguments:
- gate_logits: bfloat16 [16384, 14336], P('dp', 'tensor'), may hold values from -6 to 6
- up_projected: bfloat16 [16384, 14336], P('dp', 'tensor'), may hold values from -6 to 6
- output_gradient: bfloat16 [16384, 4096], P('dp', 'tensor'), may hold values from -6 to 6
- down_matrix: bfloat16 [14336, 4096], P('tensor', 'dp'), may hold values from -0.046875 to 0.046875
- adapter_input_factors: float32 [32, 16, 14336], P('dp', None, 'tensor'), may hold values from -0.046875 to 0.046875
- adapter_output_factors: float32 [32, 16, 4096], P('dp', None, 'tensor'), may hold values from -0.375 to 0.375
- input_moments: float32 [2, 32, 16, 14336], P(None, 'dp', None, 'tensor'), as said below
- output_moments: float32 [2, 32, 16, 4096], P(None, 'dp', None, 'tensor'), as said below
- batch_tenants: int32 [16384], P('dp'), may hold values from 0 to 15, as said below
- tenant_owner_slots: int32 [16], replicated, may hold values from 0 to 31, as said below
Outputs:
- grad_gate: bfloat16 [16384, 14336], P('dp', 'tensor')
- grad_up: bfloat16 [16384, 14336], P('dp', 'tensor')
- new_moments_a: float32 [2, 32, 16, 14336], P(None, 'dp', None, 'tensor')
- new_moments_b: float32 [2, 32, 16, 4096], P(None, 'dp', None, 'tensor')
- step_a: float32 [32, 16, 14336], P('dp', None, 'tensor')
- step_b: float32 [32, 16, 4096], P('dp', None, 'tensor')
Inputs may be any that keep to these rules, and one draw needn't show every extreme that they name: `tenant_owner_slots`: distinct slots; 16 slots own no tenant. `batch_tenants`: each micro-batch (the 512 tokens of one index of dp) is a run of one tenant followed by a run of a tenant that may differ, each run one token or more. `input_moments`: the second row (second moments) is positive. `output_moments`: the second row (second moments) is positive.
All inputs are finite; a program needn't handle non-finite values.
Results may differ from a plain program's by a relative error of at most 0.0041.
Values may be sent and summed in bfloat16 or wider, within the bound.
No kernel may reach another device: no remote copies, remote signals or barrier semaphores. Data moves between devices by JAX's collectives and lax.ppermute only.
A program may use at most 64 MiB of HBM per device.

v0:
```python
import jax
import jax.numpy as jnp
from jax import lax
from jax.sharding import PartitionSpec as P

ADAM_STEP = 10


ADAPTER_SCALE = 2.0
BETA_ONE = 0.9
BETA_TWO = 0.95
ADAM_EPS = 1e-08


def adam_update(sums, counts, moments):
    grad = sums / jnp.maximum(counts, 1.0)[:, None, None]
    active = (counts > 0.5)[:, None, None]
    first = jnp.where(active, BETA_ONE * moments[0] + (1.0 - BETA_ONE) * grad, moments[0])
    second = jnp.where(active, BETA_TWO * moments[1] + (1.0 - BETA_TWO) * grad * grad, moments[1])
    corr_one = 1.0 - BETA_ONE**ADAM_STEP
    corr_two = 1.0 - BETA_TWO**ADAM_STEP
    update = first / corr_one / (jnp.sqrt(second / corr_two) + ADAM_EPS)
    update = jnp.where(active, update, jnp.zeros_like(update))
    return (jnp.stack([first, second]), update)


def shards(
    gate_logits,
    up_projected,
    output_gradient,
    down_matrix,
    adapter_input_factors,
    adapter_output_factors,
    input_moments,
    output_moments,
    batch_tenants,
    tenant_owner_slots,
):
    tenants = tenant_owner_slots.shape[0]
    slot_count = lax.axis_size("dp")
    rank = adapter_input_factors.shape[1]
    tok_rows = gate_logits.shape[0]
    one_hot = (batch_tenants[:, None] == jnp.arange(tenants, dtype=jnp.int32)[None, :]).astype(
        jnp.int32
    )
    token_slots = jnp.sum(one_hot * tenant_owner_slots[None, :], axis=1)
    select = (token_slots[:, None] == jnp.arange(slot_count, dtype=jnp.int32)[None, :]).astype(
        jnp.float32
    )
    cot_full = lax.all_gather(output_gradient, "tensor", axis=1, tiled=True)
    factors_a, factors_b = (
        lax.all_gather(adapter_input_factors.astype(jnp.bfloat16), "dp", axis=0, tiled=True),
        lax.all_gather(adapter_output_factors.astype(jnp.bfloat16), "dp", axis=0, tiled=True),
    )
    flat_a = factors_a.reshape(slot_count * rank, factors_a.shape[2])
    flat_b = factors_b.reshape(slot_count * rank, factors_b.shape[2])
    gate_f = gate_logits.astype(jnp.float32)
    up_f = up_projected.astype(jnp.float32)
    sigmoid_gate = jax.nn.sigmoid(gate_f)
    activated = gate_f * sigmoid_gate
    hidden = (activated * up_f).astype(jnp.bfloat16)
    proj_all = jnp.dot(hidden, flat_a.T, preferred_element_type=jnp.float32).reshape(
        tok_rows, slot_count, rank
    )
    proj_part = jnp.sum(select[:, :, None] * proj_all, axis=1)
    grad_all = jnp.dot(output_gradient, flat_b.T, preferred_element_type=jnp.float32).reshape(
        tok_rows, slot_count, rank
    )
    grad_part = jnp.sum(select[:, :, None] * grad_all, axis=1)
    proj_sum, gradient_total = lax.psum((proj_part, grad_part), "tensor")
    rank_projection = proj_sum.astype(jnp.bfloat16)
    rank_gradient = (ADAPTER_SCALE * gradient_total).astype(jnp.bfloat16)
    spread_grad = (
        (select[:, :, None] * rank_gradient.astype(jnp.float32)[:, None, :])
        .astype(jnp.bfloat16)
        .reshape(tok_rows, slot_count * rank)
    )
    spread_proj = (
        (select[:, :, None] * rank_projection.astype(jnp.float32)[:, None, :])
        .astype(jnp.bfloat16)
        .reshape(tok_rows, slot_count * rank)
    )
    hidden_grad = lax.dot_general(
        cot_full,
        lax.all_gather(down_matrix, "dp", axis=1, tiled=True),
        (((1,), (1,)), ((), ())),
        preferred_element_type=jnp.float32,
    )
    hidden_grad = hidden_grad + jnp.dot(spread_grad, flat_a, preferred_element_type=jnp.float32)
    grad_gate = (hidden_grad * up_f * sigmoid_gate * (1.0 + gate_f * (1.0 - sigmoid_gate))).astype(
        jnp.bfloat16
    )
    grad_up = (hidden_grad * activated).astype(jnp.bfloat16)
    term_a = lax.dot_general(
        spread_grad, hidden, (((0,), (0,)), ((), ())), preferred_element_type=jnp.float32
    ).reshape(slot_count, rank, hidden.shape[1])
    term_b = ADAPTER_SCALE * lax.dot_general(
        spread_proj, output_gradient, (((0,), (0,)), ((), ())), preferred_element_type=jnp.float32
    ).reshape(slot_count, rank, output_gradient.shape[1])
    token_counts = jnp.sum(select, axis=0)
    sum_a, sum_b, counts = (
        lax.psum_scatter(term_a, "dp", scatter_dimension=0, tiled=True),
        lax.psum_scatter(term_b, "dp", scatter_dimension=0, tiled=True),
        lax.psum_scatter(token_counts, "dp", scatter_dimension=0, tiled=True),
    )
    new_moments_a, step_a = adam_update(sum_a, counts, input_moments)
    new_moments_b, step_b = adam_update(sum_b, counts, output_moments)
    return (grad_gate, grad_up, new_moments_a, new_moments_b, step_a, step_b)


def solution(mesh):
    placed = (
        P("dp", "tensor"),
        P("dp", "tensor"),
        P("dp", "tensor"),
        P("tensor", "dp"),
        P("dp", None, "tensor"),
        P("dp", None, "tensor"),
        P(None, "dp", None, "tensor"),
        P(None, "dp", None, "tensor"),
        P("dp"),
        P(),
    )
    return jax.shard_map(
        shards,
        mesh=mesh,
        in_specs=placed,
        out_specs=(
            P("dp", "tensor"),
            P("dp", "tensor"),
            P(None, "dp", None, "tensor"),
            P(None, "dp", None, "tensor"),
            P("dp", None, "tensor"),
            P("dp", None, "tensor"),
        ),
        check_vma=False,
    )
```

profile of v0, /device:TPU:24, one launch (start us, length us, event | category | flops | bytes accessed | tf_op | source)
XLA Modules:
  0.0 588.2 jit_solution(12871171379188541730)
XLA Ops:
  8.0 0.0 copy-start.3
  8.0 0.0 reduce-scatter.5.cloned.1.call-start
  8.1 0.0 copy-start.4
  8.1 0.9 convert_element_type.60
  9.0 48.6 %all_gather.15 = bf16[32,16,896]{2,1,0:T(8,128)(2,1)S(1)} all-gather(bf16[1,16,896]{2,1,0:T(8,128)(2,1)S(1)} %convert_element_type.60), channel_id=1, replica_groups=mesh['dp'=32,'tensor'=16] {'dp'}, dimensions={0}, use_global_device_ids=true | all-gather | bytes 946176 | tf_op jit(solution)/shard_map/all_gather | solution.py:52
  57.6 0.8 select_reduce_fusion
  58.4 0.7 convert_element_type.56
  59.1 38.9 %all_gather.14 = bf16[32,16,256]{2,1,0:T(8,128)(2,1)S(1)} all-gather(bf16[1,16,256]{2,1,0:T(8,128)(2,1)S(1)} %convert_element_type.56), channel_id=1, replica_groups=mesh['dp'=32,'tensor'=16] {'dp'}, dimensions={0}, use_global_device_ids=true | all-gather | bytes 270336 | tf_op jit(solution)/shard_map/all_gather | solution.py:53
  98.0 1.3 fusion.8
  99.3 0.0 copy-done.3
  99.3 0.0 copy-done.4
  99.3 0.0 copy-start
  99.3 1.0 fusion.9
  100.4 95.9 %all-reduce.1 = (f32[512,16]{0,1:T(8,128)S(1)}, bf16[512,16]{0,1:T(8,128)(2,1)S(1)}) all-reduce(f32[512,16]{0,1:T(8,128)S(1)} %fusion.8, f32[512,16]{0,1:T(8,128)S(1)} %fusion.9), channel_id=1, replica_groups=mesh['dp'=32,'tensor'=16] {'tensor'}, use_global_device_ids=true, to_apply=%region_2.0 | all-reduce | flops 16384 | bytes 114688 | tf_op jit(solution)/shard_map/psum | solution.py:70
  196.3 0.3 multiply_convert_fusion.1
  196.5 0.0 copy-done
  196.5 1.2 convolution_multiply_fusion.2
  197.8 0.0 reduce-scatter.5.cloned.1.call-update
  197.8 0.0 reduce-scatter.3.cloned.1.call-start
  197.8 3.6 fusion.14
  201.4 0.0 copy-start.2
  201.4 0.0 copy-start.1
  201.4 0.0 reduce-scatter.3.cloned.1.call-update
  201.4 0.0 all-gather.3.cloned.1.call-start
  201.5 0.5 all-gather.3.cloned.1.call-update
  202.0 0.0 all-gather.5.cloned.1.call-start
  202.1 0.5 all-gather.5.cloned.1.call-update
  202.6 1.3 dynamic-slice
  203.9 0.1 fusion.27
  204.0 77.7 %all-reduce = f32[32]{0:T(128)S(1)} all-reduce(f32[32]{0:T(128)S(1)} %fusion.27), channel_id=2, replica_groups=mesh['dp'=32,'tensor'=16] {'dp'}, use_global_device_ids=true, to_apply=%region_4.0.clone | all-reduce | flops 32 | bytes 256
  281.7 1.2 dynamic-slice.1
  284.3 121.4 %reduce-scatter.5.cloned.1.call-done = f32[1,16,256]{2,1,0:T(8,128)} async-done(((f32[32,16,256]{2,1,0:T(8,128)}), f32[1,16,256]{2,1,0:T(8,128)}) %reduce-scatter.5.cloned.1.call-update) | async-done | bytes 16400 | tf_op jit(solution)/shard_map/reduce_scatter | solution.py:103
  405.7 0.0 copy-done.2
  405.7 1.4 divide_select_fusion.1
  407.1 0.6 pad_maximum_fusion.1
  407.7 158.0 %reduce-scatter.3.cloned.1.call-done = f32[1,16,896]{2,1,0:T(8,128)} async-done(((f32[32,16,896]{2,1,0:T(8,128)}), f32[1,16,896]{2,1,0:T(8,128)}) %reduce-scatter.3.cloned.1.call-update) | async-done | bytes 57360 | tf_op jit(solution)/shard_map/reduce_scatter | solution.py:102
  565.7 0.0 copy-done.1
  565.7 1.5 divide_select_fusion
  567.2 0.7 pad_maximum_fusion
  567.9 0.0 copy-start.5
  567.9 0.0 all-gather.3.cloned.1.call-done
  567.9 0.0 all-gather.5.cloned.1.call-done
  567.9 10.2 %fusion.38 = f32[512,896]{1,0:T(8,128)S(1)} fusion(bf16[512,4096]{1,0:T(8,128)(2,1)} %all-gather.3.cloned.1.call-done, bf16[896,4096]{1,0:T(8,128)(2,1)} %all-gather.5.cloned.1.call-done), kind=kOutput, calls=%fused_computation.67 | convolution fusion | flops 3758096384 | bytes 13369344 | tf_op jit(solution)/shard_map/dot_general | solution.py:83
  578.1 0.0 copy-done.5
  578.1 2.7 multiply_convert_fusion
  (3 shorter events, 0.0 us)
Async XLA Ops:
  8.0 91.3 %copy-start.3 = (bf16[512,896]{1,0:T(8,128)(2,1)S(1)}, bf16[512,896]{1,0:T(8,128)(2,1)}, u32[]{:S(2)}) copy-start(bf16[512,896]{1,0:T(8,128)(2,1)} %param.10) | copy-start | bytes 2752516
  8.0 397.7 %reduce-scatter.5.cloned.1.call-start = ((), (), s32[]{:S(2)}) async-start(), calls=%async_computation.5 | async-start | bytes 540672 | tf_op jit(solution)/shard_map/reduce_scatter | solution.py:103
  8.1 91.3 %copy-start.4 = (bf16[512,896]{1,0:T(8,128)(2,1)S(1)}, bf16[512,896]{1,0:T(8,128)(2,1)}, u32[]{:S(2)}) copy-start(bf16[512,896]{1,0:T(8,128)(2,1)} %param.11) | copy-start | bytes 2752516
  99.3 97.2 %copy-start = (bf16[512,256]{1,0:T(8,128)(2,1)S(1)}, bf16[512,256]{1,0:T(8,128)(2,1)}, u32[]{:S(2)}) copy-start(bf16[512,256]{1,0:T(8,128)(2,1)} %param.12) | copy-start | bytes 786436
  197.8 367.9 %reduce-scatter.3.cloned.1.call-start = ((), (), s32[]{:S(2)}) async-start(), calls=%async_computation.4 | async-start | bytes 1892352 | tf_op jit(solution)/shard_map/reduce_scatter | solution.py:102
  201.4 204.3 %copy-start.2 = (f32[2,1,16,256]{3,2,1,0:T(8,128)S(1)}, f32[2,1,16,256]{3,2,1,0:T(8,128)}, u32[]{:S(2)}) copy-start(f32[2,1,16,256]{3,2,1,0:T(8,128)} %param.17) | copy-start | bytes 98308
  201.4 364.3 %copy-start.1 = (f32[2,1,16,896]{3,2,1,0:T(8,128)S(1)}, f32[2,1,16,896]{3,2,1,0:T(8,128)}, u32[]{:S(2)}) copy-start(f32[2,1,16,896]{3,2,1,0:T(8,128)} %param.16) | copy-start | bytes 344068
  201.4 366.4 %all-gather.3.cloned.1.call-start = ((), (), s32[]{:S(2)}) async-start(), calls=%async_computation.2 | async-start | bytes 4456448 | tf_op jit(solution)/shard_map/all_gather | solution.py:50
  202.0 365.8 %all-gather.5.cloned.1.call-start = ((), (), s32[]{:S(2)}) async-start(), calls=%async_computation.3 | async-start | bytes 7569408 | tf_op jit(solution)/shard_map/all_gather | solution.py:85
  567.9 10.2 %copy-start.5 = (bf16[512,896]{1,0:T(8,128)(2,1)S(1)}, bf16[512,896]{1,0:T(8,128)(2,1)}, u32[]{:S(2)}) copy-start(bf16[512,896]{1,0:T(8,128)(2,1)} %param.11) | copy-start | bytes 2752516
Sparse Core Ops, SparseCore 0:
  197.9 207.7 reduce-scatter.4
  408.7 156.9 reduce-scatter.2
Sparse Core Ops, SparseCore 1:
  204.9 136.2 all-gather.2
  343.1 82.6 all-gather.4
where the time goes:
time: 589 us; the launch traced here: 588 us
  waiting for transfers between devices  281 us (48%)
  blocking collectives  261 us (44%)
  matrix products  20 us (3%)
  between operations  16.9 us (3%)
  other arithmetic  6.97 us (1%)
    reduce_scatter x1, waiting for transfers between devices, shards(): lax.psum_scatter(term_a, 'dp', scatter_dimension=0, tiled=True)  158 us
    reduce_scatter x1, waiting for transfers between devices, shards(): lax.psum_scatter(term_b, 'dp', scatter_dimension=0, tiled=True)  121 us
    psum x1, blocking collectives, shards(): proj_sum, gradient_total = lax.psum((proj_part, grad_part), 'tensor')  95.9 us
    unnamed x1, blocking collectives  77.7 us
    all_gather x1, blocking collectives, shards(): lax.all_gather(adapter_input_factors.astype(jnp.bfloat16), 'dp', axis=0,...  48.6 us
    all_gather x1, blocking collectives, shards(): lax.all_gather(adapter_output_factors.astype(jnp.bfloat16), 'dp', axis=0,...  38.9 us
  transfers between devices with their start and end apart: 4, of which 2 were waited for; matrix products, arithmetic and copies ran while one was open for 2% of the time, Pallas kernels for 0%

commit v1 on v0

v1 whole, which is shorter than its diff:
```python
import jax
import jax.numpy as jnp
from jax import lax
from jax.sharding import PartitionSpec as P

ADAM_STEP = 10


ADAPTER_SCALE = 2.0
BETA_ONE = 0.9
BETA_TWO = 0.95
ADAM_EPS = 1e-08
Y, Z_HI = 4, 4
COUNT_BASE = 32


def adam_update(sums, count, moments):
    grad = sums / jnp.maximum(count, 1.0)
    active = count > 0.5
    first = jnp.where(active, BETA_ONE * moments[0] + (1.0 - BETA_ONE) * grad, moments[0])
    second = jnp.where(active, BETA_TWO * moments[1] + (1.0 - BETA_TWO) * grad * grad, moments[1])
    corr_one = 1.0 - BETA_ONE**ADAM_STEP
    corr_two = 1.0 - BETA_TWO**ADAM_STEP
    update = first / corr_one / (jnp.sqrt(second / corr_two) + ADAM_EPS)
    update = jnp.where(active, update, jnp.zeros_like(update))
    return (jnp.stack([first, second]), update)


def gather_by_exchange(block, axis, groups=None, size=None):
    size = lax.axis_size(axis) if size is None else size
    copies = jnp.broadcast_to(block[None], (size,) + block.shape)
    return lax.all_to_all(copies, axis, 0, 0, axis_index_groups=groups)


def nt_dot(left, right):
    return lax.dot_general(
        left, right, (((1,), (1,)), ((), ())), preferred_element_type=jnp.float32
    )


def shards(
    gate_logits,
    up_projected,
    output_gradient,
    down_matrix,
    adapter_input_factors,
    adapter_output_factors,
    input_moments,
    output_moments,
    batch_tenants,
    tenant_owner_slots,
):
    slot_count = lax.axis_size("dp")
    me = lax.axis_index("dp")
    rank, hid = adapter_input_factors.shape[1:]
    feat = adapter_output_factors.shape[2]
    tok = gate_logits.shape[0]
    cot_full = lax.all_gather(output_gradient, "tensor", axis=1, tiled=True)
    down_full = lax.all_gather(down_matrix, "dp", axis=1, tiled=True)

    tenant_ids = jnp.arange(tenant_owner_slots.shape[0], dtype=jnp.int32)
    slot_first = jnp.sum(jnp.where(tenant_ids == batch_tenants[0], tenant_owner_slots, 0))
    slot_last = jnp.sum(jnp.where(tenant_ids == batch_tenants[-1], tenant_owner_slots, 0))
    in_first = (batch_tenants == batch_tenants[0])[None, :]
    count_first = jnp.sum(in_first.astype(jnp.int32))
    count_last = tok - count_first
    slots = jnp.arange(slot_count, dtype=jnp.int32)
    hot_first = slots == slot_first
    hot_last = slots == slot_last
    run_counts = jnp.where(hot_first, count_first, 0) + jnp.where(hot_last, count_last, 0)
    digits = jnp.stack([run_counts // COUNT_BASE, run_counts % COUNT_BASE]).astype(jnp.bfloat16)
    digits = jnp.pad(digits, ((0, rank - 2), (0, 128 - slot_count)))

    packed = jnp.concatenate(
        [
            adapter_input_factors[0].astype(jnp.bfloat16),
            adapter_output_factors[0].astype(jnp.bfloat16),
            digits,
        ],
        axis=1,
    )
    gathered = gather_by_exchange(packed, "dp")
    mine = lax.dynamic_index_in_dim(gathered[:, :2, hid + feat :], me, axis=2, keepdims=False)
    count_parts = jnp.sum(mine.astype(jnp.float32), axis=0)
    count = COUNT_BASE * count_parts[0] + count_parts[1]
    pair = jnp.concatenate(
        [
            lax.dynamic_index_in_dim(gathered, slot_first, 0, keepdims=False),
            lax.dynamic_index_in_dim(gathered, slot_last, 0, keepdims=False),
        ],
        axis=0,
    )
    pair_a, pair_b = pair[:, :hid], pair[:, hid : hid + feat]

    gate_f = gate_logits.astype(jnp.float32)
    up_f = up_projected.astype(jnp.float32)
    sigmoid_gate = jax.nn.sigmoid(gate_f)
    activated = gate_f * sigmoid_gate
    hidden = (activated * up_f).astype(jnp.bfloat16)

    proj_pair = nt_dot(pair_a, hidden)
    grad_pair = nt_dot(pair_b, output_gradient)
    part = jnp.concatenate(
        [
            jnp.where(in_first, proj_pair[:rank], proj_pair[rank:]),
            jnp.where(in_first, grad_pair[:rank], grad_pair[rank:]),
        ],
        axis=0,
    )
    along_y = [[y * Z_HI + h for y in range(Y)] for h in range(Z_HI)]
    along_z = [[y * Z_HI + h for h in range(Z_HI)] for y in range(Y)]
    chunks = part.reshape(2 * rank, Y, tok // Y).transpose(1, 0, 2)
    chunk = jnp.sum(lax.all_to_all(chunks, "tensor", 0, 0, axis_index_groups=along_y), axis=0)
    chunk = jnp.sum(lax.all_gather(chunk, "tensor", axis_index_groups=along_z), axis=0)
    scale = jnp.where(jnp.arange(2 * rank)[:, None] < rank, 1.0, ADAPTER_SCALE)
    rounded = (scale * chunk).astype(jnp.bfloat16)
    whole = lax.all_gather(rounded, "tensor", axis_index_groups=along_y)
    whole = whole.transpose(1, 0, 2).reshape(2 * rank, tok)
    rank_projection, rank_gradient = whole[:rank], whole[rank:]
    zero = jnp.zeros((), jnp.bfloat16)
    spread_grad = jnp.concatenate(
        [jnp.where(in_first, rank_gradient, zero), jnp.where(in_first, zero, rank_gradient)]
    )
    spread_proj = jnp.concatenate(
        [jnp.where(in_first, rank_projection, zero), jnp.where(in_first, zero, rank_projection)]
    )
    term_a = jnp.dot(spread_grad, hidden, preferred_element_type=jnp.float32)
    term_b = ADAPTER_SCALE * jnp.dot(
        spread_proj, output_gradient, preferred_element_type=jnp.float32
    )
    term = jnp.concatenate([term_a, term_b], axis=1)
    outgoing = jnp.where(hot_first[:, None, None], term[:rank][None], 0.0) + jnp.where(
        hot_last[:, None, None], term[rank:][None], 0.0
    )
    incoming = lax.all_to_all(outgoing.astype(jnp.bfloat16), "dp", 0, 0)
    sums = jnp.sum(incoming.astype(jnp.float32), axis=0)
    new_moments_a, step_a = adam_update(sums[None, :, :hid], count, input_moments)
    new_moments_b, step_b = adam_update(sums[None, :, hid:], count, output_moments)

    hidden_grad = nt_dot(cot_full, down_full)
    hidden_grad = hidden_grad + lax.dot_general(
        spread_grad, pair_a, (((0,), (0,)), ((), ())), preferred_element_type=jnp.float32
    )
    grad_gate = (hidden_grad * up_f * sigmoid_gate * (1.0 + gate_f * (1.0 - sigmoid_gate))).astype(
        jnp.bfloat16
    )
    grad_up = (hidden_grad * activated).astype(jnp.bfloat16)
    return (grad_gate, grad_up, new_moments_a, new_moments_b, step_a, step_b)


def solution(mesh):
    placed = (
        P("dp", "tensor"),
        P("dp", "tensor"),
        P("dp", "tensor"),
        P("tensor", "dp"),
        P("dp", None, "tensor"),
        P("dp", None, "tensor"),
        P(None, "dp", None, "tensor"),
        P(None, "dp", None, "tensor"),
        P("dp"),
        P(),
    )
    return jax.shard_map(
        shards,
        mesh=mesh,
        in_specs=placed,
        out_specs=(
            P("dp", "tensor"),
            P("dp", "tensor"),
            P(None, "dp", None, "tensor"),
            P(None, "dp", None, "tensor"),
            P("dp", None, "tensor"),
            P("dp", None, "tensor"),
        ),
        check_vma=False,
    )
```

time: 589 us -> 289 us (0.49)
  blocking collectives: 261 us -> 52.4 us
  waiting for transfers between devices: 281 us -> 159 us
  starting transfers between devices: 0.16 us -> 17.6 us
  other arithmetic: 6.97 us -> 20.7 us
  matrix products: 20 us -> 13.2 us
    reduce_scatter x2 -> x0, waiting for transfers between devices: 279 us -> none  [the longest x1 158 us: shards(): lax.psum_scatter(term_a, 'dp', scatter_dimension=0, tiled=True)]
    psum x1 -> x0, blocking collectives: 95.9 us -> none  [shards(): proj_sum, gradient_total = lax.psum((proj_part, grad_part), 'tensor')]
    all_to_all x0 -> x3, waiting for transfers between devices: none -> 91.8 us  [the longest x1 45.9 us: shards(): incoming = lax.all_to_all(outgoing.astype(jnp.bfloat16), 'dp', 0, 0)]
    unnamed x1 -> x0, blocking collectives: 77.7 us -> none
    all_gather x1, waiting for transfers between devices: 0.01 us -> 65.5 us  [shards(): down_full = lax.all_gather(down_matrix, 'dp', axis=1, tiled=True)]
    all_gather x2, blocking collectives: 87.5 us -> 52.4 us  [the longest x1 38.4 us: shards(): lax.all_gather(chunk, 'tensor', axis_index_groups=along_z)]
    all_to_all x0 -> x3, starting transfers between devices: none -> 17.5 us  [the longest x1 8.75 us: gather_by_exchange(): return lax.all_to_all(copies, axis, 0, 0, axis_index_groups=groups)]
    dot_general x6, matrix products: 20 us -> 13.2 us  [the longest x3 10.4 us: nt_dot(): lax.dot_general(left, right, (((1,), (1,)), ((), ())), preferred_element_...]
  transfers between devices with their start and end apart: 4 -> 5, of which waited for: 2 -> 4; matrix products, arithmetic and copies ran while one was open for 2% -> 9% of each run, Pallas kernels for 0% -> 0%
where the time goes in v1:
time: 289 us; the launch traced here: 286 us
  waiting for transfers between devices  159 us (55%)
  blocking collectives  52.4 us (18%)
  other arithmetic  20.7 us (7%)
  between operations  20.1 us (7%)
  starting transfers between devices  17.6 us (6%)
  matrix products  13.2 us (5%)
  local copies, waits for them, and re-layouts  3.36 us (1%)
    all_gather x1, waiting for transfers between devices, shards(): down_full = lax.all_gather(down_matrix, 'dp', axis=1, tiled=True)  65.5 us
    all_to_all x1, waiting for transfers between devices, shards(): incoming = lax.all_to_all(outgoing.astype(jnp.bfloat16), 'dp', 0, 0)  45.9 us
    all_to_all x1, waiting for transfers between devices, gather_by_exchange(): return lax.all_to_all(copies, axis, 0, 0, axis_index_groups=groups)  42.8 us
    all_gather x1, blocking collectives, shards(): lax.all_gather(chunk, 'tensor', axis_index_groups=along_z)  38.4 us
    all_gather x1, blocking collectives, shards(): whole = lax.all_gather(rounded, 'tensor', axis_index_groups=along_y)  14 us
    dot_general x3, matrix products, nt_dot(): lax.dot_general(left, right, (((1,), (1,)), ((), ())), preferred_element_...  10.4 us
    all_to_all x1, starting transfers between devices, gather_by_exchange(): return lax.all_to_all(copies, axis, 0, 0, axis_index_groups=groups)  8.75 us
  transfers between devices with their start and end apart: 5, of which 4 were waited for; matrix products, arithmetic and copies ran while one was open for 9% of the time, Pallas kernels for 0%

profile of v1, /device:TPU:24, one launch (start us, length us, event | category | flops | bytes accessed | tf_op | source)
XLA Modules:
  0.0 286.0 jit_solution(8930348689604427091)
XLA Ops:
  7.2 0.0 all-gather.4.cloned.1.call-start
  7.2 0.7 all-gather.4.cloned.1.call-update
  7.9 0.0 all-gather.6.cloned.1.call-start
  7.9 0.7 all-gather.6.cloned.1.call-update
  8.6 1.3 fusion.46
  10.0 2.0 convert_reduce_fusion.1
  12.0 0.0 copy-start.4
  12.6 2.6 fusion.29
  15.2 2.0 fusion.33
  17.2 0.7 convert_bitcast_fusion.1
  17.9 0.8 convert_bitcast_fusion
  18.7 0.0 copy-start.1
  18.8 1.2 broadcast_in_dim.120
  19.9 8.8 %all-to-all-start = ((bf16[32,16,1280]{2,1,0:T(8,128)(2,1)}), bf16[32,16,1280]{2,1,0:T(8,128)(2,1)S(1)}, u32[]{:S(2)}, u32[]{:S(2)}) async-start(bf16[32,16,1280]{2,1,0:T(8,128)(2,1)} %broadcast_in_dim.120), calls=%async_computation | async-start | bytes 2621440 | tf_op jit(solution)/shard_map/all_to_all | solution.py:32
  28.7 0.0 copy-start
  32.6 1.9 iota_compare_fusion.2
  34.5 0.0 copy-done.1
  34.5 1.7 fusion
  36.3 42.8 %all-to-all-done = bf16[32,16,1280]{2,1,0:T(8,128)(2,1)S(1)} async-done(((bf16[32,16,1280]{2,1,0:T(8,128)(2,1)}), bf16[32,16,1280]{2,1,0:T(8,128)(2,1)S(1)}, u32[]{:S(2)}, u32[]{:S(2)}) %all-to-all-start) | async-done | bytes 1310752 | tf_op jit(solution)/shard_map/all_to_all | solution.py:32
  79.1 0.0 copy-done
  79.1 0.2 fusion.19
  79.3 0.4 fusion.41
  79.7 0.0 copy-done.4
  79.7 0.6 bitcast_bitcast_fusion
  80.4 4.7 %all-to-all-start.1 = ((f32[4,32,128]{2,1,0:T(8,128)}), f32[4,32,128]{2,1,0:T(8,128)S(1)}, u32[]{:S(2)}, u32[]{:S(2)}) async-start(f32[4,32,128]{2,1,0:T(8,128)} %bitcast_bitcast_fusion), calls=%async_computation.1 | async-start | bytes 131072 | tf_op jit(solution)/shard_map/all_to_all | solution.py:113
  85.1 0.5 compare_select_fusion.4
  85.6 3.0 %all-to-all-done.1 = f32[4,32,128]{2,1,0:T(8,128)S(1)} async-done(((f32[4,32,128]{2,1,0:T(8,128)}), f32[4,32,128]{2,1,0:T(8,128)S(1)}, u32[]{:S(2)}, u32[]{:S(2)}) %all-to-all-start.1) | async-done | bytes 65568 | tf_op jit(solution)/shard_map/all_to_all | solution.py:113
  88.6 0.6 reduce_sum.68
  89.2 38.4 %all-gather = f32[128,128]{1,0:T(8,128)S(1)} all-gather(f32[32,128]{1,0:T(8,128)} %reduce_sum.68), channel_id=2, replica_groups={{0,1,2,3},{4,5,6,7},{8,9,10,11},{12,13,14,15},{16,17,18,19},{20,21,22,2..., dimensions={0}, use_global_device_ids=true | all-gather | bytes 81920 | tf_op jit(solution)/shard_map/all_gather | solution.py:114
  127.6 0.6 reduce_sum.69
  128.2 0.0 copy-start.5
  128.2 0.0 copy-start.6
  128.2 0.8 fusion.22
  129.0 14.0 %all_gather.20 = bf16[4,32,128]{2,1,0:T(8,128)(2,1)S(1)} all-gather(bf16[1,32,128]{2,1,0:T(8,128)(2,1)S(1)} %fusion.22), channel_id=1, replica_groups={{0,4,8,12},{1,5,9,13},{2,6,10,14},{3,7,11,15},{16,20,24,28},{17,21,25,2..., dimensions={0}, use_global_device_ids=true | all-gather | bytes 40960 | tf_op jit(solution)/shard_map/all_gather | solution.py:117
  143.0 0.7 bitcast_select_fusion.2
  143.7 0.1 convolution_multiply_fusion
  143.8 0.3 fusion.16
  144.1 0.0 copy-done.5
  144.2 0.0 copy-done.6
  144.2 1.4 add_convert_fusion
  145.6 0.0 copy-start.3
  145.6 4.1 %all-to-all-start.2 = ((bf16[32,16,1152]{2,1,0:T(8,128)(2,1)}), bf16[32,16,1152]{2,1,0:T(8,128)(2,1)S(1)}, u32[]{:S(2)}, u32[]{:S(2)}) async-start(bf16[32,16,1152]{2,1,0:T(8,128)(2,1)} %add_convert_fusion), calls=%async_computation.2 | async-start | bytes 2359296 | tf_op jit(solution)/shard_map/all_to_all | solution.py:135
  149.7 0.1 constant_dynamic-slice_fusion
  149.8 0.1 copy.38
  149.9 0.1 convert_reduce_fusion.2
  150.0 0.6 fusion.47
  151.9 45.9 %all-to-all-done.2 = bf16[32,16,1152]{2,1,0:T(8,128)(2,1)S(1)} async-done(((bf16[32,16,1152]{2,1,0:T(8,128)(2,1)}), bf16[32,16,1152]{2,1,0:T(8,128)(2,1)S(1)}, u32[]{:S(2)}, u32[]{:S(2)}) %all-to-all-start.2) | async-done | bytes 1179680 | tf_op jit(solution)/shard_map/all_to_all | solution.py:135
  197.8 0.2 convert_reduce_fusion
  198.0 0.0 copy-done.3
  198.0 0.6 select_bitcast_fusion.1
  198.6 0.6 pad_maximum_fusion.4
  199.3 1.5 select_bitcast_fusion
  200.8 0.7 pad_maximum_fusion
  201.4 0.0 copy-start.2
  201.4 0.0 all-gather.4.cloned.1.call-done
  201.5 65.5 %all-gather.6.cloned.1.call-done = bf16[896,4096]{1,0:T(8,128)(2,1)} async-done(((bf16[896,128]{1,0:T(8,128)(2,1)}), bf16[896,4096]{1,0:T(8,128)(2,1)}) %all-gather.6.cloned.1.call-update) | async-done | bytes 7340048 | tf_op jit(solution)/shard_map/all_gather | solution.py:59
  267.0 9.9 %fusion.48 = f32[512,896]{1,0:T(8,128)S(1)} fusion(bf16[512,4096]{1,0:T(8,128)(2,1)} %all-gather.4.cloned.1.call-done, bf16[896,4096]{1,0:T(8,128)(2,1)} %all-gather.6.cloned.1.call-done), kind=kOutput, calls=%fused_computation.110 | convolution fusion | flops 3758096384 | bytes 13369344 | tf_op jit(solution)/shard_map/dot_general | solution.py:36
  276.9 0.0 copy-done.2
  276.9 2.3 multiply_convert_fusion
  (8 shorter events, 0.1 us)
Async XLA Ops:
  7.2 194.3 %all-gather.4.cloned.1.call-start = ((), (), s32[]{:S(2)}) async-start(), calls=%async_computation.3 | async-start | bytes 4456448 | tf_op jit(solution)/shard_map/all_gather | solution.py:58
  7.9 259.1 %all-gather.6.cloned.1.call-start = ((), (), s32[]{:S(2)}) async-start(), calls=%async_computation.4 | async-start | bytes 7569408 | tf_op jit(solution)/shard_map/all_gather | solution.py:59
  12.0 67.7 %copy-start.4 = (pred[512]{0:T(512)(128)(4,1)}, pred[512]{0:T(512)(128)(4,1)S(1)}, u32[]{:S(2)}) copy-start(pred[512]{0:T(512)(128)(4,1)S(1)} %get-tuple-element.11) | copy-start | bytes 1540
  18.7 15.8 %copy-start.1 = (bf16[512,896]{1,0:T(8,128)(2,1)S(1)}, bf16[512,896]{1,0:T(8,128)(2,1)}, u32[]{:S(2)}) copy-start(bf16[512,896]{1,0:T(8,128)(2,1)} %param.10) | copy-start | bytes 2752516
  19.9 59.2 %all-to-all-start = ((bf16[32,16,1280]{2,1,0:T(8,128)(2,1)}), bf16[32,16,1280]{2,1,0:T(8,128)(2,1)S(1)}, u32[]{:S(2)}, u32[]{:S(2)}) async-start(bf16[32,16,1280]{2,1,0:T(8,128)(2,1)} %broadcast_in_dim.120), calls=%async_computation | async-start | bytes 2621440 | tf_op jit(solution)/shard_map/all_to_all | solution.py:32
  28.7 50.4 %copy-start = (bf16[512,256]{1,0:T(8,128)(2,1)S(1)}, bf16[512,256]{1,0:T(8,128)(2,1)}, u32[]{:S(2)}) copy-start(bf16[512,256]{1,0:T(8,128)(2,1)} %param.12) | copy-start | bytes 786436
  80.4 8.2 %all-to-all-start.1 = ((f32[4,32,128]{2,1,0:T(8,128)}), f32[4,32,128]{2,1,0:T(8,128)S(1)}, u32[]{:S(2)}, u32[]{:S(2)}) async-start(f32[4,32,128]{2,1,0:T(8,128)} %bitcast_bitcast_fusion), calls=%async_computation.1 | async-start | bytes 131072 | tf_op jit(solution)/shard_map/all_to_all | solution.py:113
  128.2 15.9 %copy-start.5 = (pred[32]{0:T(512)(128)(4,1)S(1)}, pred[32]{0:T(512)(128)(4,1)}, u32[]{:S(2)}) copy-start(pred[32]{0:T(512)(128)(4,1)} %get-tuple-element.38) | copy-start | bytes 100
  128.2 15.9 %copy-start.6 = (pred[32]{0:T(512)(128)(4,1)S(1)}, pred[32]{0:T(512)(128)(4,1)}, u32[]{:S(2)}) copy-start(pred[32]{0:T(512)(128)(4,1)} %get-tuple-element.39) | copy-start | bytes 100
  145.6 52.4 %copy-start.3 = (f32[2,1,16,256]{3,2,1,0:T(8,128)S(1)}, f32[2,1,16,256]{3,2,1,0:T(8,128)}, u32[]{:S(2)}) copy-start(f32[2,1,16,256]{3,2,1,0:T(8,128)} %param.17) | copy-start | bytes 98308
  145.6 52.3 %all-to-all-start.2 = ((bf16[32,16,1152]{2,1,0:T(8,128)(2,1)}), bf16[32,16,1152]{2,1,0:T(8,128)(2,1)S(1)}, u32[]{:S(2)}, u32[]{:S(2)}) async-start(bf16[32,16,1152]{2,1,0:T(8,128)(2,1)} %add_convert_fusion), calls=%async_computation.2 | async-start | bytes 2359296 | tf_op jit(solution)/shard_map/all_to_all | solution.py:135
  201.4 75.4 %copy-start.2 = (bf16[512,896]{1,0:T(8,128)(2,1)S(1)}, bf16[512,896]{1,0:T(8,128)(2,1)}, u32[]{:S(2)}) copy-start(bf16[512,896]{1,0:T(8,128)(2,1)} %param.11) | copy-start | bytes 2752516
Sparse Core Ops, SparseCore 0:
  11.0 164.0 all-gather.3
  177.1 89.8 all-gather.5

commit v2 on v0

v2 whole, which is shorter than its diff:
```python
import functools

import jax
import jax.numpy as jnp
from jax import lax
from jax.experimental import pallas as pl
from jax.experimental.pallas import tpu as pltpu
from jax.sharding import PartitionSpec as P

ADAM_STEP = 10


ADAPTER_SCALE = 2.0
BETA_ONE = 0.9
BETA_TWO = 0.95
ADAM_EPS = 1e-08
X, Z_LO, CORES = 4, 4, 2
Y, Z_HI = 4, 4
COUNT_BASE = 32
LANES = 128
INFO_FIRST, INFO_LAST, INFO_CUT = 0, 1, 2

ALONG_X = [[(x * Z_LO + z) * CORES + c for x in range(X)] for z in range(Z_LO) for c in range(CORES)]
ALONG_Z_LO = [[(x * Z_LO + z) * CORES + c for z in range(Z_LO)] for x in range(X) for c in range(CORES)]
ALONG_Y = [[y * Z_HI + h for y in range(Y)] for h in range(Z_HI)]
ALONG_Z_HI = [[y * Z_HI + h for h in range(Z_HI)] for y in range(Y)]
OTHER_CORE = [(d, d ^ 1) for d in range(X * Z_LO * CORES)]
NEXT_Z = [(y * Z_HI + h, y * Z_HI + (h + 1) % Z_HI) for y in range(Y) for h in range(Z_HI)]
LAST_Z = [(y * Z_HI + h, y * Z_HI + (h - 1) % Z_HI) for y in range(Y) for h in range(Z_HI)]
NEXT_Y = [(y * Z_HI + h, (y + 1) % Y * Z_HI + h) for y in range(Y) for h in range(Z_HI)]
LAST_Y = [(y * Z_HI + h, (y - 1) % Y * Z_HI + h) for y in range(Y) for h in range(Z_HI)]

VMEM = pl.BlockSpec(memory_space=pltpu.VMEM)
SMEM = pl.BlockSpec(memory_space=pltpu.SMEM)


def params(mib=40):
    return pltpu.CompilerParams(vmem_limit_bytes=mib * 1024 * 1024)


def nt_dot(left, right):
    return lax.dot_general(
        left, right, (((1,), (1,)), ((), ())), preferred_element_type=jnp.float32
    )


def tn_dot(left, right):
    return lax.dot_general(
        left, right, (((0,), (0,)), ((), ())), preferred_element_type=jnp.float32
    )


def spread(copies, block):
    return jnp.broadcast_to(block[None], (copies,) + block.shape)


def prepare(tenants_s, owners_s, tenants_v, factor_a, factor_b, packed, info_v):
    tok = tenants_s.shape[0]
    rank, hid = factor_a.shape
    feat = factor_b.shape[1]
    first, last = tenants_s[0], tenants_s[tok - 1]
    slot_first, slot_last = owners_s[first], owners_s[last]
    cut = jnp.sum((tenants_v[...] == first).astype(jnp.int32))
    lane = lax.broadcasted_iota(jnp.int32, (rank, LANES), 1)
    row = lax.broadcasted_iota(jnp.int32, (rank, LANES), 0)
    counts = jnp.where(lane == slot_first, cut, 0) + jnp.where(lane == slot_last, tok - cut, 0)
    high = lax.shift_right_logical(counts, 5)
    digits = jnp.where(row == 0, high, jnp.where(row == 1, counts - COUNT_BASE * high, 0))
    digits = digits.astype(jnp.float32).astype(jnp.bfloat16)
    a = factor_a[...].astype(jnp.bfloat16)
    b = factor_b[...].astype(jnp.bfloat16)
    for copy in range(packed.shape[0]):
        packed[copy, :, :hid] = a
        packed[copy, :, hid : hid + feat] = b
        packed[copy, :, hid + feat :] = digits
    lane_i = lax.broadcasted_iota(jnp.int32, info_v.shape, 1)
    info_v[...] = jnp.where(
        lane_i == INFO_FIRST, slot_first, jnp.where(lane_i == INFO_LAST, slot_last, cut)
    )


def low_rank(info_s, core_s, own, other, hidden, cot, part, pair, totals):
    core = core_s[0]
    rank = own.shape[1]
    hid, feat = hidden.shape[1], cot.shape[1]
    for run, place in enumerate((INFO_FIRST, INFO_LAST)):
        slot = info_s[place]
        chip = lax.shift_right_logical(slot, 1)
        here = (slot & 1) == core
        rows = pl.ds(run * rank, rank)

        @pl.when(here)
        def _():
            pair[rows, :] = own[chip, :, : hid + feat]

        @pl.when(jnp.logical_not(here))
        def _():
            pair[rows, :] = other[chip, :, : hid + feat]

    tok = hidden.shape[0]
    in_first = lax.broadcasted_iota(jnp.int32, (rank, tok), 1) < info_s[INFO_CUT]
    proj = nt_dot(pair[:, :hid], hidden[...])
    grad = nt_dot(pair[:, hid:], cot[...])
    proj = jnp.where(in_first, proj[:rank], proj[rank:])
    grad = jnp.where(in_first, grad[:rank], grad[rank:])
    width = tok // Y
    for y in range(Y):
        part[y, :rank, :] = proj[:, y * width : (y + 1) * width]
        part[y, rank:, :] = grad[:, y * width : (y + 1) * width]
    digits = own[:, :, hid + feat :].astype(jnp.float32)
    digits = digits + other[:, :, hid + feat :].astype(jnp.float32)
    totals[...] = jnp.sum(digits, axis=0)


def terms(info_s, whole, hidden, cot, grad_rows, term):
    rank = whole.shape[1] // 2
    hid = hidden.shape[1]
    tok = hidden.shape[0]
    rows = jnp.concatenate([whole[y] for y in range(Y)], axis=1)
    in_first = lax.broadcasted_iota(jnp.int32, (rank, tok), 1) < info_s[INFO_CUT]
    proj = rows[:rank].astype(jnp.float32)
    grad = rows[rank:].astype(jnp.float32)
    zero = jnp.zeros_like(proj)

    def by_run(values):
        both = [jnp.where(in_first, values, zero), jnp.where(in_first, zero, values)]
        return jnp.concatenate(both, axis=0).astype(jnp.bfloat16)

    proj, grad = by_run(proj), by_run(grad)
    grad_rows[...] = grad
    term[:, :hid] = jnp.dot(grad, hidden[...], preferred_element_type=jnp.float32)
    term[:, hid:] = ADAPTER_SCALE * jnp.dot(proj, cot[...], preferred_element_type=jnp.float32)


def dense(info_s, info_other_s, core_s, term, term_other, outgoing, total):
    core = core_s[0]
    rank = outgoing.shape[1]
    total[...] = jnp.zeros_like(total)
    for info, source in ((info_s, term), (info_other_s, term_other)):
        for run, place in enumerate((INFO_FIRST, INFO_LAST)):
            slot = info[place]
            chip = lax.shift_right_logical(slot, 1)

            @pl.when((slot & 1) == core)
            def _():
                total[chip] += source[run * rank : (run + 1) * rank, :]

    outgoing[...] = total[...].astype(jnp.bfloat16)


def adam(me_s, totals, incoming, moments_a, moments_b, new_a, new_b, step_a, step_b):
    lane = lax.broadcasted_iota(jnp.int32, (1, LANES), 1)
    digit = COUNT_BASE * totals[0:1, :] + totals[1:2, :]
    count = jnp.sum(jnp.where(lane == me_s[0], digit, 0.0))
    active = count > 0.5
    divisor = jnp.maximum(count, 1.0)
    corr_one = 1.0 - BETA_ONE**ADAM_STEP
    corr_two = 1.0 - BETA_TWO**ADAM_STEP
    sums = jnp.sum(incoming[...].astype(jnp.float32), axis=0)
    hid = moments_a.shape[-1]
    for part, moments, new, step in (
        (sums[:, :hid], moments_a, new_a, step_a),
        (sums[:, hid:], moments_b, new_b, step_b),
    ):
        grad = part / divisor
        old_one, old_two = moments[0, 0], moments[1, 0]
        first = jnp.where(active, BETA_ONE * old_one + (1.0 - BETA_ONE) * grad, old_one)
        second = jnp.where(active, BETA_TWO * old_two + (1.0 - BETA_TWO) * grad * grad, old_two)
        update = first / corr_one / (jnp.sqrt(second / corr_two) + ADAM_EPS)
        new[0, 0] = first
        new[1, 0] = second
        step[0] = jnp.where(active, update, 0.0)


def finish(
    y_s, own, back, ahead, far_top, far_low, down, grad_rows, pair_a, gate, up, out_gate, out_up, total
):
    place, turn = pl.program_id(0), pl.program_id(1)
    half = far_top.shape[1]
    weights = down[...]

    @pl.when((place == 0) & (turn == 0))
    def _():
        total[...] = tn_dot(grad_rows[...], pair_a[...])

    @pl.when(turn == 0)
    def _():
        total[...] += nt_dot(own[0], weights)

    @pl.when(turn == 1)
    def _():
        total[...] += nt_dot(back[0], weights)

    @pl.when(turn == 2)
    def _():
        total[...] += nt_dot(ahead[0], weights)

    @pl.when(turn == 3)
    def _():
        total[:half, :] += nt_dot(far_top[0], weights)
        total[half:, :] += nt_dot(far_low[0], weights)

    @pl.when((place == pl.num_programs(0) - 1) & (turn == pl.num_programs(1) - 1))
    def _():
        gate_f = gate[...].astype(jnp.float32)
        up_f = up[...].astype(jnp.float32)
        sigmoid_gate = jax.nn.sigmoid(gate_f)
        grad = total[...]
        out_gate[...] = (
            grad * up_f * sigmoid_gate * (1.0 + gate_f * (1.0 - sigmoid_gate))
        ).astype(jnp.bfloat16)
        out_up[...] = (grad * (gate_f * sigmoid_gate)).astype(jnp.bfloat16)


def shards(
    gate_logits,
    up_projected,
    output_gradient,
    down_matrix,
    adapter_input_factors,
    adapter_output_factors,
    input_moments,
    output_moments,
    batch_tenants,
    tenant_owner_slots,
):
    me = lax.axis_index("dp").astype(jnp.int32)
    core_s = (me & (CORES - 1)).reshape(1)
    tensor = lax.axis_index("tensor").astype(jnp.int32)
    y_s = jnp.stack([lax.shift_right_logical(tensor, 2), tensor & (Z_HI - 1)])
    rank, hid = adapter_input_factors.shape[1:]
    feat = adapter_output_factors.shape[2]
    tok = gate_logits.shape[0]
    wide = hid + feat
    bf16, f32 = jnp.bfloat16, jnp.float32
    shape = jax.ShapeDtypeStruct

    down_full = lax.all_gather(down_matrix, "dp", axis=1, tiled=True)

    packed, info_v = pl.pallas_call(
        prepare,
        out_shape=(shape((Z_LO, rank, wide + LANES), bf16), shape((8, LANES), jnp.int32)),
        in_specs=[SMEM, SMEM, VMEM, VMEM, VMEM],
        out_specs=(VMEM, VMEM),
        compiler_params=params(),
        name="prepare",
    )(
        batch_tenants,
        tenant_owner_slots,
        batch_tenants.reshape(-1, LANES),
        adapter_input_factors[0],
        adapter_output_factors[0],
    )
    column = lax.all_to_all(packed, "dp", 0, 0, axis_index_groups=ALONG_Z_LO)
    info_other_v = lax.ppermute(info_v, "dp", OTHER_CORE)
    info_s, info_other_s = info_v[0, :8], info_other_v[0, :8]
    half = tok // 2
    z_back = lax.ppermute(output_gradient, "tensor", NEXT_Z)
    z_ahead = lax.ppermute(output_gradient, "tensor", LAST_Z)
    hidden = (
        jax.nn.silu(gate_logits.astype(f32)) * up_projected.astype(f32)
    ).astype(bf16)
    plane = lax.all_to_all(spread(X, column), "dp", 0, 0, axis_index_groups=ALONG_X)
    own = plane.reshape(X * Z_LO, rank, wide + LANES)
    other = lax.ppermute(own, "dp", OTHER_CORE)

    part, pair, totals = pl.pallas_call(
        low_rank,
        out_shape=(
            shape((Y, 2 * rank, tok // Y), f32),
            shape((2 * rank, wide), bf16),
            shape((rank, LANES), f32),
        ),
        in_specs=[SMEM, SMEM, VMEM, VMEM, VMEM, VMEM],
        out_specs=(VMEM, VMEM, VMEM),
        compiler_params=params(),
        name="low_rank",
    )(info_s, core_s, own, other, hidden, output_gradient)

    z_back, z_ahead, part = lax.optimization_barrier((z_back, z_ahead, part))
    z_far_top = lax.ppermute(z_back[:half], "tensor", NEXT_Z)
    z_far_low = lax.ppermute(z_ahead[half:], "tensor", LAST_Z)

    chunk = jnp.sum(lax.all_to_all(part, "tensor", 0, 0, axis_index_groups=ALONG_Y), axis=0)
    chunk = jnp.sum(lax.all_gather(chunk, "tensor", axis_index_groups=ALONG_Z_HI), axis=0)
    scale = jnp.where(jnp.arange(2 * rank)[:, None] < rank, 1.0, ADAPTER_SCALE)
    rounded = (scale * chunk).astype(bf16)
    whole = lax.all_to_all(spread(Y, rounded), "tensor", 0, 0, axis_index_groups=ALONG_Y)

    z_far_top, z_far_low, whole = lax.optimization_barrier((z_far_top, z_far_low, whole))
    z_far = jnp.concatenate([z_far_top, z_far_low])
    cot_z = jnp.stack([output_gradient, z_back, z_ahead, z_far])
    back = lax.ppermute(cot_z, "tensor", NEXT_Y)
    ahead = lax.ppermute(cot_z, "tensor", LAST_Y)

    grad_rows, term = pl.pallas_call(
        terms,
        out_shape=(shape((2 * rank, tok), bf16), shape((2 * rank, wide), f32)),
        in_specs=[SMEM, VMEM, VMEM, VMEM],
        out_specs=(VMEM, VMEM),
        compiler_params=params(),
        name="terms",
    )(info_s, whole, hidden, output_gradient)

    term_other = lax.ppermute(term, "dp", OTHER_CORE)
    outgoing = pl.pallas_call(
        dense,
        out_shape=shape((X * Z_LO, rank, wide), bf16),
        in_specs=[SMEM, SMEM, SMEM, VMEM, VMEM],
        out_specs=VMEM,
        scratch_shapes=[pltpu.VMEM((X * Z_LO, rank, wide), f32)],
        compiler_params=params(),
        name="dense",
    )(info_s, info_other_s, core_s, term, term_other)
    outgoing = outgoing.reshape(X, Z_LO, rank, wide)
    by_x = lax.all_to_all(outgoing, "dp", 0, 0, axis_index_groups=ALONG_X)
    by_x = jnp.sum(by_x.astype(f32), axis=0).astype(bf16)
    incoming = lax.all_to_all(by_x, "dp", 0, 0, axis_index_groups=ALONG_Z_LO)

    new_moments_a, new_moments_b, step_a, step_b = pl.pallas_call(
        adam,
        out_shape=(
            shape(input_moments.shape, f32),
            shape(output_moments.shape, f32),
            shape(adapter_input_factors.shape, f32),
            shape(adapter_output_factors.shape, f32),
        ),
        in_specs=[SMEM, VMEM, VMEM, VMEM, VMEM],
        out_specs=(VMEM,) * 4,
        compiler_params=params(),
        name="adam",
    )(me.reshape(1), totals, incoming, input_moments, output_moments)

    far_top = lax.ppermute(back[:, :half], "tensor", NEXT_Y)
    far_low = lax.ppermute(ahead[:, half:], "tensor", LAST_Y)

    def down_block(place, turn, y_ref):
        y_off = jnp.where(turn == 1, Y - 1, jnp.where(turn == 2, 1, jnp.where(turn == 3, 2, 0)))
        z_off = jnp.where(place == 1, Z_HI - 1, jnp.where(place == 2, 1, jnp.where(place == 3, 2, 0)))
        return 0, lax.rem(y_ref[0] + y_off, Y) * Z_HI + lax.rem(y_ref[1] + z_off, Z_HI)

    def by_place(rows):
        return pl.BlockSpec((1, rows, feat), lambda place, turn, y_ref: (place, 0, 0))

    def whole_of(rows, columns):
        return pl.BlockSpec((rows, columns), lambda place, turn, y_ref: (0, 0))

    grad_gate, grad_up = pl.pallas_call(
        finish,
        out_shape=(shape((tok, hid), bf16), shape((tok, hid), bf16)),
        grid_spec=pltpu.PrefetchScalarGridSpec(
            num_scalar_prefetch=1,
            grid=(Z_HI, Y),
            in_specs=[
                by_place(tok),
                by_place(tok),
                by_place(tok),
                by_place(half),
                by_place(half),
                pl.BlockSpec((hid, feat), down_block),
                whole_of(2 * rank, tok),
                whole_of(2 * rank, hid),
                whole_of(tok, hid),
                whole_of(tok, hid),
            ],
            out_specs=[whole_of(tok, hid), whole_of(tok, hid)],
            scratch_shapes=[pltpu.VMEM((tok, hid), f32)],
        ),
        compiler_params=params(),
        name="finish",
    )(
        y_s,
        cot_z,
        back,
        ahead,
        far_top,
        far_low,
        down_full,
        grad_rows,
        pair[:, :hid],
        gate_logits,
        up_projected,
    )
    return (grad_gate, grad_up, new_moments_a, new_moments_b, step_a, step_b)


def solution(mesh):
    placed = (
        P("dp", "tensor"),
        P("dp", "tensor"),
        P("dp", "tensor"),
        P("tensor", "dp"),
        P("dp", None, "tensor"),
        P("dp", None, "tensor"),
        P(None, "dp", None, "tensor"),
        P(None, "dp", None, "tensor"),
        P("dp"),
        P(),
    )
    return jax.shard_map(
        shards,
        mesh=mesh,
        in_specs=placed,
        out_specs=(
            P("dp", "tensor"),
            P("dp", "tensor"),
            P(None, "dp", None, "tensor"),
            P(None, "dp", None, "tensor"),
            P("dp", None, "tensor"),
            P("dp", None, "tensor"),
        ),
        check_vma=False,
    )
```

time: 589 us -> 216 us (0.37)
  waiting for transfers between devices: 281 us -> 25.8 us
  blocking collectives: 261 us -> 59.6 us
  starting transfers between devices: 0.16 us -> 66.7 us
  Pallas kernels: 0 us -> 22.1 us
  matrix products: 20 us -> 0 us
  local copies, waits for them, and re-layouts: 2.53 us -> 19.4 us
    reduce_scatter x2 -> x0, waiting for transfers between devices: 279 us -> none  [the longest x1 158 us: shards(): lax.psum_scatter(term_a, 'dp', scatter_dimension=0, tiled=True)]
    psum x1 -> x0, blocking collectives: 95.9 us -> none  [shards(): proj_sum, gradient_total = lax.psum((proj_part, grad_part), 'tensor')]
    unnamed x1 -> x0, blocking collectives: 77.7 us -> none
    all_gather x2 -> x1, blocking collectives: 87.5 us -> 23 us  [shards(): lax.all_gather(chunk, 'tensor', axis_index_groups=ALONG_Z_HI)]
    ppermute x0 -> x11, starting transfers between devices: none -> 44.5 us  [the longest x1 9.25 us: shards(): z_far_top = lax.ppermute(z_back[:half], 'tensor', NEXT_Z)]
    all_to_all x0 -> x3, blocking collectives: none -> 36.6 us  [the longest x1 15.9 us: shards(): lax.all_to_all(spread(X, column), 'dp', 0, 0, axis_index_groups=ALONG_X)]
    all_to_all x0 -> x3, starting transfers between devices: none -> 22.2 us  [the longest x1 13.4 us: shards(): incoming = lax.all_to_all(by_x, 'dp', 0, 0, axis_index_groups=ALONG_Z_LO)]
    pallas_call x0 -> x6, Pallas kernels: none -> 22.1 us  [the longest x1 15.5 us: shards(): pl.pallas_call(finish, out_shape=(shape((tok, hid), bf16), shape((tok, hi...]
  transfers between devices with their start and end apart: 4 -> 15, of which waited for: 2 -> 4; matrix products, arithmetic and copies ran while one was open for 2% -> 5% of each run, Pallas kernels for 0% -> 3%
where the time goes in v2:
time: 216 us; the launch traced here: 212 us
  starting transfers between devices  66.7 us (31%)
  blocking collectives  59.6 us (28%)
  waiting for transfers between devices  25.8 us (12%)
  Pallas kernels  22.1 us (10%)
  local copies, waits for them, and re-layouts  19.4 us (9%)
  between operations  14.3 us (7%)
  other arithmetic  4.39 us (2%)
    all_gather x1, blocking collectives, shards(): lax.all_gather(chunk, 'tensor', axis_index_groups=ALONG_Z_HI)  23 us
    ppermute x1, waiting for transfers between devices, shards(): z_back = lax.ppermute(output_gradient, 'tensor', NEXT_Z)  19.5 us
    all_to_all x1, blocking collectives, shards(): lax.all_to_all(spread(X, column), 'dp', 0, 0, axis_index_groups=ALONG_X)  15.9 us
    pallas_call x1, Pallas kernels, shards(): pl.pallas_call(finish, out_shape=(shape((tok, hid), bf16), shape((tok, hi...  15.5 us
    all_to_all x1, starting transfers between devices, shards(): incoming = lax.all_to_all(by_x, 'dp', 0, 0, axis_index_groups=ALONG_Z_LO)  13.4 us
    all_to_all x1, blocking collectives, shards(): column = lax.all_to_all(packed, 'dp', 0, 0, axis_index_groups=ALONG_Z_LO)  12.6 us
    unnamed x34, local copies, waits for them, and re-layouts  12.3 us
    ppermute x1, starting transfers between devices, shards(): z_far_top = lax.ppermute(z_back[:half], 'tensor', NEXT_Z)  9.25 us
  transfers between devices with their start and end apart: 15, of which 4 were waited for; matrix products, arithmetic and copies ran while one was open for 5% of the time, Pallas kernels for 3%

profile of v2, /device:TPU:24, one launch (start us, length us, event | category | flops | bytes accessed | tf_op | source)
XLA Modules:
  0.0 212.2 jit_solution(12378723358065060029)
XLA Ops:
  7.2 0.0 copy-start.2
  7.2 0.0 all-gather.3.cloned.1.call-start
  7.2 0.7 all-gather.3.cloned.1.call-update
  7.9 0.8 copy-done.6
  8.7 0.7 copy-done.11
  9.5 0.7 copy-done.14
  10.1 0.7 copy-done.15
  10.8 0.7 prepare.1
  11.5 12.6 %all_to_all.30 = bf16[4,16,1280]{2,1,0:T(8,128)(2,1)S(1)} all-to-all(bf16[4,16,1280]{2,1,0:T(8,128)(2,1)S(1)} %get-tuple-element.26), channel_id=1, replica_groups={{0,32,64,96},{16,48,80,112},{128,160,192,224},{144,176,208,240},{256,28..., dimensions={0} | all-to-all | bytes 327680 | tf_op jit(solution)/shard_map/all_to_all | solution.py:254
  24.2 15.9 %all_to_all.31 = bf16[4,4,16,1280]{3,2,1,0:T(8,128)(2,1)S(1)} all-to-all(bf16[4,4,16,1280]{3,2,1,0:T(8,128)(2,1)S(1)} %broadcast_in_dim.12), channel_id=1, replica_groups={{0,128,256,384},{16,144,272,400},{32,160,288,416},{48,176,304,432},{64,..., dimensions={0} | all-to-all | bytes 1310720 | tf_op jit(solution)/shard_map/all_to_all | solution.py:263
  40.1 1.9 collective-permute-start.2
  42.0 9.1 %collective-permute-start = (bf16[512,256]{1,0:T(8,128)(2,1)}, bf16[512,256]{1,0:T(8,128)(2,1)}, u32[]{:S(2)}, u32[]{:S(2)}) collective-permute-start(bf16[512,256]{1,0:T(8,128)(2,1)} %cot.3), channel_id=1, source_target_pairs={{0,1},{1,2},{2,3},{3,0},{4,5},{5,6},{6,7},{7,4},{8,9},{9,10},{10,1... | collective-permute-start | bytes 786440 | tf_op jit(solution)/shard_map/ppermute | solution.py:258
  51.1 3.3 %collective-permute-start.1 = (bf16[512,256]{1,0:T(8,128)(2,1)}, bf16[512,256]{1,0:T(8,128)(2,1)}, u32[]{:S(2)}, u32[]{:S(2)}) collective-permute-start(bf16[512,256]{1,0:T(8,128)(2,1)} %cot.3), channel_id=1, source_target_pairs={{0,3},{1,0},{2,1},{3,2},{4,7},{5,4},{6,5},{7,6},{8,11},{9,8},{10,9... | collective-permute-start | bytes 786440 | tf_op jit(solution)/shard_map/ppermute | solution.py:259
  54.4 0.6 fusion.4.hidden
  55.1 0.0 collective-permute-done.2.other
  55.1 2.3 %low_rank.1 = (f32[4,32,128]{2,1,0:T(8,128)}, bf16[32,1152]{1,0:T(8,128)(2,1)S(1)}, f32[16,128]{1,0:T(8,128)S(1)}) custom-call(s32[8]{0:T(128)S(1)} %slice_bitcast_fusion.1.info_s, s32[1]{0:T(128)} %bitcast.7.core_s, bf16[16,16,1280]{2,1,0:T(8,128)(2,1)S(1)} %bitcast.20, bf16[16,16,1280]{2,1,0:T(8,128)(2,1)} %collective-permute-done.2.other, ...), custom_call_target="tpu_custom_call" | custom-call | tf_op jit(solution)/shard_map/low_rank/pallas_call | solution.py:267
  57.3 0.6 copy-done.7
  58.0 0.6 copy-done.12
  58.6 19.5 %collective-permute-done = bf16[512,256]{1,0:T(8,128)(2,1)} collective-permute-done((bf16[512,256]{1,0:T(8,128)(2,1)}, bf16[512,256]{1,0:T(8,128)(2,1)}, u32[]{:S(2)}, u32[]{:S(2)}) %collective-permute-start) | collective-permute-done | bytes 262176 | tf_op jit(solution)/shard_map/ppermute | solution.py:258
  78.1 0.0 collective-permute-done.1
  78.1 4.7 %all-to-all-start.2 = ((f32[4,32,128]{2,1,0:T(8,128)}), f32[4,32,128]{2,1,0:T(8,128)S(1)}, u32[]{:S(2)}, u32[]{:S(2)}) async-start(f32[4,32,128]{2,1,0:T(8,128)} %get-tuple-element.30), calls=%async_computation.2 | async-start | bytes 131072 | tf_op jit(solution)/shard_map/all_to_all | solution.py:284
  82.8 0.9 slice.22
  83.7 9.3 %collective-permute-start.3 = (bf16[256,256]{1,0:T(8,128)(2,1)S(1)}, bf16[256,256]{1,0:T(8,128)(2,1)S(1)}, u32[]{:S(2)}, u32[]{:S(2)}) collective-permute-start(bf16[256,256]{1,0:T(8,128)(2,1)S(1)} %slice.22), channel_id=1, source_target_pairs={{0,1},{1,2},{2,3},{3,0},{4,5},{5,6},{6,7},{7,4},{8,9},{9,10},{10,1... | collective-permute-start | bytes 393224 | tf_op jit(solution)/shard_map/ppermute | solution.py:281
  93.0 0.9 slice.23
  93.9 3.4 %collective-permute-start.4 = (bf16[256,256]{1,0:T(8,128)(2,1)S(1)}, bf16[256,256]{1,0:T(8,128)(2,1)S(1)}, u32[]{:S(2)}, u32[]{:S(2)}) collective-permute-start(bf16[256,256]{1,0:T(8,128)(2,1)S(1)} %slice.23), channel_id=1, source_target_pairs={{0,3},{1,0},{2,1},{3,2},{4,7},{5,4},{6,5},{7,6},{8,11},{9,8},{10,9... | collective-permute-start | bytes 393224 | tf_op jit(solution)/shard_map/ppermute | solution.py:282
  97.3 0.0 all-to-all-done.2
  97.3 23.0 %all-gather = f32[128,128]{1,0:T(8,128)S(1)} all-gather(f32[32,128]{1,0:T(8,128)S(1)} %reduce_sum.30), channel_id=2, replica_groups={{0,1,2,3},{4,5,6,7},{8,9,10,11},{12,13,14,15},{16,17,18,19},{20,21,22,2..., dimensions={0}, use_global_device_ids=true | all-gather | bytes 81920 | tf_op jit(solution)/shard_map/all_gather | solution.py:285
  120.3 0.1 multiply_convert_fusion
  120.4 8.1 %all_to_all.32.whole = bf16[4,32,128]{2,1,0:T(8,128)(2,1)S(1)} all-to-all(bf16[4,32,128]{2,1,0:T(8,128)(2,1)S(1)} %broadcast_in_dim.24), channel_id=1, replica_groups={{0,4,8,12},{1,5,9,13},{2,6,10,14},{3,7,11,15},{16,20,24,28},{17,21,25,2..., dimensions={0} | all-to-all | bytes 65536 | tf_op jit(solution)/shard_map/all_to_all | solution.py:288
  128.5 0.0 collective-permute-done.3
  128.5 1.3 pad_maximum_fusion.own
  129.7 4.1 %collective-permute-start.5 = (bf16[4,512,256]{2,1,0:T(8,128)(2,1)S(1)}, bf16[4,512,256]{2,1,0:T(8,128)(2,1)}, u32[]{:S(2)}, u32[]{:S(2)}) collective-permute-start(bf16[4,512,256]{2,1,0:T(8,128)(2,1)S(1)} %pad_maximum_fusion.own), channel_id=1, source_target_pairs={{0,4},{1,5},{2,6},{3,7},{4,8},{5,9},{6,10},{7,11},{8,12},{9,13},{1... | collective-permute-start | bytes 3145736 | tf_op jit(solution)/shard_map/ppermute | solution.py:293
  133.9 1.9 collective-permute-start.6
  135.8 1.9 collective-permute-start.9
  137.8 1.2 terms.1
  139.0 0.0 copy-start.8
  139.0 0.6 copy-done.8
  139.6 2.4 %collective-permute-start.10 = (f32[32,1152]{1,0:T(8,128)S(1)}, f32[32,1152]{1,0:T(8,128)S(1)}, u32[]{:S(2)}, u32[]{:S(2)}) collective-permute-start(f32[32,1152]{1,0:T(8,128)S(1)} %get-tuple-element.39.term), channel_id=1, source_target_pairs={{0,16},{16,0},{32,48},{48,32},{64,80},{80,64},{96,112},{112,96},{1... | collective-permute-start | bytes 442376 | tf_op jit(solution)/shard_map/ppermute | solution.py:305
  142.0 1.0 collective-permute-done.10.term_other
  143.0 1.5 dense.1
  144.5 4.2 %all-to-all-start.4 = ((bf16[4,4,16,1152]{3,2,1,0:T(8,128)(2,1)}), bf16[4,4,16,1152]{3,2,1,0:T(8,128)(2,1)}, u32[]{:S(2)}, u32[]{:S(2)}) async-start(bf16[4,4,16,1152]{3,2,1,0:T(8,128)(2,1)} %bitcast.15), calls=%async_computation.4 | async-start | bytes 1179648 | tf_op jit(solution)/shard_map/all_to_all | solution.py:316
  148.7 0.0 copy-start.3
  148.7 0.7 collective-permute-done.5.back
  149.4 1.9 slice.28
  151.3 5.2 %collective-permute-start.7 = (bf16[4,256,256]{2,1,0:T(8,128)(2,1)}, bf16[4,256,256]{2,1,0:T(8,128)(2,1)S(1)}, u32[]{:S(2)}, u32[]{:S(2)}) collective-permute-start(bf16[4,256,256]{2,1,0:T(8,128)(2,1)} %slice.28), channel_id=1, source_target_pairs={{0,4},{1,5},{2,6},{3,7},{4,8},{5,9},{6,10},{7,11},{8,12},{9,13},{1... | collective-permute-start | bytes 1572872 | tf_op jit(solution)/shard_map/ppermute | solution.py:334
  156.4 1.9 slice.29
  158.3 1.9 collective-permute-start.8
  160.2 1.8 reduce_sum.32
  162.1 13.4 %all-to-all-start.5 = ((bf16[4,16,1152]{2,1,0:T(8,128)(2,1)}), bf16[4,16,1152]{2,1,0:T(8,128)(2,1)S(1)}, u32[]{:S(2)}, u32[]{:S(2)}) async-start(bf16[4,16,1152]{2,1,0:T(8,128)(2,1)} %reduce_sum.32), calls=%async_computation.5 | async-start | bytes 294912 | tf_op jit(solution)/shard_map/all_to_all | solution.py:318
  175.5 0.6 pad_add_fusion.y_s
  176.0 1.4 slice.26.pair_a
  177.5 3.9 %all-to-all-done.5.incoming = bf16[4,16,1152]{2,1,0:T(8,128)(2,1)S(1)} async-done(((bf16[4,16,1152]{2,1,0:T(8,128)(2,1)}), bf16[4,16,1152]{2,1,0:T(8,128)(2,1)S(1)}, u32[]{:S(2)}, u32[]{:S(2)}) %all-to-all-start.5) | async-done | bytes 147488 | tf_op jit(solution)/shard_map/all_to_all | solution.py:318
  181.4 0.9 copy-done.5
  182.3 0.8 copy-done.10
  183.1 0.7 copy-done.13
  183.8 0.8 adam.1
  184.6 0.0 collective-permute-done.7.far_top
  184.6 0.0 collective-permute-done.8.far_low
  184.6 0.0 all-gather.3.cloned.1.call-done.down
  184.7 3.1 %copy-done = bf16[896,4096]{1,0:T(8,128)(2,1)S(1)} copy-done((bf16[896,4096]{1,0:T(8,128)(2,1)S(1)}, bf16[896,4096]{1,0:T(8,128)(2,1)}, u32[]{:S(2)}) %copy-start) | copy-done | bytes 7340056
  187.7 0.8 copy-done.4
  188.5 0.8 copy-done.9
  189.3 0.6 copy-done.16
  189.9 15.5 %finish.1 = (bf16[512,896]{1,0:T(8,128)(2,1)}, bf16[512,896]{1,0:T(8,128)(2,1)}) custom-call(s32[2]{0:T(128)S(1)} %copy-done.16, bf16[4,512,256]{2,1,0:T(8,128)(2,1)S(1)} %pad_maximum_fusion.own, bf16[4,512,256]{2,1,0:T(8,128)(2,1)} %collective-permute-done.5.back, bf16[4,512,256]{2,1,0:T(8,128)(2,1)} %collective-permute-done.6.ahead, ...), custom_call_target="tpu_custom_call" | custom-call | tf_op jit(solution)/shard_map/finish/pallas_call | solution.py:348
  (29 shorter events, 0.1 us)
Async XLA Ops:
  7.2 47.3 %copy-start.1 = (bf16[512,896]{1,0:T(8,128)(2,1)S(1)}, bf16[512,896]{1,0:T(8,128)(2,1)}, u32[]{:S(2)}) copy-start(bf16[512,896]{1,0:T(8,128)(2,1)} %up.1) | copy-start | bytes 2752516
  7.2 47.3 %copy-start.2 = (bf16[512,896]{1,0:T(8,128)(2,1)S(1)}, bf16[512,896]{1,0:T(8,128)(2,1)}, u32[]{:S(2)}) copy-start(bf16[512,896]{1,0:T(8,128)(2,1)} %gate.1) | copy-start | bytes 2752516
  7.2 177.4 %all-gather.3.cloned.1.call-start = ((), (), s32[]{:S(2)}) async-start(), calls=%async_computation.6 | async-start | bytes 7569408 | tf_op jit(solution)/shard_map/all_gather | solution.py:238
  7.9 0.8 copy-start.6
  8.7 0.7 copy-start.11
  9.5 0.7 copy-start.14
  10.1 0.7 copy-start.15
  40.1 15.0 %collective-permute-start.2 = (bf16[16,16,1280]{2,1,0:T(8,128)(2,1)S(1)}, bf16[16,16,1280]{2,1,0:T(8,128)(2,1)}, u32[]{:S(2)}, u32[]{:S(2)}) collective-permute-start(bf16[16,16,1280]{2,1,0:T(8,128)(2,1)S(1)} %bitcast.19), channel_id=1, source_target_pairs={{0,16},{16,0},{32,48},{48,32},{64,80},{80,64},{96,112},{112,96},{1... | collective-permute-start | bytes 1966088 | tf_op jit(solution)/shard_map/ppermute | solution.py:265
  42.0 36.1 %collective-permute-start = (bf16[512,256]{1,0:T(8,128)(2,1)}, bf16[512,256]{1,0:T(8,128)(2,1)}, u32[]{:S(2)}, u32[]{:S(2)}) collective-permute-start(bf16[512,256]{1,0:T(8,128)(2,1)} %cot.3), channel_id=1, source_target_pairs={{0,1},{1,2},{2,3},{3,0},{4,5},{5,6},{6,7},{7,4},{8,9},{9,10},{10,1... | collective-permute-start | bytes 786440 | tf_op jit(solution)/shard_map/ppermute | solution.py:258
  51.1 27.0 %collective-permute-start.1 = (bf16[512,256]{1,0:T(8,128)(2,1)}, bf16[512,256]{1,0:T(8,128)(2,1)}, u32[]{:S(2)}, u32[]{:S(2)}) collective-permute-start(bf16[512,256]{1,0:T(8,128)(2,1)} %cot.3), channel_id=1, source_target_pairs={{0,3},{1,0},{2,1},{3,2},{4,7},{5,4},{6,5},{7,6},{8,11},{9,8},{10,9... | collective-permute-start | bytes 786440 | tf_op jit(solution)/shard_map/ppermute | solution.py:259
  57.3 0.6 copy-start.7
  58.0 0.6 copy-start.12
  78.1 19.2 %all-to-all-start.2 = ((f32[4,32,128]{2,1,0:T(8,128)}), f32[4,32,128]{2,1,0:T(8,128)S(1)}, u32[]{:S(2)}, u32[]{:S(2)}) async-start(f32[4,32,128]{2,1,0:T(8,128)} %get-tuple-element.30), calls=%async_computation.2 | async-start | bytes 131072 | tf_op jit(solution)/shard_map/all_to_all | solution.py:284
  83.7 44.8 %collective-permute-start.3 = (bf16[256,256]{1,0:T(8,128)(2,1)S(1)}, bf16[256,256]{1,0:T(8,128)(2,1)S(1)}, u32[]{:S(2)}, u32[]{:S(2)}) collective-permute-start(bf16[256,256]{1,0:T(8,128)(2,1)S(1)} %slice.22), channel_id=1, source_target_pairs={{0,1},{1,2},{2,3},{3,0},{4,5},{5,6},{6,7},{7,4},{8,9},{9,10},{10,1... | collective-permute-start | bytes 393224 | tf_op jit(solution)/shard_map/ppermute | solution.py:281
  93.9 34.6 %collective-permute-start.4 = (bf16[256,256]{1,0:T(8,128)(2,1)S(1)}, bf16[256,256]{1,0:T(8,128)(2,1)S(1)}, u32[]{:S(2)}, u32[]{:S(2)}) collective-permute-start(bf16[256,256]{1,0:T(8,128)(2,1)S(1)} %slice.23), channel_id=1, source_target_pairs={{0,3},{1,0},{2,1},{3,2},{4,7},{5,4},{6,5},{7,6},{8,11},{9,8},{10,9... | collective-permute-start | bytes 393224 | tf_op jit(solution)/shard_map/ppermute | solution.py:282
  129.7 19.6 %collective-permute-start.5 = (bf16[4,512,256]{2,1,0:T(8,128)(2,1)S(1)}, bf16[4,512,256]{2,1,0:T(8,128)(2,1)}, u32[]{:S(2)}, u32[]{:S(2)}) collective-permute-start(bf16[4,512,256]{2,1,0:T(8,128)(2,1)S(1)} %pad_maximum_fusion.own), channel_id=1, source_target_pairs={{0,4},{1,5},{2,6},{3,7},{4,8},{5,9},{6,10},{7,11},{8,12},{9,13},{1... | collective-permute-start | bytes 3145736 | tf_op jit(solution)/shard_map/ppermute | solution.py:293
  133.9 22.5 %collective-permute-start.6 = (bf16[4,512,256]{2,1,0:T(8,128)(2,1)S(1)}, bf16[4,512,256]{2,1,0:T(8,128)(2,1)}, u32[]{:S(2)}, u32[]{:S(2)}) collective-permute-start(bf16[4,512,256]{2,1,0:T(8,128)(2,1)S(1)} %pad_maximum_fusion.own), channel_id=1, source_target_pairs={{0,12},{1,13},{2,14},{3,15},{4,0},{5,1},{6,2},{7,3},{8,4},{9,5},{1... | collective-permute-start | bytes 3145736 | tf_op jit(solution)/shard_map/ppermute | solution.py:294
  135.8 6.2 %collective-permute-start.9 = (s32[8,128]{1,0:T(8,128)S(1)}, s32[8,128]{1,0:T(8,128)S(1)}, u32[]{:S(2)}, u32[]{:S(2)}) collective-permute-start(s32[8,128]{1,0:T(8,128)S(1)} %get-tuple-element.25), channel_id=1, source_target_pairs={{0,16},{16,0},{32,48},{48,32},{64,80},{80,64},{96,112},{112,96},{1... | collective-permute-start | bytes 12296 | tf_op jit(solution)/shard_map/ppermute | solution.py:255
  139.0 0.6 copy-start.8
  139.6 3.4 %collective-permute-start.10 = (f32[32,1152]{1,0:T(8,128)S(1)}, f32[32,1152]{1,0:T(8,128)S(1)}, u32[]{:S(2)}, u32[]{:S(2)}) collective-permute-start(f32[32,1152]{1,0:T(8,128)S(1)} %get-tuple-element.39.term), channel_id=1, source_target_pairs={{0,16},{16,0},{32,48},{48,32},{64,80},{80,64},{96,112},{112,96},{1... | collective-permute-start | bytes 442376 | tf_op jit(solution)/shard_map/ppermute | solution.py:305
  144.5 15.7 %all-to-all-start.4 = ((bf16[4,4,16,1152]{3,2,1,0:T(8,128)(2,1)}), bf16[4,4,16,1152]{3,2,1,0:T(8,128)(2,1)}, u32[]{:S(2)}, u32[]{:S(2)}) async-start(bf16[4,4,16,1152]{3,2,1,0:T(8,128)(2,1)} %bitcast.15), calls=%async_computation.4 | async-start | bytes 1179648 | tf_op jit(solution)/shard_map/all_to_all | solution.py:316
  148.7 35.9 %copy-start.3 = (bf16[512,896]{1,0:T(8,128)(2,1)S(1)}, bf16[512,896]{1,0:T(8,128)(2,1)}, u32[]{:S(2)}) copy-start(bf16[512,896]{1,0:T(8,128)(2,1)} %gate.1) | copy-start | bytes 2752516
  151.3 33.3 %collective-permute-start.7 = (bf16[4,256,256]{2,1,0:T(8,128)(2,1)}, bf16[4,256,256]{2,1,0:T(8,128)(2,1)S(1)}, u32[]{:S(2)}, u32[]{:S(2)}) collective-permute-start(bf16[4,256,256]{2,1,0:T(8,128)(2,1)} %slice.28), channel_id=1, source_target_pairs={{0,4},{1,5},{2,6},{3,7},{4,8},{5,9},{6,10},{7,11},{8,12},{9,13},{1... | collective-permute-start | bytes 1572872 | tf_op jit(solution)/shard_map/ppermute | solution.py:334
  158.3 26.3 %collective-permute-start.8 = (bf16[4,256,256]{2,1,0:T(8,128)(2,1)}, bf16[4,256,256]{2,1,0:T(8,128)(2,1)}, u32[]{:S(2)}, u32[]{:S(2)}) collective-permute-start(bf16[4,256,256]{2,1,0:T(8,128)(2,1)} %slice.29), channel_id=1, source_target_pairs={{0,12},{1,13},{2,14},{3,15},{4,0},{5,1},{6,2},{7,3},{8,4},{9,5},{1... | collective-permute-start | bytes 1572872 | tf_op jit(solution)/shard_map/ppermute | solution.py:335
  162.1 19.3 %all-to-all-start.5 = ((bf16[4,16,1152]{2,1,0:T(8,128)(2,1)}), bf16[4,16,1152]{2,1,0:T(8,128)(2,1)S(1)}, u32[]{:S(2)}, u32[]{:S(2)}) async-start(bf16[4,16,1152]{2,1,0:T(8,128)(2,1)} %reduce_sum.32), calls=%async_computation.5 | async-start | bytes 294912 | tf_op jit(solution)/shard_map/all_to_all | solution.py:318
  181.4 0.9 copy-start.5
  182.3 0.8 copy-start.10
  183.1 0.7 copy-start.13
  184.6 3.1 %copy-start = (bf16[896,4096]{1,0:T(8,128)(2,1)S(1)}, bf16[896,4096]{1,0:T(8,128)(2,1)}, u32[]{:S(2)}) copy-start(bf16[896,4096]{1,0:T(8,128)(2,1)} %all-gather.3.cloned.1.call-done.down) | copy-start | bytes 22020100
  187.7 0.8 copy-start.4
  188.5 0.8 copy-start.9
  189.3 0.6 copy-start.16
Sparse Core Ops, SparseCore 0:
  10.1 123.9 all-gather.2

commit v3 on v2

--- a/solution.py
+++ b/solution.py
@@ -25,12 +25,11 @@
 ALONG_Y = [[y * Z_HI + h for y in range(Y)] for h in range(Z_HI)]
 ALONG_Z_HI = [[y * Z_HI + h for h in range(Z_HI)] for y in range(Y)]
 OTHER_CORE = [(d, d ^ 1) for d in range(X * Z_LO * CORES)]
-NEXT_Z = [(y * Z_HI + h, y * Z_HI + (h + 1) % Z_HI) for y in range(Y) for h in range(Z_HI)]
-LAST_Z = [(y * Z_HI + h, y * Z_HI + (h - 1) % Z_HI) for y in range(Y) for h in range(Z_HI)]
 NEXT_Y = [(y * Z_HI + h, (y + 1) % Y * Z_HI + h) for y in range(Y) for h in range(Z_HI)]
 LAST_Y = [(y * Z_HI + h, (y - 1) % Y * Z_HI + h) for y in range(Y) for h in range(Z_HI)]
 
 VMEM = pl.BlockSpec(memory_space=pltpu.VMEM)
+WHOLE = pl.BlockSpec()
 SMEM = pl.BlockSpec(memory_space=pltpu.SMEM)
 
 
@@ -69,10 +68,9 @@
     digits = digits.astype(jnp.float32).astype(jnp.bfloat16)
     a = factor_a[...].astype(jnp.bfloat16)
     b = factor_b[...].astype(jnp.bfloat16)
-    for copy in range(packed.shape[0]):
-        packed[copy, :, :hid] = a
-        packed[copy, :, hid : hid + feat] = b
-        packed[copy, :, hid + feat :] = digits
+    packed[:, :hid] = a
+    packed[:, hid : hid + feat] = b
+    packed[:, hid + feat :] = digits
     lane_i = lax.broadcasted_iota(jnp.int32, info_v.shape, 1)
     info_v[...] = jnp.where(
         lane_i == INFO_FIRST, slot_first, jnp.where(lane_i == INFO_LAST, slot_last, cut)
@@ -103,23 +101,22 @@
     grad = nt_dot(pair[:, hid:], cot[...])
     proj = jnp.where(in_first, proj[:rank], proj[rank:])
     grad = jnp.where(in_first, grad[:rank], grad[rank:])
-    width = tok // Y
     for y in range(Y):
-        part[y, :rank, :] = proj[:, y * width : (y + 1) * width]
-        part[y, rank:, :] = grad[:, y * width : (y + 1) * width]
+        part[y, :rank, :] = proj
+        part[y, rank:, :] = grad
     digits = own[:, :, hid + feat :].astype(jnp.float32)
     digits = digits + other[:, :, hid + feat :].astype(jnp.float32)
     totals[...] = jnp.sum(digits, axis=0)
 
 
-def terms(info_s, whole, hidden, cot, grad_rows, term):
-    rank = whole.shape[1] // 2
+def terms(info_s, sums, hidden, cot, grad_rows, term):
+    rank = sums.shape[1] // 2
     hid = hidden.shape[1]
     tok = hidden.shape[0]
-    rows = jnp.concatenate([whole[y] for y in range(Y)], axis=1)
+    rows = jnp.sum(sums[...], axis=0)
     in_first = lax.broadcasted_iota(jnp.int32, (rank, tok), 1) < info_s[INFO_CUT]
-    proj = rows[:rank].astype(jnp.float32)
-    grad = rows[rank:].astype(jnp.float32)
+    proj = rows[:rank]
+    grad = ADAPTER_SCALE * rows[rank:]
     zero = jnp.zeros_like(proj)
 
     def by_run(values):
@@ -173,34 +170,31 @@
 
 
 def finish(
-    y_s, own, back, ahead, far_top, far_low, down, grad_rows, pair_a, gate, up, out_gate, out_up, total
+    place_s, own, back, ahead, far_low, far_high, down_own, down_back, down_ahead, down_far,
+    grad_rows, pair_a, gate, up, out_gate, out_up, total, far
 ):
-    place, turn = pl.program_id(0), pl.program_id(1)
-    half = far_top.shape[1]
-    weights = down[...]
-
-    @pl.when((place == 0) & (turn == 0))
+    place = pl.program_id(0)
+
+    @pl.when(place == 0)
     def _():
         total[...] = tn_dot(grad_rows[...], pair_a[...])
 
-    @pl.when(turn == 0)
+    @pl.when(place < 2)
     def _():
-        total[...] += nt_dot(own[0], weights)
-
-    @pl.when(turn == 1)
+        far[...] = far_low[0]
+
+    @pl.when(place >= 2)
     def _():
-        total[...] += nt_dot(back[0], weights)
-
-    @pl.when(turn == 2)
-    def _():
-        total[...] += nt_dot(ahead[0], weights)
-
-    @pl.when(turn == 3)
-    def _():
-        total[:half, :] += nt_dot(far_top[0], weights)
-        total[half:, :] += nt_dot(far_low[0], weights)
-
-    @pl.when((place == pl.num_programs(0) - 1) & (turn == pl.num_programs(1) - 1))
+        far[...] = far_high[0]
+
+    total[...] += (
+        nt_dot(own[0], down_own[...])
+        + nt_dot(back[0], down_back[...])
+        + nt_dot(ahead[0], down_ahead[...])
+        + nt_dot(far[...], down_far[...])
+    )
+
+    @pl.when(place == pl.num_programs(0) - 1)
     def _():
         gate_f = gate[...].astype(jnp.float32)
         up_f = up[...].astype(jnp.float32)
@@ -226,8 +220,7 @@
 ):
     me = lax.axis_index("dp").astype(jnp.int32)
     core_s = (me & (CORES - 1)).reshape(1)
-    tensor = lax.axis_index("tensor").astype(jnp.int32)
-    y_s = jnp.stack([lax.shift_right_logical(tensor, 2), tensor & (Z_HI - 1)])
+    y_s = lax.shift_right_logical(lax.axis_index("tensor").astype(jnp.int32), 2).reshape(1)
     rank, hid = adapter_input_factors.shape[1:]
     feat = adapter_output_factors.shape[2]
     tok = gate_logits.shape[0]
@@ -239,10 +232,10 @@
 
     packed, info_v = pl.pallas_call(
         prepare,
-        out_shape=(shape((Z_LO, rank, wide + LANES), bf16), shape((8, LANES), jnp.int32)),
-        in_specs=[SMEM, SMEM, VMEM, VMEM, VMEM],
-        out_specs=(VMEM, VMEM),
-        compiler_params=params(),
+        out_shape=(shape((rank, wide + LANES), bf16), shape((8, LANES), jnp.int32)),
+        in_specs=[SMEM, SMEM, WHOLE, WHOLE, WHOLE],
+        out_specs=(WHOLE, WHOLE),
+        compiler_params=params(56),
         name="prepare",
     )(
         batch_tenants,
@@ -251,23 +244,23 @@
         adapter_input_factors[0],
         adapter_output_factors[0],
     )
-    column = lax.all_to_all(packed, "dp", 0, 0, axis_index_groups=ALONG_Z_LO)
+    cot_z = lax.all_to_all(
+        spread(Z_HI, output_gradient), "tensor", 0, 0, axis_index_groups=ALONG_Z_HI
+    )
     info_other_v = lax.ppermute(info_v, "dp", OTHER_CORE)
     info_s, info_other_s = info_v[0, :8], info_other_v[0, :8]
-    half = tok // 2
-    z_back = lax.ppermute(output_gradient, "tensor", NEXT_Z)
-    z_ahead = lax.ppermute(output_gradient, "tensor", LAST_Z)
     hidden = (
         jax.nn.silu(gate_logits.astype(f32)) * up_projected.astype(f32)
     ).astype(bf16)
-    plane = lax.all_to_all(spread(X, column), "dp", 0, 0, axis_index_groups=ALONG_X)
+    column = lax.all_gather(packed, "dp", axis_index_groups=ALONG_Z_LO)
+    plane = lax.all_gather(column, "dp", axis_index_groups=ALONG_X)
     own = plane.reshape(X * Z_LO, rank, wide + LANES)
     other = lax.ppermute(own, "dp", OTHER_CORE)
 
     part, pair, totals = pl.pallas_call(
         low_rank,
         out_shape=(
-            shape((Y, 2 * rank, tok // Y), f32),
+            shape((Y, 2 * rank, tok), f32),
             shape((2 * rank, wide), bf16),
             shape((rank, LANES), f32),
         ),
@@ -277,21 +270,16 @@
         name="low_rank",
     )(info_s, core_s, own, other, hidden, output_gradient)
 
-    z_back, z_ahead, part = lax.optimization_barrier((z_back, z_ahead, part))
-    z_far_top = lax.ppermute(z_back[:half], "tensor", NEXT_Z)
-    z_far_low = lax.ppermute(z_ahead[half:], "tensor", LAST_Z)
-
-    chunk = jnp.sum(lax.all_to_all(part, "tensor", 0, 0, axis_index_groups=ALONG_Y), axis=0)
-    chunk = jnp.sum(lax.all_gather(chunk, "tensor", axis_index_groups=ALONG_Z_HI), axis=0)
-    scale = jnp.where(jnp.arange(2 * rank)[:, None] < rank, 1.0, ADAPTER_SCALE)
-    rounded = (scale * chunk).astype(bf16)
-    whole = lax.all_to_all(spread(Y, rounded), "tensor", 0, 0, axis_index_groups=ALONG_Y)
-
-    z_far_top, z_far_low, whole = lax.optimization_barrier((z_far_top, z_far_low, whole))
-    z_far = jnp.concatenate([z_far_top, z_far_low])
-    cot_z = jnp.stack([output_gradient, z_back, z_ahead, z_far])
+    cot_z, part = lax.optimization_barrier((cot_z, part))
     back = lax.ppermute(cot_z, "tensor", NEXT_Y)
     ahead = lax.ppermute(cot_z, "tensor", LAST_Y)
+
+    sums = jnp.sum(lax.all_to_all(part, "tensor", 0, 0, axis_index_groups=ALONG_Y), axis=0)
+    sums = lax.all_gather(sums, "tensor", axis_index_groups=ALONG_Z_HI)
+    back, ahead, sums = lax.optimization_barrier((back, ahead, sums))
+    half = Z_HI // 2
+    far_low = lax.ppermute(back[:half], "tensor", NEXT_Y)
+    far_high = lax.ppermute(ahead[half:], "tensor", LAST_Y)
 
     grad_rows, term = pl.pallas_call(
         terms,
@@ -300,7 +288,7 @@
         out_specs=(VMEM, VMEM),
         compiler_params=params(),
         name="terms",
-    )(info_s, whole, hidden, output_gradient)
+    )(info_s, sums, hidden, output_gradient)
 
     term_other = lax.ppermute(term, "dp", OTHER_CORE)
     outgoing = pl.pallas_call(
@@ -325,56 +313,60 @@
             shape(adapter_input_factors.shape, f32),
             shape(adapter_output_factors.shape, f32),
         ),
-        in_specs=[SMEM, VMEM, VMEM, VMEM, VMEM],
-        out_specs=(VMEM,) * 4,
-        compiler_params=params(),
+        in_specs=[SMEM, WHOLE, WHOLE, WHOLE, WHOLE],
+        out_specs=(WHOLE,) * 4,
+        compiler_params=params(56),
         name="adam",
     )(me.reshape(1), totals, incoming, input_moments, output_moments)
 
-    far_top = lax.ppermute(back[:, :half], "tensor", NEXT_Y)
-    far_low = lax.ppermute(ahead[:, half:], "tensor", LAST_Y)
-
-    def down_block(place, turn, y_ref):
-        y_off = jnp.where(turn == 1, Y - 1, jnp.where(turn == 2, 1, jnp.where(turn == 3, 2, 0)))
-        z_off = jnp.where(place == 1, Z_HI - 1, jnp.where(place == 2, 1, jnp.where(place == 3, 2, 0)))
-        return 0, lax.rem(y_ref[0] + y_off, Y) * Z_HI + lax.rem(y_ref[1] + z_off, Z_HI)
-
-    def by_place(rows):
-        return pl.BlockSpec((1, rows, feat), lambda place, turn, y_ref: (place, 0, 0))
+    def down_block(ahead_by):
+        return pl.BlockSpec(
+            (hid, feat),
+            lambda place, y_ref: (0, lax.rem(y_ref[0] + ahead_by, Y) * Z_HI + place),
+        )
+
+    def by_place(index):
+        return pl.BlockSpec((1, tok, feat), lambda place, y_ref: (index(place), 0, 0))
 
     def whole_of(rows, columns):
-        return pl.BlockSpec((rows, columns), lambda place, turn, y_ref: (0, 0))
+        return pl.BlockSpec((rows, columns), lambda place, y_ref: (0, 0))
 
     grad_gate, grad_up = pl.pallas_call(
         finish,
         out_shape=(shape((tok, hid), bf16), shape((tok, hid), bf16)),
         grid_spec=pltpu.PrefetchScalarGridSpec(
             num_scalar_prefetch=1,
-            grid=(Z_HI, Y),
+            grid=(Z_HI,),
             in_specs=[
-                by_place(tok),
-                by_place(tok),
-                by_place(tok),
-                by_place(half),
-                by_place(half),
-                pl.BlockSpec((hid, feat), down_block),
+                by_place(lambda place: place),
+                by_place(lambda place: place),
+                by_place(lambda place: place),
+                by_place(lambda place: jnp.minimum(place, half - 1)),
+                by_place(lambda place: jnp.maximum(place - half, 0)),
+                down_block(0),
+                down_block(Y - 1),
+                down_block(1),
+                down_block(2),
                 whole_of(2 * rank, tok),
                 whole_of(2 * rank, hid),
                 whole_of(tok, hid),
                 whole_of(tok, hid),
             ],
             out_specs=[whole_of(tok, hid), whole_of(tok, hid)],
-            scratch_shapes=[pltpu.VMEM((tok, hid), f32)],
+            scratch_shapes=[pltpu.VMEM((tok, hid), f32), pltpu.VMEM((tok, feat), bf16)],
         ),
-        compiler_params=params(),
+        compiler_params=params(56),
         name="finish",
     )(
         y_s,
         cot_z,
         back,
         ahead,
-        far_top,
         far_low,
+        far_high,
+        down_full,
+        down_full,
+        down_full,
         down_full,
         grad_rows,
         pair[:, :hid],

time: 216 us -> 222 us (1.028)
  blocking collectives: 59.6 us -> 101 us
  starting transfers between devices: 66.7 us -> 45.1 us
  local copies, waits for them, and re-layouts: 19.4 us -> 7.52 us
  waiting for transfers between devices: 25.8 us -> 31.1 us
  Pallas kernels: 22.1 us -> 18.6 us
    all_gather x1 -> x3, blocking collectives: 23 us -> 101 us  [the longest x1 64 us: shards(): column = lax.all_gather(packed, 'dp', axis_index_groups=ALONG_Z_LO)]
    all_to_all x3 -> x0, blocking collectives: 36.6 us -> none  [the longest x1 15.9 us: shards(): lax.all_to_all(spread(X, column), 'dp', 0, 0, axis_index_groups=ALONG_X)]
    ppermute x6 -> x2, starting transfers between devices: 32.2 us -> 5.83 us  [the longest x1 3.75 us: shards(): far_high = lax.ppermute(ahead[half:], 'tensor', LAST_Y)]
    all_to_all x1, waiting for transfers between devices: 0.01 us -> 21 us  [shards(): lax.all_to_all(part, 'tensor', 0, 0, axis_index_groups=ALONG_Y)]
    ppermute x6 -> x2, waiting for transfers between devices: 19.6 us -> 0.01 us  [the longest x1 0.01 us: shards(): far_low = lax.ppermute(back[:half], 'tensor', NEXT_Y)]
    all_to_all x0 -> x1, starting transfers between devices: none -> 15.2 us  [shards(): lax.all_to_all(spread(Z_HI, output_gradient), 'tensor', 0, 0, axis_index_...]
    unnamed x34 -> x18, local copies, waits for them, and re-layouts: 12.3 us -> 2.22 us
    all_to_all x1, starting transfers between devices: 13.4 us -> 3.84 us  [shards(): incoming = lax.all_to_all(by_x, 'dp', 0, 0, axis_index_groups=ALONG_Z_LO)]
  transfers between devices with their start and end apart: 15 -> 12, of which waited for: 4 -> 4; matrix products, arithmetic and copies ran while one was open for 5% -> 4% of each run, Pallas kernels for 3% -> 3%
where the time goes in v3:
time: 222 us; the launch traced here: 220 us
  blocking collectives  101 us (45%)
  starting transfers between devices  45.1 us (20%)
  waiting for transfers between devices  31.1 us (14%)
  Pallas kernels  18.6 us (8%)
  between operations  14.2 us (6%)
  local copies, waits for them, and re-layouts  7.52 us (3%)
  other arithmetic  2.56 us (1%)
    all_gather x1, blocking collectives, shards(): column = lax.all_gather(packed, 'dp', axis_index_groups=ALONG_Z_LO)  64 us
    all_gather x1, blocking collectives, shards(): sums = lax.all_gather(sums, 'tensor', axis_index_groups=ALONG_Z_HI)  22.8 us
    all_to_all x1, waiting for transfers between devices, shards(): lax.all_to_all(part, 'tensor', 0, 0, axis_index_groups=ALONG_Y)  21 us
    all_to_all x1, starting transfers between devices, shards(): lax.all_to_all(spread(Z_HI, output_gradient), 'tensor', 0, 0, axis_index_...  15.2 us
    all_gather x1, blocking collectives, shards(): plane = lax.all_gather(column, 'dp', axis_index_groups=ALONG_X)  13.8 us
    pallas_call x1, Pallas kernels, shards(): pl.pallas_call(finish, out_shape=(shape((tok, hid), bf16), shape((tok, hi...  11.1 us
    all_to_all x1, waiting for transfers between devices, shards(): incoming = lax.all_to_all(by_x, 'dp', 0, 0, axis_index_groups=ALONG_Z_LO)  5.38 us
    all_to_all x1, starting transfers between devices, shards(): lax.all_to_all(part, 'tensor', 0, 0, axis_index_groups=ALONG_Y)  4.85 us
  transfers between devices with their start and end apart: 12, of which 4 were waited for; matrix products, arithmetic and copies ran while one was open for 4% of the time, Pallas kernels for 3%

profile of v3, /device:TPU:24, one launch (start us, length us, event | category | flops | bytes accessed | tf_op | source)
XLA Modules:
  0.0 219.7 jit_solution(8292876190881937544)
XLA Ops:
  7.2 0.0 all-gather.5.cloned.1.call-start
  7.2 0.7 all-gather.5.cloned.1.call-update
  7.9 2.1 broadcast_in_dim.2
  10.0 0.0 copy-start.3
  10.0 15.2 %all-to-all-start = ((bf16[4,512,256]{2,1,0:T(8,128)(2,1)}), bf16[4,512,256]{2,1,0:T(8,128)(2,1)}, u32[]{:S(2)}, u32[]{:S(2)}) async-start(bf16[4,512,256]{2,1,0:T(8,128)(2,1)} %broadcast_in_dim.2), calls=%async_computation | async-start | bytes 2097152 | tf_op jit(solution)/shard_map/all_to_all | solution.py:247
  25.2 1.6 prepare.1
  26.8 64.0 %all-gather = bf16[64,1280]{1,0:T(8,128)(2,1)S(1)} all-gather(bf16[16,1280]{1,0:T(8,128)(2,1)} %get-tuple-element.25), channel_id=2, replica_groups={{0,32,64,96},{16,48,80,112},{128,160,192,224},{144,176,208,240},{256,28..., dimensions={0}, use_global_device_ids=true | all-gather | bytes 204800 | tf_op jit(solution)/shard_map/all_gather | solution.py:255
  90.8 0.0 copy-start
  90.8 13.8 %all-gather.1.own = bf16[16,16,1280]{2,1,0:T(8,128)(2,1)S(1)} all-gather(bf16[4,16,1280]{2,1,0:T(8,128)(2,1)S(1)} %bitcast.14), channel_id=3, replica_groups={{0,128,256,384},{16,144,272,400},{32,160,288,416},{48,176,304,432},{64,..., dimensions={0}, use_global_device_ids=true | all-gather | bytes 819200 | tf_op jit(solution)/shard_map/all_gather | solution.py:256
  104.6 1.9 collective-permute-start
  106.5 0.7 slice_bitcast_fusion.1.info_s
  107.2 0.0 copy-done.3
  107.2 1.8 fusion.4.hidden
  109.0 0.0 copy-start.8
  109.0 0.0 collective-permute-done.other
  109.0 0.0 copy-done
  109.0 1.7 low_rank.1
  110.8 0.0 copy-start.2
  110.8 0.6 copy-done.2
  111.4 0.0 all-to-all-done.own
  111.4 1.9 collective-permute-start.1
  113.3 3.9 %collective-permute-start.2 = (bf16[4,512,256]{2,1,0:T(8,128)(2,1)}, bf16[4,512,256]{2,1,0:T(8,128)(2,1)}, u32[]{:S(2)}, u32[]{:S(2)}) collective-permute-start(bf16[4,512,256]{2,1,0:T(8,128)(2,1)} %all-to-all-done.own), channel_id=1, source_target_pairs={{0,12},{1,13},{2,14},{3,15},{4,0},{5,1},{6,2},{7,3},{8,4},{9,5},{1... | collective-permute-start | bytes 3145736 | tf_op jit(solution)/shard_map/ppermute | solution.py:275
  117.2 4.9 %all-to-all-start.1 = ((f32[4,32,512]{2,1,0:T(8,128)}), f32[4,32,512]{2,1,0:T(8,128)S(1)}, u32[]{:S(2)}, u32[]{:S(2)}) async-start(f32[4,32,512]{2,1,0:T(8,128)} %get-tuple-element.28), calls=%async_computation.1 | async-start | bytes 524288 | tf_op jit(solution)/shard_map/all_to_all | solution.py:277
  122.1 0.0 copy-done.8
  122.1 1.9 collective-permute-start.5
  124.0 21.0 %all-to-all-done.1 = f32[4,32,512]{2,1,0:T(8,128)S(1)} async-done(((f32[4,32,512]{2,1,0:T(8,128)}), f32[4,32,512]{2,1,0:T(8,128)S(1)}, u32[]{:S(2)}, u32[]{:S(2)}) %all-to-all-start.1) | async-done | bytes 262176 | tf_op jit(solution)/shard_map/all_to_all | solution.py:277
  145.0 22.8 %all-gather.2 = f32[128,512]{1,0:T(8,128)S(1)} all-gather(f32[32,512]{1,0:T(8,128)S(1)} %reduce_sum.21), channel_id=4, replica_groups={{0,1,2,3},{4,5,6,7},{8,9,10,11},{12,13,14,15},{16,17,18,19},{20,21,22,2..., dimensions={0}, use_global_device_ids=true | all-gather | bytes 327680 | tf_op jit(solution)/shard_map/all_gather | solution.py:278
  167.7 0.0 collective-permute-done.1.back
  167.8 0.0 copy-start.4
  167.8 0.0 collective-permute-done.2.ahead
  167.8 0.8 terms.1
  168.6 0.0 copy-start.1
  168.6 1.9 collective-permute-start.6
  170.5 0.0 collective-permute-done.5
  170.6 1.3 collective-permute-done.6.term_other
  171.9 1.5 dense.1
  173.4 3.8 %all-to-all-start.2 = ((bf16[4,4,16,1152]{3,2,1,0:T(8,128)(2,1)}), bf16[4,4,16,1152]{3,2,1,0:T(8,128)(2,1)S(1)}, u32[]{:S(2)}, u32[]{:S(2)}) async-start(bf16[4,4,16,1152]{3,2,1,0:T(8,128)(2,1)} %bitcast.10), calls=%async_computation.2 | async-start | bytes 1179648 | tf_op jit(solution)/shard_map/all_to_all | solution.py:304
  177.2 0.8 slice.16
  178.0 0.0 copy-done.4
  178.0 2.1 collective-permute-start.3
  180.1 1.1 slice.17
  181.2 0.0 copy-done.1
  181.2 3.8 %collective-permute-start.4 = (bf16[2,512,256]{2,1,0:T(8,128)(2,1)S(1)}, bf16[2,512,256]{2,1,0:T(8,128)(2,1)S(1)}, u32[]{:S(2)}, u32[]{:S(2)}) collective-permute-start(bf16[2,512,256]{2,1,0:T(8,128)(2,1)S(1)} %slice.17), channel_id=1, source_target_pairs={{0,12},{1,13},{2,14},{3,15},{4,0},{5,1},{6,2},{7,3},{8,4},{9,5},{1... | collective-permute-start | bytes 1572872 | tf_op jit(solution)/shard_map/ppermute | solution.py:282
  185.0 2.7 %all-to-all-done.2 = bf16[4,4,16,1152]{3,2,1,0:T(8,128)(2,1)S(1)} async-done(((bf16[4,4,16,1152]{3,2,1,0:T(8,128)(2,1)}), bf16[4,4,16,1152]{3,2,1,0:T(8,128)(2,1)S(1)}, u32[]{:S(2)}, u32[]{:S(2)}) %all-to-all-start.2) | async-done | bytes 589856 | tf_op jit(solution)/shard_map/all_to_all | solution.py:304
  187.7 0.8 reduce_sum.22
  188.5 3.8 %all-to-all-start.3 = ((bf16[4,16,1152]{2,1,0:T(8,128)(2,1)}), bf16[4,16,1152]{2,1,0:T(8,128)(2,1)S(1)}, u32[]{:S(2)}, u32[]{:S(2)}) async-start(bf16[4,16,1152]{2,1,0:T(8,128)(2,1)} %reduce_sum.22), calls=%async_computation.3 | async-start | bytes 294912 | tf_op jit(solution)/shard_map/all_to_all | solution.py:306
  192.3 0.6 slice.18.pair_a
  192.9 5.4 %all-to-all-done.3.incoming = bf16[4,16,1152]{2,1,0:T(8,128)(2,1)S(1)} async-done(((bf16[4,16,1152]{2,1,0:T(8,128)(2,1)}), bf16[4,16,1152]{2,1,0:T(8,128)(2,1)S(1)}, u32[]{:S(2)}, u32[]{:S(2)}) %all-to-all-start.3) | async-done | bytes 147488 | tf_op jit(solution)/shard_map/all_to_all | solution.py:306
  198.3 0.0 copy-start.5
  198.3 0.7 copy-done.5
  199.0 1.8 adam.1
  200.8 0.0 collective-permute-done.3.far_low
  200.8 0.0 copy-start.6
  200.8 0.0 collective-permute-done.4.far_high
  200.8 0.0 copy-start.7
  200.8 0.0 all-gather.5.cloned.1.call-done.down_own.down_back.down_ahead.down_far
  200.8 0.8 copy-done.6
  201.6 0.2 copy-done.7
  201.8 11.1 %finish.1 = (bf16[512,896]{1,0:T(8,128)(2,1)}, bf16[512,896]{1,0:T(8,128)(2,1)}) custom-call(s32[1]{0:T(128)} %bitcast.place_s, bf16[4,512,256]{2,1,0:T(8,128)(2,1)} %all-to-all-done.own, bf16[4,512,256]{2,1,0:T(8,128)(2,1)} %copy-done.4, bf16[4,512,256]{2,1,0:T(8,128)(2,1)} %collective-permute-done.2.ahead, bf16[2,512,256]{2,1,0:T(8,128)(2,1)} %copy-done.6, ...), custom_call_target="tpu_custom_call" | custom-call | tf_op jit(solution)/shard_map/finish/pallas_call | solution.py:334
  (2 shorter events, 0.0 us)
Async XLA Ops:
  7.2 193.7 %all-gather.5.cloned.1.call-start = ((), (), s32[]{:S(2)}) async-start(), calls=%async_computation.4 | async-start | bytes 7569408 | tf_op jit(solution)/shard_map/all_gather | solution.py:231
  10.0 97.2 %copy-start.3 = (bf16[512,896]{1,0:T(8,128)(2,1)S(1)}, bf16[512,896]{1,0:T(8,128)(2,1)}, u32[]{:S(2)}) copy-start(bf16[512,896]{1,0:T(8,128)(2,1)} %up.1) | copy-start | bytes 2752516
  10.0 101.4 %all-to-all-start = ((bf16[4,512,256]{2,1,0:T(8,128)(2,1)}), bf16[4,512,256]{2,1,0:T(8,128)(2,1)}, u32[]{:S(2)}, u32[]{:S(2)}) async-start(bf16[4,512,256]{2,1,0:T(8,128)(2,1)} %broadcast_in_dim.2), calls=%async_computation | async-start | bytes 2097152 | tf_op jit(solution)/shard_map/all_to_all | solution.py:247
  90.8 18.2 %copy-start = (bf16[512,256]{1,0:T(8,128)(2,1)S(1)}, bf16[512,256]{1,0:T(8,128)(2,1)}, u32[]{:S(2)}) copy-start(bf16[512,256]{1,0:T(8,128)(2,1)} %cot.3) | copy-start | bytes 786436
  104.6 4.4 %collective-permute-start = (bf16[16,16,1280]{2,1,0:T(8,128)(2,1)S(1)}, bf16[16,16,1280]{2,1,0:T(8,128)(2,1)S(1)}, u32[]{:S(2)}, u32[]{:S(2)}) collective-permute-start(bf16[16,16,1280]{2,1,0:T(8,128)(2,1)S(1)} %all-gather.1.own), channel_id=1, source_target_pairs={{0,16},{16,0},{32,48},{48,32},{64,80},{80,64},{96,112},{112,96},{1... | collective-permute-start | bytes 1966088 | tf_op jit(solution)/shard_map/ppermute | solution.py:258
  109.0 13.1 %copy-start.8 = (s32[8,128]{1,0:T(8,128)S(1)}, s32[8,128]{1,0:T(8,128)}, u32[]{:S(2)}) copy-start(s32[8,128]{1,0:T(8,128)} %get-tuple-element.24) | copy-start | bytes 12292
  110.8 0.6 copy-start.2
  111.4 56.4 %collective-permute-start.1 = (bf16[4,512,256]{2,1,0:T(8,128)(2,1)}, bf16[4,512,256]{2,1,0:T(8,128)(2,1)S(1)}, u32[]{:S(2)}, u32[]{:S(2)}) collective-permute-start(bf16[4,512,256]{2,1,0:T(8,128)(2,1)} %all-to-all-done.own), channel_id=1, source_target_pairs={{0,4},{1,5},{2,6},{3,7},{4,8},{5,9},{6,10},{7,11},{8,12},{9,13},{1... | collective-permute-start | bytes 3145736 | tf_op jit(solution)/shard_map/ppermute | solution.py:274
  113.3 54.5 %collective-permute-start.2 = (bf16[4,512,256]{2,1,0:T(8,128)(2,1)}, bf16[4,512,256]{2,1,0:T(8,128)(2,1)}, u32[]{:S(2)}, u32[]{:S(2)}) collective-permute-start(bf16[4,512,256]{2,1,0:T(8,128)(2,1)} %all-to-all-done.own), channel_id=1, source_target_pairs={{0,12},{1,13},{2,14},{3,15},{4,0},{5,1},{6,2},{7,3},{8,4},{9,5},{1... | collective-permute-start | bytes 3145736 | tf_op jit(solution)/shard_map/ppermute | solution.py:275
  117.2 27.7 %all-to-all-start.1 = ((f32[4,32,512]{2,1,0:T(8,128)}), f32[4,32,512]{2,1,0:T(8,128)S(1)}, u32[]{:S(2)}, u32[]{:S(2)}) async-start(f32[4,32,512]{2,1,0:T(8,128)} %get-tuple-element.28), calls=%async_computation.1 | async-start | bytes 524288 | tf_op jit(solution)/shard_map/all_to_all | solution.py:277
  122.1 48.4 %collective-permute-start.5 = (s32[8,128]{1,0:T(8,128)S(1)}, s32[8,128]{1,0:T(8,128)S(1)}, u32[]{:S(2)}, u32[]{:S(2)}) collective-permute-start(s32[8,128]{1,0:T(8,128)S(1)} %copy-done.8), channel_id=1, source_target_pairs={{0,16},{16,0},{32,48},{48,32},{64,80},{80,64},{96,112},{112,96},{1... | collective-permute-start | bytes 12296 | tf_op jit(solution)/shard_map/ppermute | solution.py:250
  167.8 10.3 %copy-start.4 = (bf16[4,512,256]{2,1,0:T(8,128)(2,1)}, bf16[4,512,256]{2,1,0:T(8,128)(2,1)S(1)}, u32[]{:S(2)}) copy-start(bf16[4,512,256]{2,1,0:T(8,128)(2,1)S(1)} %collective-permute-done.1.back) | copy-start | bytes 3145732
  168.6 12.6 %copy-start.1 = (bf16[32,512]{1,0:T(8,128)(2,1)}, bf16[32,512]{1,0:T(8,128)(2,1)S(1)}, u32[]{:S(2)}) copy-start(bf16[32,512]{1,0:T(8,128)(2,1)S(1)} %get-tuple-element.32.grad_rows) | copy-start | bytes 98308
  168.6 3.3 %collective-permute-start.6 = (f32[32,1152]{1,0:T(8,128)S(1)}, f32[32,1152]{1,0:T(8,128)S(1)}, u32[]{:S(2)}, u32[]{:S(2)}) collective-permute-start(f32[32,1152]{1,0:T(8,128)S(1)} %get-tuple-element.37.term), channel_id=1, source_target_pairs={{0,16},{16,0},{32,48},{48,32},{64,80},{80,64},{96,112},{112,96},{1... | collective-permute-start | bytes 442376 | tf_op jit(solution)/shard_map/ppermute | solution.py:293
  173.4 14.3 %all-to-all-start.2 = ((bf16[4,4,16,1152]{3,2,1,0:T(8,128)(2,1)}), bf16[4,4,16,1152]{3,2,1,0:T(8,128)(2,1)S(1)}, u32[]{:S(2)}, u32[]{:S(2)}) async-start(bf16[4,4,16,1152]{3,2,1,0:T(8,128)(2,1)} %bitcast.10), calls=%async_computation.2 | async-start | bytes 1179648 | tf_op jit(solution)/shard_map/all_to_all | solution.py:304
  178.0 22.8 %collective-permute-start.3 = (bf16[2,512,256]{2,1,0:T(8,128)(2,1)}, bf16[2,512,256]{2,1,0:T(8,128)(2,1)S(1)}, u32[]{:S(2)}, u32[]{:S(2)}) collective-permute-start(bf16[2,512,256]{2,1,0:T(8,128)(2,1)} %slice.16), channel_id=1, source_target_pairs={{0,4},{1,5},{2,6},{3,7},{4,8},{5,9},{6,10},{7,11},{8,12},{9,13},{1... | collective-permute-start | bytes 1572872 | tf_op jit(solution)/shard_map/ppermute | solution.py:281
  181.2 19.6 %collective-permute-start.4 = (bf16[2,512,256]{2,1,0:T(8,128)(2,1)S(1)}, bf16[2,512,256]{2,1,0:T(8,128)(2,1)S(1)}, u32[]{:S(2)}, u32[]{:S(2)}) collective-permute-start(bf16[2,512,256]{2,1,0:T(8,128)(2,1)S(1)} %slice.17), channel_id=1, source_target_pairs={{0,12},{1,13},{2,14},{3,15},{4,0},{5,1},{6,2},{7,3},{8,4},{9,5},{1... | collective-permute-start | bytes 1572872 | tf_op jit(solution)/shard_map/ppermute | solution.py:282
  188.5 9.8 %all-to-all-start.3 = ((bf16[4,16,1152]{2,1,0:T(8,128)(2,1)}), bf16[4,16,1152]{2,1,0:T(8,128)(2,1)S(1)}, u32[]{:S(2)}, u32[]{:S(2)}) async-start(bf16[4,16,1152]{2,1,0:T(8,128)(2,1)} %reduce_sum.22), calls=%async_computation.3 | async-start | bytes 294912 | tf_op jit(solution)/shard_map/all_to_all | solution.py:306
  198.3 0.7 copy-start.5
  200.8 0.8 copy-start.6
  200.8 1.0 copy-start.7
Sparse Core Ops, SparseCore 0:
  10.1 130.7 all-gather.4

commit v4 on v3

--- a/solution.py
+++ b/solution.py
@@ -68,9 +68,10 @@
     digits = digits.astype(jnp.float32).astype(jnp.bfloat16)
     a = factor_a[...].astype(jnp.bfloat16)
     b = factor_b[...].astype(jnp.bfloat16)
-    packed[:, :hid] = a
-    packed[:, hid : hid + feat] = b
-    packed[:, hid + feat :] = digits
+    for copy in range(packed.shape[0]):
+        packed[copy, :, :hid] = a
+        packed[copy, :, hid : hid + feat] = b
+        packed[copy, :, hid + feat :] = digits
     lane_i = lax.broadcasted_iota(jnp.int32, info_v.shape, 1)
     info_v[...] = jnp.where(
         lane_i == INFO_FIRST, slot_first, jnp.where(lane_i == INFO_LAST, slot_last, cut)
@@ -101,9 +102,8 @@
     grad = nt_dot(pair[:, hid:], cot[...])
     proj = jnp.where(in_first, proj[:rank], proj[rank:])
     grad = jnp.where(in_first, grad[:rank], grad[rank:])
-    for y in range(Y):
-        part[y, :rank, :] = proj
-        part[y, rank:, :] = grad
+    part[:rank, :] = proj
+    part[rank:, :] = grad
     digits = own[:, :, hid + feat :].astype(jnp.float32)
     digits = digits + other[:, :, hid + feat :].astype(jnp.float32)
     totals[...] = jnp.sum(digits, axis=0)
@@ -126,21 +126,26 @@
     proj, grad = by_run(proj), by_run(grad)
     grad_rows[...] = grad
     term[:, :hid] = jnp.dot(grad, hidden[...], preferred_element_type=jnp.float32)
-    term[:, hid:] = ADAPTER_SCALE * jnp.dot(proj, cot[...], preferred_element_type=jnp.float32)
-
-
-def dense(info_s, info_other_s, core_s, term, term_other, outgoing, total):
+    wide = hid + cot.shape[1]
+    term[:, hid:wide] = ADAPTER_SCALE * jnp.dot(
+        proj, cot[...], preferred_element_type=jnp.float32
+    )
+    term[:rank, wide:] = jnp.full((rank, LANES), info_s[INFO_FIRST], jnp.int32).astype(jnp.float32)
+    term[rank:, wide:] = jnp.full((rank, LANES), info_s[INFO_LAST], jnp.int32).astype(jnp.float32)
+
+
+def dense(core_s, term, term_other, outgoing, total):
     core = core_s[0]
-    rank = outgoing.shape[1]
+    rank, wide = outgoing.shape[1:]
     total[...] = jnp.zeros_like(total)
-    for info, source in ((info_s, term), (info_other_s, term_other)):
-        for run, place in enumerate((INFO_FIRST, INFO_LAST)):
-            slot = info[place]
+    for source in (term, term_other):
+        for run in range(2):
+            slot = jnp.max(source[run * rank : run * rank + 8, wide:]).astype(jnp.int32)
             chip = lax.shift_right_logical(slot, 1)
 
             @pl.when((slot & 1) == core)
             def _():
-                total[chip] += source[run * rank : (run + 1) * rank, :]
+                total[chip] += source[run * rank : (run + 1) * rank, :wide]
 
     outgoing[...] = total[...].astype(jnp.bfloat16)
 
@@ -232,7 +237,7 @@
 
     packed, info_v = pl.pallas_call(
         prepare,
-        out_shape=(shape((rank, wide + LANES), bf16), shape((8, LANES), jnp.int32)),
+        out_shape=(shape((Z_LO, rank, wide + LANES), bf16), shape((8, LANES), jnp.int32)),
         in_specs=[SMEM, SMEM, WHOLE, WHOLE, WHOLE],
         out_specs=(WHOLE, WHOLE),
         compiler_params=params(56),
@@ -244,15 +249,13 @@
         adapter_input_factors[0],
         adapter_output_factors[0],
     )
-    cot_z = lax.all_to_all(
-        spread(Z_HI, output_gradient), "tensor", 0, 0, axis_index_groups=ALONG_Z_HI
-    )
-    info_other_v = lax.ppermute(info_v, "dp", OTHER_CORE)
-    info_s, info_other_s = info_v[0, :8], info_other_v[0, :8]
+    column = lax.all_to_all(packed, "dp", 0, 0, axis_index_groups=ALONG_Z_LO)
+    column, cot_copies = lax.optimization_barrier((column, spread(Z_HI, output_gradient)))
+    cot_z = lax.all_to_all(cot_copies, "tensor", 0, 0, axis_index_groups=ALONG_Z_HI)
+    info_s = info_v[0, :8]
     hidden = (
         jax.nn.silu(gate_logits.astype(f32)) * up_projected.astype(f32)
     ).astype(bf16)
-    column = lax.all_gather(packed, "dp", axis_index_groups=ALONG_Z_LO)
     plane = lax.all_gather(column, "dp", axis_index_groups=ALONG_X)
     own = plane.reshape(X * Z_LO, rank, wide + LANES)
     other = lax.ppermute(own, "dp", OTHER_CORE)
@@ -260,7 +263,7 @@
     part, pair, totals = pl.pallas_call(
         low_rank,
         out_shape=(
-            shape((Y, 2 * rank, tok), f32),
+            shape((2 * rank, tok), f32),
             shape((2 * rank, wide), bf16),
             shape((rank, LANES), f32),
         ),
@@ -270,20 +273,18 @@
         name="low_rank",
     )(info_s, core_s, own, other, hidden, output_gradient)
 
-    cot_z, part = lax.optimization_barrier((cot_z, part))
+    sums = jnp.sum(lax.all_gather(part, "tensor", axis_index_groups=ALONG_Y), axis=0)
+    cot_z, sums = lax.optimization_barrier((cot_z, sums))
     back = lax.ppermute(cot_z, "tensor", NEXT_Y)
     ahead = lax.ppermute(cot_z, "tensor", LAST_Y)
-
-    sums = jnp.sum(lax.all_to_all(part, "tensor", 0, 0, axis_index_groups=ALONG_Y), axis=0)
     sums = lax.all_gather(sums, "tensor", axis_index_groups=ALONG_Z_HI)
-    back, ahead, sums = lax.optimization_barrier((back, ahead, sums))
     half = Z_HI // 2
     far_low = lax.ppermute(back[:half], "tensor", NEXT_Y)
     far_high = lax.ppermute(ahead[half:], "tensor", LAST_Y)
 
     grad_rows, term = pl.pallas_call(
         terms,
-        out_shape=(shape((2 * rank, tok), bf16), shape((2 * rank, wide), f32)),
+        out_shape=(shape((2 * rank, tok), bf16), shape((2 * rank, wide + LANES), f32)),
         in_specs=[SMEM, VMEM, VMEM, VMEM],
         out_specs=(VMEM, VMEM),
         compiler_params=params(),
@@ -294,12 +295,12 @@
     outgoing = pl.pallas_call(
         dense,
         out_shape=shape((X * Z_LO, rank, wide), bf16),
-        in_specs=[SMEM, SMEM, SMEM, VMEM, VMEM],
+        in_specs=[SMEM, VMEM, VMEM],
         out_specs=VMEM,
         scratch_shapes=[pltpu.VMEM((X * Z_LO, rank, wide), f32)],
         compiler_params=params(),
         name="dense",
-    )(info_s, info_other_s, core_s, term, term_other)
+    )(core_s, term, term_other)
     outgoing = outgoing.reshape(X, Z_LO, rank, wide)
     by_x = lax.all_to_all(outgoing, "dp", 0, 0, axis_index_groups=ALONG_X)
     by_x = jnp.sum(by_x.astype(f32), axis=0).astype(bf16)

time: 222 us -> 181 us (0.82)
  blocking collectives: 101 us -> 59.2 us
  waiting for transfers between devices: 31.1 us -> 38.7 us
  starting transfers between devices: 45.1 us -> 41 us
    all_gather x1, blocking collectives: 64 us -> 12.3 us  [shards(): lax.all_gather(part, 'tensor', axis_index_groups=ALONG_Y)]
    all_to_all x0 -> x1, blocking collectives: none -> 12.8 us  [shards(): column = lax.all_to_all(packed, 'dp', 0, 0, axis_index_groups=ALONG_Z_LO)]
    all_to_all x2 -> x1, starting transfers between devices: 20.1 us -> 12.5 us  [shards(): lax.all_to_all(cot_copies, 'tensor', 0, 0, axis_index_groups=ALONG_Z_HI)]
    all_to_all x2 -> x1, waiting for transfers between devices: 21 us -> 27 us  [shards(): lax.all_to_all(cot_copies, 'tensor', 0, 0, axis_index_groups=ALONG_Z_HI)]
    all_to_all x1, starting transfers between devices: 3.8 us -> 9.66 us  [shards(): by_x = lax.all_to_all(outgoing, 'dp', 0, 0, axis_index_groups=ALONG_X)]
    all_gather x1, blocking collectives: 22.8 us -> 19.6 us  [shards(): sums = lax.all_gather(sums, 'tensor', axis_index_groups=ALONG_Z_HI)]
  transfers between devices with their start and end apart: 12 -> 10, of which waited for: 4 -> 4; matrix products, arithmetic and copies ran while one was open for 4% -> 4% of each run, Pallas kernels for 3% -> 4%
where the time goes in v4:
time: 181 us; the launch traced here: 179 us
  blocking collectives  59.2 us (33%)
  starting transfers between devices  41 us (23%)
  waiting for transfers between devices  38.7 us (21%)
  Pallas kernels  17.7 us (10%)
  between operations  14.2 us (8%)
  local copies, waits for them, and re-layouts  5.97 us (3%)
  other arithmetic  2.54 us (1%)
    all_to_all x1, waiting for transfers between devices, shards(): lax.all_to_all(cot_copies, 'tensor', 0, 0, axis_index_groups=ALONG_Z_HI)  27 us
    all_gather x1, blocking collectives, shards(): sums = lax.all_gather(sums, 'tensor', axis_index_groups=ALONG_Z_HI)  19.6 us
    all_gather x1, blocking collectives, shards(): plane = lax.all_gather(column, 'dp', axis_index_groups=ALONG_X)  14.5 us
    all_to_all x1, blocking collectives, shards(): column = lax.all_to_all(packed, 'dp', 0, 0, axis_index_groups=ALONG_Z_LO)  12.8 us
    all_to_all x1, starting transfers between devices, shards(): lax.all_to_all(cot_copies, 'tensor', 0, 0, axis_index_groups=ALONG_Z_HI)  12.5 us
    all_gather x1, blocking collectives, shards(): lax.all_gather(part, 'tensor', axis_index_groups=ALONG_Y)  12.3 us
    pallas_call x1, Pallas kernels, shards(): pl.pallas_call(finish, out_shape=(shape((tok, hid), bf16), shape((tok, hi...  11.1 us
    all_to_all x1, starting transfers between devices, shards(): by_x = lax.all_to_all(outgoing, 'dp', 0, 0, axis_index_groups=ALONG_X)  9.66 us
  transfers between devices with their start and end apart: 10, of which 4 were waited for; matrix products, arithmetic and copies ran while one was open for 4% of the time, Pallas kernels for 4%

profile of v4, /device:TPU:24, one launch (start us, length us, event | category | flops | bytes accessed | tf_op | source)
XLA Modules:
  0.0 179.4 jit_solution(3741484551553116386)
XLA Ops:
  7.2 0.0 all-gather.5.cloned.1.call-start
  7.2 0.7 all-gather.5.cloned.1.call-update
  7.9 1.6 prepare.1
  9.5 12.8 %all_to_all.20 = bf16[4,16,1280]{2,1,0:T(8,128)(2,1)S(1)} all-to-all(bf16[4,16,1280]{2,1,0:T(8,128)(2,1)} %get-tuple-element.23), channel_id=1, replica_groups={{0,32,64,96},{16,48,80,112},{128,160,192,224},{144,176,208,240},{256,28..., dimensions={0} | all-to-all | bytes 327680 | tf_op jit(solution)/shard_map/all_to_all | solution.py:252
  22.4 0.0 copy-start.3
  22.4 2.2 %broadcast_in_dim.2 = bf16[4,512,256]{2,1,0:T(8,128)(2,1)} broadcast(bf16[512,256]{1,0:T(8,128)(2,1)} %cot.3), dimensions={1,2} | broadcast | bytes 1310720 | tf_op jit(solution)/shard_map/broadcast_in_dim | solution.py:53
  24.6 12.5 %all-to-all-start.1 = ((bf16[4,512,256]{2,1,0:T(8,128)(2,1)}), bf16[4,512,256]{2,1,0:T(8,128)(2,1)}, u32[]{:S(2)}, u32[]{:S(2)}) async-start(bf16[4,512,256]{2,1,0:T(8,128)(2,1)} %broadcast_in_dim.2), calls=%async_computation.1 | async-start | bytes 2097152 | tf_op jit(solution)/shard_map/all_to_all | solution.py:254
  37.1 0.0 copy-start
  37.1 14.5 %all-gather.own = bf16[16,16,1280]{2,1,0:T(8,128)(2,1)S(1)} all-gather(bf16[4,16,1280]{2,1,0:T(8,128)(2,1)S(1)} %all_to_all.20), channel_id=2, replica_groups={{0,128,256,384},{16,144,272,400},{32,160,288,416},{48,176,304,432},{64,..., dimensions={0}, use_global_device_ids=true | all-gather | bytes 819200 | tf_op jit(solution)/shard_map/all_gather | solution.py:259
  51.6 1.9 %collective-permute-start = (bf16[16,16,1280]{2,1,0:T(8,128)(2,1)S(1)}, bf16[16,16,1280]{2,1,0:T(8,128)(2,1)S(1)}, u32[]{:S(2)}, u32[]{:S(2)}) collective-permute-start(bf16[16,16,1280]{2,1,0:T(8,128)(2,1)S(1)} %all-gather.own), channel_id=1, source_target_pairs={{0,16},{16,0},{32,48},{48,32},{64,80},{80,64},{96,112},{112,96},{1... | collective-permute-start | bytes 1966088 | tf_op jit(solution)/shard_map/ppermute | solution.py:261
  53.5 0.7 slice_bitcast_fusion.info_s
  54.2 0.0 copy-done.3
  54.2 1.8 fusion.4.hidden
  56.0 0.0 collective-permute-done.other
  56.0 0.0 copy-done
  56.0 1.0 low_rank.1
  57.0 0.0 copy-start.2
  57.0 12.3 %all-gather.1 = f32[128,512]{1,0:T(8,128)S(1)} all-gather(f32[32,512]{1,0:T(8,128)S(1)} %get-tuple-element.27), channel_id=3, replica_groups={{0,4,8,12},{1,5,9,13},{2,6,10,14},{3,7,11,15},{16,20,24,28},{17,21,25,2..., dimensions={0}, use_global_device_ids=true | all-gather | bytes 327680 | tf_op jit(solution)/shard_map/all_gather | solution.py:276
  69.3 0.0 copy-done.2
  69.3 27.0 %all-to-all-done.1.own = bf16[4,512,256]{2,1,0:T(8,128)(2,1)} async-done(((bf16[4,512,256]{2,1,0:T(8,128)(2,1)}), bf16[4,512,256]{2,1,0:T(8,128)(2,1)}, u32[]{:S(2)}, u32[]{:S(2)}) %all-to-all-start.1) | async-done | bytes 1048608 | tf_op jit(solution)/shard_map/all_to_all | solution.py:254
  96.3 3.0 %collective-permute-start.1 = (bf16[4,512,256]{2,1,0:T(8,128)(2,1)}, bf16[4,512,256]{2,1,0:T(8,128)(2,1)S(1)}, u32[]{:S(2)}, u32[]{:S(2)}) collective-permute-start(bf16[4,512,256]{2,1,0:T(8,128)(2,1)} %all-to-all-done.1.own), channel_id=1, source_target_pairs={{0,4},{1,5},{2,6},{3,7},{4,8},{5,9},{6,10},{7,11},{8,12},{9,13},{1... | collective-permute-start | bytes 3145736 | tf_op jit(solution)/shard_map/ppermute | solution.py:278
  99.3 2.8 %collective-permute-start.2 = (bf16[4,512,256]{2,1,0:T(8,128)(2,1)}, bf16[4,512,256]{2,1,0:T(8,128)(2,1)S(1)}, u32[]{:S(2)}, u32[]{:S(2)}) collective-permute-start(bf16[4,512,256]{2,1,0:T(8,128)(2,1)} %all-to-all-done.1.own), channel_id=1, source_target_pairs={{0,12},{1,13},{2,14},{3,15},{4,0},{5,1},{6,2},{7,3},{8,4},{9,5},{1... | collective-permute-start | bytes 3145736 | tf_op jit(solution)/shard_map/ppermute | solution.py:279
  102.1 19.6 %all-gather.2 = f32[128,512]{1,0:T(8,128)S(1)} all-gather(f32[32,512]{1,0:T(8,128)S(1)} %reduce_sum.21), channel_id=4, replica_groups={{0,1,2,3},{4,5,6,7},{8,9,10,11},{12,13,14,15},{16,17,18,19},{20,21,22,2..., dimensions={0}, use_global_device_ids=true | all-gather | bytes 327680 | tf_op jit(solution)/shard_map/all_gather | solution.py:280
  121.7 0.8 terms.1
  122.6 0.0 copy-start.1
  122.6 1.9 %collective-permute-start.5 = (f32[32,1280]{1,0:T(8,128)S(1)}, f32[32,1280]{1,0:T(8,128)S(1)}, u32[]{:S(2)}, u32[]{:S(2)}) collective-permute-start(f32[32,1280]{1,0:T(8,128)S(1)} %get-tuple-element.35.term), channel_id=1, source_target_pairs={{0,16},{16,0},{32,48},{48,32},{64,80},{80,64},{96,112},{112,96},{1... | collective-permute-start | bytes 491528 | tf_op jit(solution)/shard_map/ppermute | solution.py:294
  124.5 1.4 collective-permute-done.5.term_other
  125.9 1.4 dense.1
  127.3 9.7 %all-to-all-start.2 = ((bf16[4,4,16,1152]{3,2,1,0:T(8,128)(2,1)}), bf16[4,4,16,1152]{3,2,1,0:T(8,128)(2,1)S(1)}, u32[]{:S(2)}, u32[]{:S(2)}) async-start(bf16[4,4,16,1152]{3,2,1,0:T(8,128)(2,1)} %bitcast.9), calls=%async_computation.2 | async-start | bytes 1179648 | tf_op jit(solution)/shard_map/all_to_all | solution.py:305
  136.9 0.0 collective-permute-done.1.back
  136.9 0.0 copy-start.4
  136.9 0.9 slice.16
  137.8 3.7 %collective-permute-start.3 = (bf16[2,512,256]{2,1,0:T(8,128)(2,1)}, bf16[2,512,256]{2,1,0:T(8,128)(2,1)}, u32[]{:S(2)}, u32[]{:S(2)}) collective-permute-start(bf16[2,512,256]{2,1,0:T(8,128)(2,1)} %slice.16), channel_id=1, source_target_pairs={{0,4},{1,5},{2,6},{3,7},{4,8},{5,9},{6,10},{7,11},{8,12},{9,13},{1... | collective-permute-start | bytes 1572872 | tf_op jit(solution)/shard_map/ppermute | solution.py:282
  141.6 0.0 collective-permute-done.2.ahead
  141.6 0.0 copy-start.5
  141.6 0.9 slice.17
  142.5 0.0 copy-done.1
  142.5 2.1 %collective-permute-start.4 = (bf16[2,512,256]{2,1,0:T(8,128)(2,1)}, bf16[2,512,256]{2,1,0:T(8,128)(2,1)}, u32[]{:S(2)}, u32[]{:S(2)}) collective-permute-start(bf16[2,512,256]{2,1,0:T(8,128)(2,1)} %slice.17), channel_id=1, source_target_pairs={{0,12},{1,13},{2,14},{3,15},{4,0},{5,1},{6,2},{7,3},{8,4},{9,5},{1... | collective-permute-start | bytes 1572872 | tf_op jit(solution)/shard_map/ppermute | solution.py:283
  144.6 4.0 %all-to-all-done.2 = bf16[4,4,16,1152]{3,2,1,0:T(8,128)(2,1)S(1)} async-done(((bf16[4,4,16,1152]{3,2,1,0:T(8,128)(2,1)}), bf16[4,4,16,1152]{3,2,1,0:T(8,128)(2,1)S(1)}, u32[]{:S(2)}, u32[]{:S(2)}) %all-to-all-start.2) | async-done | bytes 589856 | tf_op jit(solution)/shard_map/all_to_all | solution.py:305
  148.6 0.8 reduce_sum.22
  149.4 3.3 %all-to-all-start.3 = ((bf16[4,16,1152]{2,1,0:T(8,128)(2,1)}), bf16[4,16,1152]{2,1,0:T(8,128)(2,1)S(1)}, u32[]{:S(2)}, u32[]{:S(2)}) async-start(bf16[4,16,1152]{2,1,0:T(8,128)(2,1)} %reduce_sum.22), calls=%async_computation.3 | async-start | bytes 294912 | tf_op jit(solution)/shard_map/all_to_all | solution.py:307
  152.8 0.6 slice.15.pair_a
  153.4 5.6 %all-to-all-done.3.incoming = bf16[4,16,1152]{2,1,0:T(8,128)(2,1)S(1)} async-done(((bf16[4,16,1152]{2,1,0:T(8,128)(2,1)}), bf16[4,16,1152]{2,1,0:T(8,128)(2,1)S(1)}, u32[]{:S(2)}, u32[]{:S(2)}) %all-to-all-start.3) | async-done | bytes 147488 | tf_op jit(solution)/shard_map/all_to_all | solution.py:307
  158.9 0.0 copy-start.6
  158.9 0.7 copy-done.6
  159.6 1.8 %adam.1 = (f32[2,1,16,896]{3,2,1,0:T(8,128)}, f32[2,1,16,256]{3,2,1,0:T(8,128)}, f32[1,16,896]{2,1,0:T(8,128)}, f32[1,16,256]{2,1,0:T(8,128)}) custom-call(s32[1]{0:T(128)} %bitcast.8.me_s, f32[16,128]{1,0:T(8,128)} %copy-done.2, bf16[4,16,1152]{2,1,0:T(8,128)(2,1)} %copy-done.6, f32[2,1,16,896]{3,2,1,0:T(8,128)} %moments_a.1, f32[2,1,16,256]{3,2,1,0:T(8,128)} %moments_b.1), custom_call_target="tpu_custom_call" | custom-call | tf_op jit(solution)/shard_map/adam/pallas_call | solution.py:309
  161.4 0.0 collective-permute-done.3.far_low
  161.4 0.0 collective-permute-done.4.far_high
  161.4 0.0 all-gather.5.cloned.1.call-done.down_own.down_back.down_ahead.down_far
  161.4 0.0 copy-done.4
  161.5 0.0 copy-done.5
  161.5 11.1 %finish.1 = (bf16[512,896]{1,0:T(8,128)(2,1)}, bf16[512,896]{1,0:T(8,128)(2,1)}) custom-call(s32[1]{0:T(128)} %bitcast.place_s, bf16[4,512,256]{2,1,0:T(8,128)(2,1)} %all-to-all-done.1.own, bf16[4,512,256]{2,1,0:T(8,128)(2,1)} %copy-done.4, bf16[4,512,256]{2,1,0:T(8,128)(2,1)} %copy-done.5, bf16[2,512,256]{2,1,0:T(8,128)(2,1)} %collective-permute-done.3.far_low, ...), custom_call_target="tpu_custom_call" | custom-call | tf_op jit(solution)/shard_map/finish/pallas_call | solution.py:335
  (1 shorter events, 0.0 us)
Async XLA Ops:
  7.2 154.3 %all-gather.5.cloned.1.call-start = ((), (), s32[]{:S(2)}) async-start(), calls=%async_computation.4 | async-start | bytes 7569408 | tf_op jit(solution)/shard_map/all_gather | solution.py:236
  22.4 31.8 %copy-start.3 = (bf16[512,896]{1,0:T(8,128)(2,1)S(1)}, bf16[512,896]{1,0:T(8,128)(2,1)}, u32[]{:S(2)}) copy-start(bf16[512,896]{1,0:T(8,128)(2,1)} %up.1) | copy-start | bytes 2752516
  24.6 71.7 %all-to-all-start.1 = ((bf16[4,512,256]{2,1,0:T(8,128)(2,1)}), bf16[4,512,256]{2,1,0:T(8,128)(2,1)}, u32[]{:S(2)}, u32[]{:S(2)}) async-start(bf16[4,512,256]{2,1,0:T(8,128)(2,1)} %broadcast_in_dim.2), calls=%async_computation.1 | async-start | bytes 2097152 | tf_op jit(solution)/shard_map/all_to_all | solution.py:254
  37.1 18.9 %copy-start = (bf16[512,256]{1,0:T(8,128)(2,1)S(1)}, bf16[512,256]{1,0:T(8,128)(2,1)}, u32[]{:S(2)}) copy-start(bf16[512,256]{1,0:T(8,128)(2,1)} %cot.3) | copy-start | bytes 786436
  51.6 4.4 %collective-permute-start = (bf16[16,16,1280]{2,1,0:T(8,128)(2,1)S(1)}, bf16[16,16,1280]{2,1,0:T(8,128)(2,1)S(1)}, u32[]{:S(2)}, u32[]{:S(2)}) collective-permute-start(bf16[16,16,1280]{2,1,0:T(8,128)(2,1)S(1)} %all-gather.own), channel_id=1, source_target_pairs={{0,16},{16,0},{32,48},{48,32},{64,80},{80,64},{96,112},{112,96},{1... | collective-permute-start | bytes 1966088 | tf_op jit(solution)/shard_map/ppermute | solution.py:261
  57.0 12.3 %copy-start.2 = (f32[16,128]{1,0:T(8,128)}, f32[16,128]{1,0:T(8,128)S(1)}, u32[]{:S(2)}) copy-start(f32[16,128]{1,0:T(8,128)S(1)} %get-tuple-element.34.totals) | copy-start | bytes 24580
  96.3 40.7 %collective-permute-start.1 = (bf16[4,512,256]{2,1,0:T(8,128)(2,1)}, bf16[4,512,256]{2,1,0:T(8,128)(2,1)S(1)}, u32[]{:S(2)}, u32[]{:S(2)}) collective-permute-start(bf16[4,512,256]{2,1,0:T(8,128)(2,1)} %all-to-all-done.1.own), channel_id=1, source_target_pairs={{0,4},{1,5},{2,6},{3,7},{4,8},{5,9},{6,10},{7,11},{8,12},{9,13},{1... | collective-permute-start | bytes 3145736 | tf_op jit(solution)/shard_map/ppermute | solution.py:278
  99.3 42.3 %collective-permute-start.2 = (bf16[4,512,256]{2,1,0:T(8,128)(2,1)}, bf16[4,512,256]{2,1,0:T(8,128)(2,1)S(1)}, u32[]{:S(2)}, u32[]{:S(2)}) collective-permute-start(bf16[4,512,256]{2,1,0:T(8,128)(2,1)} %all-to-all-done.1.own), channel_id=1, source_target_pairs={{0,12},{1,13},{2,14},{3,15},{4,0},{5,1},{6,2},{7,3},{8,4},{9,5},{1... | collective-permute-start | bytes 3145736 | tf_op jit(solution)/shard_map/ppermute | solution.py:279
  122.6 19.9 %copy-start.1 = (bf16[32,512]{1,0:T(8,128)(2,1)}, bf16[32,512]{1,0:T(8,128)(2,1)S(1)}, u32[]{:S(2)}) copy-start(bf16[32,512]{1,0:T(8,128)(2,1)S(1)} %get-tuple-element.30.grad_rows) | copy-start | bytes 98308
  122.6 3.3 %collective-permute-start.5 = (f32[32,1280]{1,0:T(8,128)S(1)}, f32[32,1280]{1,0:T(8,128)S(1)}, u32[]{:S(2)}, u32[]{:S(2)}) collective-permute-start(f32[32,1280]{1,0:T(8,128)S(1)} %get-tuple-element.35.term), channel_id=1, source_target_pairs={{0,16},{16,0},{32,48},{48,32},{64,80},{80,64},{96,112},{112,96},{1... | collective-permute-start | bytes 491528 | tf_op jit(solution)/shard_map/ppermute | solution.py:294
  127.3 21.4 %all-to-all-start.2 = ((bf16[4,4,16,1152]{3,2,1,0:T(8,128)(2,1)}), bf16[4,4,16,1152]{3,2,1,0:T(8,128)(2,1)S(1)}, u32[]{:S(2)}, u32[]{:S(2)}) async-start(bf16[4,4,16,1152]{3,2,1,0:T(8,128)(2,1)} %bitcast.9), calls=%async_computation.2 | async-start | bytes 1179648 | tf_op jit(solution)/shard_map/all_to_all | solution.py:305
  136.9 24.5 %copy-start.4 = (bf16[4,512,256]{2,1,0:T(8,128)(2,1)}, bf16[4,512,256]{2,1,0:T(8,128)(2,1)S(1)}, u32[]{:S(2)}) copy-start(bf16[4,512,256]{2,1,0:T(8,128)(2,1)S(1)} %collective-permute-done.1.back) | copy-start | bytes 3145732
  137.8 23.6 %collective-permute-start.3 = (bf16[2,512,256]{2,1,0:T(8,128)(2,1)}, bf16[2,512,256]{2,1,0:T(8,128)(2,1)}, u32[]{:S(2)}, u32[]{:S(2)}) collective-permute-start(bf16[2,512,256]{2,1,0:T(8,128)(2,1)} %slice.16), channel_id=1, source_target_pairs={{0,4},{1,5},{2,6},{3,7},{4,8},{5,9},{6,10},{7,11},{8,12},{9,13},{1... | collective-permute-start | bytes 1572872 | tf_op jit(solution)/shard_map/ppermute | solution.py:282
  141.6 19.9 %copy-start.5 = (bf16[4,512,256]{2,1,0:T(8,128)(2,1)}, bf16[4,512,256]{2,1,0:T(8,128)(2,1)S(1)}, u32[]{:S(2)}) copy-start(bf16[4,512,256]{2,1,0:T(8,128)(2,1)S(1)} %collective-permute-done.2.ahead) | copy-start | bytes 3145732
  142.5 18.9 %collective-permute-start.4 = (bf16[2,512,256]{2,1,0:T(8,128)(2,1)}, bf16[2,512,256]{2,1,0:T(8,128)(2,1)}, u32[]{:S(2)}, u32[]{:S(2)}) collective-permute-start(bf16[2,512,256]{2,1,0:T(8,128)(2,1)} %slice.17), channel_id=1, source_target_pairs={{0,12},{1,13},{2,14},{3,15},{4,0},{5,1},{6,2},{7,3},{8,4},{9,5},{1... | collective-permute-start | bytes 1572872 | tf_op jit(solution)/shard_map/ppermute | solution.py:283
  149.4 9.5 %all-to-all-start.3 = ((bf16[4,16,1152]{2,1,0:T(8,128)(2,1)}), bf16[4,16,1152]{2,1,0:T(8,128)(2,1)S(1)}, u32[]{:S(2)}, u32[]{:S(2)}) async-start(bf16[4,16,1152]{2,1,0:T(8,128)(2,1)} %reduce_sum.22), calls=%async_computation.3 | async-start | bytes 294912 | tf_op jit(solution)/shard_map/all_to_all | solution.py:307
  158.9 0.7 copy-start.6
Sparse Core Ops, SparseCore 0:
  10.1 136.8 all-gather.4

commit v5 on v4

--- a/solution.py
+++ b/solution.py
@@ -25,8 +25,26 @@
 ALONG_Y = [[y * Z_HI + h for y in range(Y)] for h in range(Z_HI)]
 ALONG_Z_HI = [[y * Z_HI + h for h in range(Z_HI)] for y in range(Y)]
 OTHER_CORE = [(d, d ^ 1) for d in range(X * Z_LO * CORES)]
-NEXT_Y = [(y * Z_HI + h, (y + 1) % Y * Z_HI + h) for y in range(Y) for h in range(Z_HI)]
-LAST_Y = [(y * Z_HI + h, (y - 1) % Y * Z_HI + h) for y in range(Y) for h in range(Z_HI)]
+SAME_CORE = [[(x * Z_LO + z) * CORES + c for x in range(X) for z in range(Z_LO)] for c in range(CORES)]
+
+
+def shift_x(by):
+    return [
+        ((x * Z_LO + z) * CORES + c, ((x + by) % X * Z_LO + z) * CORES + c)
+        for x in range(X)
+        for z in range(Z_LO)
+        for c in range(CORES)
+    ]
+
+
+def shift_z_lo(by):
+    return [
+        ((x * Z_LO + z) * CORES + c, (x * Z_LO + (z + by) % Z_LO) * CORES + c)
+        for x in range(X)
+        for z in range(Z_LO)
+        for c in range(CORES)
+    ]
+
 
 VMEM = pl.BlockSpec(memory_space=pltpu.VMEM)
 WHOLE = pl.BlockSpec()
@@ -78,8 +96,8 @@
     )
 
 
-def low_rank(info_s, core_s, own, other, hidden, cot, part, pair, totals):
-    core = core_s[0]
+def low_rank(info_s, place_s, own, other, hidden, cot, part, pair, totals):
+    core = place_s[0]
     rank = own.shape[1]
     hid, feat = hidden.shape[1], cot.shape[1]
     for run, place in enumerate((INFO_FIRST, INFO_LAST)):
@@ -134,9 +152,9 @@
     term[rank:, wide:] = jnp.full((rank, LANES), info_s[INFO_LAST], jnp.int32).astype(jnp.float32)
 
 
-def dense(core_s, term, term_other, outgoing, total):
-    core = core_s[0]
-    rank, wide = outgoing.shape[1:]
+def dense(place_s, term, term_other, stay, next_one, next_two, next_three, total):
+    core, x = place_s[0], place_s[1]
+    rank, wide = stay.shape[1:]
     total[...] = jnp.zeros_like(total)
     for source in (term, term_other):
         for run in range(2):
@@ -147,18 +165,37 @@
             def _():
                 total[chip] += source[run * rank : (run + 1) * rank, :wide]
 
-    outgoing[...] = total[...].astype(jnp.bfloat16)
-
-
-def adam(me_s, totals, incoming, moments_a, moments_b, new_a, new_b, step_a, step_b):
+    for distance, out in enumerate((stay, next_one, next_two, next_three)):
+        target = (x + distance) & (X - 1)
+        out[...] = total[pl.ds(target * Z_LO, Z_LO)].astype(jnp.bfloat16)
+
+
+def merge(place_s, one, two, three, four, stay, next_one, next_two, next_three, total):
+    z = place_s[2]
+    total[...] = (
+        one[...].astype(jnp.float32)
+        + two[...].astype(jnp.float32)
+        + three[...].astype(jnp.float32)
+        + four[...].astype(jnp.float32)
+    )
+    for distance, out in enumerate((stay, next_one, next_two, next_three)):
+        out[...] = total[(z + distance) & (Z_LO - 1)].astype(jnp.bfloat16)
+
+
+def adam(place_s, totals, one, two, three, four, moments_a, moments_b, new_a, new_b, step_a, step_b):
     lane = lax.broadcasted_iota(jnp.int32, (1, LANES), 1)
     digit = COUNT_BASE * totals[0:1, :] + totals[1:2, :]
-    count = jnp.sum(jnp.where(lane == me_s[0], digit, 0.0))
+    count = jnp.sum(jnp.where(lane == place_s[3], digit, 0.0))
     active = count > 0.5
     divisor = jnp.maximum(count, 1.0)
     corr_one = 1.0 - BETA_ONE**ADAM_STEP
     corr_two = 1.0 - BETA_TWO**ADAM_STEP
-    sums = jnp.sum(incoming[...].astype(jnp.float32), axis=0)
+    sums = (
+        one[...].astype(jnp.float32)
+        + two[...].astype(jnp.float32)
+        + three[...].astype(jnp.float32)
+        + four[...].astype(jnp.float32)
+    )
     hid = moments_a.shape[-1]
     for part, moments, new, step in (
         (sums[:, :hid], moments_a, new_a, step_a),
@@ -175,29 +212,25 @@
 
 
 def finish(
-    place_s, own, back, ahead, far_low, far_high, down_own, down_back, down_ahead, down_far,
-    grad_rows, pair_a, gate, up, out_gate, out_up, total, far
+    place_s, cot, down_own, down_other, grad_rows, pair_a, gate, up, out_gate, out_up, total, weights
 ):
     place = pl.program_id(0)
+    core = place_s[0]
+    half = cot.shape[2] // CORES
 
     @pl.when(place == 0)
     def _():
         total[...] = tn_dot(grad_rows[...], pair_a[...])
 
-    @pl.when(place < 2)
-    def _():
-        far[...] = far_low[0]
-
-    @pl.when(place >= 2)
-    def _():
-        far[...] = far_high[0]
-
-    total[...] += (
-        nt_dot(own[0], down_own[...])
-        + nt_dot(back[0], down_back[...])
-        + nt_dot(ahead[0], down_ahead[...])
-        + nt_dot(far[...], down_far[...])
-    )
+    mine = pl.ds(pl.multiple_of(core * half, half), half)
+    theirs = pl.ds(pl.multiple_of((1 - core) * half, half), half)
+    for block in range(cot.shape[0]):
+        weights[block, :, mine] = down_own[:, block * half : (block + 1) * half]
+        weights[block, :, theirs] = down_other[:, block * half : (block + 1) * half]
+    added = nt_dot(cot[0], weights[0])
+    for block in range(1, cot.shape[0]):
+        added += nt_dot(cot[block], weights[block])
+    total[...] += added
 
     @pl.when(place == pl.num_programs(0) - 1)
     def _():
@@ -224,8 +257,8 @@
     tenant_owner_slots,
 ):
     me = lax.axis_index("dp").astype(jnp.int32)
-    core_s = (me & (CORES - 1)).reshape(1)
-    y_s = lax.shift_right_logical(lax.axis_index("tensor").astype(jnp.int32), 2).reshape(1)
+    chip = lax.shift_right_logical(me, 1)
+    place_s = jnp.stack([me & (CORES - 1), lax.shift_right_logical(chip, 2), chip & (Z_LO - 1), me])
     rank, hid = adapter_input_factors.shape[1:]
     feat = adapter_output_factors.shape[2]
     tok = gate_logits.shape[0]
@@ -233,7 +266,9 @@
     bf16, f32 = jnp.bfloat16, jnp.float32
     shape = jax.ShapeDtypeStruct
 
-    down_full = lax.all_gather(down_matrix, "dp", axis=1, tiled=True)
+    down_own = lax.all_gather(
+        down_matrix, "dp", axis=1, tiled=True, axis_index_groups=SAME_CORE
+    )
 
     packed, info_v = pl.pallas_call(
         prepare,
@@ -271,16 +306,12 @@
         out_specs=(VMEM, VMEM, VMEM),
         compiler_params=params(),
         name="low_rank",
-    )(info_s, core_s, own, other, hidden, output_gradient)
+    )(info_s, place_s, own, other, hidden, output_gradient)
 
     sums = jnp.sum(lax.all_gather(part, "tensor", axis_index_groups=ALONG_Y), axis=0)
     cot_z, sums = lax.optimization_barrier((cot_z, sums))
-    back = lax.ppermute(cot_z, "tensor", NEXT_Y)
-    ahead = lax.ppermute(cot_z, "tensor", LAST_Y)
+    cot_all = lax.all_to_all(spread(Y, cot_z), "tensor", 0, 0, axis_index_groups=ALONG_Y)
     sums = lax.all_gather(sums, "tensor", axis_index_groups=ALONG_Z_HI)
-    half = Z_HI // 2
-    far_low = lax.ppermute(back[:half], "tensor", NEXT_Y)
-    far_high = lax.ppermute(ahead[half:], "tensor", LAST_Y)
 
     grad_rows, term = pl.pallas_call(
         terms,
@@ -292,19 +323,30 @@
     )(info_s, sums, hidden, output_gradient)
 
     term_other = lax.ppermute(term, "dp", OTHER_CORE)
-    outgoing = pl.pallas_call(
+    down_own, term_other = lax.optimization_barrier((down_own, term_other))
+    down_other = lax.ppermute(down_own, "dp", OTHER_CORE)
+    block = shape((Z_LO, rank, wide), bf16)
+    stay, *leave = pl.pallas_call(
         dense,
-        out_shape=shape((X * Z_LO, rank, wide), bf16),
+        out_shape=(block,) * X,
         in_specs=[SMEM, VMEM, VMEM],
-        out_specs=VMEM,
+        out_specs=(VMEM,) * X,
         scratch_shapes=[pltpu.VMEM((X * Z_LO, rank, wide), f32)],
         compiler_params=params(),
         name="dense",
-    )(core_s, term, term_other)
-    outgoing = outgoing.reshape(X, Z_LO, rank, wide)
-    by_x = lax.all_to_all(outgoing, "dp", 0, 0, axis_index_groups=ALONG_X)
-    by_x = jnp.sum(by_x.astype(f32), axis=0).astype(bf16)
-    incoming = lax.all_to_all(by_x, "dp", 0, 0, axis_index_groups=ALONG_Z_LO)
+    )(place_s, term, term_other)
+    arrived = [lax.ppermute(part, "dp", shift_x(by + 1)) for by, part in enumerate(leave)]
+    block = shape((rank, wide), bf16)
+    stay, *leave = pl.pallas_call(
+        merge,
+        out_shape=(block,) * Z_LO,
+        in_specs=[SMEM] + [VMEM] * X,
+        out_specs=(VMEM,) * Z_LO,
+        scratch_shapes=[pltpu.VMEM((Z_LO, rank, wide), f32)],
+        compiler_params=params(),
+        name="merge",
+    )(place_s, stay, *arrived)
+    arrived = [lax.ppermute(part, "dp", shift_z_lo(by + 1)) for by, part in enumerate(leave)]
 
     new_moments_a, new_moments_b, step_a, step_b = pl.pallas_call(
         adam,
@@ -314,61 +356,43 @@
             shape(adapter_input_factors.shape, f32),
             shape(adapter_output_factors.shape, f32),
         ),
-        in_specs=[SMEM, WHOLE, WHOLE, WHOLE, WHOLE],
+        in_specs=[SMEM] + [WHOLE] * 7,
         out_specs=(WHOLE,) * 4,
         compiler_params=params(56),
         name="adam",
-    )(me.reshape(1), totals, incoming, input_moments, output_moments)
-
-    def down_block(ahead_by):
-        return pl.BlockSpec(
-            (hid, feat),
-            lambda place, y_ref: (0, lax.rem(y_ref[0] + ahead_by, Y) * Z_HI + place),
-        )
-
-    def by_place(index):
-        return pl.BlockSpec((1, tok, feat), lambda place, y_ref: (index(place), 0, 0))
+    )(place_s, totals, stay, *arrived, input_moments, output_moments)
 
     def whole_of(rows, columns):
-        return pl.BlockSpec((rows, columns), lambda place, y_ref: (0, 0))
+        return pl.BlockSpec((rows, columns), lambda place, place_ref: (0, 0))
+
+    def down_part():
+        return pl.BlockSpec((hid, Z_HI * feat // CORES), lambda place, place_ref: (0, place))
 
     grad_gate, grad_up = pl.pallas_call(
         finish,
         out_shape=(shape((tok, hid), bf16), shape((tok, hid), bf16)),
         grid_spec=pltpu.PrefetchScalarGridSpec(
             num_scalar_prefetch=1,
-            grid=(Z_HI,),
+            grid=(Y,),
             in_specs=[
-                by_place(lambda place: place),
-                by_place(lambda place: place),
-                by_place(lambda place: place),
-                by_place(lambda place: jnp.minimum(place, half - 1)),
-                by_place(lambda place: jnp.maximum(place - half, 0)),
-                down_block(0),
-                down_block(Y - 1),
-                down_block(1),
-                down_block(2),
+                pl.BlockSpec((Z_HI, tok, feat), lambda place, place_ref: (place, 0, 0)),
+                down_part(),
+                down_part(),
                 whole_of(2 * rank, tok),
                 whole_of(2 * rank, hid),
                 whole_of(tok, hid),
                 whole_of(tok, hid),
             ],
             out_specs=[whole_of(tok, hid), whole_of(tok, hid)],
-            scratch_shapes=[pltpu.VMEM((tok, hid), f32), pltpu.VMEM((tok, feat), bf16)],
+            scratch_shapes=[pltpu.VMEM((tok, hid), f32), pltpu.VMEM((Z_HI, hid, feat), bf16)],
         ),
         compiler_params=params(56),
         name="finish",
     )(
-        y_s,
-        cot_z,
-        back,
-        ahead,
-        far_low,
-        far_high,
-        down_full,
-        down_full,
-        down_full,
-        down_full,
+        place_s,
+        cot_all.reshape(Y * Z_HI, tok, feat),
+        down_own,
+        down_other,
         grad_rows,
         pair[:, :hid],
         gate_logits,

time: 181 us -> 254 us (1.40)
  waiting for transfers between devices: 38.7 us -> 105 us
  starting transfers between devices: 41 us -> 43.9 us
    all_gather x1, waiting for transfers between devices: 0.02 us -> 53.6 us  [shards(): lax.all_gather(down_matrix, 'dp', axis=1, tiled=True, axis_index_groups=S...]
    ppermute x4 -> x7, starting transfers between devices: 11.7 us -> 22.7 us  [the longest x3 10.8 us: shards(): lax.ppermute(part, 'dp', shift_z_lo(by + 1))]
    all_to_all x2 -> x1, starting transfers between devices: 13 us -> 4.81 us  [shards(): lax.all_to_all(spread(Y, cot_z), 'tensor', 0, 0, axis_index_groups=ALONG_Y)]
    all_to_all x2 -> x1, waiting for transfers between devices: 9.61 us -> 16.9 us  [shards(): lax.all_to_all(spread(Y, cot_z), 'tensor', 0, 0, axis_index_groups=ALONG_Y)]
    ppermute x4 -> x7, waiting for transfers between devices: 0.01 us -> 5.95 us  [the longest x3 4.96 us: shards(): lax.ppermute(part, 'dp', shift_x(by + 1))]
  transfers between devices with their start and end apart: 10 -> 12, of which waited for: 4 -> 7; matrix products, arithmetic and copies ran while one was open for 4% -> 3% of each run, Pallas kernels for 4% -> 3%
where the time goes in v5:
time: 254 us; the launch traced here: 251 us
  waiting for transfers between devices  105 us (41%)
  blocking collectives  59.7 us (24%)
  starting transfers between devices  43.9 us (17%)
  Pallas kernels  19.6 us (8%)
  between operations  14.2 us (6%)
  local copies, waits for them, and re-layouts  7.06 us (3%)
    all_gather x1, waiting for transfers between devices, shards(): lax.all_gather(down_matrix, 'dp', axis=1, tiled=True, axis_index_groups=S...  53.6 us
    all_to_all x1, waiting for transfers between devices, shards(): lax.all_to_all(cot_copies, 'tensor', 0, 0, axis_index_groups=ALONG_Z_HI)  26.4 us
    all_gather x1, blocking collectives, shards(): sums = lax.all_gather(sums, 'tensor', axis_index_groups=ALONG_Z_HI)  19.9 us
    all_to_all x1, waiting for transfers between devices, shards(): lax.all_to_all(spread(Y, cot_z), 'tensor', 0, 0, axis_index_groups=ALONG_Y)  16.9 us
    all_gather x1, blocking collectives, shards(): plane = lax.all_gather(column, 'dp', axis_index_groups=ALONG_X)  14.8 us
    all_to_all x1, blocking collectives, shards(): column = lax.all_to_all(packed, 'dp', 0, 0, axis_index_groups=ALONG_Z_LO)  12.8 us
    pallas_call x1, Pallas kernels, shards(): pl.pallas_call(finish, out_shape=(shape((tok, hid), bf16), shape((tok, hi...  12.6 us
    all_to_all x1, starting transfers between devices, shards(): lax.all_to_all(cot_copies, 'tensor', 0, 0, axis_index_groups=ALONG_Z_HI)  12.5 us
  transfers between devices with their start and end apart: 12, of which 7 were waited for; matrix products, arithmetic and copies ran while one was open for 3% of the time, Pallas kernels for 3%

profile of v5, /device:TPU:24, one launch (start us, length us, event | category | flops | bytes accessed | tf_op | source)
XLA Modules:
  0.0 251.2 jit_solution(15493079523142520431)
XLA Ops:
  7.2 0.0 all-gather.5.cloned.1.call-start
  7.2 0.7 all-gather.5.cloned.1.call-update
  7.9 1.6 prepare.1
  9.5 12.8 %all_to_all.15 = bf16[4,16,1280]{2,1,0:T(8,128)(2,1)S(1)} all-to-all(bf16[4,16,1280]{2,1,0:T(8,128)(2,1)} %get-tuple-element.33), channel_id=1, replica_groups={{0,32,64,96},{16,48,80,112},{128,160,192,224},{144,176,208,240},{256,28..., dimensions={0} | all-to-all | bytes 327680 | tf_op jit(solution)/shard_map/all_to_all | solution.py:287
  22.4 0.0 copy-start.5
  22.4 2.1 broadcast_in_dim.4
  24.5 12.5 %all-to-all-start.1 = ((bf16[4,512,256]{2,1,0:T(8,128)(2,1)}), bf16[4,512,256]{2,1,0:T(8,128)(2,1)S(1)}, u32[]{:S(2)}, u32[]{:S(2)}) async-start(bf16[4,512,256]{2,1,0:T(8,128)(2,1)} %broadcast_in_dim.4), calls=%async_computation.1 | async-start | bytes 2097152 | tf_op jit(solution)/shard_map/all_to_all | solution.py:289
  37.0 0.0 copy-start
  37.0 14.8 %all-gather.own = bf16[16,16,1280]{2,1,0:T(8,128)(2,1)S(1)} all-gather(bf16[4,16,1280]{2,1,0:T(8,128)(2,1)S(1)} %all_to_all.15), channel_id=2, replica_groups={{0,128,256,384},{16,144,272,400},{32,160,288,416},{48,176,304,432},{64,..., dimensions={0}, use_global_device_ids=true | all-gather | bytes 819200 | tf_op jit(solution)/shard_map/all_gather | solution.py:294
  51.8 1.9 collective-permute-start
  53.7 0.1 pad_add_fusion.place_s
  53.8 0.0 copy-start.3
  53.8 0.7 slice_bitcast_fusion.info_s
  54.5 0.0 copy-done.5
  54.5 1.8 fusion.4.hidden
  56.2 0.0 collective-permute-done.other
  56.2 0.0 copy-done
  56.2 1.0 low_rank.1
  57.3 0.0 copy-start.4
  57.3 12.3 %all-gather.1 = f32[128,512]{1,0:T(8,128)S(1)} all-gather(f32[32,512]{1,0:T(8,128)S(1)} %get-tuple-element.37), channel_id=3, replica_groups={{0,4,8,12},{1,5,9,13},{2,6,10,14},{3,7,11,15},{16,20,24,28},{17,21,25,2..., dimensions={0}, use_global_device_ids=true | all-gather | bytes 327680 | tf_op jit(solution)/shard_map/all_gather | solution.py:311
  69.6 26.4 %all-to-all-done.1 = bf16[4,512,256]{2,1,0:T(8,128)(2,1)S(1)} async-done(((bf16[4,512,256]{2,1,0:T(8,128)(2,1)}), bf16[4,512,256]{2,1,0:T(8,128)(2,1)S(1)}, u32[]{:S(2)}, u32[]{:S(2)}) %all-to-all-start.1) | async-done | bytes 1048608 | tf_op jit(solution)/shard_map/all_to_all | solution.py:289
  95.9 19.9 %all-gather.2 = f32[128,512]{1,0:T(8,128)S(1)} all-gather(f32[32,512]{1,0:T(8,128)S(1)} %reduce_sum.9), channel_id=4, replica_groups={{0,1,2,3},{4,5,6,7},{8,9,10,11},{12,13,14,15},{16,17,18,19},{20,21,22,2..., dimensions={0}, use_global_device_ids=true | all-gather | bytes 327680 | tf_op jit(solution)/shard_map/all_gather | solution.py:314
  115.8 0.0 copy-done.4
  115.8 0.8 terms.1
  116.6 0.0 copy-start.2
  116.6 0.6 copy-done.2
  117.2 1.9 collective-permute-start.1
  119.2 1.4 collective-permute-done.1.term_other
  120.5 53.6 %all-gather.5.cloned.1.call-done.down_own = bf16[896,2048]{1,0:T(8,128)(2,1)} async-done(((bf16[896,128]{1,0:T(8,128)(2,1)}), bf16[896,2048]{1,0:T(8,128)(2,1)}) %all-gather.5.cloned.1.call-update) | async-done | bytes 3670032 | tf_op jit(solution)/shard_map/all_gather | solution.py:269
  174.1 1.9 collective-permute-start.2
  176.1 2.4 broadcast_in_dim.5
  178.5 4.8 %all-to-all-start.2 = ((bf16[4,4,512,256]{3,2,1,0:T(8,128)(2,1)}), bf16[4,4,512,256]{3,2,1,0:T(8,128)(2,1)}, u32[]{:S(2)}, u32[]{:S(2)}) async-start(bf16[4,4,512,256]{3,2,1,0:T(8,128)(2,1)} %broadcast_in_dim.5), calls=%async_computation.2 | async-start | bytes 8388608 | tf_op jit(solution)/shard_map/all_to_all | solution.py:313
  183.3 1.1 dense.1
  184.4 1.9 collective-permute-start.3
  186.3 4.6 %collective-permute-start.4 = (bf16[4,16,1152]{2,1,0:T(8,128)(2,1)S(1)}, bf16[4,16,1152]{2,1,0:T(8,128)(2,1)S(1)}, u32[]{:S(2)}, u32[]{:S(2)}) collective-permute-start(bf16[4,16,1152]{2,1,0:T(8,128)(2,1)S(1)} %get-tuple-element.50), channel_id=1, source_target_pairs={{0,256},{16,272},{32,288},{48,304},{64,320},{80,336},{96,352},{112... | collective-permute-start | bytes 442376 | tf_op jit(solution)/shard_map/ppermute | solution.py:338
  191.0 3.5 %collective-permute-start.5 = (bf16[4,16,1152]{2,1,0:T(8,128)(2,1)S(1)}, bf16[4,16,1152]{2,1,0:T(8,128)(2,1)S(1)}, u32[]{:S(2)}, u32[]{:S(2)}) collective-permute-start(bf16[4,16,1152]{2,1,0:T(8,128)(2,1)S(1)} %get-tuple-element.51), channel_id=1, source_target_pairs={{0,384},{16,400},{32,416},{48,432},{64,448},{80,464},{96,480},{112... | collective-permute-start | bytes 442376 | tf_op jit(solution)/shard_map/ppermute | solution.py:338
  194.5 2.5 collective-permute-done.3.two
  197.0 0.0 collective-permute-done.4.three
  197.0 2.5 collective-permute-done.5.four
  199.4 0.0 copy-done.3
  199.4 0.7 merge.1
  200.1 0.0 copy-start.1
  200.1 2.3 collective-permute-start.6
  202.4 4.0 %collective-permute-start.7 = (bf16[16,1152]{1,0:T(8,128)(2,1)S(1)}, bf16[16,1152]{1,0:T(8,128)(2,1)S(1)}, u32[]{:S(2)}, u32[]{:S(2)}) collective-permute-start(bf16[16,1152]{1,0:T(8,128)(2,1)S(1)} %get-tuple-element.54), channel_id=1, source_target_pairs={{0,64},{16,80},{32,96},{48,112},{64,0},{80,16},{96,32},{112,48},{1... | collective-permute-start | bytes 110600 | tf_op jit(solution)/shard_map/ppermute | solution.py:349
  206.4 4.5 %collective-permute-start.8 = (bf16[16,1152]{1,0:T(8,128)(2,1)S(1)}, bf16[16,1152]{1,0:T(8,128)(2,1)S(1)}, u32[]{:S(2)}, u32[]{:S(2)}) collective-permute-start(bf16[16,1152]{1,0:T(8,128)(2,1)S(1)} %get-tuple-element.55), channel_id=1, source_target_pairs={{0,96},{16,112},{32,0},{48,16},{64,32},{80,48},{96,64},{112,80},{1... | collective-permute-start | bytes 110600 | tf_op jit(solution)/shard_map/ppermute | solution.py:349
  210.9 0.6 slice.7.pair_a
  211.6 0.0 copy-done.1
  211.6 0.0 collective-permute-done.6.two
  211.6 0.0 copy-start.6
  211.6 0.0 collective-permute-done.7.three
  211.6 0.0 copy-start.7
  211.6 1.0 collective-permute-done.8.four
  212.6 0.0 copy-start.8
  212.6 0.0 copy-done.6
  212.6 0.0 copy-done.7
  212.6 0.6 copy-done.8
  213.2 1.8 adam.1
  214.9 16.9 %all-to-all-done.2 = bf16[4,4,512,256]{3,2,1,0:T(8,128)(2,1)} async-done(((bf16[4,4,512,256]{3,2,1,0:T(8,128)(2,1)}), bf16[4,4,512,256]{3,2,1,0:T(8,128)(2,1)}, u32[]{:S(2)}, u32[]{:S(2)}) %all-to-all-start.2) | async-done | bytes 4194336 | tf_op jit(solution)/shard_map/all_to_all | solution.py:313
  231.8 0.0 collective-permute-done.2.down_other
  231.8 12.6 %finish.1 = (bf16[512,896]{1,0:T(8,128)(2,1)}, bf16[512,896]{1,0:T(8,128)(2,1)}) custom-call(s32[4]{0:T(128)} %copy-done.3, bf16[16,512,256]{2,1,0:T(8,128)(2,1)} %bitcast.9.cot, bf16[896,2048]{1,0:T(8,128)(2,1)} %all-gather.5.cloned.1.call-done.down_own, bf16[896,2048]{1,0:T(8,128)(2,1)} %collective-permute-done.2.down_other, bf16[32,512]{1,0:T(8,128)(2,1)} %copy-done.2, ...), custom_call_target="tpu_custom_call" | custom-call | tf_op jit(solution)/shard_map/finish/pallas_call | solution.py:371
  (1 shorter events, 0.0 us)
Async XLA Ops:
  7.2 167.0 %all-gather.5.cloned.1.call-start = ((), (), s32[]{:S(2)}) async-start(), calls=%async_computation.3 | async-start | bytes 3899392 | tf_op jit(solution)/shard_map/all_gather | solution.py:269
  22.4 32.1 %copy-start.5 = (bf16[512,896]{1,0:T(8,128)(2,1)S(1)}, bf16[512,896]{1,0:T(8,128)(2,1)}, u32[]{:S(2)}) copy-start(bf16[512,896]{1,0:T(8,128)(2,1)} %up.1) | copy-start | bytes 2752516
  24.5 71.4 %all-to-all-start.1 = ((bf16[4,512,256]{2,1,0:T(8,128)(2,1)}), bf16[4,512,256]{2,1,0:T(8,128)(2,1)S(1)}, u32[]{:S(2)}, u32[]{:S(2)}) async-start(bf16[4,512,256]{2,1,0:T(8,128)(2,1)} %broadcast_in_dim.4), calls=%async_computation.1 | async-start | bytes 2097152 | tf_op jit(solution)/shard_map/all_to_all | solution.py:289
  37.0 19.2 %copy-start = (bf16[512,256]{1,0:T(8,128)(2,1)S(1)}, bf16[512,256]{1,0:T(8,128)(2,1)}, u32[]{:S(2)}) copy-start(bf16[512,256]{1,0:T(8,128)(2,1)} %cot.3) | copy-start | bytes 786436
  51.8 4.5 %collective-permute-start = (bf16[16,16,1280]{2,1,0:T(8,128)(2,1)S(1)}, bf16[16,16,1280]{2,1,0:T(8,128)(2,1)S(1)}, u32[]{:S(2)}, u32[]{:S(2)}) collective-permute-start(bf16[16,16,1280]{2,1,0:T(8,128)(2,1)S(1)} %all-gather.own), channel_id=1, source_target_pairs={{0,16},{16,0},{32,48},{48,32},{64,80},{80,64},{96,112},{112,96},{1... | collective-permute-start | bytes 1966088 | tf_op jit(solution)/shard_map/ppermute | solution.py:296
  53.8 145.7 %copy-start.3 = (s32[4]{0:T(128)}, s32[4]{0:T(128)S(1)}, u32[]{:S(2)}) copy-start(s32[4]{0:T(128)S(1)} %pad_add_fusion.place_s) | copy-start | bytes 52
  57.3 58.5 %copy-start.4 = (f32[16,128]{1,0:T(8,128)}, f32[16,128]{1,0:T(8,128)S(1)}, u32[]{:S(2)}) copy-start(f32[16,128]{1,0:T(8,128)S(1)} %get-tuple-element.46.totals) | copy-start | bytes 24580
  116.6 0.6 copy-start.2
  117.2 3.3 %collective-permute-start.1 = (f32[32,1280]{1,0:T(8,128)S(1)}, f32[32,1280]{1,0:T(8,128)S(1)}, u32[]{:S(2)}, u32[]{:S(2)}) collective-permute-start(f32[32,1280]{1,0:T(8,128)S(1)} %get-tuple-element.40.term), channel_id=1, source_target_pairs={{0,16},{16,0},{32,48},{48,32},{64,80},{80,64},{96,112},{112,96},{1... | collective-permute-start | bytes 491528 | tf_op jit(solution)/shard_map/ppermute | solution.py:325
  174.1 57.7 %collective-permute-start.2 = (bf16[896,2048]{1,0:T(8,128)(2,1)}, bf16[896,2048]{1,0:T(8,128)(2,1)}, u32[]{:S(2)}, u32[]{:S(2)}) collective-permute-start(bf16[896,2048]{1,0:T(8,128)(2,1)} %all-gather.5.cloned.1.call-done.down_own), channel_id=1, source_target_pairs={{0,16},{16,0},{32,48},{48,32},{64,80},{80,64},{96,112},{112,96},{1... | collective-permute-start | bytes 11010056 | tf_op jit(solution)/shard_map/ppermute | solution.py:327
  178.5 53.3 %all-to-all-start.2 = ((bf16[4,4,512,256]{3,2,1,0:T(8,128)(2,1)}), bf16[4,4,512,256]{3,2,1,0:T(8,128)(2,1)}, u32[]{:S(2)}, u32[]{:S(2)}) async-start(bf16[4,4,512,256]{3,2,1,0:T(8,128)(2,1)} %broadcast_in_dim.5), calls=%async_computation.2 | async-start | bytes 8388608 | tf_op jit(solution)/shard_map/all_to_all | solution.py:313
  184.4 12.5 %collective-permute-start.3 = (bf16[4,16,1152]{2,1,0:T(8,128)(2,1)S(1)}, bf16[4,16,1152]{2,1,0:T(8,128)(2,1)S(1)}, u32[]{:S(2)}, u32[]{:S(2)}) collective-permute-start(bf16[4,16,1152]{2,1,0:T(8,128)(2,1)S(1)} %get-tuple-element.49), channel_id=1, source_target_pairs={{0,128},{16,144},{32,160},{48,176},{64,192},{80,208},{96,224},{112... | collective-permute-start | bytes 442376 | tf_op jit(solution)/shard_map/ppermute | solution.py:338
  186.3 10.6 %collective-permute-start.4 = (bf16[4,16,1152]{2,1,0:T(8,128)(2,1)S(1)}, bf16[4,16,1152]{2,1,0:T(8,128)(2,1)S(1)}, u32[]{:S(2)}, u32[]{:S(2)}) collective-permute-start(bf16[4,16,1152]{2,1,0:T(8,128)(2,1)S(1)} %get-tuple-element.50), channel_id=1, source_target_pairs={{0,256},{16,272},{32,288},{48,304},{64,320},{80,336},{96,352},{112... | collective-permute-start | bytes 442376 | tf_op jit(solution)/shard_map/ppermute | solution.py:338
  191.0 8.5 %collective-permute-start.5 = (bf16[4,16,1152]{2,1,0:T(8,128)(2,1)S(1)}, bf16[4,16,1152]{2,1,0:T(8,128)(2,1)S(1)}, u32[]{:S(2)}, u32[]{:S(2)}) collective-permute-start(bf16[4,16,1152]{2,1,0:T(8,128)(2,1)S(1)} %get-tuple-element.51), channel_id=1, source_target_pairs={{0,384},{16,400},{32,416},{48,432},{64,448},{80,464},{96,480},{112... | collective-permute-start | bytes 442376 | tf_op jit(solution)/shard_map/ppermute | solution.py:338
  200.1 11.4 %copy-start.1 = (bf16[16,1152]{1,0:T(8,128)(2,1)}, bf16[16,1152]{1,0:T(8,128)(2,1)S(1)}, u32[]{:S(2)}) copy-start(bf16[16,1152]{1,0:T(8,128)(2,1)S(1)} %get-tuple-element.52.one) | copy-start | bytes 110596
  200.1 11.4 %collective-permute-start.6 = (bf16[16,1152]{1,0:T(8,128)(2,1)S(1)}, bf16[16,1152]{1,0:T(8,128)(2,1)S(1)}, u32[]{:S(2)}, u32[]{:S(2)}) collective-permute-start(bf16[16,1152]{1,0:T(8,128)(2,1)S(1)} %get-tuple-element.53), channel_id=1, source_target_pairs={{0,32},{16,48},{32,64},{48,80},{64,96},{80,112},{96,0},{112,16},{1... | collective-permute-start | bytes 110600 | tf_op jit(solution)/shard_map/ppermute | solution.py:349
  202.4 9.2 %collective-permute-start.7 = (bf16[16,1152]{1,0:T(8,128)(2,1)S(1)}, bf16[16,1152]{1,0:T(8,128)(2,1)S(1)}, u32[]{:S(2)}, u32[]{:S(2)}) collective-permute-start(bf16[16,1152]{1,0:T(8,128)(2,1)S(1)} %get-tuple-element.54), channel_id=1, source_target_pairs={{0,64},{16,80},{32,96},{48,112},{64,0},{80,16},{96,32},{112,48},{1... | collective-permute-start | bytes 110600 | tf_op jit(solution)/shard_map/ppermute | solution.py:349
  206.4 6.1 %collective-permute-start.8 = (bf16[16,1152]{1,0:T(8,128)(2,1)S(1)}, bf16[16,1152]{1,0:T(8,128)(2,1)S(1)}, u32[]{:S(2)}, u32[]{:S(2)}) collective-permute-start(bf16[16,1152]{1,0:T(8,128)(2,1)S(1)} %get-tuple-element.55), channel_id=1, source_target_pairs={{0,96},{16,112},{32,0},{48,16},{64,32},{80,48},{96,64},{112,80},{1... | collective-permute-start | bytes 110600 | tf_op jit(solution)/shard_map/ppermute | solution.py:349
  211.6 1.0 copy-start.6
  211.6 1.0 copy-start.7
  212.6 0.6 copy-start.8
Sparse Core Ops, SparseCore 0:
  10.0 164.0 all-gather.4

commit v6 on v4

--- a/solution.py
+++ b/solution.py
@@ -110,10 +110,11 @@
 
 
 def terms(info_s, sums, hidden, cot, grad_rows, term):
-    rank = sums.shape[1] // 2
+    rank = sums.shape[1] // 4
     hid = hidden.shape[1]
     tok = hidden.shape[0]
-    rows = jnp.sum(sums[...], axis=0)
+    rows = jnp.sum(sums[...].astype(jnp.float32), axis=0)
+    rows = rows[: 2 * rank] + rows[2 * rank :]
     in_first = lax.broadcasted_iota(jnp.int32, (rank, tok), 1) < info_s[INFO_CUT]
     proj = rows[:rank]
     grad = ADAPTER_SCALE * rows[rank:]
@@ -174,30 +175,33 @@
         step[0] = jnp.where(active, update, 0.0)
 
 
-def finish(
-    place_s, own, back, ahead, far_low, far_high, down_own, down_back, down_ahead, down_far,
-    grad_rows, pair_a, gate, up, out_gate, out_up, total, far
-):
+def finish(place_s, *refs):
+    halves, refs = (refs[0:5], refs[5:10]), refs[10:]
+    down, refs = refs[:4], refs[4:]
+    grad_rows, pair_a, gate, up, out_gate, out_up, total, far = refs
     place = pl.program_id(0)
+    rows = far.shape[0]
 
     @pl.when(place == 0)
     def _():
         total[...] = tn_dot(grad_rows[...], pair_a[...])
 
-    @pl.when(place < 2)
-    def _():
-        far[...] = far_low[0]
-
-    @pl.when(place >= 2)
-    def _():
-        far[...] = far_high[0]
-
-    total[...] += (
-        nt_dot(own[0], down_own[...])
-        + nt_dot(back[0], down_back[...])
-        + nt_dot(ahead[0], down_ahead[...])
-        + nt_dot(far[...], down_far[...])
-    )
+    for half, (own, back, ahead, far_low, far_high) in enumerate(halves):
+
+        @pl.when(place < 2)
+        def _():
+            far[...] = far_low[0]
+
+        @pl.when(place >= 2)
+        def _():
+            far[...] = far_high[0]
+
+        total[half * rows : (half + 1) * rows, :] += (
+            nt_dot(own[0], down[0][...])
+            + nt_dot(back[0], down[1][...])
+            + nt_dot(ahead[0], down[2][...])
+            + nt_dot(far[...], down[3][...])
+        )
 
     @pl.when(place == pl.num_programs(0) - 1)
     def _():
@@ -233,8 +237,6 @@
     bf16, f32 = jnp.bfloat16, jnp.float32
     shape = jax.ShapeDtypeStruct
 
-    down_full = lax.all_gather(down_matrix, "dp", axis=1, tiled=True)
-
     packed, info_v = pl.pallas_call(
         prepare,
         out_shape=(shape((Z_LO, rank, wide + LANES), bf16), shape((8, LANES), jnp.int32)),
@@ -250,14 +252,17 @@
         adapter_output_factors[0],
     )
     column = lax.all_to_all(packed, "dp", 0, 0, axis_index_groups=ALONG_Z_LO)
-    column, cot_copies = lax.optimization_barrier((column, spread(Z_HI, output_gradient)))
-    cot_z = lax.all_to_all(cot_copies, "tensor", 0, 0, axis_index_groups=ALONG_Z_HI)
+    half = tok // 2
+    column, first_half, down = lax.optimization_barrier(
+        (column, spread(Z_HI, output_gradient[:half]), down_matrix)
+    )
+    cot_first = lax.all_to_all(first_half, "tensor", 0, 0, axis_index_groups=ALONG_Z_HI)
     info_s = info_v[0, :8]
-    hidden = (
-        jax.nn.silu(gate_logits.astype(f32)) * up_projected.astype(f32)
-    ).astype(bf16)
+    gate_f = gate_logits.astype(f32)
+    hidden = (jax.nn.silu(gate_f) * up_projected.astype(f32)).astype(bf16)
     plane = lax.all_gather(column, "dp", axis_index_groups=ALONG_X)
     own = plane.reshape(X * Z_LO, rank, wide + LANES)
+    down_full = lax.all_gather(down, "dp", axis=1, tiled=True)
     other = lax.ppermute(own, "dp", OTHER_CORE)
 
     part, pair, totals = pl.pallas_call(
@@ -274,13 +279,29 @@
     )(info_s, core_s, own, other, hidden, output_gradient)
 
     sums = jnp.sum(lax.all_gather(part, "tensor", axis_index_groups=ALONG_Y), axis=0)
-    cot_z, sums = lax.optimization_barrier((cot_z, sums))
-    back = lax.ppermute(cot_z, "tensor", NEXT_Y)
-    ahead = lax.ppermute(cot_z, "tensor", LAST_Y)
-    sums = lax.all_gather(sums, "tensor", axis_index_groups=ALONG_Z_HI)
-    half = Z_HI // 2
-    far_low = lax.ppermute(back[:half], "tensor", NEXT_Y)
-    far_high = lax.ppermute(ahead[half:], "tensor", LAST_Y)
+    value = sums.astype(bf16)
+    remainder = (sums - value.astype(f32)).astype(bf16)
+    packed_sums = jnp.concatenate([value, remainder]).reshape(-1, feat)
+    second_half = jnp.concatenate([output_gradient[half:], packed_sums])
+    cot_first, second_half = lax.optimization_barrier((cot_first, second_half))
+    arrived = lax.all_to_all(
+        spread(Z_HI, second_half), "tensor", 0, 0, axis_index_groups=ALONG_Z_HI
+    )
+    cot_second = arrived[:, :half]
+    sums = arrived[:, half:].reshape(Z_HI, 4 * rank, tok)
+
+    def near_y(blocks):
+        return lax.ppermute(blocks, "tensor", NEXT_Y), lax.ppermute(blocks, "tensor", LAST_Y)
+
+    def far_y(back, ahead):
+        low = lax.ppermute(back[: Z_HI // 2], "tensor", NEXT_Y)
+        high = lax.ppermute(ahead[Z_HI // 2 :], "tensor", LAST_Y)
+        return low, high
+
+    near_first, sums = lax.optimization_barrier((near_y(cot_first), sums))
+    far_first = far_y(*near_first)
+    near_second = near_y(cot_second)
+    far_second = far_y(*near_second)
 
     grad_rows, term = pl.pallas_call(
         terms,
@@ -304,6 +325,7 @@
     outgoing = outgoing.reshape(X, Z_LO, rank, wide)
     by_x = lax.all_to_all(outgoing, "dp", 0, 0, axis_index_groups=ALONG_X)
     by_x = jnp.sum(by_x.astype(f32), axis=0).astype(bf16)
+    far_first, by_x = lax.optimization_barrier((far_first, by_x))
     incoming = lax.all_to_all(by_x, "dp", 0, 0, axis_index_groups=ALONG_Z_LO)
 
     new_moments_a, new_moments_b, step_a, step_b = pl.pallas_call(
@@ -327,7 +349,15 @@
         )
 
     def by_place(index):
-        return pl.BlockSpec((1, tok, feat), lambda place, y_ref: (index(place), 0, 0))
+        return pl.BlockSpec((1, half, feat), lambda place, y_ref: (index(place), 0, 0))
+
+    half_specs = [
+        by_place(lambda place: place),
+        by_place(lambda place: place),
+        by_place(lambda place: place),
+        by_place(lambda place: jnp.minimum(place, Z_HI // 2 - 1)),
+        by_place(lambda place: jnp.maximum(place - Z_HI // 2, 0)),
+    ]
 
     def whole_of(rows, columns):
         return pl.BlockSpec((rows, columns), lambda place, y_ref: (0, 0))
@@ -339,11 +369,8 @@
             num_scalar_prefetch=1,
             grid=(Z_HI,),
             in_specs=[
-                by_place(lambda place: place),
-                by_place(lambda place: place),
-                by_place(lambda place: place),
-                by_place(lambda place: jnp.minimum(place, half - 1)),
-                by_place(lambda place: jnp.maximum(place - half, 0)),
+                *half_specs,
+                *half_specs,
                 down_block(0),
                 down_block(Y - 1),
                 down_block(1),
@@ -354,17 +381,18 @@
                 whole_of(tok, hid),
             ],
             out_specs=[whole_of(tok, hid), whole_of(tok, hid)],
-            scratch_shapes=[pltpu.VMEM((tok, hid), f32), pltpu.VMEM((tok, feat), bf16)],
+            scratch_shapes=[pltpu.VMEM((tok, hid), f32), pltpu.VMEM((half, feat), bf16)],
         ),
         compiler_params=params(56),
         name="finish",
     )(
         y_s,
-        cot_z,
-        back,
-        ahead,
-        far_low,
-        far_high,
+        cot_first,
+        *near_first,
+        *far_first,
+        cot_second,
+        *near_second,
+        *far_second,
         down_full,
         down_full,
         down_full,

time: 181 us -> 201 us (1.11)
  blocking collectives: 59.2 us -> 27.3 us
  starting transfers between devices: 41 us -> 67.4 us
  waiting for transfers between devices: 38.7 us -> 61.8 us
  local copies, waits for them, and re-layouts: 5.97 us -> 8.05 us
    all_gather x1 -> x0, blocking collectives: 19.6 us -> none  [shards(): sums = lax.all_gather(sums, 'tensor', axis_index_groups=ALONG_Z_HI)]
    all_to_all x1 -> x3, waiting for transfers between devices: 27 us -> 46.3 us  [the longest x1 41.5 us: shards(): lax.all_to_all(spread(Z_HI, second_half), 'tensor', 0, 0, axis_index_grou...]
    all_to_all x1 -> x3, starting transfers between devices: 12.5 us -> 30.5 us  [the longest x1 12.7 us: shards(): lax.all_to_all(first_half, 'tensor', 0, 0, axis_index_groups=ALONG_Z_HI)]
    ppermute x4 -> x8, waiting for transfers between devices: 0.01 us -> 14.2 us  [the longest x2 7.7 us: far_y(): low = lax.ppermute(back[:Z_HI // 2], 'tensor', NEXT_Y)]
    all_to_all x1 -> x0, blocking collectives: 12.8 us -> none  [shards(): column = lax.all_to_all(packed, 'dp', 0, 0, axis_index_groups=ALONG_Z_LO)]
    ppermute x4 -> x8, starting transfers between devices: 11.7 us -> 23.3 us  [the longest x2 7 us: near_y(): lax.ppermute(blocks, 'tensor', LAST_Y)]
    all_to_all x1, waiting for transfers between devices: 5.57 us -> 0.01 us  [shards(): incoming = lax.all_to_all(by_x, 'dp', 0, 0, axis_index_groups=ALONG_Z_LO)]
    all_to_all x1, waiting for transfers between devices: 4.04 us -> 0.01 us  [shards(): by_x = lax.all_to_all(outgoing, 'dp', 0, 0, axis_index_groups=ALONG_X)]
  transfers between devices with their start and end apart: 10 -> 16, of which waited for: 4 -> 6; matrix products, arithmetic and copies ran while one was open for 4% -> 4% of each run, Pallas kernels for 4% -> 3%
where the time goes in v6:
time: 201 us; the launch traced here: 200 us
  starting transfers between devices  67.4 us (34%)
  waiting for transfers between devices  61.8 us (31%)
  blocking collectives  27.3 us (14%)
  Pallas kernels  18.5 us (9%)
  between operations  14.4 us (7%)
  local copies, waits for them, and re-layouts  8.05 us (4%)
  other arithmetic  2.57 us (1%)
    all_to_all x1, waiting for transfers between devices, shards(): lax.all_to_all(spread(Z_HI, second_half), 'tensor', 0, 0, axis_index_grou...  41.5 us
    all_gather x1, blocking collectives, shards(): plane = lax.all_gather(column, 'dp', axis_index_groups=ALONG_X)  14.7 us
    all_to_all x1, starting transfers between devices, shards(): lax.all_to_all(first_half, 'tensor', 0, 0, axis_index_groups=ALONG_Z_HI)  12.7 us
    all_gather x1, blocking collectives, shards(): lax.all_gather(part, 'tensor', axis_index_groups=ALONG_Y)  12.5 us
    all_to_all x1, starting transfers between devices, shards(): lax.all_to_all(spread(Z_HI, second_half), 'tensor', 0, 0, axis_index_grou...  11.9 us
    pallas_call x1, Pallas kernels, shards(): pl.pallas_call(finish, out_shape=(shape((tok, hid), bf16), shape((tok, hi...  11.8 us
    ppermute x2, waiting for transfers between devices, far_y(): low = lax.ppermute(back[:Z_HI // 2], 'tensor', NEXT_Y)  7.7 us
    ppermute x2, starting transfers between devices, near_y(): lax.ppermute(blocks, 'tensor', LAST_Y)  7 us
  transfers between devices with their start and end apart: 16, of which 6 were waited for; matrix products, arithmetic and copies ran while one was open for 4% of the time, Pallas kernels for 3%

profile of v6, /device:TPU:24, one launch (start us, length us, event | category | flops | bytes accessed | tf_op | source)
XLA Modules:
  0.0 200.1 jit_solution(14146474678188069452)
XLA Ops:
  7.2 0.0 copy-start.3
  7.2 1.7 prepare.1
  8.9 5.9 %all-to-all-start = ((bf16[4,16,1280]{2,1,0:T(8,128)(2,1)}), bf16[4,16,1280]{2,1,0:T(8,128)(2,1)S(1)}, u32[]{:S(2)}, u32[]{:S(2)}) async-start(bf16[4,16,1280]{2,1,0:T(8,128)(2,1)} %get-tuple-element.30), calls=%async_computation | async-start | bytes 327680 | tf_op jit(solution)/shard_map/all_to_all | solution.py:254
  14.8 0.0 all-gather.4.cloned.1.call-start
  14.8 1.6 fusion.5
  16.4 4.8 %all-to-all-done = bf16[4,16,1280]{2,1,0:T(8,128)(2,1)S(1)} async-done(((bf16[4,16,1280]{2,1,0:T(8,128)(2,1)}), bf16[4,16,1280]{2,1,0:T(8,128)(2,1)S(1)}, u32[]{:S(2)}, u32[]{:S(2)}) %all-to-all-start) | async-done | bytes 163872 | tf_op jit(solution)/shard_map/all_to_all | solution.py:254
  21.2 0.8 broadcast_in_dim.4
  22.0 0.0 all-gather.4.cloned.1.call-update
  22.1 12.7 %all-to-all-start.1 = ((bf16[4,256,256]{2,1,0:T(8,128)(2,1)}), bf16[4,256,256]{2,1,0:T(8,128)(2,1)}, u32[]{:S(2)}, u32[]{:S(2)}) async-start(bf16[4,256,256]{2,1,0:T(8,128)(2,1)} %broadcast_in_dim.4), calls=%async_computation.1 | async-start | bytes 1048576 | tf_op jit(solution)/shard_map/all_to_all | solution.py:259
  34.8 14.7 %all-gather.own = bf16[16,16,1280]{2,1,0:T(8,128)(2,1)S(1)} all-gather(bf16[4,16,1280]{2,1,0:T(8,128)(2,1)S(1)} %all-to-all-done), channel_id=2, replica_groups={{0,128,256,384},{16,144,272,400},{32,160,288,416},{48,176,304,432},{64,..., dimensions={0}, use_global_device_ids=true | all-gather | bytes 819200 | tf_op jit(solution)/shard_map/all_gather | solution.py:263
  49.5 1.9 collective-permute-start
  51.4 0.7 slice_bitcast_fusion.info_s
  52.1 0.0 copy-done.3
  52.1 1.8 fusion.4.hidden
  53.9 0.0 copy-start.9
  53.9 0.0 collective-permute-done.other
  53.9 0.0 copy-done
  53.9 1.0 low_rank.1
  54.9 12.5 %all-gather.1 = f32[128,512]{1,0:T(8,128)S(1)} all-gather(f32[32,512]{1,0:T(8,128)S(1)} %get-tuple-element.34), channel_id=3, replica_groups={{0,4,8,12},{1,5,9,13},{2,6,10,14},{3,7,11,15},{16,20,24,28},{17,21,25,2..., dimensions={0}, use_global_device_ids=true | all-gather | bytes 327680 | tf_op jit(solution)/shard_map/all_gather | solution.py:281
  67.5 0.0 copy-done.2
  67.6 0.0 copy-done.9
  67.6 0.0 all-to-all-done.1.refs_0_
  67.6 0.9 broadcast_in_dim.5
  68.5 11.9 %all-to-all-start.2 = ((bf16[4,384,256]{2,1,0:T(8,128)(2,1)}), bf16[4,384,256]{2,1,0:T(8,128)(2,1)S(1)}, u32[]{:S(2)}, u32[]{:S(2)}) async-start(bf16[4,384,256]{2,1,0:T(8,128)(2,1)} %broadcast_in_dim.5), calls=%async_computation.2 | async-start | bytes 1572864 | tf_op jit(solution)/shard_map/all_to_all | solution.py:287
  80.4 2.3 %collective-permute-start.1 = (bf16[4,256,256]{2,1,0:T(8,128)(2,1)}, bf16[4,256,256]{2,1,0:T(8,128)(2,1)S(1)}, u32[]{:S(2)}, u32[]{:S(2)}) collective-permute-start(bf16[4,256,256]{2,1,0:T(8,128)(2,1)} %all-to-all-done.1.refs_0_), channel_id=1, source_target_pairs={{0,4},{1,5},{2,6},{3,7},{4,8},{5,9},{6,10},{7,11},{8,12},{9,13},{1... | collective-permute-start | bytes 1572872 | tf_op jit(solution)/shard_map/ppermute | solution.py:294
  82.7 3.5 %collective-permute-start.2 = (bf16[4,256,256]{2,1,0:T(8,128)(2,1)}, bf16[4,256,256]{2,1,0:T(8,128)(2,1)}, u32[]{:S(2)}, u32[]{:S(2)}) collective-permute-start(bf16[4,256,256]{2,1,0:T(8,128)(2,1)} %all-to-all-done.1.refs_0_), channel_id=1, source_target_pairs={{0,12},{1,13},{2,14},{3,15},{4,0},{5,1},{6,2},{7,3},{8,4},{9,5},{1... | collective-permute-start | bytes 1572872 | tf_op jit(solution)/shard_map/ppermute | solution.py:294
  86.3 41.5 %all-to-all-done.2 = bf16[4,384,256]{2,1,0:T(8,128)(2,1)S(1)} async-done(((bf16[4,384,256]{2,1,0:T(8,128)(2,1)}), bf16[4,384,256]{2,1,0:T(8,128)(2,1)S(1)}, u32[]{:S(2)}, u32[]{:S(2)}) %all-to-all-start.2) | async-done | bytes 786464 | tf_op jit(solution)/shard_map/all_to_all | solution.py:287
  127.8 0.1 reshape.43.sums
  127.9 0.0 collective-permute-done.1.refs_1_
  127.9 0.0 copy-start.5
  127.9 0.0 collective-permute-done.2.refs_2_
  127.9 0.8 terms.1
  128.7 0.0 copy-start.1
  128.8 1.9 collective-permute-start.5
  130.7 1.4 collective-permute-done.5.term_other
  132.0 1.4 dense.1
  133.4 6.4 %all-to-all-start.3 = ((bf16[4,4,16,1152]{3,2,1,0:T(8,128)(2,1)}), bf16[4,4,16,1152]{3,2,1,0:T(8,128)(2,1)S(1)}, u32[]{:S(2)}, u32[]{:S(2)}) async-start(bf16[4,4,16,1152]{3,2,1,0:T(8,128)(2,1)} %bitcast.7), calls=%async_computation.3 | async-start | bytes 1179648 | tf_op jit(solution)/shard_map/all_to_all | solution.py:326
  139.9 2.4 %collective-permute-start.6 = (bf16[4,256,256]{2,1,0:T(8,128)(2,1)S(1)}, bf16[4,256,256]{2,1,0:T(8,128)(2,1)S(1)}, u32[]{:S(2)}, u32[]{:S(2)}) collective-permute-start(bf16[4,256,256]{2,1,0:T(8,128)(2,1)S(1)} %slice.41.refs_5_), channel_id=1, source_target_pairs={{0,4},{1,5},{2,6},{3,7},{4,8},{5,9},{6,10},{7,11},{8,12},{9,13},{1... | collective-permute-start | bytes 1572872 | tf_op jit(solution)/shard_map/ppermute | solution.py:294
  142.3 3.5 %collective-permute-start.7 = (bf16[4,256,256]{2,1,0:T(8,128)(2,1)S(1)}, bf16[4,256,256]{2,1,0:T(8,128)(2,1)S(1)}, u32[]{:S(2)}, u32[]{:S(2)}) collective-permute-start(bf16[4,256,256]{2,1,0:T(8,128)(2,1)S(1)} %slice.41.refs_5_), channel_id=1, source_target_pairs={{0,12},{1,13},{2,14},{3,15},{4,0},{5,1},{6,2},{7,3},{8,4},{9,5},{1... | collective-permute-start | bytes 1572872 | tf_op jit(solution)/shard_map/ppermute | solution.py:294
  145.8 0.0 copy-done.1
  145.8 3.6 %collective-permute-start.3 = (bf16[2,256,256]{2,1,0:T(8,128)(2,1)S(1)}, bf16[2,256,256]{2,1,0:T(8,128)(2,1)S(1)}, u32[]{:S(2)}, u32[]{:S(2)}) collective-permute-start(bf16[2,256,256]{2,1,0:T(8,128)(2,1)S(1)} %slice.34), channel_id=1, source_target_pairs={{0,4},{1,5},{2,6},{3,7},{4,8},{5,9},{6,10},{7,11},{8,12},{9,13},{1... | collective-permute-start | bytes 786440 | tf_op jit(solution)/shard_map/ppermute | solution.py:297
  149.4 1.0 slice.35
  150.4 2.3 %collective-permute-start.4 = (bf16[2,256,256]{2,1,0:T(8,128)(2,1)S(1)}, bf16[2,256,256]{2,1,0:T(8,128)(2,1)S(1)}, u32[]{:S(2)}, u32[]{:S(2)}) collective-permute-start(bf16[2,256,256]{2,1,0:T(8,128)(2,1)S(1)} %slice.35), channel_id=1, source_target_pairs={{0,12},{1,13},{2,14},{3,15},{4,0},{5,1},{6,2},{7,3},{8,4},{9,5},{1... | collective-permute-start | bytes 786440 | tf_op jit(solution)/shard_map/ppermute | solution.py:298
  152.6 0.0 all-to-all-done.3
  152.7 0.8 reduce_sum.22
  153.4 7.7 %collective-permute-done.3.refs_3_ = bf16[2,256,256]{2,1,0:T(8,128)(2,1)S(1)} collective-permute-done((bf16[2,256,256]{2,1,0:T(8,128)(2,1)S(1)}, bf16[2,256,256]{2,1,0:T(8,128)(2,1)S(1)}, u32[]{:S(2)}, u32[]{:S(2)}) %collective-permute-start.3) | collective-permute-done | bytes 262176 | tf_op jit(solution)/shard_map/ppermute | solution.py:297
  161.1 3.3 %collective-permute-done.4.refs_4_ = bf16[2,256,256]{2,1,0:T(8,128)(2,1)S(1)} collective-permute-done((bf16[2,256,256]{2,1,0:T(8,128)(2,1)S(1)}, bf16[2,256,256]{2,1,0:T(8,128)(2,1)S(1)}, u32[]{:S(2)}, u32[]{:S(2)}) %collective-permute-start.4) | collective-permute-done | bytes 262176 | tf_op jit(solution)/shard_map/ppermute | solution.py:298
  164.4 3.3 %all-to-all-start.4 = ((bf16[4,16,1152]{2,1,0:T(8,128)(2,1)}), bf16[4,16,1152]{2,1,0:T(8,128)(2,1)S(1)}, u32[]{:S(2)}, u32[]{:S(2)}) async-start(bf16[4,16,1152]{2,1,0:T(8,128)(2,1)} %reduce_sum.22), calls=%async_computation.4 | async-start | bytes 294912 | tf_op jit(solution)/shard_map/all_to_all | solution.py:329
  167.8 0.0 collective-permute-done.6.refs_6_
  167.8 0.0 copy-start.6
  167.8 2.1 %collective-permute-start.8 = (bf16[2,256,256]{2,1,0:T(8,128)(2,1)S(1)}, bf16[2,256,256]{2,1,0:T(8,128)(2,1)S(1)}, u32[]{:S(2)}, u32[]{:S(2)}) collective-permute-start(bf16[2,256,256]{2,1,0:T(8,128)(2,1)S(1)} %slice.42), channel_id=1, source_target_pairs={{0,4},{1,5},{2,6},{3,7},{4,8},{5,9},{6,10},{7,11},{8,12},{9,13},{1... | collective-permute-start | bytes 786440 | tf_op jit(solution)/shard_map/ppermute | solution.py:297
  170.0 0.0 collective-permute-done.7.refs_7_
  170.0 0.0 copy-start.7
  170.0 0.8 slice.43
  170.8 3.7 %collective-permute-start.9 = (bf16[2,256,256]{2,1,0:T(8,128)(2,1)}, bf16[2,256,256]{2,1,0:T(8,128)(2,1)S(1)}, u32[]{:S(2)}, u32[]{:S(2)}) collective-permute-start(bf16[2,256,256]{2,1,0:T(8,128)(2,1)} %slice.43), channel_id=1, source_target_pairs={{0,12},{1,13},{2,14},{3,15},{4,0},{5,1},{6,2},{7,3},{8,4},{9,5},{1... | collective-permute-start | bytes 786440 | tf_op jit(solution)/shard_map/ppermute | solution.py:298
  174.5 0.6 slice.39.refs_15_
  175.1 0.0 all-to-all-done.4.incoming
  175.1 0.7 copy-done.8
  175.8 1.8 adam.1
  177.6 0.0 collective-permute-done.8.refs_8_
  177.6 3.2 %collective-permute-done.9.refs_9_ = bf16[2,256,256]{2,1,0:T(8,128)(2,1)S(1)} collective-permute-done((bf16[2,256,256]{2,1,0:T(8,128)(2,1)}, bf16[2,256,256]{2,1,0:T(8,128)(2,1)S(1)}, u32[]{:S(2)}, u32[]{:S(2)}) %collective-permute-start.9) | collective-permute-done | bytes 262176 | tf_op jit(solution)/shard_map/ppermute | solution.py:298
  180.7 0.0 copy-done.10
  180.8 0.6 copy-done.13
  181.4 11.8 %finish.1 = (bf16[512,896]{1,0:T(8,128)(2,1)}, bf16[512,896]{1,0:T(8,128)(2,1)}) custom-call(s32[1]{0:T(128)} %bitcast.place_s, bf16[4,256,256]{2,1,0:T(8,128)(2,1)} %all-to-all-done.1.refs_0_, bf16[4,256,256]{2,1,0:T(8,128)(2,1)} %copy-done.5, bf16[4,256,256]{2,1,0:T(8,128)(2,1)} %collective-permute-done.2.refs_2_, bf16[2,256,256]{2,1,0:T(8,128)(2,1)} %copy-done.10, ...), custom_call_target="tpu_custom_call" | custom-call | tf_op jit(solution)/shard_map/finish/pallas_call | solution.py:365
  (24 shorter events, 0.2 us)
Async XLA Ops:
  7.2 45.0 %copy-start.3 = (bf16[512,896]{1,0:T(8,128)(2,1)S(1)}, bf16[512,896]{1,0:T(8,128)(2,1)}, u32[]{:S(2)}) copy-start(bf16[512,896]{1,0:T(8,128)(2,1)} %refs_17_.1) | copy-start | bytes 2752516
  8.9 12.3 %all-to-all-start = ((bf16[4,16,1280]{2,1,0:T(8,128)(2,1)}), bf16[4,16,1280]{2,1,0:T(8,128)(2,1)S(1)}, u32[]{:S(2)}, u32[]{:S(2)}) async-start(bf16[4,16,1280]{2,1,0:T(8,128)(2,1)} %get-tuple-element.30), calls=%async_computation | async-start | bytes 327680 | tf_op jit(solution)/shard_map/all_to_all | solution.py:254
  14.8 166.0 %all-gather.4.cloned.1.call-start = ((), (), s32[]{:S(2)}) async-start(), calls=%async_computation.5 | async-start | bytes 7569408 | tf_op jit(solution)/shard_map/all_gather | solution.py:265
  22.1 45.5 %all-to-all-start.1 = ((bf16[4,256,256]{2,1,0:T(8,128)(2,1)}), bf16[4,256,256]{2,1,0:T(8,128)(2,1)}, u32[]{:S(2)}, u32[]{:S(2)}) async-start(bf16[4,256,256]{2,1,0:T(8,128)(2,1)} %broadcast_in_dim.4), calls=%async_computation.1 | async-start | bytes 1048576 | tf_op jit(solution)/shard_map/all_to_all | solution.py:259
  34.8 19.1 %copy-start = (bf16[512,256]{1,0:T(8,128)(2,1)S(1)}, bf16[512,256]{1,0:T(8,128)(2,1)}, u32[]{:S(2)}) copy-start(bf16[512,256]{1,0:T(8,128)(2,1)} %cot.3) | copy-start | bytes 786436
  49.5 4.4 %collective-permute-start = (bf16[16,16,1280]{2,1,0:T(8,128)(2,1)S(1)}, bf16[16,16,1280]{2,1,0:T(8,128)(2,1)S(1)}, u32[]{:S(2)}, u32[]{:S(2)}) collective-permute-start(bf16[16,16,1280]{2,1,0:T(8,128)(2,1)S(1)} %all-gather.own), channel_id=1, source_target_pairs={{0,16},{16,0},{32,48},{48,32},{64,80},{80,64},{96,112},{112,96},{1... | collective-permute-start | bytes 1966088 | tf_op jit(solution)/shard_map/ppermute | solution.py:266
  53.9 13.7 %copy-start.9 = (bf16[256,256]{1,0:T(8,128)(2,1)S(1)}, bf16[256,256]{1,0:T(8,128)(2,1)}, u32[]{:S(2)}) copy-start(bf16[256,256]{1,0:T(8,128)(2,1)} %get-tuple-element.56) | copy-start | bytes 393220
  54.9 12.6 %copy-start.2 = (f32[16,128]{1,0:T(8,128)}, f32[16,128]{1,0:T(8,128)S(1)}, u32[]{:S(2)}) copy-start(f32[16,128]{1,0:T(8,128)S(1)} %get-tuple-element.48.totals) | copy-start | bytes 24580
  68.5 59.2 %all-to-all-start.2 = ((bf16[4,384,256]{2,1,0:T(8,128)(2,1)}), bf16[4,384,256]{2,1,0:T(8,128)(2,1)S(1)}, u32[]{:S(2)}, u32[]{:S(2)}) async-start(bf16[4,384,256]{2,1,0:T(8,128)(2,1)} %broadcast_in_dim.5), calls=%async_computation.2 | async-start | bytes 1572864 | tf_op jit(solution)/shard_map/all_to_all | solution.py:287
  80.4 47.5 %collective-permute-start.1 = (bf16[4,256,256]{2,1,0:T(8,128)(2,1)}, bf16[4,256,256]{2,1,0:T(8,128)(2,1)S(1)}, u32[]{:S(2)}, u32[]{:S(2)}) collective-permute-start(bf16[4,256,256]{2,1,0:T(8,128)(2,1)} %all-to-all-done.1.refs_0_), channel_id=1, source_target_pairs={{0,4},{1,5},{2,6},{3,7},{4,8},{5,9},{6,10},{7,11},{8,12},{9,13},{1... | collective-permute-start | bytes 1572872 | tf_op jit(solution)/shard_map/ppermute | solution.py:294
  82.7 45.2 %collective-permute-start.2 = (bf16[4,256,256]{2,1,0:T(8,128)(2,1)}, bf16[4,256,256]{2,1,0:T(8,128)(2,1)}, u32[]{:S(2)}, u32[]{:S(2)}) collective-permute-start(bf16[4,256,256]{2,1,0:T(8,128)(2,1)} %all-to-all-done.1.refs_0_), channel_id=1, source_target_pairs={{0,12},{1,13},{2,14},{3,15},{4,0},{5,1},{6,2},{7,3},{8,4},{9,5},{1... | collective-permute-start | bytes 1572872 | tf_op jit(solution)/shard_map/ppermute | solution.py:294
  127.9 17.9 %copy-start.5 = (bf16[4,256,256]{2,1,0:T(8,128)(2,1)}, bf16[4,256,256]{2,1,0:T(8,128)(2,1)S(1)}, u32[]{:S(2)}) copy-start(bf16[4,256,256]{2,1,0:T(8,128)(2,1)S(1)} %collective-permute-done.1.refs_1_) | copy-start | bytes 1572868
  128.7 17.1 %copy-start.1 = (bf16[32,512]{1,0:T(8,128)(2,1)}, bf16[32,512]{1,0:T(8,128)(2,1)S(1)}, u32[]{:S(2)}) copy-start(bf16[32,512]{1,0:T(8,128)(2,1)S(1)} %get-tuple-element.44.refs_14_) | copy-start | bytes 98308
  128.8 3.3 %collective-permute-start.5 = (f32[32,1280]{1,0:T(8,128)S(1)}, f32[32,1280]{1,0:T(8,128)S(1)}, u32[]{:S(2)}, u32[]{:S(2)}) collective-permute-start(f32[32,1280]{1,0:T(8,128)S(1)} %get-tuple-element.40.term), channel_id=1, source_target_pairs={{0,16},{16,0},{32,48},{48,32},{64,80},{80,64},{96,112},{112,96},{1... | collective-permute-start | bytes 491528 | tf_op jit(solution)/shard_map/ppermute | solution.py:315
  133.4 19.2 %all-to-all-start.3 = ((bf16[4,4,16,1152]{3,2,1,0:T(8,128)(2,1)}), bf16[4,4,16,1152]{3,2,1,0:T(8,128)(2,1)S(1)}, u32[]{:S(2)}, u32[]{:S(2)}) async-start(bf16[4,4,16,1152]{3,2,1,0:T(8,128)(2,1)} %bitcast.7), calls=%async_computation.3 | async-start | bytes 1179648 | tf_op jit(solution)/shard_map/all_to_all | solution.py:326
  139.9 40.9 %copy-start.4 = (bf16[4,256,256]{2,1,0:T(8,128)(2,1)}, bf16[4,256,256]{2,1,0:T(8,128)(2,1)S(1)}, u32[]{:S(2)}) copy-start(bf16[4,256,256]{2,1,0:T(8,128)(2,1)S(1)} %slice.41.refs_5_) | copy-start | bytes 1572868
  139.9 27.9 %collective-permute-start.6 = (bf16[4,256,256]{2,1,0:T(8,128)(2,1)S(1)}, bf16[4,256,256]{2,1,0:T(8,128)(2,1)S(1)}, u32[]{:S(2)}, u32[]{:S(2)}) collective-permute-start(bf16[4,256,256]{2,1,0:T(8,128)(2,1)S(1)} %slice.41.refs_5_), channel_id=1, source_target_pairs={{0,4},{1,5},{2,6},{3,7},{4,8},{5,9},{6,10},{7,11},{8,12},{9,13},{1... | collective-permute-start | bytes 1572872 | tf_op jit(solution)/shard_map/ppermute | solution.py:294
  142.3 27.7 %collective-permute-start.7 = (bf16[4,256,256]{2,1,0:T(8,128)(2,1)S(1)}, bf16[4,256,256]{2,1,0:T(8,128)(2,1)S(1)}, u32[]{:S(2)}, u32[]{:S(2)}) collective-permute-start(bf16[4,256,256]{2,1,0:T(8,128)(2,1)S(1)} %slice.41.refs_5_), channel_id=1, source_target_pairs={{0,12},{1,13},{2,14},{3,15},{4,0},{5,1},{6,2},{7,3},{8,4},{9,5},{1... | collective-permute-start | bytes 1572872 | tf_op jit(solution)/shard_map/ppermute | solution.py:294
  145.8 15.3 %collective-permute-start.3 = (bf16[2,256,256]{2,1,0:T(8,128)(2,1)S(1)}, bf16[2,256,256]{2,1,0:T(8,128)(2,1)S(1)}, u32[]{:S(2)}, u32[]{:S(2)}) collective-permute-start(bf16[2,256,256]{2,1,0:T(8,128)(2,1)S(1)} %slice.34), channel_id=1, source_target_pairs={{0,4},{1,5},{2,6},{3,7},{4,8},{5,9},{6,10},{7,11},{8,12},{9,13},{1... | collective-permute-start | bytes 786440 | tf_op jit(solution)/shard_map/ppermute | solution.py:297
  150.4 14.1 %collective-permute-start.4 = (bf16[2,256,256]{2,1,0:T(8,128)(2,1)S(1)}, bf16[2,256,256]{2,1,0:T(8,128)(2,1)S(1)}, u32[]{:S(2)}, u32[]{:S(2)}) collective-permute-start(bf16[2,256,256]{2,1,0:T(8,128)(2,1)S(1)} %slice.35), channel_id=1, source_target_pairs={{0,12},{1,13},{2,14},{3,15},{4,0},{5,1},{6,2},{7,3},{8,4},{9,5},{1... | collective-permute-start | bytes 786440 | tf_op jit(solution)/shard_map/ppermute | solution.py:298
  161.1 19.6 %copy-start.10 = (bf16[2,256,256]{2,1,0:T(8,128)(2,1)}, bf16[2,256,256]{2,1,0:T(8,128)(2,1)S(1)}, u32[]{:S(2)}) copy-start(bf16[2,256,256]{2,1,0:T(8,128)(2,1)S(1)} %collective-permute-done.3.refs_3_) | copy-start | bytes 786436
  164.4 16.3 %copy-start.11 = (bf16[2,256,256]{2,1,0:T(8,128)(2,1)}, bf16[2,256,256]{2,1,0:T(8,128)(2,1)S(1)}, u32[]{:S(2)}) copy-start(bf16[2,256,256]{2,1,0:T(8,128)(2,1)S(1)} %collective-permute-done.4.refs_4_) | copy-start | bytes 786436
  164.4 10.7 %all-to-all-start.4 = ((bf16[4,16,1152]{2,1,0:T(8,128)(2,1)}), bf16[4,16,1152]{2,1,0:T(8,128)(2,1)S(1)}, u32[]{:S(2)}, u32[]{:S(2)}) async-start(bf16[4,16,1152]{2,1,0:T(8,128)(2,1)} %reduce_sum.22), calls=%async_computation.4 | async-start | bytes 294912 | tf_op jit(solution)/shard_map/all_to_all | solution.py:329
  167.8 13.0 %copy-start.6 = (bf16[4,256,256]{2,1,0:T(8,128)(2,1)}, bf16[4,256,256]{2,1,0:T(8,128)(2,1)S(1)}, u32[]{:S(2)}) copy-start(bf16[4,256,256]{2,1,0:T(8,128)(2,1)S(1)} %collective-permute-done.6.refs_6_) | copy-start | bytes 1572868
  167.8 9.8 %collective-permute-start.8 = (bf16[2,256,256]{2,1,0:T(8,128)(2,1)S(1)}, bf16[2,256,256]{2,1,0:T(8,128)(2,1)S(1)}, u32[]{:S(2)}, u32[]{:S(2)}) collective-permute-start(bf16[2,256,256]{2,1,0:T(8,128)(2,1)S(1)} %slice.42), channel_id=1, source_target_pairs={{0,4},{1,5},{2,6},{3,7},{4,8},{5,9},{6,10},{7,11},{8,12},{9,13},{1... | collective-permute-start | bytes 786440 | tf_op jit(solution)/shard_map/ppermute | solution.py:297
  170.0 10.8 %copy-start.7 = (bf16[4,256,256]{2,1,0:T(8,128)(2,1)}, bf16[4,256,256]{2,1,0:T(8,128)(2,1)S(1)}, u32[]{:S(2)}) copy-start(bf16[4,256,256]{2,1,0:T(8,128)(2,1)S(1)} %collective-permute-done.7.refs_7_) | copy-start | bytes 1572868
  170.8 10.0 %collective-permute-start.9 = (bf16[2,256,256]{2,1,0:T(8,128)(2,1)}, bf16[2,256,256]{2,1,0:T(8,128)(2,1)S(1)}, u32[]{:S(2)}, u32[]{:S(2)}) collective-permute-start(bf16[2,256,256]{2,1,0:T(8,128)(2,1)} %slice.43), channel_id=1, source_target_pairs={{0,12},{1,13},{2,14},{3,15},{4,0},{5,1},{6,2},{7,3},{8,4},{9,5},{1... | collective-permute-start | bytes 786440 | tf_op jit(solution)/shard_map/ppermute | solution.py:298
  175.1 0.7 copy-start.8
  177.6 3.2 %copy-start.12 = (bf16[2,256,256]{2,1,0:T(8,128)(2,1)}, bf16[2,256,256]{2,1,0:T(8,128)(2,1)S(1)}, u32[]{:S(2)}) copy-start(bf16[2,256,256]{2,1,0:T(8,128)(2,1)S(1)} %collective-permute-done.8.refs_8_) | copy-start | bytes 786436
  180.7 0.7 copy-start.13
Sparse Core Ops, SparseCore 0:
  22.2 135.3 all-gather.3

commit v7 on v4

--- a/solution.py
+++ b/solution.py
@@ -274,13 +274,10 @@
     )(info_s, core_s, own, other, hidden, output_gradient)
 
     sums = jnp.sum(lax.all_gather(part, "tensor", axis_index_groups=ALONG_Y), axis=0)
+    sums = lax.all_gather(sums, "tensor", axis_index_groups=ALONG_Z_HI)
     cot_z, sums = lax.optimization_barrier((cot_z, sums))
     back = lax.ppermute(cot_z, "tensor", NEXT_Y)
     ahead = lax.ppermute(cot_z, "tensor", LAST_Y)
-    sums = lax.all_gather(sums, "tensor", axis_index_groups=ALONG_Z_HI)
-    half = Z_HI // 2
-    far_low = lax.ppermute(back[:half], "tensor", NEXT_Y)
-    far_high = lax.ppermute(ahead[half:], "tensor", LAST_Y)
 
     grad_rows, term = pl.pallas_call(
         terms,
@@ -304,6 +301,10 @@
     outgoing = outgoing.reshape(X, Z_LO, rank, wide)
     by_x = lax.all_to_all(outgoing, "dp", 0, 0, axis_index_groups=ALONG_X)
     by_x = jnp.sum(by_x.astype(f32), axis=0).astype(bf16)
+    back, ahead, by_x = lax.optimization_barrier((back, ahead, by_x))
+    half = Z_HI // 2
+    far_low = lax.ppermute(back[:half], "tensor", NEXT_Y)
+    far_high = lax.ppermute(ahead[half:], "tensor", LAST_Y)
     incoming = lax.all_to_all(by_x, "dp", 0, 0, axis_index_groups=ALONG_Z_LO)
 
     new_moments_a, new_moments_b, step_a, step_b = pl.pallas_call(

time: 181 us -> 183 us (1.011)
  blocking collectives: 59.2 us -> 100 us
  waiting for transfers between devices: 38.7 us -> 8.18 us
  starting transfers between devices: 41 us -> 31.9 us
    all_to_all x1, waiting for transfers between devices: 27 us -> 0.01 us  [shards(): lax.all_to_all(cot_copies, 'tensor', 0, 0, axis_index_groups=ALONG_Z_HI)]
    all_to_all x0 -> x1, blocking collectives: none -> 23.7 us  [shards(): by_x = lax.all_to_all(outgoing, 'dp', 0, 0, axis_index_groups=ALONG_X)]
    all_gather x1, blocking collectives: 19.6 us -> 36.9 us  [shards(): sums = lax.all_gather(sums, 'tensor', axis_index_groups=ALONG_Z_HI)]
    all_to_all x1 -> x0, starting transfers between devices: 9.66 us -> none  [shards(): by_x = lax.all_to_all(outgoing, 'dp', 0, 0, axis_index_groups=ALONG_X)]
    all_to_all x1 -> x0, waiting for transfers between devices: 4.04 us -> none  [shards(): by_x = lax.all_to_all(outgoing, 'dp', 0, 0, axis_index_groups=ALONG_X)]
  transfers between devices with their start and end apart: 10 -> 9, of which waited for: 4 -> 3; matrix products, arithmetic and copies ran while one was open for 4% -> 4% of each run, Pallas kernels for 4% -> 3%
where the time goes in v7:
time: 183 us; the launch traced here: 181 us
  blocking collectives  100 us (55%)
  starting transfers between devices  31.9 us (17%)
  Pallas kernels  16.9 us (9%)
  between operations  14.2 us (8%)
  waiting for transfers between devices  8.18 us (4%)
  local copies, waits for them, and re-layouts  6.86 us (4%)
  other arithmetic  2.54 us (1%)
    all_gather x1, blocking collectives, shards(): sums = lax.all_gather(sums, 'tensor', axis_index_groups=ALONG_Z_HI)  36.9 us
    all_to_all x1, blocking collectives, shards(): by_x = lax.all_to_all(outgoing, 'dp', 0, 0, axis_index_groups=ALONG_X)  23.7 us
    all_gather x1, blocking collectives, shards(): plane = lax.all_gather(column, 'dp', axis_index_groups=ALONG_X)  14.5 us
    all_to_all x1, blocking collectives, shards(): column = lax.all_to_all(packed, 'dp', 0, 0, axis_index_groups=ALONG_Z_LO)  12.8 us
    all_to_all x1, starting transfers between devices, shards(): lax.all_to_all(cot_copies, 'tensor', 0, 0, axis_index_groups=ALONG_Z_HI)  12.5 us
    all_gather x1, blocking collectives, shards(): lax.all_gather(part, 'tensor', axis_index_groups=ALONG_Y)  12.3 us
    pallas_call x1, Pallas kernels, shards(): pl.pallas_call(finish, out_shape=(shape((tok, hid), bf16), shape((tok, hi...  11.1 us
    all_to_all x1, waiting for transfers between devices, shards(): incoming = lax.all_to_all(by_x, 'dp', 0, 0, axis_index_groups=ALONG_Z_LO)  5.34 us
  transfers between devices with their start and end apart: 9, of which 3 were waited for; matrix products, arithmetic and copies ran while one was open for 4% of the time, Pallas kernels for 3%

profile of v7, /device:TPU:24, one launch (start us, length us, event | category | flops | bytes accessed | tf_op | source)
XLA Modules:
  0.0 180.7 jit_solution(13970970122436646602)
XLA Ops:
  7.2 0.0 all-gather.5.cloned.1.call-start
  7.2 0.7 all-gather.5.cloned.1.call-update
  7.9 1.6 prepare.1
  9.5 12.8 %all_to_all.20 = bf16[4,16,1280]{2,1,0:T(8,128)(2,1)S(1)} all-to-all(bf16[4,16,1280]{2,1,0:T(8,128)(2,1)} %get-tuple-element.26), channel_id=1, replica_groups={{0,32,64,96},{16,48,80,112},{128,160,192,224},{144,176,208,240},{256,28..., dimensions={0} | all-to-all | bytes 327680 | tf_op jit(solution)/shard_map/all_to_all | solution.py:252
  22.4 0.0 copy-start.3
  22.4 2.2 %broadcast_in_dim.2 = bf16[4,512,256]{2,1,0:T(8,128)(2,1)} broadcast(bf16[512,256]{1,0:T(8,128)(2,1)} %cot.3), dimensions={1,2} | broadcast | bytes 1310720 | tf_op jit(solution)/shard_map/broadcast_in_dim | solution.py:53
  24.6 12.5 %all-to-all-start.1 = ((bf16[4,512,256]{2,1,0:T(8,128)(2,1)}), bf16[4,512,256]{2,1,0:T(8,128)(2,1)}, u32[]{:S(2)}, u32[]{:S(2)}) async-start(bf16[4,512,256]{2,1,0:T(8,128)(2,1)} %broadcast_in_dim.2), calls=%async_computation.1 | async-start | bytes 2097152 | tf_op jit(solution)/shard_map/all_to_all | solution.py:254
  37.1 0.0 copy-start
  37.1 14.5 %all-gather.own = bf16[16,16,1280]{2,1,0:T(8,128)(2,1)S(1)} all-gather(bf16[4,16,1280]{2,1,0:T(8,128)(2,1)S(1)} %all_to_all.20), channel_id=2, replica_groups={{0,128,256,384},{16,144,272,400},{32,160,288,416},{48,176,304,432},{64,..., dimensions={0}, use_global_device_ids=true | all-gather | bytes 819200 | tf_op jit(solution)/shard_map/all_gather | solution.py:259
  51.6 1.9 %collective-permute-start = (bf16[16,16,1280]{2,1,0:T(8,128)(2,1)S(1)}, bf16[16,16,1280]{2,1,0:T(8,128)(2,1)S(1)}, u32[]{:S(2)}, u32[]{:S(2)}) collective-permute-start(bf16[16,16,1280]{2,1,0:T(8,128)(2,1)S(1)} %all-gather.own), channel_id=1, source_target_pairs={{0,16},{16,0},{32,48},{48,32},{64,80},{80,64},{96,112},{112,96},{1... | collective-permute-start | bytes 1966088 | tf_op jit(solution)/shard_map/ppermute | solution.py:261
  53.5 0.7 slice_bitcast_fusion.info_s
  54.2 0.0 copy-done.3
  54.2 1.8 fusion.4.hidden
  55.9 0.0 collective-permute-done.other
  56.0 0.0 copy-done
  56.0 1.0 low_rank.1
  57.0 0.0 copy-start.2
  57.0 12.3 %all-gather.1 = f32[128,512]{1,0:T(8,128)S(1)} all-gather(f32[32,512]{1,0:T(8,128)S(1)} %get-tuple-element.30), channel_id=3, replica_groups={{0,4,8,12},{1,5,9,13},{2,6,10,14},{3,7,11,15},{16,20,24,28},{17,21,25,2..., dimensions={0}, use_global_device_ids=true | all-gather | bytes 327680 | tf_op jit(solution)/shard_map/all_gather | solution.py:276
  69.2 0.0 copy-done.2
  69.3 36.9 %all-gather.2 = f32[128,512]{1,0:T(8,128)S(1)} all-gather(f32[32,512]{1,0:T(8,128)S(1)} %reduce_sum.21), channel_id=4, replica_groups={{0,1,2,3},{4,5,6,7},{8,9,10,11},{12,13,14,15},{16,17,18,19},{20,21,22,2..., dimensions={0}, use_global_device_ids=true | all-gather | bytes 327680 | tf_op jit(solution)/shard_map/all_gather | solution.py:277
  106.2 0.0 all-to-all-done.1.own
  106.2 3.5 %collective-permute-start.1 = (bf16[4,512,256]{2,1,0:T(8,128)(2,1)}, bf16[4,512,256]{2,1,0:T(8,128)(2,1)S(1)}, u32[]{:S(2)}, u32[]{:S(2)}) collective-permute-start(bf16[4,512,256]{2,1,0:T(8,128)(2,1)} %all-to-all-done.1.own), channel_id=1, source_target_pairs={{0,4},{1,5},{2,6},{3,7},{4,8},{5,9},{6,10},{7,11},{8,12},{9,13},{1... | collective-permute-start | bytes 3145736 | tf_op jit(solution)/shard_map/ppermute | solution.py:279
  109.8 2.3 %collective-permute-start.2 = (bf16[4,512,256]{2,1,0:T(8,128)(2,1)}, bf16[4,512,256]{2,1,0:T(8,128)(2,1)}, u32[]{:S(2)}, u32[]{:S(2)}) collective-permute-start(bf16[4,512,256]{2,1,0:T(8,128)(2,1)} %all-to-all-done.1.own), channel_id=1, source_target_pairs={{0,12},{1,13},{2,14},{3,15},{4,0},{5,1},{6,2},{7,3},{8,4},{9,5},{1... | collective-permute-start | bytes 3145736 | tf_op jit(solution)/shard_map/ppermute | solution.py:280
  112.0 0.8 terms.1
  112.9 0.0 copy-start.1
  112.9 1.9 %collective-permute-start.3 = (f32[32,1280]{1,0:T(8,128)S(1)}, f32[32,1280]{1,0:T(8,128)S(1)}, u32[]{:S(2)}, u32[]{:S(2)}) collective-permute-start(f32[32,1280]{1,0:T(8,128)S(1)} %get-tuple-element.33.term), channel_id=1, source_target_pairs={{0,16},{16,0},{32,48},{48,32},{64,80},{80,64},{96,112},{112,96},{1... | collective-permute-start | bytes 491528 | tf_op jit(solution)/shard_map/ppermute | solution.py:291
  114.8 1.4 collective-permute-done.3.term_other
  116.2 0.6 dense.1
  116.8 23.7 %all_to_all.21 = bf16[4,4,16,1152]{3,2,1,0:T(8,128)(2,1)S(1)} all-to-all(bf16[4,4,16,1152]{3,2,1,0:T(8,128)(2,1)S(1)} %bitcast.11), channel_id=1, replica_groups={{0,128,256,384},{16,144,272,400},{32,160,288,416},{48,176,304,432},{64,..., dimensions={0} | all-to-all | bytes 1179648 | tf_op jit(solution)/shard_map/all_to_all | solution.py:302
  140.4 0.8 reduce_sum.22
  141.2 0.0 collective-permute-done.1.back
  141.2 0.0 copy-start.4
  141.2 0.0 collective-permute-done.2.ahead
  141.2 0.0 copy-done.1
  141.3 2.8 %collective-permute-start.4 = (bf16[2,512,256]{2,1,0:T(8,128)(2,1)S(1)}, bf16[2,512,256]{2,1,0:T(8,128)(2,1)S(1)}, u32[]{:S(2)}, u32[]{:S(2)}) collective-permute-start(bf16[2,512,256]{2,1,0:T(8,128)(2,1)S(1)} %slice.13), channel_id=1, source_target_pairs={{0,4},{1,5},{2,6},{3,7},{4,8},{5,9},{6,10},{7,11},{8,12},{9,13},{1... | collective-permute-start | bytes 1572872 | tf_op jit(solution)/shard_map/ppermute | solution.py:306
  144.0 1.9 %slice.14 = bf16[2,512,256]{2,1,0:T(8,128)(2,1)} slice(bf16[4,512,256]{2,1,0:T(8,128)(2,1)} %collective-permute-done.2.ahead), slice={[2:4], [0:512], [0:256]} | slice | bytes 1048576 | tf_op jit(solution)/shard_map/slice | solution.py:307
  145.9 3.1 %collective-permute-start.5 = (bf16[2,512,256]{2,1,0:T(8,128)(2,1)}, bf16[2,512,256]{2,1,0:T(8,128)(2,1)S(1)}, u32[]{:S(2)}, u32[]{:S(2)}) collective-permute-start(bf16[2,512,256]{2,1,0:T(8,128)(2,1)} %slice.14), channel_id=1, source_target_pairs={{0,12},{1,13},{2,14},{3,15},{4,0},{5,1},{6,2},{7,3},{8,4},{9,5},{1... | collective-permute-start | bytes 1572872 | tf_op jit(solution)/shard_map/ppermute | solution.py:307
  149.0 3.8 %all-to-all-start.3 = ((bf16[4,16,1152]{2,1,0:T(8,128)(2,1)}), bf16[4,16,1152]{2,1,0:T(8,128)(2,1)S(1)}, u32[]{:S(2)}, u32[]{:S(2)}) async-start(bf16[4,16,1152]{2,1,0:T(8,128)(2,1)} %reduce_sum.22), calls=%async_computation.3 | async-start | bytes 294912 | tf_op jit(solution)/shard_map/all_to_all | solution.py:308
  152.8 0.6 slice.15.pair_a
  153.4 5.3 %all-to-all-done.3.incoming = bf16[4,16,1152]{2,1,0:T(8,128)(2,1)S(1)} async-done(((bf16[4,16,1152]{2,1,0:T(8,128)(2,1)}), bf16[4,16,1152]{2,1,0:T(8,128)(2,1)S(1)}, u32[]{:S(2)}, u32[]{:S(2)}) %all-to-all-start.3) | async-done | bytes 147488 | tf_op jit(solution)/shard_map/all_to_all | solution.py:308
  158.7 0.0 copy-start.5
  158.7 0.7 copy-done.5
  159.4 1.8 adam.1
  161.2 0.0 collective-permute-done.4.far_low
  161.2 0.0 copy-start.6
  161.2 0.8 collective-permute-done.5.far_high
  162.0 0.0 copy-start.7
  162.0 0.0 all-gather.5.cloned.1.call-done.down_own.down_back.down_ahead.down_far
  162.0 0.0 copy-done.4
  162.0 0.0 copy-done.6
  162.0 0.8 copy-done.7
  162.8 11.1 %finish.1 = (bf16[512,896]{1,0:T(8,128)(2,1)}, bf16[512,896]{1,0:T(8,128)(2,1)}) custom-call(s32[1]{0:T(128)} %bitcast.place_s, bf16[4,512,256]{2,1,0:T(8,128)(2,1)} %all-to-all-done.1.own, bf16[4,512,256]{2,1,0:T(8,128)(2,1)} %copy-done.4, bf16[4,512,256]{2,1,0:T(8,128)(2,1)} %collective-permute-done.2.ahead, bf16[2,512,256]{2,1,0:T(8,128)(2,1)} %copy-done.6, ...), custom_call_target="tpu_custom_call" | custom-call | tf_op jit(solution)/shard_map/finish/pallas_call | solution.py:336
  (2 shorter events, 0.1 us)
Async XLA Ops:
  7.2 154.8 %all-gather.5.cloned.1.call-start = ((), (), s32[]{:S(2)}) async-start(), calls=%async_computation.4 | async-start | bytes 7569408 | tf_op jit(solution)/shard_map/all_gather | solution.py:236
  22.4 31.8 %copy-start.3 = (bf16[512,896]{1,0:T(8,128)(2,1)S(1)}, bf16[512,896]{1,0:T(8,128)(2,1)}, u32[]{:S(2)}) copy-start(bf16[512,896]{1,0:T(8,128)(2,1)} %up.1) | copy-start | bytes 2752516
  24.6 81.6 %all-to-all-start.1 = ((bf16[4,512,256]{2,1,0:T(8,128)(2,1)}), bf16[4,512,256]{2,1,0:T(8,128)(2,1)}, u32[]{:S(2)}, u32[]{:S(2)}) async-start(bf16[4,512,256]{2,1,0:T(8,128)(2,1)} %broadcast_in_dim.2), calls=%async_computation.1 | async-start | bytes 2097152 | tf_op jit(solution)/shard_map/all_to_all | solution.py:254
  37.1 18.9 %copy-start = (bf16[512,256]{1,0:T(8,128)(2,1)S(1)}, bf16[512,256]{1,0:T(8,128)(2,1)}, u32[]{:S(2)}) copy-start(bf16[512,256]{1,0:T(8,128)(2,1)} %cot.3) | copy-start | bytes 786436
  51.6 4.4 %collective-permute-start = (bf16[16,16,1280]{2,1,0:T(8,128)(2,1)S(1)}, bf16[16,16,1280]{2,1,0:T(8,128)(2,1)S(1)}, u32[]{:S(2)}, u32[]{:S(2)}) collective-permute-start(bf16[16,16,1280]{2,1,0:T(8,128)(2,1)S(1)} %all-gather.own), channel_id=1, source_target_pairs={{0,16},{16,0},{32,48},{48,32},{64,80},{80,64},{96,112},{112,96},{1... | collective-permute-start | bytes 1966088 | tf_op jit(solution)/shard_map/ppermute | solution.py:261
  57.0 12.3 %copy-start.2 = (f32[16,128]{1,0:T(8,128)}, f32[16,128]{1,0:T(8,128)S(1)}, u32[]{:S(2)}) copy-start(f32[16,128]{1,0:T(8,128)S(1)} %get-tuple-element.40.totals) | copy-start | bytes 24580
  106.2 35.0 %collective-permute-start.1 = (bf16[4,512,256]{2,1,0:T(8,128)(2,1)}, bf16[4,512,256]{2,1,0:T(8,128)(2,1)S(1)}, u32[]{:S(2)}, u32[]{:S(2)}) collective-permute-start(bf16[4,512,256]{2,1,0:T(8,128)(2,1)} %all-to-all-done.1.own), channel_id=1, source_target_pairs={{0,4},{1,5},{2,6},{3,7},{4,8},{5,9},{6,10},{7,11},{8,12},{9,13},{1... | collective-permute-start | bytes 3145736 | tf_op jit(solution)/shard_map/ppermute | solution.py:279
  109.8 31.4 %collective-permute-start.2 = (bf16[4,512,256]{2,1,0:T(8,128)(2,1)}, bf16[4,512,256]{2,1,0:T(8,128)(2,1)}, u32[]{:S(2)}, u32[]{:S(2)}) collective-permute-start(bf16[4,512,256]{2,1,0:T(8,128)(2,1)} %all-to-all-done.1.own), channel_id=1, source_target_pairs={{0,12},{1,13},{2,14},{3,15},{4,0},{5,1},{6,2},{7,3},{8,4},{9,5},{1... | collective-permute-start | bytes 3145736 | tf_op jit(solution)/shard_map/ppermute | solution.py:280
  112.9 28.4 %copy-start.1 = (bf16[32,512]{1,0:T(8,128)(2,1)}, bf16[32,512]{1,0:T(8,128)(2,1)S(1)}, u32[]{:S(2)}) copy-start(bf16[32,512]{1,0:T(8,128)(2,1)S(1)} %get-tuple-element.36.grad_rows) | copy-start | bytes 98308
  112.9 3.3 %collective-permute-start.3 = (f32[32,1280]{1,0:T(8,128)S(1)}, f32[32,1280]{1,0:T(8,128)S(1)}, u32[]{:S(2)}, u32[]{:S(2)}) collective-permute-start(f32[32,1280]{1,0:T(8,128)S(1)} %get-tuple-element.33.term), channel_id=1, source_target_pairs={{0,16},{16,0},{32,48},{48,32},{64,80},{80,64},{96,112},{112,96},{1... | collective-permute-start | bytes 491528 | tf_op jit(solution)/shard_map/ppermute | solution.py:291
  141.2 20.8 %copy-start.4 = (bf16[4,512,256]{2,1,0:T(8,128)(2,1)}, bf16[4,512,256]{2,1,0:T(8,128)(2,1)S(1)}, u32[]{:S(2)}) copy-start(bf16[4,512,256]{2,1,0:T(8,128)(2,1)S(1)} %collective-permute-done.1.back) | copy-start | bytes 3145732
  141.3 20.0 %collective-permute-start.4 = (bf16[2,512,256]{2,1,0:T(8,128)(2,1)S(1)}, bf16[2,512,256]{2,1,0:T(8,128)(2,1)S(1)}, u32[]{:S(2)}, u32[]{:S(2)}) collective-permute-start(bf16[2,512,256]{2,1,0:T(8,128)(2,1)S(1)} %slice.13), channel_id=1, source_target_pairs={{0,4},{1,5},{2,6},{3,7},{4,8},{5,9},{6,10},{7,11},{8,12},{9,13},{1... | collective-permute-start | bytes 1572872 | tf_op jit(solution)/shard_map/ppermute | solution.py:306
  145.9 16.1 %collective-permute-start.5 = (bf16[2,512,256]{2,1,0:T(8,128)(2,1)}, bf16[2,512,256]{2,1,0:T(8,128)(2,1)S(1)}, u32[]{:S(2)}, u32[]{:S(2)}) collective-permute-start(bf16[2,512,256]{2,1,0:T(8,128)(2,1)} %slice.14), channel_id=1, source_target_pairs={{0,12},{1,13},{2,14},{3,15},{4,0},{5,1},{6,2},{7,3},{8,4},{9,5},{1... | collective-permute-start | bytes 1572872 | tf_op jit(solution)/shard_map/ppermute | solution.py:307
  149.0 9.8 %all-to-all-start.3 = ((bf16[4,16,1152]{2,1,0:T(8,128)(2,1)}), bf16[4,16,1152]{2,1,0:T(8,128)(2,1)S(1)}, u32[]{:S(2)}, u32[]{:S(2)}) async-start(bf16[4,16,1152]{2,1,0:T(8,128)(2,1)} %reduce_sum.22), calls=%async_computation.3 | async-start | bytes 294912 | tf_op jit(solution)/shard_map/all_to_all | solution.py:308
  158.7 0.7 copy-start.5
  161.2 0.8 copy-start.6
  162.0 0.8 copy-start.7
Sparse Core Ops, SparseCore 0:
  10.1 138.7 all-gather.4

commit v8 on v4

--- a/solution.py
+++ b/solution.py
@@ -274,10 +274,10 @@
     )(info_s, core_s, own, other, hidden, output_gradient)
 
     sums = jnp.sum(lax.all_gather(part, "tensor", axis_index_groups=ALONG_Y), axis=0)
+    sums = lax.all_gather(sums, "tensor", axis_index_groups=ALONG_Z_HI)
     cot_z, sums = lax.optimization_barrier((cot_z, sums))
     back = lax.ppermute(cot_z, "tensor", NEXT_Y)
     ahead = lax.ppermute(cot_z, "tensor", LAST_Y)
-    sums = lax.all_gather(sums, "tensor", axis_index_groups=ALONG_Z_HI)
     half = Z_HI // 2
     far_low = lax.ppermute(back[:half], "tensor", NEXT_Y)
     far_high = lax.ppermute(ahead[half:], "tensor", LAST_Y)
@@ -370,7 +370,7 @@
         down_full,
         down_full,
         grad_rows,
-        pair[:, :hid],
+        pair,
         gate_logits,
         up_projected,
     )

time: 181 us -> 182 us (level)
  the two profiles are of different devices: /device:TPU:24 before, /device:TPU:6 now
where the time goes in v8:
time: 182 us; the launch traced here: 181 us
  blocking collectives  82.7 us (45%)
  starting transfers between devices  38.5 us (21%)
  waiting for transfers between devices  17.7 us (10%)
  Pallas kernels  17.7 us (10%)
  between operations  14.2 us (8%)
  local copies, waits for them, and re-layouts  7.18 us (4%)
  other arithmetic  2.81 us (2%)
    all_gather x1, blocking collectives, shards(): sums = lax.all_gather(sums, 'tensor', axis_index_groups=ALONG_Z_HI)  43.3 us
    all_gather x1, blocking collectives, shards(): plane = lax.all_gather(column, 'dp', axis_index_groups=ALONG_X)  13.6 us
    all_gather x1, blocking collectives, shards(): lax.all_gather(part, 'tensor', axis_index_groups=ALONG_Y)  12.9 us
    all_to_all x1, blocking collectives, shards(): column = lax.all_to_all(packed, 'dp', 0, 0, axis_index_groups=ALONG_Z_LO)  12.8 us
    all_to_all x1, starting transfers between devices, shards(): lax.all_to_all(cot_copies, 'tensor', 0, 0, axis_index_groups=ALONG_Z_HI)  12.5 us
    pallas_call x1, Pallas kernels, shards(): pl.pallas_call(finish, out_shape=(shape((tok, hid), bf16), shape((tok, hi...  11.1 us
    ppermute x1, waiting for transfers between devices, shards(): back = lax.ppermute(cot_z, 'tensor', NEXT_Y)  9.65 us
    all_to_all x1, waiting for transfers between devices, shards(): incoming = lax.all_to_all(by_x, 'dp', 0, 0, axis_index_groups=ALONG_Z_LO)  5.93 us
  transfers between devices with their start and end apart: 10, of which 3 were waited for; matrix products, arithmetic and copies ran while one was open for 4% of the time, Pallas kernels for 4%

profile of v8, /device:TPU:6, one launch (start us, length us, event | category | flops | bytes accessed | tf_op | source)
XLA Modules:
  0.0 180.7 jit_solution(13589585010190616255)
XLA Ops:
  7.2 0.0 all-gather.5.cloned.1.call-start
  7.2 0.7 all-gather.5.cloned.1.call-update
  7.9 1.6 prepare.1
  9.5 12.8 %all_to_all.20 = bf16[4,16,1280]{2,1,0:T(8,128)(2,1)S(1)} all-to-all(bf16[4,16,1280]{2,1,0:T(8,128)(2,1)} %get-tuple-element.23), channel_id=1, replica_groups={{0,32,64,96},{16,48,80,112},{128,160,192,224},{144,176,208,240},{256,28..., dimensions={0} | all-to-all | bytes 327680 | tf_op jit(solution)/shard_map/all_to_all | solution.py:252
  22.4 2.1 %broadcast_in_dim.2 = bf16[4,512,256]{2,1,0:T(8,128)(2,1)} broadcast(bf16[512,256]{1,0:T(8,128)(2,1)} %cot.3), dimensions={1,2} | broadcast | bytes 1310720 | tf_op jit(solution)/shard_map/broadcast_in_dim | solution.py:53
  24.5 12.5 %all-to-all-start.1 = ((bf16[4,512,256]{2,1,0:T(8,128)(2,1)}), bf16[4,512,256]{2,1,0:T(8,128)(2,1)S(1)}, u32[]{:S(2)}, u32[]{:S(2)}) async-start(bf16[4,512,256]{2,1,0:T(8,128)(2,1)} %broadcast_in_dim.2), calls=%async_computation.1 | async-start | bytes 2097152 | tf_op jit(solution)/shard_map/all_to_all | solution.py:254
  37.0 0.0 copy-start
  37.0 13.6 %all-gather.own = bf16[16,16,1280]{2,1,0:T(8,128)(2,1)S(1)} all-gather(bf16[4,16,1280]{2,1,0:T(8,128)(2,1)S(1)} %all_to_all.20), channel_id=2, replica_groups={{0,128,256,384},{16,144,272,400},{32,160,288,416},{48,176,304,432},{64,..., dimensions={0}, use_global_device_ids=true | all-gather | bytes 819200 | tf_op jit(solution)/shard_map/all_gather | solution.py:259
  50.6 1.9 %collective-permute-start = (bf16[16,16,1280]{2,1,0:T(8,128)(2,1)S(1)}, bf16[16,16,1280]{2,1,0:T(8,128)(2,1)S(1)}, u32[]{:S(2)}, u32[]{:S(2)}) collective-permute-start(bf16[16,16,1280]{2,1,0:T(8,128)(2,1)S(1)} %all-gather.own), channel_id=1, source_target_pairs={{0,16},{16,0},{32,48},{48,32},{64,80},{80,64},{96,112},{112,96},{1... | collective-permute-start | bytes 1966088 | tf_op jit(solution)/shard_map/ppermute | solution.py:261
  52.5 0.7 slice_bitcast_fusion.info_s
  53.2 2.0 %fusion.4.hidden = bf16[512,896]{1,0:T(8,128)(2,1)S(1)} fusion(bf16[512,896]{1,0:T(8,128)(2,1)} %up.1, bf16[512,896]{1,0:T(8,128)(2,1)} %gate.1), kind=kLoop, calls=%fused_computation.6 | loop fusion | flops 3670016 | bytes 2752512 | tf_op jit(solution)/shard_map/convert_element_type | solution.py:258
  55.2 0.0 collective-permute-done.other
  55.3 0.0 copy-done
  55.3 1.0 low_rank.1
  56.3 0.0 copy-start.1
  56.3 0.7 copy-done.1
  56.9 0.0 copy-start.3
  56.9 12.9 %all-gather.1 = f32[128,512]{1,0:T(8,128)S(1)} all-gather(f32[32,512]{1,0:T(8,128)S(1)} %get-tuple-element.27), channel_id=3, replica_groups={{0,4,8,12},{1,5,9,13},{2,6,10,14},{3,7,11,15},{16,20,24,28},{17,21,25,2..., dimensions={0}, use_global_device_ids=true | all-gather | bytes 327680 | tf_op jit(solution)/shard_map/all_gather | solution.py:276
  69.8 0.0 copy-done.3
  69.9 43.3 %all-gather.2 = f32[128,512]{1,0:T(8,128)S(1)} all-gather(f32[32,512]{1,0:T(8,128)S(1)} %reduce_sum.21), channel_id=4, replica_groups={{0,1,2,3},{4,5,6,7},{8,9,10,11},{12,13,14,15},{16,17,18,19},{20,21,22,2..., dimensions={0}, use_global_device_ids=true | all-gather | bytes 327680 | tf_op jit(solution)/shard_map/all_gather | solution.py:277
  113.2 0.0 all-to-all-done.1.own
  113.2 0.0 copy-start.4
  113.2 3.4 %collective-permute-start.1 = (bf16[4,512,256]{2,1,0:T(8,128)(2,1)S(1)}, bf16[4,512,256]{2,1,0:T(8,128)(2,1)}, u32[]{:S(2)}, u32[]{:S(2)}) collective-permute-start(bf16[4,512,256]{2,1,0:T(8,128)(2,1)S(1)} %all-to-all-done.1.own), channel_id=1, source_target_pairs={{0,4},{1,5},{2,6},{3,7},{4,8},{5,9},{6,10},{7,11},{8,12},{9,13},{1... | collective-permute-start | bytes 3145736 | tf_op jit(solution)/shard_map/ppermute | solution.py:279
  116.6 3.8 %collective-permute-start.2 = (bf16[4,512,256]{2,1,0:T(8,128)(2,1)S(1)}, bf16[4,512,256]{2,1,0:T(8,128)(2,1)}, u32[]{:S(2)}, u32[]{:S(2)}) collective-permute-start(bf16[4,512,256]{2,1,0:T(8,128)(2,1)S(1)} %all-to-all-done.1.own), channel_id=1, source_target_pairs={{0,12},{1,13},{2,14},{3,15},{4,0},{5,1},{6,2},{7,3},{8,4},{9,5},{1... | collective-permute-start | bytes 3145736 | tf_op jit(solution)/shard_map/ppermute | solution.py:280
  120.3 0.8 terms.1
  121.2 0.0 copy-start.2
  121.2 1.9 %collective-permute-start.5 = (f32[32,1280]{1,0:T(8,128)S(1)}, f32[32,1280]{1,0:T(8,128)S(1)}, u32[]{:S(2)}, u32[]{:S(2)}) collective-permute-start(f32[32,1280]{1,0:T(8,128)S(1)} %get-tuple-element.35.term), channel_id=1, source_target_pairs={{0,16},{16,0},{32,48},{48,32},{64,80},{80,64},{96,112},{112,96},{1... | collective-permute-start | bytes 491528 | tf_op jit(solution)/shard_map/ppermute | solution.py:294
  123.1 1.4 collective-permute-done.5.term_other
  124.5 1.4 dense.1
  125.8 4.5 %all-to-all-start.2 = ((bf16[4,4,16,1152]{3,2,1,0:T(8,128)(2,1)}), bf16[4,4,16,1152]{3,2,1,0:T(8,128)(2,1)S(1)}, u32[]{:S(2)}, u32[]{:S(2)}) async-start(bf16[4,4,16,1152]{3,2,1,0:T(8,128)(2,1)} %bitcast.9), calls=%async_computation.2 | async-start | bytes 1179648 | tf_op jit(solution)/shard_map/all_to_all | solution.py:305
  130.3 9.6 %collective-permute-done.1.back = bf16[4,512,256]{2,1,0:T(8,128)(2,1)} collective-permute-done((bf16[4,512,256]{2,1,0:T(8,128)(2,1)S(1)}, bf16[4,512,256]{2,1,0:T(8,128)(2,1)}, u32[]{:S(2)}, u32[]{:S(2)}) %collective-permute-start.1) | collective-permute-done | bytes 1048608 | tf_op jit(solution)/shard_map/ppermute | solution.py:279
  140.0 1.1 slice.12
  141.1 0.0 copy-done.4
  141.1 1.9 %collective-permute-start.3 = (bf16[2,512,256]{2,1,0:T(8,128)(2,1)S(1)}, bf16[2,512,256]{2,1,0:T(8,128)(2,1)S(1)}, u32[]{:S(2)}, u32[]{:S(2)}) collective-permute-start(bf16[2,512,256]{2,1,0:T(8,128)(2,1)S(1)} %slice.12), channel_id=1, source_target_pairs={{0,4},{1,5},{2,6},{3,7},{4,8},{5,9},{6,10},{7,11},{8,12},{9,13},{1... | collective-permute-start | bytes 1572872 | tf_op jit(solution)/shard_map/ppermute | solution.py:282
  143.0 0.0 collective-permute-done.2.ahead
  143.0 1.1 slice.13
  144.1 0.0 copy-done.2
  144.1 5.2 %collective-permute-start.4 = (bf16[2,512,256]{2,1,0:T(8,128)(2,1)S(1)}, bf16[2,512,256]{2,1,0:T(8,128)(2,1)S(1)}, u32[]{:S(2)}, u32[]{:S(2)}) collective-permute-start(bf16[2,512,256]{2,1,0:T(8,128)(2,1)S(1)} %slice.13), channel_id=1, source_target_pairs={{0,12},{1,13},{2,14},{3,15},{4,0},{5,1},{6,2},{7,3},{8,4},{9,5},{1... | collective-permute-start | bytes 1572872 | tf_op jit(solution)/shard_map/ppermute | solution.py:283
  149.3 0.0 all-to-all-done.2
  149.3 0.8 reduce_sum.22
  150.1 3.3 %all-to-all-start.3 = ((bf16[4,16,1152]{2,1,0:T(8,128)(2,1)}), bf16[4,16,1152]{2,1,0:T(8,128)(2,1)S(1)}, u32[]{:S(2)}, u32[]{:S(2)}) async-start(bf16[4,16,1152]{2,1,0:T(8,128)(2,1)} %reduce_sum.22), calls=%async_computation.3 | async-start | bytes 294912 | tf_op jit(solution)/shard_map/all_to_all | solution.py:307
  153.5 5.9 %all-to-all-done.3.incoming = bf16[4,16,1152]{2,1,0:T(8,128)(2,1)S(1)} async-done(((bf16[4,16,1152]{2,1,0:T(8,128)(2,1)}), bf16[4,16,1152]{2,1,0:T(8,128)(2,1)S(1)}, u32[]{:S(2)}, u32[]{:S(2)}) %all-to-all-start.3) | async-done | bytes 147488 | tf_op jit(solution)/shard_map/all_to_all | solution.py:307
  159.4 0.0 copy-start.5
  159.4 0.7 copy-done.5
  160.0 1.8 adam.1
  161.8 0.0 collective-permute-done.3.far_low
  161.8 0.0 copy-start.6
  161.9 0.0 collective-permute-done.4.far_high
  161.9 0.0 copy-start.7
  161.9 0.0 all-gather.5.cloned.1.call-done.down_own.down_back.down_ahead.down_far
  161.9 0.7 copy-done.6
  162.7 0.2 copy-done.7
  162.8 11.1 %finish.1 = (bf16[512,896]{1,0:T(8,128)(2,1)}, bf16[512,896]{1,0:T(8,128)(2,1)}) custom-call(s32[1]{0:T(128)} %bitcast.place_s, bf16[4,512,256]{2,1,0:T(8,128)(2,1)} %copy-done.4, bf16[4,512,256]{2,1,0:T(8,128)(2,1)} %collective-permute-done.1.back, bf16[4,512,256]{2,1,0:T(8,128)(2,1)} %collective-permute-done.2.ahead, bf16[2,512,256]{2,1,0:T(8,128)(2,1)} %copy-done.6, ...), custom_call_target="tpu_custom_call" | custom-call | tf_op jit(solution)/shard_map/finish/pallas_call | solution.py:335
  (1 shorter events, 0.0 us)
Async XLA Ops:
  7.2 154.7 %all-gather.5.cloned.1.call-start = ((), (), s32[]{:S(2)}) async-start(), calls=%async_computation.4 | async-start | bytes 7569408 | tf_op jit(solution)/shard_map/all_gather | solution.py:236
  24.5 88.7 %all-to-all-start.1 = ((bf16[4,512,256]{2,1,0:T(8,128)(2,1)}), bf16[4,512,256]{2,1,0:T(8,128)(2,1)S(1)}, u32[]{:S(2)}, u32[]{:S(2)}) async-start(bf16[4,512,256]{2,1,0:T(8,128)(2,1)} %broadcast_in_dim.2), calls=%async_computation.1 | async-start | bytes 2097152 | tf_op jit(solution)/shard_map/all_to_all | solution.py:254
  37.0 18.3 %copy-start = (bf16[512,256]{1,0:T(8,128)(2,1)S(1)}, bf16[512,256]{1,0:T(8,128)(2,1)}, u32[]{:S(2)}) copy-start(bf16[512,256]{1,0:T(8,128)(2,1)} %cot.3) | copy-start | bytes 786436
  50.6 4.6 %collective-permute-start = (bf16[16,16,1280]{2,1,0:T(8,128)(2,1)S(1)}, bf16[16,16,1280]{2,1,0:T(8,128)(2,1)S(1)}, u32[]{:S(2)}, u32[]{:S(2)}) collective-permute-start(bf16[16,16,1280]{2,1,0:T(8,128)(2,1)S(1)} %all-gather.own), channel_id=1, source_target_pairs={{0,16},{16,0},{32,48},{48,32},{64,80},{80,64},{96,112},{112,96},{1... | collective-permute-start | bytes 1966088 | tf_op jit(solution)/shard_map/ppermute | solution.py:261
  56.3 0.7 copy-start.1
  56.9 12.9 %copy-start.3 = (f32[16,128]{1,0:T(8,128)}, f32[16,128]{1,0:T(8,128)S(1)}, u32[]{:S(2)}) copy-start(f32[16,128]{1,0:T(8,128)S(1)} %get-tuple-element.34.totals) | copy-start | bytes 24580
  113.2 27.9 %copy-start.4 = (bf16[4,512,256]{2,1,0:T(8,128)(2,1)}, bf16[4,512,256]{2,1,0:T(8,128)(2,1)S(1)}, u32[]{:S(2)}) copy-start(bf16[4,512,256]{2,1,0:T(8,128)(2,1)S(1)} %all-to-all-done.1.own) | copy-start | bytes 3145732
  113.2 26.8 %collective-permute-start.1 = (bf16[4,512,256]{2,1,0:T(8,128)(2,1)S(1)}, bf16[4,512,256]{2,1,0:T(8,128)(2,1)}, u32[]{:S(2)}, u32[]{:S(2)}) collective-permute-start(bf16[4,512,256]{2,1,0:T(8,128)(2,1)S(1)} %all-to-all-done.1.own), channel_id=1, source_target_pairs={{0,4},{1,5},{2,6},{3,7},{4,8},{5,9},{6,10},{7,11},{8,12},{9,13},{1... | collective-permute-start | bytes 3145736 | tf_op jit(solution)/shard_map/ppermute | solution.py:279
  116.6 26.5 %collective-permute-start.2 = (bf16[4,512,256]{2,1,0:T(8,128)(2,1)S(1)}, bf16[4,512,256]{2,1,0:T(8,128)(2,1)}, u32[]{:S(2)}, u32[]{:S(2)}) collective-permute-start(bf16[4,512,256]{2,1,0:T(8,128)(2,1)S(1)} %all-to-all-done.1.own), channel_id=1, source_target_pairs={{0,12},{1,13},{2,14},{3,15},{4,0},{5,1},{6,2},{7,3},{8,4},{9,5},{1... | collective-permute-start | bytes 3145736 | tf_op jit(solution)/shard_map/ppermute | solution.py:280
  121.2 22.9 %copy-start.2 = (bf16[32,512]{1,0:T(8,128)(2,1)}, bf16[32,512]{1,0:T(8,128)(2,1)S(1)}, u32[]{:S(2)}) copy-start(bf16[32,512]{1,0:T(8,128)(2,1)S(1)} %get-tuple-element.30.grad_rows) | copy-start | bytes 98308
  121.2 3.3 %collective-permute-start.5 = (f32[32,1280]{1,0:T(8,128)S(1)}, f32[32,1280]{1,0:T(8,128)S(1)}, u32[]{:S(2)}, u32[]{:S(2)}) collective-permute-start(f32[32,1280]{1,0:T(8,128)S(1)} %get-tuple-element.35.term), channel_id=1, source_target_pairs={{0,16},{16,0},{32,48},{48,32},{64,80},{80,64},{96,112},{112,96},{1... | collective-permute-start | bytes 491528 | tf_op jit(solution)/shard_map/ppermute | solution.py:294
  125.8 23.5 %all-to-all-start.2 = ((bf16[4,4,16,1152]{3,2,1,0:T(8,128)(2,1)}), bf16[4,4,16,1152]{3,2,1,0:T(8,128)(2,1)S(1)}, u32[]{:S(2)}, u32[]{:S(2)}) async-start(bf16[4,4,16,1152]{3,2,1,0:T(8,128)(2,1)} %bitcast.9), calls=%async_computation.2 | async-start | bytes 1179648 | tf_op jit(solution)/shard_map/all_to_all | solution.py:305
  141.1 20.8 %collective-permute-start.3 = (bf16[2,512,256]{2,1,0:T(8,128)(2,1)S(1)}, bf16[2,512,256]{2,1,0:T(8,128)(2,1)S(1)}, u32[]{:S(2)}, u32[]{:S(2)}) collective-permute-start(bf16[2,512,256]{2,1,0:T(8,128)(2,1)S(1)} %slice.12), channel_id=1, source_target_pairs={{0,4},{1,5},{2,6},{3,7},{4,8},{5,9},{6,10},{7,11},{8,12},{9,13},{1... | collective-permute-start | bytes 1572872 | tf_op jit(solution)/shard_map/ppermute | solution.py:282
  144.1 17.7 %collective-permute-start.4 = (bf16[2,512,256]{2,1,0:T(8,128)(2,1)S(1)}, bf16[2,512,256]{2,1,0:T(8,128)(2,1)S(1)}, u32[]{:S(2)}, u32[]{:S(2)}) collective-permute-start(bf16[2,512,256]{2,1,0:T(8,128)(2,1)S(1)} %slice.13), channel_id=1, source_target_pairs={{0,12},{1,13},{2,14},{3,15},{4,0},{5,1},{6,2},{7,3},{8,4},{9,5},{1... | collective-permute-start | bytes 1572872 | tf_op jit(solution)/shard_map/ppermute | solution.py:283
  150.1 9.3 %all-to-all-start.3 = ((bf16[4,16,1152]{2,1,0:T(8,128)(2,1)}), bf16[4,16,1152]{2,1,0:T(8,128)(2,1)S(1)}, u32[]{:S(2)}, u32[]{:S(2)}) async-start(bf16[4,16,1152]{2,1,0:T(8,128)(2,1)} %reduce_sum.22), calls=%async_computation.3 | async-start | bytes 294912 | tf_op jit(solution)/shard_map/all_to_all | solution.py:307
  159.4 0.7 copy-start.5
  161.8 0.8 copy-start.6
  161.9 1.0 copy-start.7
Sparse Core Ops, SparseCore 0:
  10.1 140.5 all-gather.4

commit v9 on v4

--- a/solution.py
+++ b/solution.py
@@ -24,6 +24,9 @@
 ALONG_Z_LO = [[(x * Z_LO + z) * CORES + c for z in range(Z_LO)] for x in range(X) for c in range(CORES)]
 ALONG_Y = [[y * Z_HI + h for y in range(Y)] for h in range(Z_HI)]
 ALONG_Z_HI = [[y * Z_HI + h for h in range(Z_HI)] for y in range(Y)]
+SAME_CORE = [
+    [(x * Z_LO + z) * CORES + c for x in range(X) for z in range(Z_LO)] for c in range(CORES)
+]
 OTHER_CORE = [(d, d ^ 1) for d in range(X * Z_LO * CORES)]
 NEXT_Y = [(y * Z_HI + h, (y + 1) % Y * Z_HI + h) for y in range(Y) for h in range(Z_HI)]
 LAST_Y = [(y * Z_HI + h, (y - 1) % Y * Z_HI + h) for y in range(Y) for h in range(Z_HI)]
@@ -174,41 +177,31 @@
         step[0] = jnp.where(active, update, 0.0)
 
 
-def finish(
-    place_s, own, back, ahead, far_low, far_high, down_own, down_back, down_ahead, down_far,
-    grad_rows, pair_a, gate, up, out_gate, out_up, total, far
-):
-    place = pl.program_id(0)
-
-    @pl.when(place == 0)
+def near(place_s, own, back, ahead, down_own, down_back, down_ahead, grad_rows, pair_a, total):
+    @pl.when(pl.program_id(0) == 0)
     def _():
         total[...] = tn_dot(grad_rows[...], pair_a[...])
-
-    @pl.when(place < 2)
-    def _():
-        far[...] = far_low[0]
-
-    @pl.when(place >= 2)
-    def _():
-        far[...] = far_high[0]
 
     total[...] += (
         nt_dot(own[0], down_own[...])
         + nt_dot(back[0], down_back[...])
         + nt_dot(ahead[0], down_ahead[...])
-        + nt_dot(far[...], down_far[...])
-    )
-
-    @pl.when(place == pl.num_programs(0) - 1)
-    def _():
-        gate_f = gate[...].astype(jnp.float32)
-        up_f = up[...].astype(jnp.float32)
-        sigmoid_gate = jax.nn.sigmoid(gate_f)
-        grad = total[...]
-        out_gate[...] = (
-            grad * up_f * sigmoid_gate * (1.0 + gate_f * (1.0 - sigmoid_gate))
-        ).astype(jnp.bfloat16)
-        out_up[...] = (grad * (gate_f * sigmoid_gate)).astype(jnp.bfloat16)
+    )
+
+
+def finish(place_s, far_low, far_high, down_far, total, gate, up, out_gate, out_up):
+    feat = far_low.shape[2]
+    blocks = [far_low[0], far_low[1], far_high[0], far_high[1]]
+    grad = total[...]
+    for place, block in enumerate(blocks):
+        grad += nt_dot(block, down_far[:, place * feat : (place + 1) * feat])
+    gate_f = gate[...].astype(jnp.float32)
+    up_f = up[...].astype(jnp.float32)
+    sigmoid_gate = jax.nn.sigmoid(gate_f)
+    out_gate[...] = (
+        grad * up_f * sigmoid_gate * (1.0 + gate_f * (1.0 - sigmoid_gate))
+    ).astype(jnp.bfloat16)
+    out_up[...] = (grad * (gate_f * sigmoid_gate)).astype(jnp.bfloat16)
 
 
 def shards(
@@ -278,6 +271,7 @@
     back = lax.ppermute(cot_z, "tensor", NEXT_Y)
     ahead = lax.ppermute(cot_z, "tensor", LAST_Y)
     sums = lax.all_gather(sums, "tensor", axis_index_groups=ALONG_Z_HI)
+    back, ahead, sums = lax.optimization_barrier((back, ahead, sums))
     half = Z_HI // 2
     far_low = lax.ppermute(back[:half], "tensor", NEXT_Y)
     far_high = lax.ppermute(ahead[half:], "tensor", LAST_Y)
@@ -301,11 +295,40 @@
         compiler_params=params(),
         name="dense",
     )(core_s, term, term_other)
-    outgoing = outgoing.reshape(X, Z_LO, rank, wide)
-    by_x = lax.all_to_all(outgoing, "dp", 0, 0, axis_index_groups=ALONG_X)
-    by_x = jnp.sum(by_x.astype(f32), axis=0).astype(bf16)
-    incoming = lax.all_to_all(by_x, "dp", 0, 0, axis_index_groups=ALONG_Z_LO)
-
+    incoming = lax.all_to_all(outgoing, "dp", 0, 0, axis_index_groups=SAME_CORE)
+
+    def down_block(ahead_by):
+        return pl.BlockSpec(
+            (hid, feat),
+            lambda place, y_ref: (0, lax.rem(y_ref[0] + ahead_by, Y) * Z_HI + place),
+        )
+
+    def fixed(*block):
+        return pl.BlockSpec(block, lambda step, y_ref: (0,) * len(block))
+
+    by_place = pl.BlockSpec((1, tok, feat), lambda place, y_ref: (place, 0, 0))
+    total = pl.pallas_call(
+        near,
+        out_shape=shape((tok, hid), f32),
+        grid_spec=pltpu.PrefetchScalarGridSpec(
+            num_scalar_prefetch=1,
+            grid=(Z_HI,),
+            in_specs=[
+                by_place,
+                by_place,
+                by_place,
+                down_block(0),
+                down_block(Y - 1),
+                down_block(1),
+                fixed(2 * rank, tok),
+                fixed(2 * rank, hid),
+            ],
+            out_specs=fixed(tok, hid),
+        ),
+        compiler_params=params(56),
+        name="near",
+    )(y_s, cot_z, back, ahead, down_full, down_full, down_full, grad_rows, pair)
+    total, incoming = lax.optimization_barrier((total, incoming))
     new_moments_a, new_moments_b, step_a, step_b = pl.pallas_call(
         adam,
         out_shape=(
@@ -320,60 +343,30 @@
         name="adam",
     )(me.reshape(1), totals, incoming, input_moments, output_moments)
 
-    def down_block(ahead_by):
-        return pl.BlockSpec(
-            (hid, feat),
-            lambda place, y_ref: (0, lax.rem(y_ref[0] + ahead_by, Y) * Z_HI + place),
-        )
-
-    def by_place(index):
-        return pl.BlockSpec((1, tok, feat), lambda place, y_ref: (index(place), 0, 0))
-
-    def whole_of(rows, columns):
-        return pl.BlockSpec((rows, columns), lambda place, y_ref: (0, 0))
-
+    rows = tok // 4
+    far_rows = pl.BlockSpec((half, rows, feat), lambda step, y_ref: (0, step, 0))
+    wide_rows = pl.BlockSpec((rows, hid), lambda step, y_ref: (step, 0))
     grad_gate, grad_up = pl.pallas_call(
         finish,
         out_shape=(shape((tok, hid), bf16), shape((tok, hid), bf16)),
         grid_spec=pltpu.PrefetchScalarGridSpec(
             num_scalar_prefetch=1,
-            grid=(Z_HI,),
+            grid=(tok // rows,),
             in_specs=[
-                by_place(lambda place: place),
-                by_place(lambda place: place),
-                by_place(lambda place: place),
-                by_place(lambda place: jnp.minimum(place, half - 1)),
-                by_place(lambda place: jnp.maximum(place - half, 0)),
-                down_block(0),
-                down_block(Y - 1),
-                down_block(1),
-                down_block(2),
-                whole_of(2 * rank, tok),
-                whole_of(2 * rank, hid),
-                whole_of(tok, hid),
-                whole_of(tok, hid),
+                far_rows,
+                far_rows,
+                pl.BlockSpec(
+                    (hid, Z_HI * feat), lambda step, y_ref: (0, lax.rem(y_ref[0] + 2, Y))
+                ),
+                wide_rows,
+                wide_rows,
+                wide_rows,
             ],
-            out_specs=[whole_of(tok, hid), whole_of(tok, hid)],
-            scratch_shapes=[pltpu.VMEM((tok, hid), f32), pltpu.VMEM((tok, feat), bf16)],
+            out_specs=[wide_rows, wide_rows],
         ),
         compiler_params=params(56),
         name="finish",
-    )(
-        y_s,
-        cot_z,
-        back,
-        ahead,
-        far_low,
-        far_high,
-        down_full,
-        down_full,
-        down_full,
-        down_full,
-        grad_rows,
-        pair[:, :hid],
-        gate_logits,
-        up_projected,
-    )
+    )(y_s, far_low, far_high, down_full, total, gate_logits, up_projected)
     return (grad_gate, grad_up, new_moments_a, new_moments_b, step_a, step_b)
 
 

time: 181 us -> 182 us (level)
  the two profiles are of different devices: /device:TPU:24 before, /device:TPU:73 now
where the time goes in v9:
time: 182 us; the launch traced here: 181 us
  blocking collectives  49.7 us (27%)
  waiting for transfers between devices  46.3 us (25%)
  starting transfers between devices  39.9 us (22%)
  Pallas kernels  21.6 us (12%)
  between operations  14.2 us (8%)
  local copies, waits for them, and re-layouts  6.93 us (4%)
  other arithmetic  2.07 us (1%)
    all_to_all x1, waiting for transfers between devices, shards(): lax.all_to_all(cot_copies, 'tensor', 0, 0, axis_index_groups=ALONG_Z_HI)  32.1 us
    all_gather x1, blocking collectives, shards(): sums = lax.all_gather(sums, 'tensor', axis_index_groups=ALONG_Z_HI)  17.2 us
    all_to_all x1, starting transfers between devices, shards(): lax.all_to_all(cot_copies, 'tensor', 0, 0, axis_index_groups=ALONG_Z_HI)  12.6 us
    all_gather x1, blocking collectives, shards(): plane = lax.all_gather(column, 'dp', axis_index_groups=ALONG_X)  12.4 us
    all_gather x1, blocking collectives, shards(): lax.all_gather(part, 'tensor', axis_index_groups=ALONG_Y)  10.6 us
    all_to_all x1, blocking collectives, shards(): column = lax.all_to_all(packed, 'dp', 0, 0, axis_index_groups=ALONG_Z_LO)  9.49 us
    pallas_call x1, Pallas kernels, shards(): pl.pallas_call(near, out_shape=shape((tok, hid), f32), grid_spec=pltpu.Pr...  8.25 us
    all_to_all x1, starting transfers between devices, shards(): incoming = lax.all_to_all(outgoing, 'dp', 0, 0, axis_index_groups=SAME_CORE)  7.64 us
  transfers between devices with their start and end apart: 9, of which 5 were waited for; matrix products, arithmetic and copies ran while one was open for 3% of the time, Pallas kernels for 8%

profile of v9, /device:TPU:73, one launch (start us, length us, event | category | flops | bytes accessed | tf_op | source)
XLA Modules:
  0.0 180.8 jit_solution(4736148602901923792)
XLA Ops:
  7.2 0.0 all-gather.5.cloned.1.call-start
  7.2 0.7 all-gather.5.cloned.1.call-update
  7.9 1.6 prepare.1
  9.5 9.5 %all_to_all.15 = bf16[4,16,1280]{2,1,0:T(8,128)(2,1)S(1)} all-to-all(bf16[4,16,1280]{2,1,0:T(8,128)(2,1)} %get-tuple-element.28), channel_id=1, replica_groups={{0,32,64,96},{16,48,80,112},{128,160,192,224},{144,176,208,240},{256,28..., dimensions={0} | all-to-all | bytes 327680 | tf_op jit(solution)/shard_map/all_to_all | solution.py:245
  19.0 2.1 %broadcast_in_dim.2 = bf16[4,512,256]{2,1,0:T(8,128)(2,1)} broadcast(bf16[512,256]{1,0:T(8,128)(2,1)} %cot.3), dimensions={1,2} | broadcast | bytes 1310720 | tf_op jit(solution)/shard_map/broadcast_in_dim | solution.py:56
  21.1 12.6 %all-to-all-start.1 = ((bf16[4,512,256]{2,1,0:T(8,128)(2,1)}), bf16[4,512,256]{2,1,0:T(8,128)(2,1)S(1)}, u32[]{:S(2)}, u32[]{:S(2)}) async-start(bf16[4,512,256]{2,1,0:T(8,128)(2,1)} %broadcast_in_dim.2), calls=%async_computation.1 | async-start | bytes 2097152 | tf_op jit(solution)/shard_map/all_to_all | solution.py:247
  33.7 0.0 copy-start
  33.7 12.4 %all-gather.own = bf16[16,16,1280]{2,1,0:T(8,128)(2,1)S(1)} all-gather(bf16[4,16,1280]{2,1,0:T(8,128)(2,1)S(1)} %all_to_all.15), channel_id=2, replica_groups={{0,128,256,384},{16,144,272,400},{32,160,288,416},{48,176,304,432},{64,..., dimensions={0}, use_global_device_ids=true | all-gather | bytes 819200 | tf_op jit(solution)/shard_map/all_gather | solution.py:252
  46.1 5.3 %collective-permute-start = (bf16[16,16,1280]{2,1,0:T(8,128)(2,1)S(1)}, bf16[16,16,1280]{2,1,0:T(8,128)(2,1)S(1)}, u32[]{:S(2)}, u32[]{:S(2)}) collective-permute-start(bf16[16,16,1280]{2,1,0:T(8,128)(2,1)S(1)} %all-gather.own), channel_id=1, source_target_pairs={{0,16},{16,0},{32,48},{48,32},{64,80},{80,64},{96,112},{112,96},{1... | collective-permute-start | bytes 1966088 | tf_op jit(solution)/shard_map/ppermute | solution.py:254
  51.4 0.7 slice_bitcast_fusion.info_s
  52.1 2.0 %fusion.4.hidden = bf16[512,896]{1,0:T(8,128)(2,1)S(1)} fusion(bf16[512,896]{1,0:T(8,128)(2,1)} %up.1, bf16[512,896]{1,0:T(8,128)(2,1)} %gate.1), kind=kLoop, calls=%fused_computation.6 | loop fusion | flops 3670016 | bytes 2752512 | tf_op jit(solution)/shard_map/convert_element_type | solution.py:251
  54.2 0.0 collective-permute-done.other
  54.2 0.0 copy-done
  54.2 1.0 low_rank.1
  55.2 0.0 copy-start.1
  55.2 0.7 copy-done.1
  55.8 0.0 copy-start.3
  55.8 10.6 %all-gather.1 = f32[128,512]{1,0:T(8,128)S(1)} all-gather(f32[32,512]{1,0:T(8,128)S(1)} %get-tuple-element.32), channel_id=3, replica_groups={{0,4,8,12},{1,5,9,13},{2,6,10,14},{3,7,11,15},{16,20,24,28},{17,21,25,2..., dimensions={0}, use_global_device_ids=true | all-gather | bytes 327680 | tf_op jit(solution)/shard_map/all_gather | solution.py:269
  66.4 0.0 copy-done.3
  66.4 32.1 %all-to-all-done.1.own = bf16[4,512,256]{2,1,0:T(8,128)(2,1)S(1)} async-done(((bf16[4,512,256]{2,1,0:T(8,128)(2,1)}), bf16[4,512,256]{2,1,0:T(8,128)(2,1)S(1)}, u32[]{:S(2)}, u32[]{:S(2)}) %all-to-all-start.1) | async-done | bytes 1048608 | tf_op jit(solution)/shard_map/all_to_all | solution.py:247
  98.5 0.0 copy-start.4
  98.5 2.3 %collective-permute-start.1 = (bf16[4,512,256]{2,1,0:T(8,128)(2,1)S(1)}, bf16[4,512,256]{2,1,0:T(8,128)(2,1)S(1)}, u32[]{:S(2)}, u32[]{:S(2)}) collective-permute-start(bf16[4,512,256]{2,1,0:T(8,128)(2,1)S(1)} %all-to-all-done.1.own), channel_id=1, source_target_pairs={{0,4},{1,5},{2,6},{3,7},{4,8},{5,9},{6,10},{7,11},{8,12},{9,13},{1... | collective-permute-start | bytes 3145736 | tf_op jit(solution)/shard_map/ppermute | solution.py:271
  100.8 3.0 %collective-permute-start.2 = (bf16[4,512,256]{2,1,0:T(8,128)(2,1)S(1)}, bf16[4,512,256]{2,1,0:T(8,128)(2,1)}, u32[]{:S(2)}, u32[]{:S(2)}) collective-permute-start(bf16[4,512,256]{2,1,0:T(8,128)(2,1)S(1)} %all-to-all-done.1.own), channel_id=1, source_target_pairs={{0,12},{1,13},{2,14},{3,15},{4,0},{5,1},{6,2},{7,3},{8,4},{9,5},{1... | collective-permute-start | bytes 3145736 | tf_op jit(solution)/shard_map/ppermute | solution.py:272
  103.8 17.2 %all-gather.2 = f32[128,512]{1,0:T(8,128)S(1)} all-gather(f32[32,512]{1,0:T(8,128)S(1)} %reduce_sum.9), channel_id=4, replica_groups={{0,1,2,3},{4,5,6,7},{8,9,10,11},{12,13,14,15},{16,17,18,19},{20,21,22,2..., dimensions={0}, use_global_device_ids=true | all-gather | bytes 327680 | tf_op jit(solution)/shard_map/all_gather | solution.py:273
  121.1 3.8 %collective-permute-done.1.back = bf16[4,512,256]{2,1,0:T(8,128)(2,1)S(1)} collective-permute-done((bf16[4,512,256]{2,1,0:T(8,128)(2,1)S(1)}, bf16[4,512,256]{2,1,0:T(8,128)(2,1)S(1)}, u32[]{:S(2)}, u32[]{:S(2)}) %collective-permute-start.1) | collective-permute-done | bytes 1048608 | tf_op jit(solution)/shard_map/ppermute | solution.py:271
  124.9 0.0 copy-start.5
  124.9 1.6 collective-permute-done.2.ahead
  126.4 0.8 terms.1
  127.3 0.0 copy-start.2
  127.3 3.8 %collective-permute-start.5 = (f32[32,1280]{1,0:T(8,128)S(1)}, f32[32,1280]{1,0:T(8,128)S(1)}, u32[]{:S(2)}, u32[]{:S(2)}) collective-permute-start(f32[32,1280]{1,0:T(8,128)S(1)} %get-tuple-element.40.term), channel_id=1, source_target_pairs={{0,16},{16,0},{32,48},{48,32},{64,80},{80,64},{96,112},{112,96},{1... | collective-permute-start | bytes 491528 | tf_op jit(solution)/shard_map/ppermute | solution.py:288
  131.1 1.0 collective-permute-done.5.term_other
  132.1 1.4 dense.1
  133.5 0.0 copy-done.4
  133.5 7.6 %all-to-all-start.2 = ((bf16[16,16,1152]{2,1,0:T(8,128)(2,1)}), bf16[16,16,1152]{2,1,0:T(8,128)(2,1)S(1)}, u32[]{:S(2)}, u32[]{:S(2)}) async-start(bf16[16,16,1152]{2,1,0:T(8,128)(2,1)} %dense.1), calls=%async_computation.2 | async-start | bytes 1179648 | tf_op jit(solution)/shard_map/all_to_all | solution.py:298
  141.2 0.0 copy-done.5
  141.2 2.9 %collective-permute-start.3 = (bf16[2,512,256]{2,1,0:T(8,128)(2,1)S(1)}, bf16[2,512,256]{2,1,0:T(8,128)(2,1)S(1)}, u32[]{:S(2)}, u32[]{:S(2)}) collective-permute-start(bf16[2,512,256]{2,1,0:T(8,128)(2,1)S(1)} %slice.10), channel_id=1, source_target_pairs={{0,4},{1,5},{2,6},{3,7},{4,8},{5,9},{6,10},{7,11},{8,12},{9,13},{1... | collective-permute-start | bytes 1572872 | tf_op jit(solution)/shard_map/ppermute | solution.py:276
  144.1 1.1 slice.11
  145.2 0.0 copy-done.2
  145.2 2.4 %collective-permute-start.4 = (bf16[2,512,256]{2,1,0:T(8,128)(2,1)S(1)}, bf16[2,512,256]{2,1,0:T(8,128)(2,1)S(1)}, u32[]{:S(2)}, u32[]{:S(2)}) collective-permute-start(bf16[2,512,256]{2,1,0:T(8,128)(2,1)S(1)} %slice.11), channel_id=1, source_target_pairs={{0,12},{1,13},{2,14},{3,15},{4,0},{5,1},{6,2},{7,3},{8,4},{9,5},{1... | collective-permute-start | bytes 1572872 | tf_op jit(solution)/shard_map/ppermute | solution.py:277
  147.6 7.2 %all-gather.5.cloned.1.call-done.down_own.down_back.down_ahead.down_far = bf16[896,4096]{1,0:T(8,128)(2,1)} async-done(((bf16[896,128]{1,0:T(8,128)(2,1)}), bf16[896,4096]{1,0:T(8,128)(2,1)}) %all-gather.5.cloned.1.call-update) | async-done | bytes 7340048 | tf_op jit(solution)/shard_map/all_gather | solution.py:229
  154.8 8.3 %near.1.total = f32[512,896]{1,0:T(8,128)} custom-call(s32[1]{0:T(128)} %bitcast.place_s, bf16[4,512,256]{2,1,0:T(8,128)(2,1)} %copy-done.4, bf16[4,512,256]{2,1,0:T(8,128)(2,1)} %copy-done.5, bf16[4,512,256]{2,1,0:T(8,128)(2,1)} %collective-permute-done.2.ahead, bf16[896,4096]{1,0:T(8,128)(2,1)} %all-gather.5.cloned.1.call-done.down_own.down_back.down_ahead.down_far, ...), custom_call_target="tpu_custom_call" | custom-call | tf_op jit(solution)/shard_map/near/pallas_call | solution.py:310
  163.0 0.0 all-to-all-done.2.incoming
  163.0 0.0 copy-start.6
  163.0 0.8 copy-done.6
  163.8 1.9 %adam.1 = (f32[2,1,16,896]{3,2,1,0:T(8,128)}, f32[2,1,16,256]{3,2,1,0:T(8,128)}, f32[1,16,896]{2,1,0:T(8,128)}, f32[1,16,256]{2,1,0:T(8,128)}) custom-call(s32[1]{0:T(128)} %bitcast.8.me_s, f32[16,128]{1,0:T(8,128)} %copy-done.3, bf16[16,16,1152]{2,1,0:T(8,128)(2,1)} %copy-done.6, f32[2,1,16,896]{3,2,1,0:T(8,128)} %moments_a.1, f32[2,1,16,256]{3,2,1,0:T(8,128)} %moments_b.1), custom_call_target="tpu_custom_call" | custom-call | tf_op jit(solution)/shard_map/adam/pallas_call | solution.py:332
  165.8 0.0 collective-permute-done.3.far_low
  165.8 0.0 copy-start.7
  165.8 0.0 collective-permute-done.4.far_high
  165.8 0.8 copy-done.7
  166.6 0.0 copy-start.8
  166.6 0.8 copy-done.8
  167.4 6.6 %finish.1 = (bf16[512,896]{1,0:T(8,128)(2,1)}, bf16[512,896]{1,0:T(8,128)(2,1)}) custom-call(s32[1]{0:T(128)} %bitcast.place_s, bf16[2,512,256]{2,1,0:T(8,128)(2,1)} %copy-done.7, bf16[2,512,256]{2,1,0:T(8,128)(2,1)} %copy-done.8, bf16[896,4096]{1,0:T(8,128)(2,1)} %all-gather.5.cloned.1.call-done.down_own.down_back.down_ahead.down_far, ...), custom_call_target="tpu_custom_call" | custom-call | tf_op jit(solution)/shard_map/finish/pallas_call | solution.py:349
  (2 shorter events, 0.1 us)
Async XLA Ops:
  7.2 147.6 %all-gather.5.cloned.1.call-start = ((), (), s32[]{:S(2)}) async-start(), calls=%async_computation.3 | async-start | bytes 7569408 | tf_op jit(solution)/shard_map/all_gather | solution.py:229
  21.1 77.4 %all-to-all-start.1 = ((bf16[4,512,256]{2,1,0:T(8,128)(2,1)}), bf16[4,512,256]{2,1,0:T(8,128)(2,1)S(1)}, u32[]{:S(2)}, u32[]{:S(2)}) async-start(bf16[4,512,256]{2,1,0:T(8,128)(2,1)} %broadcast_in_dim.2), calls=%async_computation.1 | async-start | bytes 2097152 | tf_op jit(solution)/shard_map/all_to_all | solution.py:247
  33.7 20.4 %copy-start = (bf16[512,256]{1,0:T(8,128)(2,1)S(1)}, bf16[512,256]{1,0:T(8,128)(2,1)}, u32[]{:S(2)}) copy-start(bf16[512,256]{1,0:T(8,128)(2,1)} %cot.3) | copy-start | bytes 786436
  46.1 8.0 %collective-permute-start = (bf16[16,16,1280]{2,1,0:T(8,128)(2,1)S(1)}, bf16[16,16,1280]{2,1,0:T(8,128)(2,1)S(1)}, u32[]{:S(2)}, u32[]{:S(2)}) collective-permute-start(bf16[16,16,1280]{2,1,0:T(8,128)(2,1)S(1)} %all-gather.own), channel_id=1, source_target_pairs={{0,16},{16,0},{32,48},{48,32},{64,80},{80,64},{96,112},{112,96},{1... | collective-permute-start | bytes 1966088 | tf_op jit(solution)/shard_map/ppermute | solution.py:254
  55.2 0.7 copy-start.1
  55.8 10.6 %copy-start.3 = (f32[16,128]{1,0:T(8,128)}, f32[16,128]{1,0:T(8,128)S(1)}, u32[]{:S(2)}) copy-start(f32[16,128]{1,0:T(8,128)S(1)} %get-tuple-element.44.totals) | copy-start | bytes 24580
  98.5 35.0 %copy-start.4 = (bf16[4,512,256]{2,1,0:T(8,128)(2,1)}, bf16[4,512,256]{2,1,0:T(8,128)(2,1)S(1)}, u32[]{:S(2)}) copy-start(bf16[4,512,256]{2,1,0:T(8,128)(2,1)S(1)} %all-to-all-done.1.own) | copy-start | bytes 3145732
  98.5 26.3 %collective-permute-start.1 = (bf16[4,512,256]{2,1,0:T(8,128)(2,1)S(1)}, bf16[4,512,256]{2,1,0:T(8,128)(2,1)S(1)}, u32[]{:S(2)}, u32[]{:S(2)}) collective-permute-start(bf16[4,512,256]{2,1,0:T(8,128)(2,1)S(1)} %all-to-all-done.1.own), channel_id=1, source_target_pairs={{0,4},{1,5},{2,6},{3,7},{4,8},{5,9},{6,10},{7,11},{8,12},{9,13},{1... | collective-permute-start | bytes 3145736 | tf_op jit(solution)/shard_map/ppermute | solution.py:271
  100.8 25.6 %collective-permute-start.2 = (bf16[4,512,256]{2,1,0:T(8,128)(2,1)S(1)}, bf16[4,512,256]{2,1,0:T(8,128)(2,1)}, u32[]{:S(2)}, u32[]{:S(2)}) collective-permute-start(bf16[4,512,256]{2,1,0:T(8,128)(2,1)S(1)} %all-to-all-done.1.own), channel_id=1, source_target_pairs={{0,12},{1,13},{2,14},{3,15},{4,0},{5,1},{6,2},{7,3},{8,4},{9,5},{1... | collective-permute-start | bytes 3145736 | tf_op jit(solution)/shard_map/ppermute | solution.py:272
  124.9 16.3 %copy-start.5 = (bf16[4,512,256]{2,1,0:T(8,128)(2,1)}, bf16[4,512,256]{2,1,0:T(8,128)(2,1)S(1)}, u32[]{:S(2)}) copy-start(bf16[4,512,256]{2,1,0:T(8,128)(2,1)S(1)} %collective-permute-done.1.back) | copy-start | bytes 3145732
  127.3 17.9 %copy-start.2 = (bf16[32,512]{1,0:T(8,128)(2,1)}, bf16[32,512]{1,0:T(8,128)(2,1)S(1)}, u32[]{:S(2)}) copy-start(bf16[32,512]{1,0:T(8,128)(2,1)S(1)} %get-tuple-element.38.grad_rows) | copy-start | bytes 98308
  127.3 4.9 %collective-permute-start.5 = (f32[32,1280]{1,0:T(8,128)S(1)}, f32[32,1280]{1,0:T(8,128)S(1)}, u32[]{:S(2)}, u32[]{:S(2)}) collective-permute-start(f32[32,1280]{1,0:T(8,128)S(1)} %get-tuple-element.40.term), channel_id=1, source_target_pairs={{0,16},{16,0},{32,48},{48,32},{64,80},{80,64},{96,112},{112,96},{1... | collective-permute-start | bytes 491528 | tf_op jit(solution)/shard_map/ppermute | solution.py:288
  133.5 29.5 %all-to-all-start.2 = ((bf16[16,16,1152]{2,1,0:T(8,128)(2,1)}), bf16[16,16,1152]{2,1,0:T(8,128)(2,1)S(1)}, u32[]{:S(2)}, u32[]{:S(2)}) async-start(bf16[16,16,1152]{2,1,0:T(8,128)(2,1)} %dense.1), calls=%async_computation.2 | async-start | bytes 1179648 | tf_op jit(solution)/shard_map/all_to_all | solution.py:298
  141.2 24.6 %collective-permute-start.3 = (bf16[2,512,256]{2,1,0:T(8,128)(2,1)S(1)}, bf16[2,512,256]{2,1,0:T(8,128)(2,1)S(1)}, u32[]{:S(2)}, u32[]{:S(2)}) collective-permute-start(bf16[2,512,256]{2,1,0:T(8,128)(2,1)S(1)} %slice.10), channel_id=1, source_target_pairs={{0,4},{1,5},{2,6},{3,7},{4,8},{5,9},{6,10},{7,11},{8,12},{9,13},{1... | collective-permute-start | bytes 1572872 | tf_op jit(solution)/shard_map/ppermute | solution.py:276
  145.2 20.6 %collective-permute-start.4 = (bf16[2,512,256]{2,1,0:T(8,128)(2,1)S(1)}, bf16[2,512,256]{2,1,0:T(8,128)(2,1)S(1)}, u32[]{:S(2)}, u32[]{:S(2)}) collective-permute-start(bf16[2,512,256]{2,1,0:T(8,128)(2,1)S(1)} %slice.11), channel_id=1, source_target_pairs={{0,12},{1,13},{2,14},{3,15},{4,0},{5,1},{6,2},{7,3},{8,4},{9,5},{1... | collective-permute-start | bytes 1572872 | tf_op jit(solution)/shard_map/ppermute | solution.py:277
  163.0 0.8 copy-start.6
  165.8 0.8 copy-start.7
  166.6 0.8 copy-start.8
Sparse Core Ops, SparseCore 0:
  10.1 144.6 all-gather.4

commit v10 on v8

--- a/solution.py
+++ b/solution.py
@@ -25,6 +25,12 @@
 ALONG_Y = [[y * Z_HI + h for y in range(Y)] for h in range(Z_HI)]
 ALONG_Z_HI = [[y * Z_HI + h for h in range(Z_HI)] for y in range(Y)]
 OTHER_CORE = [(d, d ^ 1) for d in range(X * Z_LO * CORES)]
+
+
+def shift_z_hi(by):
+    return [(y * Z_HI + h, y * Z_HI + (h + by) % Z_HI) for y in range(Y) for h in range(Z_HI)]
+
+
 NEXT_Y = [(y * Z_HI + h, (y + 1) % Y * Z_HI + h) for y in range(Y) for h in range(Z_HI)]
 LAST_Y = [(y * Z_HI + h, (y - 1) % Y * Z_HI + h) for y in range(Y) for h in range(Z_HI)]
 
@@ -53,7 +59,9 @@
     return jnp.broadcast_to(block[None], (copies,) + block.shape)
 
 
-def prepare(tenants_s, owners_s, tenants_v, factor_a, factor_b, packed, info_v):
+def prepare(tenants_s, owners_s, tenants_v, factor_a, factor_b, cot, packed, info_v, cot_copies):
+    for copy in range(cot_copies.shape[0]):
+        cot_copies[copy] = cot[...]
     tok = tenants_s.shape[0]
     rank, hid = factor_a.shape
     feat = factor_b.shape[1]
@@ -109,11 +117,11 @@
     totals[...] = jnp.sum(digits, axis=0)
 
 
-def terms(info_s, sums, hidden, cot, grad_rows, term):
-    rank = sums.shape[1] // 2
+def terms(info_s, sums, one, two, three, hidden, cot, grad_rows, term):
+    rank = sums.shape[0] // 2
     hid = hidden.shape[1]
     tok = hidden.shape[0]
-    rows = jnp.sum(sums[...], axis=0)
+    rows = sums[...] + one[...] + two[...] + three[...]
     in_first = lax.broadcasted_iota(jnp.int32, (rank, tok), 1) < info_s[INFO_CUT]
     proj = rows[:rank]
     grad = ADAPTER_SCALE * rows[rank:]
@@ -235,11 +243,15 @@
 
     down_full = lax.all_gather(down_matrix, "dp", axis=1, tiled=True)
 
-    packed, info_v = pl.pallas_call(
+    packed, info_v, cot_copies = pl.pallas_call(
         prepare,
-        out_shape=(shape((Z_LO, rank, wide + LANES), bf16), shape((8, LANES), jnp.int32)),
-        in_specs=[SMEM, SMEM, WHOLE, WHOLE, WHOLE],
-        out_specs=(WHOLE, WHOLE),
+        out_shape=(
+            shape((Z_LO, rank, wide + LANES), bf16),
+            shape((8, LANES), jnp.int32),
+            shape((Z_HI, tok, feat), bf16),
+        ),
+        in_specs=[SMEM, SMEM, WHOLE, WHOLE, WHOLE, WHOLE],
+        out_specs=(WHOLE, WHOLE, WHOLE),
         compiler_params=params(56),
         name="prepare",
     )(
@@ -248,9 +260,10 @@
         batch_tenants.reshape(-1, LANES),
         adapter_input_factors[0],
         adapter_output_factors[0],
+        output_gradient,
     )
     column = lax.all_to_all(packed, "dp", 0, 0, axis_index_groups=ALONG_Z_LO)
-    column, cot_copies = lax.optimization_barrier((column, spread(Z_HI, output_gradient)))
+    column, cot_copies = lax.optimization_barrier((column, cot_copies))
     cot_z = lax.all_to_all(cot_copies, "tensor", 0, 0, axis_index_groups=ALONG_Z_HI)
     info_s = info_v[0, :8]
     hidden = (
@@ -274,8 +287,8 @@
     )(info_s, core_s, own, other, hidden, output_gradient)
 
     sums = jnp.sum(lax.all_gather(part, "tensor", axis_index_groups=ALONG_Y), axis=0)
-    sums = lax.all_gather(sums, "tensor", axis_index_groups=ALONG_Z_HI)
-    cot_z, sums = lax.optimization_barrier((cot_z, sums))
+    others = [lax.ppermute(sums, "tensor", shift_z_hi(by)) for by in (1, 3, 2)]
+    cot_z, sums, others = lax.optimization_barrier((cot_z, sums, others))
     back = lax.ppermute(cot_z, "tensor", NEXT_Y)
     ahead = lax.ppermute(cot_z, "tensor", LAST_Y)
     half = Z_HI // 2
@@ -285,11 +298,11 @@
     grad_rows, term = pl.pallas_call(
         terms,
         out_shape=(shape((2 * rank, tok), bf16), shape((2 * rank, wide + LANES), f32)),
-        in_specs=[SMEM, VMEM, VMEM, VMEM],
+        in_specs=[SMEM] + [VMEM] * 6,
         out_specs=(VMEM, VMEM),
         compiler_params=params(),
         name="terms",
-    )(info_s, sums, hidden, output_gradient)
+    )(info_s, sums, *others, hidden, output_gradient)
 
     term_other = lax.ppermute(term, "dp", OTHER_CORE)
     outgoing = pl.pallas_call(

time: 182 us -> 183 us (level)
  the two profiles are of different devices: /device:TPU:6 before, /device:TPU:24 now
where the time goes in v10:
time: 183 us; the launch traced here: 180 us
  starting transfers between devices  64.9 us (35%)
  blocking collectives  39.5 us (22%)
  waiting for transfers between devices  34.9 us (19%)
  Pallas kernels  18.3 us (10%)
  between operations  14.2 us (8%)
  local copies, waits for them, and re-layouts  5.7 us (3%)
  other arithmetic  2.8 us (2%)
    ppermute x3, waiting for transfers between devices, shards(): others = [lax.ppermute(sums, 'tensor', shift_z_hi(by)) for by in (1, 3, 2)]  22.6 us
    ppermute x3, starting transfers between devices, shards(): others = [lax.ppermute(sums, 'tensor', shift_z_hi(by)) for by in (1, 3, 2)]  22.6 us
    all_gather x1, blocking collectives, shards(): plane = lax.all_gather(column, 'dp', axis_index_groups=ALONG_X)  14.4 us
    all_to_all x1, blocking collectives, shards(): column = lax.all_to_all(packed, 'dp', 0, 0, axis_index_groups=ALONG_Z_LO)  12.8 us
    all_to_all x1, starting transfers between devices, shards(): lax.all_to_all(cot_copies, 'tensor', 0, 0, axis_index_groups=ALONG_Z_HI)  12.5 us
    all_gather x1, blocking collectives, shards(): lax.all_gather(part, 'tensor', axis_index_groups=ALONG_Y)  12.3 us
    pallas_call x1, Pallas kernels, shards(): pl.pallas_call(finish, out_shape=(shape((tok, hid), bf16), shape((tok, hi...  11.1 us
    all_to_all x1, starting transfers between devices, shards(): incoming = lax.all_to_all(by_x, 'dp', 0, 0, axis_index_groups=ALONG_Z_LO)  9.9 us
  transfers between devices with their start and end apart: 13, of which 5 were waited for; matrix products, arithmetic and copies ran while one was open for 3% of the time, Pallas kernels for 4%

profile of v10, /device:TPU:24, one launch (start us, length us, event | category | flops | bytes accessed | tf_op | source)
XLA Modules:
  0.0 180.3 jit_solution(9631565764743362443)
XLA Ops:
  7.2 0.0 all-gather.4.cloned.1.call-start
  7.2 0.7 all-gather.4.cloned.1.call-update
  7.9 2.2 %prepare.1 = (bf16[4,16,1280]{2,1,0:T(8,128)(2,1)}, s32[8,128]{1,0:T(8,128)}, bf16[4,512,256]{2,1,0:T(8,128)(2,1)}) custom-call(s32[512]{0:T(512)} %tenants_s.1, s32[16]{0:T(128)} %owners_s.1, s32[4,128]{1,0:T(4,128)} %bitcast.13, f32[16,896]{1,0:T(8,128)} %bitcast.11, f32[16,256]{1,0:T(8,128)} %bitcast.12, bf16[512,256]{1,0:T(8,128)(2,1)} %cot.5), custom_call_target="tpu_custom_call" | custom-call | tf_op jit(solution)/shard_map/prepare/pallas_call | solution.py:246
  10.1 12.8 %all_to_all.20 = bf16[4,16,1280]{2,1,0:T(8,128)(2,1)S(1)} all-to-all(bf16[4,16,1280]{2,1,0:T(8,128)(2,1)} %get-tuple-element.27), channel_id=1, replica_groups={{0,32,64,96},{16,48,80,112},{128,160,192,224},{144,176,208,240},{256,28..., dimensions={0} | all-to-all | bytes 327680 | tf_op jit(solution)/shard_map/all_to_all | solution.py:265
  23.0 12.5 %all-to-all-start.1 = ((bf16[4,512,256]{2,1,0:T(8,128)(2,1)}), bf16[4,512,256]{2,1,0:T(8,128)(2,1)S(1)}, u32[]{:S(2)}, u32[]{:S(2)}) async-start(bf16[4,512,256]{2,1,0:T(8,128)(2,1)} %get-tuple-element.29), calls=%async_computation.1 | async-start | bytes 2097152 | tf_op jit(solution)/shard_map/all_to_all | solution.py:267
  35.5 0.0 copy-start
  35.5 14.4 %all-gather.own = bf16[16,16,1280]{2,1,0:T(8,128)(2,1)S(1)} all-gather(bf16[4,16,1280]{2,1,0:T(8,128)(2,1)S(1)} %all_to_all.20), channel_id=2, replica_groups={{0,128,256,384},{16,144,272,400},{32,160,288,416},{48,176,304,432},{64,..., dimensions={0}, use_global_device_ids=true | all-gather | bytes 819200 | tf_op jit(solution)/shard_map/all_gather | solution.py:272
  49.9 1.9 %collective-permute-start = (bf16[16,16,1280]{2,1,0:T(8,128)(2,1)S(1)}, bf16[16,16,1280]{2,1,0:T(8,128)(2,1)S(1)}, u32[]{:S(2)}, u32[]{:S(2)}) collective-permute-start(bf16[16,16,1280]{2,1,0:T(8,128)(2,1)S(1)} %all-gather.own), channel_id=1, source_target_pairs={{0,16},{16,0},{32,48},{48,32},{64,80},{80,64},{96,112},{112,96},{1... | collective-permute-start | bytes 1966088 | tf_op jit(solution)/shard_map/ppermute | solution.py:274
  51.8 0.7 slice_bitcast_fusion.info_s
  52.5 2.0 %fusion.4.hidden = bf16[512,896]{1,0:T(8,128)(2,1)S(1)} fusion(bf16[512,896]{1,0:T(8,128)(2,1)} %up.1, bf16[512,896]{1,0:T(8,128)(2,1)} %gate.1), kind=kLoop, calls=%fused_computation.6 | loop fusion | flops 3670016 | bytes 2752512 | tf_op jit(solution)/shard_map/convert_element_type | solution.py:271
  54.6 0.0 collective-permute-done.other
  54.6 0.0 copy-done
  54.6 1.0 low_rank.1
  55.6 0.0 copy-start.1
  55.6 0.0 copy-start.3
  55.6 12.3 %all-gather.1 = f32[128,512]{1,0:T(8,128)S(1)} all-gather(f32[32,512]{1,0:T(8,128)S(1)} %get-tuple-element.32), channel_id=3, replica_groups={{0,4,8,12},{1,5,9,13},{2,6,10,14},{3,7,11,15},{16,20,24,28},{17,21,25,2..., dimensions={0}, use_global_device_ids=true | all-gather | bytes 327680 | tf_op jit(solution)/shard_map/all_gather | solution.py:289
  67.9 0.0 copy-done.1
  67.9 0.0 copy-done.3
  67.9 8.0 %collective-permute-start.1 = (f32[32,512]{1,0:T(8,128)S(1)}, f32[32,512]{1,0:T(8,128)S(1)}, u32[]{:S(2)}, u32[]{:S(2)}) collective-permute-start(f32[32,512]{1,0:T(8,128)S(1)} %reduce_sum.21.sums), channel_id=1, source_target_pairs={{0,1},{1,2},{2,3},{3,0},{4,5},{5,6},{6,7},{7,4},{8,9},{9,10},{10,1... | collective-permute-start | bytes 196616 | tf_op jit(solution)/shard_map/ppermute | solution.py:290
  75.9 1.9 %collective-permute-start.2 = (f32[32,512]{1,0:T(8,128)S(1)}, f32[32,512]{1,0:T(8,128)S(1)}, u32[]{:S(2)}, u32[]{:S(2)}) collective-permute-start(f32[32,512]{1,0:T(8,128)S(1)} %reduce_sum.21.sums), channel_id=1, source_target_pairs={{0,3},{1,0},{2,1},{3,2},{4,7},{5,4},{6,5},{7,6},{8,11},{9,8},{10,9... | collective-permute-start | bytes 196616 | tf_op jit(solution)/shard_map/ppermute | solution.py:290
  77.8 12.6 %collective-permute-start.3 = (f32[32,512]{1,0:T(8,128)S(1)}, f32[32,512]{1,0:T(8,128)S(1)}, u32[]{:S(2)}, u32[]{:S(2)}) collective-permute-start(f32[32,512]{1,0:T(8,128)S(1)} %reduce_sum.21.sums), channel_id=1, source_target_pairs={{0,2},{1,3},{2,0},{3,1},{4,6},{5,7},{6,4},{7,5},{8,10},{9,11},{10,... | collective-permute-start | bytes 196616 | tf_op jit(solution)/shard_map/ppermute | solution.py:290
  90.5 0.0 collective-permute-done.1.one
  90.5 0.0 collective-permute-done.2.two
  90.5 22.6 %collective-permute-done.3.three = f32[32,512]{1,0:T(8,128)S(1)} collective-permute-done((f32[32,512]{1,0:T(8,128)S(1)}, f32[32,512]{1,0:T(8,128)S(1)}, u32[]{:S(2)}, u32[]{:S(2)}) %collective-permute-start.3) | collective-permute-done | bytes 65568 | tf_op jit(solution)/shard_map/ppermute | solution.py:290
  113.1 0.0 all-to-all-done.1.own
  113.1 0.0 copy-start.4
  113.1 2.7 %collective-permute-start.4 = (bf16[4,512,256]{2,1,0:T(8,128)(2,1)S(1)}, bf16[4,512,256]{2,1,0:T(8,128)(2,1)S(1)}, u32[]{:S(2)}, u32[]{:S(2)}) collective-permute-start(bf16[4,512,256]{2,1,0:T(8,128)(2,1)S(1)} %all-to-all-done.1.own), channel_id=1, source_target_pairs={{0,4},{1,5},{2,6},{3,7},{4,8},{5,9},{6,10},{7,11},{8,12},{9,13},{1... | collective-permute-start | bytes 3145736 | tf_op jit(solution)/shard_map/ppermute | solution.py:292
  115.8 3.2 %collective-permute-start.5 = (bf16[4,512,256]{2,1,0:T(8,128)(2,1)S(1)}, bf16[4,512,256]{2,1,0:T(8,128)(2,1)}, u32[]{:S(2)}, u32[]{:S(2)}) collective-permute-start(bf16[4,512,256]{2,1,0:T(8,128)(2,1)S(1)} %all-to-all-done.1.own), channel_id=1, source_target_pairs={{0,12},{1,13},{2,14},{3,15},{4,0},{5,1},{6,2},{7,3},{8,4},{9,5},{1... | collective-permute-start | bytes 3145736 | tf_op jit(solution)/shard_map/ppermute | solution.py:293
  119.0 0.8 terms.1
  119.8 0.0 copy-start.2
  119.8 0.6 copy-done.2
  120.4 1.9 %collective-permute-start.8 = (f32[32,1280]{1,0:T(8,128)S(1)}, f32[32,1280]{1,0:T(8,128)S(1)}, u32[]{:S(2)}, u32[]{:S(2)}) collective-permute-start(f32[32,1280]{1,0:T(8,128)S(1)} %get-tuple-element.43.term), channel_id=1, source_target_pairs={{0,16},{16,0},{32,48},{48,32},{64,80},{80,64},{96,112},{112,96},{1... | collective-permute-start | bytes 491528 | tf_op jit(solution)/shard_map/ppermute | solution.py:307
  122.3 1.4 collective-permute-done.8.term_other
  123.7 1.4 dense.1
  125.1 4.3 %all-to-all-start.2 = ((bf16[4,4,16,1152]{3,2,1,0:T(8,128)(2,1)}), bf16[4,4,16,1152]{3,2,1,0:T(8,128)(2,1)S(1)}, u32[]{:S(2)}, u32[]{:S(2)}) async-start(bf16[4,4,16,1152]{3,2,1,0:T(8,128)(2,1)} %bitcast.8), calls=%async_computation.2 | async-start | bytes 1179648 | tf_op jit(solution)/shard_map/all_to_all | solution.py:318
  129.4 0.4 collective-permute-done.4.back
  129.8 0.0 copy-start.5
  129.8 0.9 slice.12
  130.7 0.0 copy-done.4
  130.7 4.0 %collective-permute-start.6 = (bf16[2,512,256]{2,1,0:T(8,128)(2,1)}, bf16[2,512,256]{2,1,0:T(8,128)(2,1)S(1)}, u32[]{:S(2)}, u32[]{:S(2)}) collective-permute-start(bf16[2,512,256]{2,1,0:T(8,128)(2,1)} %slice.12), channel_id=1, source_target_pairs={{0,4},{1,5},{2,6},{3,7},{4,8},{5,9},{6,10},{7,11},{8,12},{9,13},{1... | collective-permute-start | bytes 1572872 | tf_op jit(solution)/shard_map/ppermute | solution.py:295
  134.7 0.0 collective-permute-done.5.ahead
  134.7 1.9 %slice.13 = bf16[2,512,256]{2,1,0:T(8,128)(2,1)} slice(bf16[4,512,256]{2,1,0:T(8,128)(2,1)} %collective-permute-done.5.ahead), slice={[2:4], [0:512], [0:256]} | slice | bytes 1048576 | tf_op jit(solution)/shard_map/slice | solution.py:296
  136.6 1.9 %collective-permute-start.7 = (bf16[2,512,256]{2,1,0:T(8,128)(2,1)}, bf16[2,512,256]{2,1,0:T(8,128)(2,1)S(1)}, u32[]{:S(2)}, u32[]{:S(2)}) collective-permute-start(bf16[2,512,256]{2,1,0:T(8,128)(2,1)} %slice.13), channel_id=1, source_target_pairs={{0,12},{1,13},{2,14},{3,15},{4,0},{5,1},{6,2},{7,3},{8,4},{9,5},{1... | collective-permute-start | bytes 1572872 | tf_op jit(solution)/shard_map/ppermute | solution.py:296
  138.5 3.8 %all-to-all-done.2 = bf16[4,4,16,1152]{3,2,1,0:T(8,128)(2,1)S(1)} async-done(((bf16[4,4,16,1152]{3,2,1,0:T(8,128)(2,1)}), bf16[4,4,16,1152]{3,2,1,0:T(8,128)(2,1)S(1)}, u32[]{:S(2)}, u32[]{:S(2)}) %all-to-all-start.2) | async-done | bytes 589856 | tf_op jit(solution)/shard_map/all_to_all | solution.py:318
  142.3 0.8 reduce_sum.22
  143.1 9.9 %all-to-all-start.3 = ((bf16[4,16,1152]{2,1,0:T(8,128)(2,1)}), bf16[4,16,1152]{2,1,0:T(8,128)(2,1)S(1)}, u32[]{:S(2)}, u32[]{:S(2)}) async-start(bf16[4,16,1152]{2,1,0:T(8,128)(2,1)} %reduce_sum.22), calls=%async_computation.3 | async-start | bytes 294912 | tf_op jit(solution)/shard_map/all_to_all | solution.py:320
  153.0 6.0 %all-to-all-done.3.incoming = bf16[4,16,1152]{2,1,0:T(8,128)(2,1)S(1)} async-done(((bf16[4,16,1152]{2,1,0:T(8,128)(2,1)}), bf16[4,16,1152]{2,1,0:T(8,128)(2,1)S(1)}, u32[]{:S(2)}, u32[]{:S(2)}) %all-to-all-start.3) | async-done | bytes 147488 | tf_op jit(solution)/shard_map/all_to_all | solution.py:320
  158.9 0.0 copy-start.6
  158.9 0.7 copy-done.6
  159.6 1.8 %adam.1 = (f32[2,1,16,896]{3,2,1,0:T(8,128)}, f32[2,1,16,256]{3,2,1,0:T(8,128)}, f32[1,16,896]{2,1,0:T(8,128)}, f32[1,16,256]{2,1,0:T(8,128)}) custom-call(s32[1]{0:T(128)} %bitcast.7.me_s, f32[16,128]{1,0:T(8,128)} %copy-done.3, bf16[4,16,1152]{2,1,0:T(8,128)(2,1)} %copy-done.6, f32[2,1,16,896]{3,2,1,0:T(8,128)} %moments_a.1, f32[2,1,16,256]{3,2,1,0:T(8,128)} %moments_b.1), custom_call_target="tpu_custom_call" | custom-call | tf_op jit(solution)/shard_map/adam/pallas_call | solution.py:322
  161.4 0.0 collective-permute-done.6.far_low
  161.4 0.0 copy-start.7
  161.4 0.0 collective-permute-done.7.far_high
  161.4 0.0 copy-start.8
  161.4 0.0 all-gather.4.cloned.1.call-done.down_own.down_back.down_ahead.down_far
  161.5 0.0 copy-done.5
  161.5 0.8 copy-done.7
  162.2 0.2 copy-done.8
  162.4 11.1 %finish.1 = (bf16[512,896]{1,0:T(8,128)(2,1)}, bf16[512,896]{1,0:T(8,128)(2,1)}) custom-call(s32[1]{0:T(128)} %bitcast.place_s, bf16[4,512,256]{2,1,0:T(8,128)(2,1)} %copy-done.4, bf16[4,512,256]{2,1,0:T(8,128)(2,1)} %copy-done.5, bf16[4,512,256]{2,1,0:T(8,128)(2,1)} %collective-permute-done.5.ahead, bf16[2,512,256]{2,1,0:T(8,128)(2,1)} %copy-done.7, ...), custom_call_target="tpu_custom_call" | custom-call | tf_op jit(solution)/shard_map/finish/pallas_call | solution.py:348
  (1 shorter events, 0.0 us)
Async XLA Ops:
  7.2 154.3 %all-gather.4.cloned.1.call-start = ((), (), s32[]{:S(2)}) async-start(), calls=%async_computation.4 | async-start | bytes 7569408 | tf_op jit(solution)/shard_map/all_gather | solution.py:244
  23.0 90.1 %all-to-all-start.1 = ((bf16[4,512,256]{2,1,0:T(8,128)(2,1)}), bf16[4,512,256]{2,1,0:T(8,128)(2,1)S(1)}, u32[]{:S(2)}, u32[]{:S(2)}) async-start(bf16[4,512,256]{2,1,0:T(8,128)(2,1)} %get-tuple-element.29), calls=%async_computation.1 | async-start | bytes 2097152 | tf_op jit(solution)/shard_map/all_to_all | solution.py:267
  35.5 19.0 %copy-start = (bf16[512,256]{1,0:T(8,128)(2,1)S(1)}, bf16[512,256]{1,0:T(8,128)(2,1)}, u32[]{:S(2)}) copy-start(bf16[512,256]{1,0:T(8,128)(2,1)} %cot.5) | copy-start | bytes 786436
  49.9 4.6 %collective-permute-start = (bf16[16,16,1280]{2,1,0:T(8,128)(2,1)S(1)}, bf16[16,16,1280]{2,1,0:T(8,128)(2,1)S(1)}, u32[]{:S(2)}, u32[]{:S(2)}) collective-permute-start(bf16[16,16,1280]{2,1,0:T(8,128)(2,1)S(1)} %all-gather.own), channel_id=1, source_target_pairs={{0,16},{16,0},{32,48},{48,32},{64,80},{80,64},{96,112},{112,96},{1... | collective-permute-start | bytes 1966088 | tf_op jit(solution)/shard_map/ppermute | solution.py:274
  55.6 12.3 %copy-start.1 = (bf16[32,1152]{1,0:T(8,128)(2,1)}, bf16[32,1152]{1,0:T(8,128)(2,1)S(1)}, u32[]{:S(2)}) copy-start(bf16[32,1152]{1,0:T(8,128)(2,1)S(1)} %get-tuple-element.39.pair_a) | copy-start | bytes 221188
  55.6 12.3 %copy-start.3 = (f32[16,128]{1,0:T(8,128)}, f32[16,128]{1,0:T(8,128)S(1)}, u32[]{:S(2)}) copy-start(f32[16,128]{1,0:T(8,128)S(1)} %get-tuple-element.42.totals) | copy-start | bytes 24580
  67.9 22.6 %collective-permute-start.1 = (f32[32,512]{1,0:T(8,128)S(1)}, f32[32,512]{1,0:T(8,128)S(1)}, u32[]{:S(2)}, u32[]{:S(2)}) collective-permute-start(f32[32,512]{1,0:T(8,128)S(1)} %reduce_sum.21.sums), channel_id=1, source_target_pairs={{0,1},{1,2},{2,3},{3,0},{4,5},{5,6},{6,7},{7,4},{8,9},{9,10},{10,1... | collective-permute-start | bytes 196616 | tf_op jit(solution)/shard_map/ppermute | solution.py:290
  75.9 14.6 %collective-permute-start.2 = (f32[32,512]{1,0:T(8,128)S(1)}, f32[32,512]{1,0:T(8,128)S(1)}, u32[]{:S(2)}, u32[]{:S(2)}) collective-permute-start(f32[32,512]{1,0:T(8,128)S(1)} %reduce_sum.21.sums), channel_id=1, source_target_pairs={{0,3},{1,0},{2,1},{3,2},{4,7},{5,4},{6,5},{7,6},{8,11},{9,8},{10,9... | collective-permute-start | bytes 196616 | tf_op jit(solution)/shard_map/ppermute | solution.py:290
  77.8 35.3 %collective-permute-start.3 = (f32[32,512]{1,0:T(8,128)S(1)}, f32[32,512]{1,0:T(8,128)S(1)}, u32[]{:S(2)}, u32[]{:S(2)}) collective-permute-start(f32[32,512]{1,0:T(8,128)S(1)} %reduce_sum.21.sums), channel_id=1, source_target_pairs={{0,2},{1,3},{2,0},{3,1},{4,6},{5,7},{6,4},{7,5},{8,10},{9,11},{10,... | collective-permute-start | bytes 196616 | tf_op jit(solution)/shard_map/ppermute | solution.py:290
  113.1 17.6 %copy-start.4 = (bf16[4,512,256]{2,1,0:T(8,128)(2,1)}, bf16[4,512,256]{2,1,0:T(8,128)(2,1)S(1)}, u32[]{:S(2)}) copy-start(bf16[4,512,256]{2,1,0:T(8,128)(2,1)S(1)} %all-to-all-done.1.own) | copy-start | bytes 3145732
  113.1 16.7 %collective-permute-start.4 = (bf16[4,512,256]{2,1,0:T(8,128)(2,1)S(1)}, bf16[4,512,256]{2,1,0:T(8,128)(2,1)S(1)}, u32[]{:S(2)}, u32[]{:S(2)}) collective-permute-start(bf16[4,512,256]{2,1,0:T(8,128)(2,1)S(1)} %all-to-all-done.1.own), channel_id=1, source_target_pairs={{0,4},{1,5},{2,6},{3,7},{4,8},{5,9},{6,10},{7,11},{8,12},{9,13},{1... | collective-permute-start | bytes 3145736 | tf_op jit(solution)/shard_map/ppermute | solution.py:292
  115.8 18.9 %collective-permute-start.5 = (bf16[4,512,256]{2,1,0:T(8,128)(2,1)S(1)}, bf16[4,512,256]{2,1,0:T(8,128)(2,1)}, u32[]{:S(2)}, u32[]{:S(2)}) collective-permute-start(bf16[4,512,256]{2,1,0:T(8,128)(2,1)S(1)} %all-to-all-done.1.own), channel_id=1, source_target_pairs={{0,12},{1,13},{2,14},{3,15},{4,0},{5,1},{6,2},{7,3},{8,4},{9,5},{1... | collective-permute-start | bytes 3145736 | tf_op jit(solution)/shard_map/ppermute | solution.py:293
  119.8 0.6 copy-start.2
  120.4 3.3 %collective-permute-start.8 = (f32[32,1280]{1,0:T(8,128)S(1)}, f32[32,1280]{1,0:T(8,128)S(1)}, u32[]{:S(2)}, u32[]{:S(2)}) collective-permute-start(f32[32,1280]{1,0:T(8,128)S(1)} %get-tuple-element.43.term), channel_id=1, source_target_pairs={{0,16},{16,0},{32,48},{48,32},{64,80},{80,64},{96,112},{112,96},{1... | collective-permute-start | bytes 491528 | tf_op jit(solution)/shard_map/ppermute | solution.py:307
  125.1 17.2 %all-to-all-start.2 = ((bf16[4,4,16,1152]{3,2,1,0:T(8,128)(2,1)}), bf16[4,4,16,1152]{3,2,1,0:T(8,128)(2,1)S(1)}, u32[]{:S(2)}, u32[]{:S(2)}) async-start(bf16[4,4,16,1152]{3,2,1,0:T(8,128)(2,1)} %bitcast.8), calls=%async_computation.2 | async-start | bytes 1179648 | tf_op jit(solution)/shard_map/all_to_all | solution.py:318
  129.8 31.7 %copy-start.5 = (bf16[4,512,256]{2,1,0:T(8,128)(2,1)}, bf16[4,512,256]{2,1,0:T(8,128)(2,1)S(1)}, u32[]{:S(2)}) copy-start(bf16[4,512,256]{2,1,0:T(8,128)(2,1)S(1)} %collective-permute-done.4.back) | copy-start | bytes 3145732
  130.7 30.7 %collective-permute-start.6 = (bf16[2,512,256]{2,1,0:T(8,128)(2,1)}, bf16[2,512,256]{2,1,0:T(8,128)(2,1)S(1)}, u32[]{:S(2)}, u32[]{:S(2)}) collective-permute-start(bf16[2,512,256]{2,1,0:T(8,128)(2,1)} %slice.12), channel_id=1, source_target_pairs={{0,4},{1,5},{2,6},{3,7},{4,8},{5,9},{6,10},{7,11},{8,12},{9,13},{1... | collective-permute-start | bytes 1572872 | tf_op jit(solution)/shard_map/ppermute | solution.py:295
  136.6 24.8 %collective-permute-start.7 = (bf16[2,512,256]{2,1,0:T(8,128)(2,1)}, bf16[2,512,256]{2,1,0:T(8,128)(2,1)S(1)}, u32[]{:S(2)}, u32[]{:S(2)}) collective-permute-start(bf16[2,512,256]{2,1,0:T(8,128)(2,1)} %slice.13), channel_id=1, source_target_pairs={{0,12},{1,13},{2,14},{3,15},{4,0},{5,1},{6,2},{7,3},{8,4},{9,5},{1... | collective-permute-start | bytes 1572872 | tf_op jit(solution)/shard_map/ppermute | solution.py:296
  143.1 15.9 %all-to-all-start.3 = ((bf16[4,16,1152]{2,1,0:T(8,128)(2,1)}), bf16[4,16,1152]{2,1,0:T(8,128)(2,1)S(1)}, u32[]{:S(2)}, u32[]{:S(2)}) async-start(bf16[4,16,1152]{2,1,0:T(8,128)(2,1)} %reduce_sum.22), calls=%async_computation.3 | async-start | bytes 294912 | tf_op jit(solution)/shard_map/all_to_all | solution.py:320
  158.9 0.7 copy-start.6
  161.4 0.8 copy-start.7
  161.4 1.0 copy-start.8
Sparse Core Ops, SparseCore 0:
  10.1 145.4 all-gather.3

commit v11 on v9

--- a/solution.py
+++ b/solution.py
@@ -52,11 +52,9 @@
     )
 
 
-def spread(copies, block):
-    return jnp.broadcast_to(block[None], (copies,) + block.shape)
-
-
-def prepare(tenants_s, owners_s, tenants_v, factor_a, factor_b, packed, info_v):
+def prepare(tenants_s, owners_s, tenants_v, factor_a, factor_b, cot, packed, info_v, cot_copies):
+    for copy in range(cot_copies.shape[0]):
+        cot_copies[copy] = cot[...]
     tok = tenants_s.shape[0]
     rank, hid = factor_a.shape
     feat = factor_b.shape[1]
@@ -228,11 +226,15 @@
 
     down_full = lax.all_gather(down_matrix, "dp", axis=1, tiled=True)
 
-    packed, info_v = pl.pallas_call(
+    packed, info_v, cot_copies = pl.pallas_call(
         prepare,
-        out_shape=(shape((Z_LO, rank, wide + LANES), bf16), shape((8, LANES), jnp.int32)),
-        in_specs=[SMEM, SMEM, WHOLE, WHOLE, WHOLE],
-        out_specs=(WHOLE, WHOLE),
+        out_shape=(
+            shape((Z_LO, rank, wide + LANES), bf16),
+            shape((8, LANES), jnp.int32),
+            shape((Z_HI, tok, feat), bf16),
+        ),
+        in_specs=[SMEM, SMEM, WHOLE, WHOLE, WHOLE, WHOLE],
+        out_specs=(WHOLE, WHOLE, WHOLE),
         compiler_params=params(56),
         name="prepare",
     )(
@@ -241,9 +243,10 @@
         batch_tenants.reshape(-1, LANES),
         adapter_input_factors[0],
         adapter_output_factors[0],
+        output_gradient,
     )
     column = lax.all_to_all(packed, "dp", 0, 0, axis_index_groups=ALONG_Z_LO)
-    column, cot_copies = lax.optimization_barrier((column, spread(Z_HI, output_gradient)))
+    column, cot_copies = lax.optimization_barrier((column, cot_copies))
     cot_z = lax.all_to_all(cot_copies, "tensor", 0, 0, axis_index_groups=ALONG_Z_HI)
     info_s = info_v[0, :8]
     hidden = (
@@ -339,7 +342,7 @@
         ),
         in_specs=[SMEM, WHOLE, WHOLE, WHOLE, WHOLE],
         out_specs=(WHOLE,) * 4,
-        compiler_params=params(56),
+        compiler_params=params(24),
         name="adam",
     )(me.reshape(1), totals, incoming, input_moments, output_moments)
 

time: 182 us -> 178 us (0.978)
  the two profiles are of different devices: /device:TPU:73 before, /device:TPU:24 now
where the time goes in v11:
time: 178 us; the launch traced here: 176 us
  blocking collectives  58.8 us (33%)
  starting transfers between devices  37.2 us (21%)
  waiting for transfers between devices  36.7 us (21%)
  Pallas kernels  21.3 us (12%)
  between operations  14.2 us (8%)
  local copies, waits for them, and re-layouts  5.48 us (3%)
  other arithmetic  2.04 us (1%)
    all_to_all x1, waiting for transfers between devices, shards(): lax.all_to_all(cot_copies, 'tensor', 0, 0, axis_index_groups=ALONG_Z_HI)  30.8 us
    all_gather x1, blocking collectives, shards(): sums = lax.all_gather(sums, 'tensor', axis_index_groups=ALONG_Z_HI)  19.3 us
    all_gather x1, blocking collectives, shards(): plane = lax.all_gather(column, 'dp', axis_index_groups=ALONG_X)  14.4 us
    all_to_all x1, blocking collectives, shards(): column = lax.all_to_all(packed, 'dp', 0, 0, axis_index_groups=ALONG_Z_LO)  12.8 us
    all_to_all x1, starting transfers between devices, shards(): lax.all_to_all(cot_copies, 'tensor', 0, 0, axis_index_groups=ALONG_Z_HI)  12.5 us
    all_gather x1, blocking collectives, shards(): lax.all_gather(part, 'tensor', axis_index_groups=ALONG_Y)  12.2 us
    all_to_all x1, starting transfers between devices, shards(): incoming = lax.all_to_all(outgoing, 'dp', 0, 0, axis_index_groups=SAME_CORE)  9.12 us
    pallas_call x1, Pallas kernels, shards(): pl.pallas_call(near, out_shape=shape((tok, hid), f32), grid_spec=pltpu.Pr...  8.37 us
  transfers between devices with their start and end apart: 9, of which 4 were waited for; matrix products, arithmetic and copies ran while one was open for 3% of the time, Pallas kernels for 8%

profile of v11, /device:TPU:24, one launch (start us, length us, event | category | flops | bytes accessed | tf_op | source)
XLA Modules:
  0.0 175.6 jit_solution(697476850204017210)
XLA Ops:
  7.2 0.0 all-gather.5.cloned.1.call-start
  7.2 0.7 all-gather.5.cloned.1.call-update
  7.9 2.2 %prepare.1 = (bf16[4,16,1280]{2,1,0:T(8,128)(2,1)}, s32[8,128]{1,0:T(8,128)}, bf16[4,512,256]{2,1,0:T(8,128)(2,1)}) custom-call(s32[512]{0:T(512)} %tenants_s.1, s32[16]{0:T(128)} %owners_s.1, s32[4,128]{1,0:T(4,128)} %bitcast.14, f32[16,896]{1,0:T(8,128)} %bitcast.12, f32[16,256]{1,0:T(8,128)} %bitcast.13, bf16[512,256]{1,0:T(8,128)(2,1)} %cot.5), custom_call_target="tpu_custom_call" | custom-call | tf_op jit(solution)/shard_map/prepare/pallas_call | solution.py:229
  10.1 12.8 %all_to_all.15 = bf16[4,16,1280]{2,1,0:T(8,128)(2,1)S(1)} all-to-all(bf16[4,16,1280]{2,1,0:T(8,128)(2,1)} %get-tuple-element.29), channel_id=1, replica_groups={{0,32,64,96},{16,48,80,112},{128,160,192,224},{144,176,208,240},{256,28..., dimensions={0} | all-to-all | bytes 327680 | tf_op jit(solution)/shard_map/all_to_all | solution.py:248
  23.0 12.5 %all-to-all-start.1 = ((bf16[4,512,256]{2,1,0:T(8,128)(2,1)}), bf16[4,512,256]{2,1,0:T(8,128)(2,1)S(1)}, u32[]{:S(2)}, u32[]{:S(2)}) async-start(bf16[4,512,256]{2,1,0:T(8,128)(2,1)} %get-tuple-element.31), calls=%async_computation.1 | async-start | bytes 2097152 | tf_op jit(solution)/shard_map/all_to_all | solution.py:250
  35.5 0.0 copy-start
  35.5 14.4 %all-gather.own = bf16[16,16,1280]{2,1,0:T(8,128)(2,1)S(1)} all-gather(bf16[4,16,1280]{2,1,0:T(8,128)(2,1)S(1)} %all_to_all.15), channel_id=2, replica_groups={{0,128,256,384},{16,144,272,400},{32,160,288,416},{48,176,304,432},{64,..., dimensions={0}, use_global_device_ids=true | all-gather | bytes 819200 | tf_op jit(solution)/shard_map/all_gather | solution.py:255
  49.9 1.9 %collective-permute-start = (bf16[16,16,1280]{2,1,0:T(8,128)(2,1)S(1)}, bf16[16,16,1280]{2,1,0:T(8,128)(2,1)S(1)}, u32[]{:S(2)}, u32[]{:S(2)}) collective-permute-start(bf16[16,16,1280]{2,1,0:T(8,128)(2,1)S(1)} %all-gather.own), channel_id=1, source_target_pairs={{0,16},{16,0},{32,48},{48,32},{64,80},{80,64},{96,112},{112,96},{1... | collective-permute-start | bytes 1966088 | tf_op jit(solution)/shard_map/ppermute | solution.py:257
  51.8 0.7 slice_bitcast_fusion.info_s
  52.5 2.0 %fusion.4.hidden = bf16[512,896]{1,0:T(8,128)(2,1)S(1)} fusion(bf16[512,896]{1,0:T(8,128)(2,1)} %up.1, bf16[512,896]{1,0:T(8,128)(2,1)} %gate.1), kind=kLoop, calls=%fused_computation.6 | loop fusion | flops 3670016 | bytes 2752512 | tf_op jit(solution)/shard_map/convert_element_type | solution.py:254
  54.5 0.0 collective-permute-done.other
  54.5 0.0 copy-done
  54.6 1.0 low_rank.1
  55.6 0.0 copy-start.2
  55.6 0.6 copy-done.2
  56.2 12.2 %all-gather.1 = f32[128,512]{1,0:T(8,128)S(1)} all-gather(f32[32,512]{1,0:T(8,128)S(1)} %get-tuple-element.34), channel_id=3, replica_groups={{0,4,8,12},{1,5,9,13},{2,6,10,14},{3,7,11,15},{16,20,24,28},{17,21,25,2..., dimensions={0}, use_global_device_ids=true | all-gather | bytes 327680 | tf_op jit(solution)/shard_map/all_gather | solution.py:272
  68.5 30.8 %all-to-all-done.1.own = bf16[4,512,256]{2,1,0:T(8,128)(2,1)S(1)} async-done(((bf16[4,512,256]{2,1,0:T(8,128)(2,1)}), bf16[4,512,256]{2,1,0:T(8,128)(2,1)S(1)}, u32[]{:S(2)}, u32[]{:S(2)}) %all-to-all-start.1) | async-done | bytes 1048608 | tf_op jit(solution)/shard_map/all_to_all | solution.py:250
  99.3 0.0 copy-start.5
  99.3 2.5 %collective-permute-start.1 = (bf16[4,512,256]{2,1,0:T(8,128)(2,1)S(1)}, bf16[4,512,256]{2,1,0:T(8,128)(2,1)S(1)}, u32[]{:S(2)}, u32[]{:S(2)}) collective-permute-start(bf16[4,512,256]{2,1,0:T(8,128)(2,1)S(1)} %all-to-all-done.1.own), channel_id=1, source_target_pairs={{0,4},{1,5},{2,6},{3,7},{4,8},{5,9},{6,10},{7,11},{8,12},{9,13},{1... | collective-permute-start | bytes 3145736 | tf_op jit(solution)/shard_map/ppermute | solution.py:274
  101.8 3.4 %collective-permute-start.2 = (bf16[4,512,256]{2,1,0:T(8,128)(2,1)S(1)}, bf16[4,512,256]{2,1,0:T(8,128)(2,1)}, u32[]{:S(2)}, u32[]{:S(2)}) collective-permute-start(bf16[4,512,256]{2,1,0:T(8,128)(2,1)S(1)} %all-to-all-done.1.own), channel_id=1, source_target_pairs={{0,12},{1,13},{2,14},{3,15},{4,0},{5,1},{6,2},{7,3},{8,4},{9,5},{1... | collective-permute-start | bytes 3145736 | tf_op jit(solution)/shard_map/ppermute | solution.py:275
  105.2 19.3 %all-gather.2 = f32[128,512]{1,0:T(8,128)S(1)} all-gather(f32[32,512]{1,0:T(8,128)S(1)} %reduce_sum.9), channel_id=4, replica_groups={{0,1,2,3},{4,5,6,7},{8,9,10,11},{12,13,14,15},{16,17,18,19},{20,21,22,2..., dimensions={0}, use_global_device_ids=true | all-gather | bytes 327680 | tf_op jit(solution)/shard_map/all_gather | solution.py:276
  124.5 0.0 collective-permute-done.1.back
  124.5 0.0 copy-start.6
  124.5 0.0 collective-permute-done.2.ahead
  124.5 0.8 terms.1
  125.3 0.0 copy-start.3
  125.3 0.6 copy-done.3
  126.0 1.9 %collective-permute-start.5 = (f32[32,1280]{1,0:T(8,128)S(1)}, f32[32,1280]{1,0:T(8,128)S(1)}, u32[]{:S(2)}, u32[]{:S(2)}) collective-permute-start(f32[32,1280]{1,0:T(8,128)S(1)} %get-tuple-element.42.term), channel_id=1, source_target_pairs={{0,16},{16,0},{32,48},{48,32},{64,80},{80,64},{96,112},{112,96},{1... | collective-permute-start | bytes 491528 | tf_op jit(solution)/shard_map/ppermute | solution.py:291
  127.9 1.4 collective-permute-done.5.term_other
  129.2 1.4 dense.1
  130.6 0.0 copy-done.5
  130.6 9.1 %all-to-all-start.2 = ((bf16[16,16,1152]{2,1,0:T(8,128)(2,1)}), bf16[16,16,1152]{2,1,0:T(8,128)(2,1)S(1)}, u32[]{:S(2)}, u32[]{:S(2)}) async-start(bf16[16,16,1152]{2,1,0:T(8,128)(2,1)} %dense.1), calls=%async_computation.2 | async-start | bytes 1179648 | tf_op jit(solution)/shard_map/all_to_all | solution.py:301
  139.7 0.8 slice.10
  140.6 2.2 %collective-permute-start.3 = (bf16[2,512,256]{2,1,0:T(8,128)(2,1)}, bf16[2,512,256]{2,1,0:T(8,128)(2,1)S(1)}, u32[]{:S(2)}, u32[]{:S(2)}) collective-permute-start(bf16[2,512,256]{2,1,0:T(8,128)(2,1)} %slice.10), channel_id=1, source_target_pairs={{0,4},{1,5},{2,6},{3,7},{4,8},{5,9},{6,10},{7,11},{8,12},{9,13},{1... | collective-permute-start | bytes 1572872 | tf_op jit(solution)/shard_map/ppermute | solution.py:279
  142.7 1.9 %slice.11 = bf16[2,512,256]{2,1,0:T(8,128)(2,1)} slice(bf16[4,512,256]{2,1,0:T(8,128)(2,1)} %collective-permute-done.2.ahead), slice={[2:4], [0:512], [0:256]} | slice | bytes 1048576 | tf_op jit(solution)/shard_map/slice | solution.py:280
  144.6 3.7 %collective-permute-start.4 = (bf16[2,512,256]{2,1,0:T(8,128)(2,1)}, bf16[2,512,256]{2,1,0:T(8,128)(2,1)S(1)}, u32[]{:S(2)}, u32[]{:S(2)}) collective-permute-start(bf16[2,512,256]{2,1,0:T(8,128)(2,1)} %slice.11), channel_id=1, source_target_pairs={{0,12},{1,13},{2,14},{3,15},{4,0},{5,1},{6,2},{7,3},{8,4},{9,5},{1... | collective-permute-start | bytes 1572872 | tf_op jit(solution)/shard_map/ppermute | solution.py:280
  148.3 0.0 all-gather.5.cloned.1.call-done.down_own.down_back.down_ahead.down_far
  148.3 0.0 copy-done.6
  148.4 0.0 copy-start.1
  148.4 0.0 copy-start.4
  148.4 8.4 %near.1.total = f32[512,896]{1,0:T(8,128)} custom-call(s32[1]{0:T(128)} %bitcast.place_s, bf16[4,512,256]{2,1,0:T(8,128)(2,1)} %copy-done.5, bf16[4,512,256]{2,1,0:T(8,128)(2,1)} %copy-done.6, bf16[4,512,256]{2,1,0:T(8,128)(2,1)} %collective-permute-done.2.ahead, bf16[896,4096]{1,0:T(8,128)(2,1)} %all-gather.5.cloned.1.call-done.down_own.down_back.down_ahead.down_far, ...), custom_call_target="tpu_custom_call" | custom-call | tf_op jit(solution)/shard_map/near/pallas_call | solution.py:313
  156.7 1.2 all-to-all-done.2.incoming
  158.0 0.0 copy-done.1
  158.0 0.0 copy-done.4
  158.0 0.8 adam.1
  158.8 0.0 collective-permute-done.3.far_low
  158.8 0.0 copy-start.7
  158.8 2.6 %collective-permute-done.4.far_high = bf16[2,512,256]{2,1,0:T(8,128)(2,1)S(1)} collective-permute-done((bf16[2,512,256]{2,1,0:T(8,128)(2,1)}, bf16[2,512,256]{2,1,0:T(8,128)(2,1)S(1)}, u32[]{:S(2)}, u32[]{:S(2)}) %collective-permute-start.4) | collective-permute-done | bytes 524320 | tf_op jit(solution)/shard_map/ppermute | solution.py:280
  161.4 0.0 copy-done.7
  161.4 0.0 copy-start.8
  161.4 0.8 copy-done.8
  162.2 6.6 %finish.1 = (bf16[512,896]{1,0:T(8,128)(2,1)}, bf16[512,896]{1,0:T(8,128)(2,1)}) custom-call(s32[1]{0:T(128)} %bitcast.place_s, bf16[2,512,256]{2,1,0:T(8,128)(2,1)} %copy-done.7, bf16[2,512,256]{2,1,0:T(8,128)(2,1)} %copy-done.8, bf16[896,4096]{1,0:T(8,128)(2,1)} %all-gather.5.cloned.1.call-done.down_own.down_back.down_ahead.down_far, ...), custom_call_target="tpu_custom_call" | custom-call | tf_op jit(solution)/shard_map/finish/pallas_call | solution.py:352
  (1 shorter events, 0.0 us)
Async XLA Ops:
  7.2 141.2 %all-gather.5.cloned.1.call-start = ((), (), s32[]{:S(2)}) async-start(), calls=%async_computation.3 | async-start | bytes 7569408 | tf_op jit(solution)/shard_map/all_gather | solution.py:227
  23.0 76.3 %all-to-all-start.1 = ((bf16[4,512,256]{2,1,0:T(8,128)(2,1)}), bf16[4,512,256]{2,1,0:T(8,128)(2,1)S(1)}, u32[]{:S(2)}, u32[]{:S(2)}) async-start(bf16[4,512,256]{2,1,0:T(8,128)(2,1)} %get-tuple-element.31), calls=%async_computation.1 | async-start | bytes 2097152 | tf_op jit(solution)/shard_map/all_to_all | solution.py:250
  35.5 19.1 %copy-start = (bf16[512,256]{1,0:T(8,128)(2,1)S(1)}, bf16[512,256]{1,0:T(8,128)(2,1)}, u32[]{:S(2)}) copy-start(bf16[512,256]{1,0:T(8,128)(2,1)} %cot.5) | copy-start | bytes 786436
  49.9 4.6 %collective-permute-start = (bf16[16,16,1280]{2,1,0:T(8,128)(2,1)S(1)}, bf16[16,16,1280]{2,1,0:T(8,128)(2,1)S(1)}, u32[]{:S(2)}, u32[]{:S(2)}) collective-permute-start(bf16[16,16,1280]{2,1,0:T(8,128)(2,1)S(1)} %all-gather.own), channel_id=1, source_target_pairs={{0,16},{16,0},{32,48},{48,32},{64,80},{80,64},{96,112},{112,96},{1... | collective-permute-start | bytes 1966088 | tf_op jit(solution)/shard_map/ppermute | solution.py:257
  55.6 0.6 copy-start.2
  99.3 31.3 %copy-start.5 = (bf16[4,512,256]{2,1,0:T(8,128)(2,1)}, bf16[4,512,256]{2,1,0:T(8,128)(2,1)S(1)}, u32[]{:S(2)}) copy-start(bf16[4,512,256]{2,1,0:T(8,128)(2,1)S(1)} %all-to-all-done.1.own) | copy-start | bytes 3145732
  99.3 25.2 %collective-permute-start.1 = (bf16[4,512,256]{2,1,0:T(8,128)(2,1)S(1)}, bf16[4,512,256]{2,1,0:T(8,128)(2,1)S(1)}, u32[]{:S(2)}, u32[]{:S(2)}) collective-permute-start(bf16[4,512,256]{2,1,0:T(8,128)(2,1)S(1)} %all-to-all-done.1.own), channel_id=1, source_target_pairs={{0,4},{1,5},{2,6},{3,7},{4,8},{5,9},{6,10},{7,11},{8,12},{9,13},{1... | collective-permute-start | bytes 3145736 | tf_op jit(solution)/shard_map/ppermute | solution.py:274
  101.8 22.7 %collective-permute-start.2 = (bf16[4,512,256]{2,1,0:T(8,128)(2,1)S(1)}, bf16[4,512,256]{2,1,0:T(8,128)(2,1)}, u32[]{:S(2)}, u32[]{:S(2)}) collective-permute-start(bf16[4,512,256]{2,1,0:T(8,128)(2,1)S(1)} %all-to-all-done.1.own), channel_id=1, source_target_pairs={{0,12},{1,13},{2,14},{3,15},{4,0},{5,1},{6,2},{7,3},{8,4},{9,5},{1... | collective-permute-start | bytes 3145736 | tf_op jit(solution)/shard_map/ppermute | solution.py:275
  124.5 23.9 %copy-start.6 = (bf16[4,512,256]{2,1,0:T(8,128)(2,1)}, bf16[4,512,256]{2,1,0:T(8,128)(2,1)S(1)}, u32[]{:S(2)}) copy-start(bf16[4,512,256]{2,1,0:T(8,128)(2,1)S(1)} %collective-permute-done.1.back) | copy-start | bytes 3145732
  125.3 0.6 copy-start.3
  126.0 3.3 %collective-permute-start.5 = (f32[32,1280]{1,0:T(8,128)S(1)}, f32[32,1280]{1,0:T(8,128)S(1)}, u32[]{:S(2)}, u32[]{:S(2)}) collective-permute-start(f32[32,1280]{1,0:T(8,128)S(1)} %get-tuple-element.42.term), channel_id=1, source_target_pairs={{0,16},{16,0},{32,48},{48,32},{64,80},{80,64},{96,112},{112,96},{1... | collective-permute-start | bytes 491528 | tf_op jit(solution)/shard_map/ppermute | solution.py:291
  130.6 27.3 %all-to-all-start.2 = ((bf16[16,16,1152]{2,1,0:T(8,128)(2,1)}), bf16[16,16,1152]{2,1,0:T(8,128)(2,1)S(1)}, u32[]{:S(2)}, u32[]{:S(2)}) async-start(bf16[16,16,1152]{2,1,0:T(8,128)(2,1)} %dense.1), calls=%async_computation.2 | async-start | bytes 1179648 | tf_op jit(solution)/shard_map/all_to_all | solution.py:301
  140.6 18.2 %collective-permute-start.3 = (bf16[2,512,256]{2,1,0:T(8,128)(2,1)}, bf16[2,512,256]{2,1,0:T(8,128)(2,1)S(1)}, u32[]{:S(2)}, u32[]{:S(2)}) collective-permute-start(bf16[2,512,256]{2,1,0:T(8,128)(2,1)} %slice.10), channel_id=1, source_target_pairs={{0,4},{1,5},{2,6},{3,7},{4,8},{5,9},{6,10},{7,11},{8,12},{9,13},{1... | collective-permute-start | bytes 1572872 | tf_op jit(solution)/shard_map/ppermute | solution.py:279
  144.6 16.7 %collective-permute-start.4 = (bf16[2,512,256]{2,1,0:T(8,128)(2,1)}, bf16[2,512,256]{2,1,0:T(8,128)(2,1)S(1)}, u32[]{:S(2)}, u32[]{:S(2)}) collective-permute-start(bf16[2,512,256]{2,1,0:T(8,128)(2,1)} %slice.11), channel_id=1, source_target_pairs={{0,12},{1,13},{2,14},{3,15},{4,0},{5,1},{6,2},{7,3},{8,4},{9,5},{1... | collective-permute-start | bytes 1572872 | tf_op jit(solution)/shard_map/ppermute | solution.py:280
  148.4 9.6 %copy-start.1 = (f32[2,1,16,896]{3,2,1,0:T(8,128)S(1)}, f32[2,1,16,896]{3,2,1,0:T(8,128)}, u32[]{:S(2)}) copy-start(f32[2,1,16,896]{3,2,1,0:T(8,128)} %moments_a.1) | copy-start | bytes 344068
  148.4 9.6 %copy-start.4 = (f32[2,1,16,256]{3,2,1,0:T(8,128)S(1)}, f32[2,1,16,256]{3,2,1,0:T(8,128)}, u32[]{:S(2)}) copy-start(f32[2,1,16,256]{3,2,1,0:T(8,128)} %moments_b.1) | copy-start | bytes 98308
  158.8 2.6 %copy-start.7 = (bf16[2,512,256]{2,1,0:T(8,128)(2,1)}, bf16[2,512,256]{2,1,0:T(8,128)(2,1)S(1)}, u32[]{:S(2)}) copy-start(bf16[2,512,256]{2,1,0:T(8,128)(2,1)S(1)} %collective-permute-done.3.far_low) | copy-start | bytes 1572868
  161.4 0.8 copy-start.8
Sparse Core Ops, SparseCore 0:
  10.1 132.9 all-gather.4

commit v12 on v11

--- a/solution.py
+++ b/solution.py
@@ -180,19 +180,14 @@
     def _():
         total[...] = tn_dot(grad_rows[...], pair_a[...])
 
-    total[...] += (
-        nt_dot(own[0], down_own[...])
-        + nt_dot(back[0], down_back[...])
-        + nt_dot(ahead[0], down_ahead[...])
-    )
+    blocks = jnp.concatenate([own[0], back[0], ahead[0]], axis=1)
+    weights = jnp.concatenate([down_own[...], down_back[...], down_ahead[...]], axis=1)
+    total[...] += nt_dot(blocks, weights)
 
 
 def finish(place_s, far_low, far_high, down_far, total, gate, up, out_gate, out_up):
-    feat = far_low.shape[2]
-    blocks = [far_low[0], far_low[1], far_high[0], far_high[1]]
-    grad = total[...]
-    for place, block in enumerate(blocks):
-        grad += nt_dot(block, down_far[:, place * feat : (place + 1) * feat])
+    blocks = jnp.concatenate([far_low[0], far_low[1], far_high[0], far_high[1]], axis=1)
+    grad = total[...] + nt_dot(blocks, down_far[...])
     gate_f = gate[...].astype(jnp.float32)
     up_f = up[...].astype(jnp.float32)
     sigmoid_gate = jax.nn.sigmoid(gate_f)
@@ -346,7 +341,7 @@
         name="adam",
     )(me.reshape(1), totals, incoming, input_moments, output_moments)
 
-    rows = tok // 4
+    rows = tok // 2
     far_rows = pl.BlockSpec((half, rows, feat), lambda step, y_ref: (0, step, 0))
     wide_rows = pl.BlockSpec((rows, hid), lambda step, y_ref: (step, 0))
     grad_gate, grad_up = pl.pallas_call(

time: 178 us -> 177 us (level)
  no operation moved by 1% of the time
where the time goes in v12:
time: 177 us; the launch traced here: 174 us
  blocking collectives  58.8 us (33%)
  starting transfers between devices  37.2 us (21%)
  waiting for transfers between devices  36.7 us (21%)
  Pallas kernels  19.8 us (11%)
  between operations  14.2 us (8%)
  local copies, waits for them, and re-layouts  5.48 us (3%)
  other arithmetic  2.04 us (1%)
    all_to_all x1, waiting for transfers between devices, shards(): lax.all_to_all(cot_copies, 'tensor', 0, 0, axis_index_groups=ALONG_Z_HI)  30.8 us
    all_gather x1, blocking collectives, shards(): sums = lax.all_gather(sums, 'tensor', axis_index_groups=ALONG_Z_HI)  19.3 us
    all_gather x1, blocking collectives, shards(): plane = lax.all_gather(column, 'dp', axis_index_groups=ALONG_X)  14.4 us
    all_to_all x1, blocking collectives, shards(): column = lax.all_to_all(packed, 'dp', 0, 0, axis_index_groups=ALONG_Z_LO)  12.8 us
    all_to_all x1, starting transfers between devices, shards(): lax.all_to_all(cot_copies, 'tensor', 0, 0, axis_index_groups=ALONG_Z_HI)  12.5 us
    all_gather x1, blocking collectives, shards(): lax.all_gather(part, 'tensor', axis_index_groups=ALONG_Y)  12.2 us
    all_to_all x1, starting transfers between devices, shards(): incoming = lax.all_to_all(outgoing, 'dp', 0, 0, axis_index_groups=SAME_CORE)  9.13 us
    pallas_call x1, Pallas kernels, shards(): pl.pallas_call(near, out_shape=shape((tok, hid), f32), grid_spec=pltpu.Pr...  8.37 us
  transfers between devices with their start and end apart: 9, of which 4 were waited for; matrix products, arithmetic and copies ran while one was open for 3% of the time, Pallas kernels for 8%

profile of v12, /device:TPU:24, one launch (start us, length us, event | category | flops | bytes accessed | tf_op | source)
XLA Modules:
  0.0 174.2 jit_solution(9700734075183207567)
XLA Ops:
  7.2 0.0 all-gather.5.cloned.1.call-start
  7.2 0.7 all-gather.5.cloned.1.call-update
  7.9 2.2 %prepare.1 = (bf16[4,16,1280]{2,1,0:T(8,128)(2,1)}, s32[8,128]{1,0:T(8,128)}, bf16[4,512,256]{2,1,0:T(8,128)(2,1)}) custom-call(s32[512]{0:T(512)} %tenants_s.1, s32[16]{0:T(128)} %owners_s.1, s32[4,128]{1,0:T(4,128)} %bitcast.14, f32[16,896]{1,0:T(8,128)} %bitcast.12, f32[16,256]{1,0:T(8,128)} %bitcast.13, bf16[512,256]{1,0:T(8,128)(2,1)} %cot.5), custom_call_target="tpu_custom_call" | custom-call | tf_op jit(solution)/shard_map/prepare/pallas_call | solution.py:224
  10.1 12.8 %all_to_all.15 = bf16[4,16,1280]{2,1,0:T(8,128)(2,1)S(1)} all-to-all(bf16[4,16,1280]{2,1,0:T(8,128)(2,1)} %get-tuple-element.29), channel_id=1, replica_groups={{0,32,64,96},{16,48,80,112},{128,160,192,224},{144,176,208,240},{256,28..., dimensions={0} | all-to-all | bytes 327680 | tf_op jit(solution)/shard_map/all_to_all | solution.py:243
  23.0 12.5 %all-to-all-start.1 = ((bf16[4,512,256]{2,1,0:T(8,128)(2,1)}), bf16[4,512,256]{2,1,0:T(8,128)(2,1)S(1)}, u32[]{:S(2)}, u32[]{:S(2)}) async-start(bf16[4,512,256]{2,1,0:T(8,128)(2,1)} %get-tuple-element.31), calls=%async_computation.1 | async-start | bytes 2097152 | tf_op jit(solution)/shard_map/all_to_all | solution.py:245
  35.5 0.0 copy-start
  35.5 14.4 %all-gather.own = bf16[16,16,1280]{2,1,0:T(8,128)(2,1)S(1)} all-gather(bf16[4,16,1280]{2,1,0:T(8,128)(2,1)S(1)} %all_to_all.15), channel_id=2, replica_groups={{0,128,256,384},{16,144,272,400},{32,160,288,416},{48,176,304,432},{64,..., dimensions={0}, use_global_device_ids=true | all-gather | bytes 819200 | tf_op jit(solution)/shard_map/all_gather | solution.py:250
  49.9 1.9 %collective-permute-start = (bf16[16,16,1280]{2,1,0:T(8,128)(2,1)S(1)}, bf16[16,16,1280]{2,1,0:T(8,128)(2,1)S(1)}, u32[]{:S(2)}, u32[]{:S(2)}) collective-permute-start(bf16[16,16,1280]{2,1,0:T(8,128)(2,1)S(1)} %all-gather.own), channel_id=1, source_target_pairs={{0,16},{16,0},{32,48},{48,32},{64,80},{80,64},{96,112},{112,96},{1... | collective-permute-start | bytes 1966088 | tf_op jit(solution)/shard_map/ppermute | solution.py:252
  51.8 0.7 slice_bitcast_fusion.info_s
  52.5 2.0 %fusion.4.hidden = bf16[512,896]{1,0:T(8,128)(2,1)S(1)} fusion(bf16[512,896]{1,0:T(8,128)(2,1)} %up.1, bf16[512,896]{1,0:T(8,128)(2,1)} %gate.1), kind=kLoop, calls=%fused_computation.6 | loop fusion | flops 3670016 | bytes 2752512 | tf_op jit(solution)/shard_map/convert_element_type | solution.py:249
  54.5 0.0 collective-permute-done.other
  54.5 0.0 copy-done
  54.6 1.0 low_rank.1
  55.6 0.0 copy-start.2
  55.6 0.6 copy-done.2
  56.2 12.2 %all-gather.1 = f32[128,512]{1,0:T(8,128)S(1)} all-gather(f32[32,512]{1,0:T(8,128)S(1)} %get-tuple-element.34), channel_id=3, replica_groups={{0,4,8,12},{1,5,9,13},{2,6,10,14},{3,7,11,15},{16,20,24,28},{17,21,25,2..., dimensions={0}, use_global_device_ids=true | all-gather | bytes 327680 | tf_op jit(solution)/shard_map/all_gather | solution.py:267
  68.5 30.8 %all-to-all-done.1.own = bf16[4,512,256]{2,1,0:T(8,128)(2,1)S(1)} async-done(((bf16[4,512,256]{2,1,0:T(8,128)(2,1)}), bf16[4,512,256]{2,1,0:T(8,128)(2,1)S(1)}, u32[]{:S(2)}, u32[]{:S(2)}) %all-to-all-start.1) | async-done | bytes 1048608 | tf_op jit(solution)/shard_map/all_to_all | solution.py:245
  99.3 0.0 copy-start.5
  99.3 2.5 %collective-permute-start.1 = (bf16[4,512,256]{2,1,0:T(8,128)(2,1)S(1)}, bf16[4,512,256]{2,1,0:T(8,128)(2,1)S(1)}, u32[]{:S(2)}, u32[]{:S(2)}) collective-permute-start(bf16[4,512,256]{2,1,0:T(8,128)(2,1)S(1)} %all-to-all-done.1.own), channel_id=1, source_target_pairs={{0,4},{1,5},{2,6},{3,7},{4,8},{5,9},{6,10},{7,11},{8,12},{9,13},{1... | collective-permute-start | bytes 3145736 | tf_op jit(solution)/shard_map/ppermute | solution.py:269
  101.8 3.4 %collective-permute-start.2 = (bf16[4,512,256]{2,1,0:T(8,128)(2,1)S(1)}, bf16[4,512,256]{2,1,0:T(8,128)(2,1)}, u32[]{:S(2)}, u32[]{:S(2)}) collective-permute-start(bf16[4,512,256]{2,1,0:T(8,128)(2,1)S(1)} %all-to-all-done.1.own), channel_id=1, source_target_pairs={{0,12},{1,13},{2,14},{3,15},{4,0},{5,1},{6,2},{7,3},{8,4},{9,5},{1... | collective-permute-start | bytes 3145736 | tf_op jit(solution)/shard_map/ppermute | solution.py:270
  105.2 19.3 %all-gather.2 = f32[128,512]{1,0:T(8,128)S(1)} all-gather(f32[32,512]{1,0:T(8,128)S(1)} %reduce_sum.9), channel_id=4, replica_groups={{0,1,2,3},{4,5,6,7},{8,9,10,11},{12,13,14,15},{16,17,18,19},{20,21,22,2..., dimensions={0}, use_global_device_ids=true | all-gather | bytes 327680 | tf_op jit(solution)/shard_map/all_gather | solution.py:271
  124.5 0.0 collective-permute-done.1.back
  124.5 0.0 copy-start.6
  124.5 0.0 collective-permute-done.2.ahead
  124.5 0.8 terms.1
  125.3 0.0 copy-start.3
  125.3 0.6 copy-done.3
  126.0 1.9 %collective-permute-start.5 = (f32[32,1280]{1,0:T(8,128)S(1)}, f32[32,1280]{1,0:T(8,128)S(1)}, u32[]{:S(2)}, u32[]{:S(2)}) collective-permute-start(f32[32,1280]{1,0:T(8,128)S(1)} %get-tuple-element.42.term), channel_id=1, source_target_pairs={{0,16},{16,0},{32,48},{48,32},{64,80},{80,64},{96,112},{112,96},{1... | collective-permute-start | bytes 491528 | tf_op jit(solution)/shard_map/ppermute | solution.py:286
  127.9 1.4 collective-permute-done.5.term_other
  129.2 1.4 dense.1
  130.6 0.0 copy-done.5
  130.6 9.1 %all-to-all-start.2 = ((bf16[16,16,1152]{2,1,0:T(8,128)(2,1)}), bf16[16,16,1152]{2,1,0:T(8,128)(2,1)S(1)}, u32[]{:S(2)}, u32[]{:S(2)}) async-start(bf16[16,16,1152]{2,1,0:T(8,128)(2,1)} %dense.1), calls=%async_computation.2 | async-start | bytes 1179648 | tf_op jit(solution)/shard_map/all_to_all | solution.py:296
  139.7 0.8 slice.10
  140.6 2.2 %collective-permute-start.3 = (bf16[2,512,256]{2,1,0:T(8,128)(2,1)}, bf16[2,512,256]{2,1,0:T(8,128)(2,1)S(1)}, u32[]{:S(2)}, u32[]{:S(2)}) collective-permute-start(bf16[2,512,256]{2,1,0:T(8,128)(2,1)} %slice.10), channel_id=1, source_target_pairs={{0,4},{1,5},{2,6},{3,7},{4,8},{5,9},{6,10},{7,11},{8,12},{9,13},{1... | collective-permute-start | bytes 1572872 | tf_op jit(solution)/shard_map/ppermute | solution.py:274
  142.7 1.9 %slice.11 = bf16[2,512,256]{2,1,0:T(8,128)(2,1)} slice(bf16[4,512,256]{2,1,0:T(8,128)(2,1)} %collective-permute-done.2.ahead), slice={[2:4], [0:512], [0:256]} | slice | bytes 1048576 | tf_op jit(solution)/shard_map/slice | solution.py:275
  144.6 3.7 %collective-permute-start.4 = (bf16[2,512,256]{2,1,0:T(8,128)(2,1)}, bf16[2,512,256]{2,1,0:T(8,128)(2,1)S(1)}, u32[]{:S(2)}, u32[]{:S(2)}) collective-permute-start(bf16[2,512,256]{2,1,0:T(8,128)(2,1)} %slice.11), channel_id=1, source_target_pairs={{0,12},{1,13},{2,14},{3,15},{4,0},{5,1},{6,2},{7,3},{8,4},{9,5},{1... | collective-permute-start | bytes 1572872 | tf_op jit(solution)/shard_map/ppermute | solution.py:275
  148.3 0.0 all-gather.5.cloned.1.call-done.down_own.down_back.down_ahead.down_far
  148.3 0.0 copy-done.6
  148.4 0.0 copy-start.1
  148.4 0.0 copy-start.4
  148.4 8.4 %near.1.total = f32[512,896]{1,0:T(8,128)} custom-call(s32[1]{0:T(128)} %bitcast.place_s, bf16[4,512,256]{2,1,0:T(8,128)(2,1)} %copy-done.5, bf16[4,512,256]{2,1,0:T(8,128)(2,1)} %copy-done.6, bf16[4,512,256]{2,1,0:T(8,128)(2,1)} %collective-permute-done.2.ahead, bf16[896,4096]{1,0:T(8,128)(2,1)} %all-gather.5.cloned.1.call-done.down_own.down_back.down_ahead.down_far, ...), custom_call_target="tpu_custom_call" | custom-call | tf_op jit(solution)/shard_map/near/pallas_call | solution.py:308
  156.7 1.2 all-to-all-done.2.incoming
  158.0 0.0 copy-done.1
  158.0 0.0 copy-done.4
  158.0 0.8 adam.1
  158.8 0.0 collective-permute-done.3.far_low
  158.8 0.0 copy-start.7
  158.8 2.6 %collective-permute-done.4.far_high = bf16[2,512,256]{2,1,0:T(8,128)(2,1)S(1)} collective-permute-done((bf16[2,512,256]{2,1,0:T(8,128)(2,1)}, bf16[2,512,256]{2,1,0:T(8,128)(2,1)S(1)}, u32[]{:S(2)}, u32[]{:S(2)}) %collective-permute-start.4) | collective-permute-done | bytes 524320 | tf_op jit(solution)/shard_map/ppermute | solution.py:275
  161.4 0.0 copy-done.7
  161.4 0.0 copy-start.8
  161.4 0.8 copy-done.8
  162.2 5.2 %finish.1 = (bf16[512,896]{1,0:T(8,128)(2,1)}, bf16[512,896]{1,0:T(8,128)(2,1)}) custom-call(s32[1]{0:T(128)} %bitcast.place_s, bf16[2,512,256]{2,1,0:T(8,128)(2,1)} %copy-done.7, bf16[2,512,256]{2,1,0:T(8,128)(2,1)} %copy-done.8, bf16[896,4096]{1,0:T(8,128)(2,1)} %all-gather.5.cloned.1.call-done.down_own.down_back.down_ahead.down_far, ...), custom_call_target="tpu_custom_call" | custom-call | tf_op jit(solution)/shard_map/finish/pallas_call | solution.py:347
  (1 shorter events, 0.0 us)
Async XLA Ops:
  7.2 141.2 %all-gather.5.cloned.1.call-start = ((), (), s32[]{:S(2)}) async-start(), calls=%async_computation.3 | async-start | bytes 7569408 | tf_op jit(solution)/shard_map/all_gather | solution.py:222
  23.0 76.3 %all-to-all-start.1 = ((bf16[4,512,256]{2,1,0:T(8,128)(2,1)}), bf16[4,512,256]{2,1,0:T(8,128)(2,1)S(1)}, u32[]{:S(2)}, u32[]{:S(2)}) async-start(bf16[4,512,256]{2,1,0:T(8,128)(2,1)} %get-tuple-element.31), calls=%async_computation.1 | async-start | bytes 2097152 | tf_op jit(solution)/shard_map/all_to_all | solution.py:245
  35.5 19.1 %copy-start = (bf16[512,256]{1,0:T(8,128)(2,1)S(1)}, bf16[512,256]{1,0:T(8,128)(2,1)}, u32[]{:S(2)}) copy-start(bf16[512,256]{1,0:T(8,128)(2,1)} %cot.5) | copy-start | bytes 786436
  49.9 4.6 %collective-permute-start = (bf16[16,16,1280]{2,1,0:T(8,128)(2,1)S(1)}, bf16[16,16,1280]{2,1,0:T(8,128)(2,1)S(1)}, u32[]{:S(2)}, u32[]{:S(2)}) collective-permute-start(bf16[16,16,1280]{2,1,0:T(8,128)(2,1)S(1)} %all-gather.own), channel_id=1, source_target_pairs={{0,16},{16,0},{32,48},{48,32},{64,80},{80,64},{96,112},{112,96},{1... | collective-permute-start | bytes 1966088 | tf_op jit(solution)/shard_map/ppermute | solution.py:252
  55.6 0.6 copy-start.2
  99.3 31.3 %copy-start.5 = (bf16[4,512,256]{2,1,0:T(8,128)(2,1)}, bf16[4,512,256]{2,1,0:T(8,128)(2,1)S(1)}, u32[]{:S(2)}) copy-start(bf16[4,512,256]{2,1,0:T(8,128)(2,1)S(1)} %all-to-all-done.1.own) | copy-start | bytes 3145732
  99.3 25.2 %collective-permute-start.1 = (bf16[4,512,256]{2,1,0:T(8,128)(2,1)S(1)}, bf16[4,512,256]{2,1,0:T(8,128)(2,1)S(1)}, u32[]{:S(2)}, u32[]{:S(2)}) collective-permute-start(bf16[4,512,256]{2,1,0:T(8,128)(2,1)S(1)} %all-to-all-done.1.own), channel_id=1, source_target_pairs={{0,4},{1,5},{2,6},{3,7},{4,8},{5,9},{6,10},{7,11},{8,12},{9,13},{1... | collective-permute-start | bytes 3145736 | tf_op jit(solution)/shard_map/ppermute | solution.py:269
  101.8 22.7 %collective-permute-start.2 = (bf16[4,512,256]{2,1,0:T(8,128)(2,1)S(1)}, bf16[4,512,256]{2,1,0:T(8,128)(2,1)}, u32[]{:S(2)}, u32[]{:S(2)}) collective-permute-start(bf16[4,512,256]{2,1,0:T(8,128)(2,1)S(1)} %all-to-all-done.1.own), channel_id=1, source_target_pairs={{0,12},{1,13},{2,14},{3,15},{4,0},{5,1},{6,2},{7,3},{8,4},{9,5},{1... | collective-permute-start | bytes 3145736 | tf_op jit(solution)/shard_map/ppermute | solution.py:270
  124.5 23.9 %copy-start.6 = (bf16[4,512,256]{2,1,0:T(8,128)(2,1)}, bf16[4,512,256]{2,1,0:T(8,128)(2,1)S(1)}, u32[]{:S(2)}) copy-start(bf16[4,512,256]{2,1,0:T(8,128)(2,1)S(1)} %collective-permute-done.1.back) | copy-start | bytes 3145732
  125.3 0.6 copy-start.3
  126.0 3.3 %collective-permute-start.5 = (f32[32,1280]{1,0:T(8,128)S(1)}, f32[32,1280]{1,0:T(8,128)S(1)}, u32[]{:S(2)}, u32[]{:S(2)}) collective-permute-start(f32[32,1280]{1,0:T(8,128)S(1)} %get-tuple-element.42.term), channel_id=1, source_target_pairs={{0,16},{16,0},{32,48},{48,32},{64,80},{80,64},{96,112},{112,96},{1... | collective-permute-start | bytes 491528 | tf_op jit(solution)/shard_map/ppermute | solution.py:286
  130.6 27.3 %all-to-all-start.2 = ((bf16[16,16,1152]{2,1,0:T(8,128)(2,1)}), bf16[16,16,1152]{2,1,0:T(8,128)(2,1)S(1)}, u32[]{:S(2)}, u32[]{:S(2)}) async-start(bf16[16,16,1152]{2,1,0:T(8,128)(2,1)} %dense.1), calls=%async_computation.2 | async-start | bytes 1179648 | tf_op jit(solution)/shard_map/all_to_all | solution.py:296
  140.6 18.2 %collective-permute-start.3 = (bf16[2,512,256]{2,1,0:T(8,128)(2,1)}, bf16[2,512,256]{2,1,0:T(8,128)(2,1)S(1)}, u32[]{:S(2)}, u32[]{:S(2)}) collective-permute-start(bf16[2,512,256]{2,1,0:T(8,128)(2,1)} %slice.10), channel_id=1, source_target_pairs={{0,4},{1,5},{2,6},{3,7},{4,8},{5,9},{6,10},{7,11},{8,12},{9,13},{1... | collective-permute-start | bytes 1572872 | tf_op jit(solution)/shard_map/ppermute | solution.py:274
  144.6 16.7 %collective-permute-start.4 = (bf16[2,512,256]{2,1,0:T(8,128)(2,1)}, bf16[2,512,256]{2,1,0:T(8,128)(2,1)S(1)}, u32[]{:S(2)}, u32[]{:S(2)}) collective-permute-start(bf16[2,512,256]{2,1,0:T(8,128)(2,1)} %slice.11), channel_id=1, source_target_pairs={{0,12},{1,13},{2,14},{3,15},{4,0},{5,1},{6,2},{7,3},{8,4},{9,5},{1... | collective-permute-start | bytes 1572872 | tf_op jit(solution)/shard_map/ppermute | solution.py:275
  148.4 9.6 %copy-start.1 = (f32[2,1,16,896]{3,2,1,0:T(8,128)S(1)}, f32[2,1,16,896]{3,2,1,0:T(8,128)}, u32[]{:S(2)}) copy-start(f32[2,1,16,896]{3,2,1,0:T(8,128)} %moments_a.1) | copy-start | bytes 344068
  148.4 9.6 %copy-start.4 = (f32[2,1,16,256]{3,2,1,0:T(8,128)S(1)}, f32[2,1,16,256]{3,2,1,0:T(8,128)}, u32[]{:S(2)}) copy-start(f32[2,1,16,256]{3,2,1,0:T(8,128)} %moments_b.1) | copy-start | bytes 98308
  158.8 2.6 %copy-start.7 = (bf16[2,512,256]{2,1,0:T(8,128)(2,1)}, bf16[2,512,256]{2,1,0:T(8,128)(2,1)S(1)}, u32[]{:S(2)}) copy-start(bf16[2,512,256]{2,1,0:T(8,128)(2,1)S(1)} %collective-permute-done.3.far_low) | copy-start | bytes 1572868
  161.4 0.8 copy-start.8
Sparse Core Ops, SparseCore 0:
  10.1 132.9 all-gather.4

commit v13 on v12

--- a/solution.py
+++ b/solution.py
@@ -185,8 +185,22 @@
     total[...] += nt_dot(blocks, weights)
 
 
-def finish(place_s, far_low, far_high, down_far, total, gate, up, out_gate, out_up):
-    blocks = jnp.concatenate([far_low[0], far_low[1], far_high[0], far_high[1]], axis=1)
+def finish(place_s, far_low, far_high, down_far, total, gate, up, out_gate, out_up, joined):
+    rows, cut = total.shape[0], far_low.shape[1]
+    places = range(far_low.shape[0])
+
+    @pl.when(pl.program_id(0) == 0)
+    def _():
+        for place in places:
+            joined[place] = far_low[place, :rows]
+
+    @pl.when(pl.program_id(0) == 1)
+    def _():
+        for place in places:
+            joined[place, : cut - rows] = far_low[place, rows:]
+            joined[place, cut - rows :] = far_high[place]
+
+    blocks = jnp.concatenate([joined[place] for place in places], axis=1)
     grad = total[...] + nt_dot(blocks, down_far[...])
     gate_f = gate[...].astype(jnp.float32)
     up_f = up[...].astype(jnp.float32)
@@ -270,9 +284,9 @@
     ahead = lax.ppermute(cot_z, "tensor", LAST_Y)
     sums = lax.all_gather(sums, "tensor", axis_index_groups=ALONG_Z_HI)
     back, ahead, sums = lax.optimization_barrier((back, ahead, sums))
-    half = Z_HI // 2
-    far_low = lax.ppermute(back[:half], "tensor", NEXT_Y)
-    far_high = lax.ppermute(ahead[half:], "tensor", LAST_Y)
+    cut = tok * 5 // 8
+    far_low = lax.ppermute(back[:, :cut], "tensor", NEXT_Y)
+    far_high = lax.ppermute(ahead[:, cut:], "tensor", LAST_Y)
 
     grad_rows, term = pl.pallas_call(
         terms,
@@ -342,7 +356,6 @@
     )(me.reshape(1), totals, incoming, input_moments, output_moments)
 
     rows = tok // 2
-    far_rows = pl.BlockSpec((half, rows, feat), lambda step, y_ref: (0, step, 0))
     wide_rows = pl.BlockSpec((rows, hid), lambda step, y_ref: (step, 0))
     grad_gate, grad_up = pl.pallas_call(
         finish,
@@ -351,8 +364,8 @@
             num_scalar_prefetch=1,
             grid=(tok // rows,),
             in_specs=[
-                far_rows,
-                far_rows,
+                fixed(Z_HI, cut, feat),
+                fixed(Z_HI, tok - cut, feat),
                 pl.BlockSpec(
                     (hid, Z_HI * feat), lambda step, y_ref: (0, lax.rem(y_ref[0] + 2, Y))
                 ),
@@ -361,6 +374,7 @@
                 wide_rows,
             ],
             out_specs=[wide_rows, wide_rows],
+            scratch_shapes=[pltpu.VMEM((Z_HI, rows, feat), bf16)],
         ),
         compiler_params=params(56),
         name="finish",

time: 177 us -> 177 us (level)
  the two profiles are of different devices: /device:TPU:24 before, /device:TPU:89 now
where the time goes in v13:
time: 177 us; the launch traced here: 176 us
  waiting for transfers between devices  49.1 us (28%)
  blocking collectives  49 us (28%)
  starting transfers between devices  35.6 us (20%)
  Pallas kernels  20.2 us (11%)
  between operations  14.2 us (8%)
  local copies, waits for them, and re-layouts  6.26 us (4%)
  other arithmetic  2.04 us (1%)
    all_to_all x1, waiting for transfers between devices, shards(): lax.all_to_all(cot_copies, 'tensor', 0, 0, axis_index_groups=ALONG_Z_HI)  33.9 us
    all_gather x1, blocking collectives, shards(): sums = lax.all_gather(sums, 'tensor', axis_index_groups=ALONG_Z_HI)  16.3 us
    all_gather x1, blocking collectives, shards(): plane = lax.all_gather(column, 'dp', axis_index_groups=ALONG_X)  12.9 us
    all_to_all x1, starting transfers between devices, shards(): lax.all_to_all(cot_copies, 'tensor', 0, 0, axis_index_groups=ALONG_Z_HI)  12.6 us
    all_gather x1, blocking collectives, shards(): lax.all_gather(part, 'tensor', axis_index_groups=ALONG_Y)  10.2 us
    all_to_all x1, blocking collectives, shards(): column = lax.all_to_all(packed, 'dp', 0, 0, axis_index_groups=ALONG_Z_LO)  9.49 us
    pallas_call x1, Pallas kernels, shards(): pl.pallas_call(near, out_shape=shape((tok, hid), f32), grid_spec=pltpu.Pr...  8.35 us
    all_gather x1, waiting for transfers between devices, shards(): down_full = lax.all_gather(down_matrix, 'dp', axis=1, tiled=True)  6.05 us
  transfers between devices with their start and end apart: 9, of which 5 were waited for; matrix products, arithmetic and copies ran while one was open for 3% of the time, Pallas kernels for 8%

profile of v13, /device:TPU:89, one launch (start us, length us, event | category | flops | bytes accessed | tf_op | source)
XLA Modules:
  0.0 176.3 jit_solution(12865464539917275043)
XLA Ops:
  7.2 0.0 all-gather.5.cloned.1.call-start
  7.2 0.7 all-gather.5.cloned.1.call-update
  7.9 2.2 %prepare.1 = (bf16[4,16,1280]{2,1,0:T(8,128)(2,1)}, s32[8,128]{1,0:T(8,128)}, bf16[4,512,256]{2,1,0:T(8,128)(2,1)}) custom-call(s32[512]{0:T(512)} %tenants_s.1, s32[16]{0:T(128)} %owners_s.1, s32[4,128]{1,0:T(4,128)} %bitcast.14, f32[16,896]{1,0:T(8,128)} %bitcast.12, f32[16,256]{1,0:T(8,128)} %bitcast.13, bf16[512,256]{1,0:T(8,128)(2,1)} %cot.5), custom_call_target="tpu_custom_call" | custom-call | tf_op jit(solution)/shard_map/prepare/pallas_call | solution.py:238
  10.1 9.5 %all_to_all.15 = bf16[4,16,1280]{2,1,0:T(8,128)(2,1)S(1)} all-to-all(bf16[4,16,1280]{2,1,0:T(8,128)(2,1)} %get-tuple-element.29), channel_id=1, replica_groups={{0,32,64,96},{16,48,80,112},{128,160,192,224},{144,176,208,240},{256,28..., dimensions={0} | all-to-all | bytes 327680 | tf_op jit(solution)/shard_map/all_to_all | solution.py:257
  19.6 12.6 %all-to-all-start.1 = ((bf16[4,512,256]{2,1,0:T(8,128)(2,1)}), bf16[4,512,256]{2,1,0:T(8,128)(2,1)S(1)}, u32[]{:S(2)}, u32[]{:S(2)}) async-start(bf16[4,512,256]{2,1,0:T(8,128)(2,1)} %get-tuple-element.31), calls=%async_computation.1 | async-start | bytes 2097152 | tf_op jit(solution)/shard_map/all_to_all | solution.py:259
  32.2 0.0 copy-start
  32.2 12.9 %all-gather.own = bf16[16,16,1280]{2,1,0:T(8,128)(2,1)S(1)} all-gather(bf16[4,16,1280]{2,1,0:T(8,128)(2,1)S(1)} %all_to_all.15), channel_id=2, replica_groups={{0,128,256,384},{16,144,272,400},{32,160,288,416},{48,176,304,432},{64,..., dimensions={0}, use_global_device_ids=true | all-gather | bytes 819200 | tf_op jit(solution)/shard_map/all_gather | solution.py:264
  45.1 5.0 %collective-permute-start = (bf16[16,16,1280]{2,1,0:T(8,128)(2,1)S(1)}, bf16[16,16,1280]{2,1,0:T(8,128)(2,1)S(1)}, u32[]{:S(2)}, u32[]{:S(2)}) collective-permute-start(bf16[16,16,1280]{2,1,0:T(8,128)(2,1)S(1)} %all-gather.own), channel_id=1, source_target_pairs={{0,16},{16,0},{32,48},{48,32},{64,80},{80,64},{96,112},{112,96},{1... | collective-permute-start | bytes 1966088 | tf_op jit(solution)/shard_map/ppermute | solution.py:266
  50.2 0.7 slice_bitcast_fusion.info_s
  50.9 2.0 %fusion.4.hidden = bf16[512,896]{1,0:T(8,128)(2,1)S(1)} fusion(bf16[512,896]{1,0:T(8,128)(2,1)} %up.1, bf16[512,896]{1,0:T(8,128)(2,1)} %gate.1), kind=kLoop, calls=%fused_computation.6 | loop fusion | flops 3670016 | bytes 2752512 | tf_op jit(solution)/shard_map/convert_element_type | solution.py:263
  52.9 0.0 collective-permute-done.other
  52.9 0.0 copy-done
  52.9 1.0 low_rank.1
  53.9 0.0 copy-start.2
  53.9 0.7 copy-done.2
  54.6 10.2 %all-gather.1 = f32[128,512]{1,0:T(8,128)S(1)} all-gather(f32[32,512]{1,0:T(8,128)S(1)} %get-tuple-element.34), channel_id=3, replica_groups={{0,4,8,12},{1,5,9,13},{2,6,10,14},{3,7,11,15},{16,20,24,28},{17,21,25,2..., dimensions={0}, use_global_device_ids=true | all-gather | bytes 327680 | tf_op jit(solution)/shard_map/all_gather | solution.py:281
  64.9 33.9 %all-to-all-done.1.own = bf16[4,512,256]{2,1,0:T(8,128)(2,1)S(1)} async-done(((bf16[4,512,256]{2,1,0:T(8,128)(2,1)}), bf16[4,512,256]{2,1,0:T(8,128)(2,1)S(1)}, u32[]{:S(2)}, u32[]{:S(2)}) %all-to-all-start.1) | async-done | bytes 1048608 | tf_op jit(solution)/shard_map/all_to_all | solution.py:259
  98.7 0.0 copy-start.5
  98.7 1.9 %collective-permute-start.1 = (bf16[4,512,256]{2,1,0:T(8,128)(2,1)S(1)}, bf16[4,512,256]{2,1,0:T(8,128)(2,1)S(1)}, u32[]{:S(2)}, u32[]{:S(2)}) collective-permute-start(bf16[4,512,256]{2,1,0:T(8,128)(2,1)S(1)} %all-to-all-done.1.own), channel_id=1, source_target_pairs={{0,4},{1,5},{2,6},{3,7},{4,8},{5,9},{6,10},{7,11},{8,12},{9,13},{1... | collective-permute-start | bytes 3145736 | tf_op jit(solution)/shard_map/ppermute | solution.py:283
  100.6 3.4 %collective-permute-start.2 = (bf16[4,512,256]{2,1,0:T(8,128)(2,1)S(1)}, bf16[4,512,256]{2,1,0:T(8,128)(2,1)}, u32[]{:S(2)}, u32[]{:S(2)}) collective-permute-start(bf16[4,512,256]{2,1,0:T(8,128)(2,1)S(1)} %all-to-all-done.1.own), channel_id=1, source_target_pairs={{0,12},{1,13},{2,14},{3,15},{4,0},{5,1},{6,2},{7,3},{8,4},{9,5},{1... | collective-permute-start | bytes 3145736 | tf_op jit(solution)/shard_map/ppermute | solution.py:284
  104.0 16.3 %all-gather.2 = f32[128,512]{1,0:T(8,128)S(1)} all-gather(f32[32,512]{1,0:T(8,128)S(1)} %reduce_sum.9), channel_id=4, replica_groups={{0,1,2,3},{4,5,6,7},{8,9,10,11},{12,13,14,15},{16,17,18,19},{20,21,22,2..., dimensions={0}, use_global_device_ids=true | all-gather | bytes 327680 | tf_op jit(solution)/shard_map/all_gather | solution.py:285
  120.3 4.3 %collective-permute-done.1.back = bf16[4,512,256]{2,1,0:T(8,128)(2,1)S(1)} collective-permute-done((bf16[4,512,256]{2,1,0:T(8,128)(2,1)S(1)}, bf16[4,512,256]{2,1,0:T(8,128)(2,1)S(1)}, u32[]{:S(2)}, u32[]{:S(2)}) %collective-permute-start.1) | collective-permute-done | bytes 1048608 | tf_op jit(solution)/shard_map/ppermute | solution.py:283
  124.7 0.0 copy-start.6
  124.7 3.0 %collective-permute-done.2.ahead = bf16[4,512,256]{2,1,0:T(8,128)(2,1)} collective-permute-done((bf16[4,512,256]{2,1,0:T(8,128)(2,1)S(1)}, bf16[4,512,256]{2,1,0:T(8,128)(2,1)}, u32[]{:S(2)}, u32[]{:S(2)}) %collective-permute-start.2) | collective-permute-done | bytes 1048608 | tf_op jit(solution)/shard_map/ppermute | solution.py:284
  127.7 0.8 terms.1
  128.5 0.0 copy-start.3
  128.5 0.6 copy-done.3
  129.1 3.7 %collective-permute-start.5 = (f32[32,1280]{1,0:T(8,128)S(1)}, f32[32,1280]{1,0:T(8,128)S(1)}, u32[]{:S(2)}, u32[]{:S(2)}) collective-permute-start(f32[32,1280]{1,0:T(8,128)S(1)} %get-tuple-element.42.term), channel_id=1, source_target_pairs={{0,16},{16,0},{32,48},{48,32},{64,80},{80,64},{96,112},{112,96},{1... | collective-permute-start | bytes 491528 | tf_op jit(solution)/shard_map/ppermute | solution.py:300
  132.8 1.1 collective-permute-done.5.term_other
  133.9 1.4 dense.1
  135.3 0.0 copy-done.5
  135.3 3.7 %all-to-all-start.2 = ((bf16[16,16,1152]{2,1,0:T(8,128)(2,1)}), bf16[16,16,1152]{2,1,0:T(8,128)(2,1)S(1)}, u32[]{:S(2)}, u32[]{:S(2)}) async-start(bf16[16,16,1152]{2,1,0:T(8,128)(2,1)} %dense.1), calls=%async_computation.2 | async-start | bytes 1179648 | tf_op jit(solution)/shard_map/all_to_all | solution.py:310
  139.0 0.9 slice.10
  139.9 1.9 %collective-permute-start.3 = (bf16[4,320,256]{2,1,0:T(8,128)(2,1)}, bf16[4,320,256]{2,1,0:T(8,128)(2,1)S(1)}, u32[]{:S(2)}, u32[]{:S(2)}) collective-permute-start(bf16[4,320,256]{2,1,0:T(8,128)(2,1)} %slice.10), channel_id=1, source_target_pairs={{0,4},{1,5},{2,6},{3,7},{4,8},{5,9},{6,10},{7,11},{8,12},{9,13},{1... | collective-permute-start | bytes 1966088 | tf_op jit(solution)/shard_map/ppermute | solution.py:288
  141.8 1.8 %slice.11 = bf16[4,192,256]{2,1,0:T(8,128)(2,1)} slice(bf16[4,512,256]{2,1,0:T(8,128)(2,1)} %collective-permute-done.2.ahead), slice={[0:4], [320:512], [0:256]} | slice | bytes 786432 | tf_op jit(solution)/shard_map/slice | solution.py:289
  143.6 3.3 %collective-permute-start.4 = (bf16[4,192,256]{2,1,0:T(8,128)(2,1)}, bf16[4,192,256]{2,1,0:T(8,128)(2,1)S(1)}, u32[]{:S(2)}, u32[]{:S(2)}) collective-permute-start(bf16[4,192,256]{2,1,0:T(8,128)(2,1)} %slice.11), channel_id=1, source_target_pairs={{0,12},{1,13},{2,14},{3,15},{4,0},{5,1},{6,2},{7,3},{8,4},{9,5},{1... | collective-permute-start | bytes 1179656 | tf_op jit(solution)/shard_map/ppermute | solution.py:289
  147.0 6.0 %all-gather.5.cloned.1.call-done.down_own.down_back.down_ahead.down_far = bf16[896,4096]{1,0:T(8,128)(2,1)} async-done(((bf16[896,128]{1,0:T(8,128)(2,1)}), bf16[896,4096]{1,0:T(8,128)(2,1)}) %all-gather.5.cloned.1.call-update) | async-done | bytes 7340048 | tf_op jit(solution)/shard_map/all_gather | solution.py:236
  153.0 0.0 copy-done.6
  153.0 0.0 copy-start.1
  153.1 0.0 copy-start.4
  153.1 8.4 %near.1.total = f32[512,896]{1,0:T(8,128)} custom-call(s32[1]{0:T(128)} %bitcast.place_s, bf16[4,512,256]{2,1,0:T(8,128)(2,1)} %copy-done.5, bf16[4,512,256]{2,1,0:T(8,128)(2,1)} %copy-done.6, bf16[4,512,256]{2,1,0:T(8,128)(2,1)} %collective-permute-done.2.ahead, bf16[896,4096]{1,0:T(8,128)(2,1)} %all-gather.5.cloned.1.call-done.down_own.down_back.down_ahead.down_far, ...), custom_call_target="tpu_custom_call" | custom-call | tf_op jit(solution)/shard_map/near/pallas_call | solution.py:322
  161.4 0.0 all-to-all-done.2.incoming
  161.4 0.0 copy-done.1
  161.4 0.0 copy-done.4
  161.4 0.8 adam.1
  162.3 0.0 collective-permute-done.4.far_high
  162.3 0.0 copy-start.8
  162.3 0.0 collective-permute-done.3.far_low
  162.3 0.7 copy-done.8
  163.0 0.0 copy-start.7
  163.0 0.8 copy-done.7
  163.9 5.5 %finish.1 = (bf16[512,896]{1,0:T(8,128)(2,1)}, bf16[512,896]{1,0:T(8,128)(2,1)}) custom-call(s32[1]{0:T(128)} %bitcast.place_s, bf16[4,320,256]{2,1,0:T(8,128)(2,1)} %copy-done.7, bf16[4,192,256]{2,1,0:T(8,128)(2,1)} %copy-done.8, bf16[896,4096]{1,0:T(8,128)(2,1)} %all-gather.5.cloned.1.call-done.down_own.down_back.down_ahead.down_far, ...), custom_call_target="tpu_custom_call" | custom-call | tf_op jit(solution)/shard_map/finish/pallas_call | solution.py:360
  (1 shorter events, 0.0 us)
Async XLA Ops:
  7.2 145.9 %all-gather.5.cloned.1.call-start = ((), (), s32[]{:S(2)}) async-start(), calls=%async_computation.3 | async-start | bytes 7569408 | tf_op jit(solution)/shard_map/all_gather | solution.py:236
  19.6 79.1 %all-to-all-start.1 = ((bf16[4,512,256]{2,1,0:T(8,128)(2,1)}), bf16[4,512,256]{2,1,0:T(8,128)(2,1)S(1)}, u32[]{:S(2)}, u32[]{:S(2)}) async-start(bf16[4,512,256]{2,1,0:T(8,128)(2,1)} %get-tuple-element.31), calls=%async_computation.1 | async-start | bytes 2097152 | tf_op jit(solution)/shard_map/all_to_all | solution.py:259
  32.2 20.7 %copy-start = (bf16[512,256]{1,0:T(8,128)(2,1)S(1)}, bf16[512,256]{1,0:T(8,128)(2,1)}, u32[]{:S(2)}) copy-start(bf16[512,256]{1,0:T(8,128)(2,1)} %cot.5) | copy-start | bytes 786436
  45.1 7.8 %collective-permute-start = (bf16[16,16,1280]{2,1,0:T(8,128)(2,1)S(1)}, bf16[16,16,1280]{2,1,0:T(8,128)(2,1)S(1)}, u32[]{:S(2)}, u32[]{:S(2)}) collective-permute-start(bf16[16,16,1280]{2,1,0:T(8,128)(2,1)S(1)} %all-gather.own), channel_id=1, source_target_pairs={{0,16},{16,0},{32,48},{48,32},{64,80},{80,64},{96,112},{112,96},{1... | collective-permute-start | bytes 1966088 | tf_op jit(solution)/shard_map/ppermute | solution.py:266
  53.9 0.7 copy-start.2
  98.7 36.6 %copy-start.5 = (bf16[4,512,256]{2,1,0:T(8,128)(2,1)}, bf16[4,512,256]{2,1,0:T(8,128)(2,1)S(1)}, u32[]{:S(2)}) copy-start(bf16[4,512,256]{2,1,0:T(8,128)(2,1)S(1)} %all-to-all-done.1.own) | copy-start | bytes 3145732
  98.7 25.9 %collective-permute-start.1 = (bf16[4,512,256]{2,1,0:T(8,128)(2,1)S(1)}, bf16[4,512,256]{2,1,0:T(8,128)(2,1)S(1)}, u32[]{:S(2)}, u32[]{:S(2)}) collective-permute-start(bf16[4,512,256]{2,1,0:T(8,128)(2,1)S(1)} %all-to-all-done.1.own), channel_id=1, source_target_pairs={{0,4},{1,5},{2,6},{3,7},{4,8},{5,9},{6,10},{7,11},{8,12},{9,13},{1... | collective-permute-start | bytes 3145736 | tf_op jit(solution)/shard_map/ppermute | solution.py:283
  100.6 27.0 %collective-permute-start.2 = (bf16[4,512,256]{2,1,0:T(8,128)(2,1)S(1)}, bf16[4,512,256]{2,1,0:T(8,128)(2,1)}, u32[]{:S(2)}, u32[]{:S(2)}) collective-permute-start(bf16[4,512,256]{2,1,0:T(8,128)(2,1)S(1)} %all-to-all-done.1.own), channel_id=1, source_target_pairs={{0,12},{1,13},{2,14},{3,15},{4,0},{5,1},{6,2},{7,3},{8,4},{9,5},{1... | collective-permute-start | bytes 3145736 | tf_op jit(solution)/shard_map/ppermute | solution.py:284
  124.7 28.4 %copy-start.6 = (bf16[4,512,256]{2,1,0:T(8,128)(2,1)}, bf16[4,512,256]{2,1,0:T(8,128)(2,1)S(1)}, u32[]{:S(2)}) copy-start(bf16[4,512,256]{2,1,0:T(8,128)(2,1)S(1)} %collective-permute-done.1.back) | copy-start | bytes 3145732
  128.5 0.6 copy-start.3
  129.1 4.8 %collective-permute-start.5 = (f32[32,1280]{1,0:T(8,128)S(1)}, f32[32,1280]{1,0:T(8,128)S(1)}, u32[]{:S(2)}, u32[]{:S(2)}) collective-permute-start(f32[32,1280]{1,0:T(8,128)S(1)} %get-tuple-element.42.term), channel_id=1, source_target_pairs={{0,16},{16,0},{32,48},{48,32},{64,80},{80,64},{96,112},{112,96},{1... | collective-permute-start | bytes 491528 | tf_op jit(solution)/shard_map/ppermute | solution.py:300
  135.3 26.1 %all-to-all-start.2 = ((bf16[16,16,1152]{2,1,0:T(8,128)(2,1)}), bf16[16,16,1152]{2,1,0:T(8,128)(2,1)S(1)}, u32[]{:S(2)}, u32[]{:S(2)}) async-start(bf16[16,16,1152]{2,1,0:T(8,128)(2,1)} %dense.1), calls=%async_computation.2 | async-start | bytes 1179648 | tf_op jit(solution)/shard_map/all_to_all | solution.py:310
  139.9 22.4 %collective-permute-start.3 = (bf16[4,320,256]{2,1,0:T(8,128)(2,1)}, bf16[4,320,256]{2,1,0:T(8,128)(2,1)S(1)}, u32[]{:S(2)}, u32[]{:S(2)}) collective-permute-start(bf16[4,320,256]{2,1,0:T(8,128)(2,1)} %slice.10), channel_id=1, source_target_pairs={{0,4},{1,5},{2,6},{3,7},{4,8},{5,9},{6,10},{7,11},{8,12},{9,13},{1... | collective-permute-start | bytes 1966088 | tf_op jit(solution)/shard_map/ppermute | solution.py:288
  143.6 18.6 %collective-permute-start.4 = (bf16[4,192,256]{2,1,0:T(8,128)(2,1)}, bf16[4,192,256]{2,1,0:T(8,128)(2,1)S(1)}, u32[]{:S(2)}, u32[]{:S(2)}) collective-permute-start(bf16[4,192,256]{2,1,0:T(8,128)(2,1)} %slice.11), channel_id=1, source_target_pairs={{0,12},{1,13},{2,14},{3,15},{4,0},{5,1},{6,2},{7,3},{8,4},{9,5},{1... | collective-permute-start | bytes 1179656 | tf_op jit(solution)/shard_map/ppermute | solution.py:289
  153.0 8.4 %copy-start.1 = (f32[2,1,16,896]{3,2,1,0:T(8,128)S(1)}, f32[2,1,16,896]{3,2,1,0:T(8,128)}, u32[]{:S(2)}) copy-start(f32[2,1,16,896]{3,2,1,0:T(8,128)} %moments_a.1) | copy-start | bytes 344068
  153.1 8.4 %copy-start.4 = (f32[2,1,16,256]{3,2,1,0:T(8,128)S(1)}, f32[2,1,16,256]{3,2,1,0:T(8,128)}, u32[]{:S(2)}) copy-start(f32[2,1,16,256]{3,2,1,0:T(8,128)} %moments_b.1) | copy-start | bytes 98308
  162.3 0.8 copy-start.8
  163.0 0.9 copy-start.7
Sparse Core Ops, SparseCore 0:
  10.1 142.9 all-gather.4
